TPU v7x, 32 devices: a whole 2x2x4 slice. The times are simulated.
32 devices in a mesh: dp: 8 (over z, y), expert: 4 (over x, core).
Axes of the slice: x: 2, y: 2, z: 4, core: 2. Of those that a mesh axis runs over, the one named last changes fastest.
Arguments:
- tokens: bfloat16 [8192, 1024], P(('dp', 'expert')), may hold values from -6 to 6
- out_grad: bfloat16 [8192, 1024], P(('dp', 'expert')), may hold values from -3 to 3
- gate_prob: bfloat16 [8192], P(('dp', 'expert')), may hold values from 0.19921875 to 1
- expert_id: int32 [8192], P(('dp', 'expert')), may hold values from 0 to 3, as said below
- up_weight: bfloat16 [4, 1024, 2048], P('expert'), may hold values from -0.1875 to 0.1875
- down_weight: bfloat16 [4, 2048, 1024], P('expert'), may hold values from -0.125 to 0.125
Outputs:
- tokens_grad: bfloat16 [8192, 1024], P(('dp', 'expert'))
- gate_grad: bfloat16 [8192], P(('dp', 'expert'))
- up_weight_grad: float32 [4, 1024, 2048], P('expert', 'dp')
- down_weight_grad: float32 [4, 2048, 1024], P('expert', 'dp')
Inputs may be any that keep to these rules, and one draw needn't show every extreme that they name: `expert_id`: among the 256 tokens of one device each expert is named at most 128 times; in every data group one expert is named exactly 128 times by every device of the group.
All inputs are finite; a program needn't handle non-finite values.
Results may differ from a plain program's by a relative error of at most 0.017.
Values may be sent and summed in bfloat16 or wider, within the bound.
No kernel may reach another device: no remote copies, remote signals or barrier semaphores. Data moves between devices by JAX's collectives and lax.ppermute only.
A program may use at most 64 MiB of HBM per device.

v0:
```python
import jax
import jax.numpy as jnp
from jax import lax
from jax.sharding import PartitionSpec as P

SQRT_HALF = 0.7071067811865476
INV_ROOT_TAU = 0.3989422804014327


def gelu_value(pre_act):
    return 0.5 * pre_act * (1.0 + jax.scipy.special.erf(pre_act * SQRT_HALF))


def gelu_slope(pre_act):
    normal_cdf = 0.5 * (1.0 + jax.scipy.special.erf(pre_act * SQRT_HALF))
    return normal_cdf + pre_act * jnp.exp(-0.5 * pre_act * pre_act) * INV_ROOT_TAU


def contract_rows(left, right):
    return lax.dot_general(
        left, right, (((0,), (0,)), ((), ())), preferred_element_type=jnp.float32
    )


def expert_rows(feat_rows, grad_rows, gate_rows, up_matrix, down_matrix):
    pre_act = jnp.dot(feat_rows, up_matrix, preferred_element_type=jnp.float32)
    hidden = gelu_value(pre_act).astype(jnp.bfloat16)
    expert_out = jnp.dot(hidden, down_matrix, preferred_element_type=jnp.float32)
    gate_grad = jnp.sum(grad_rows.astype(jnp.float32) * expert_out, axis=1).astype(jnp.bfloat16)
    scaled = (gate_rows.astype(jnp.float32)[:, None] * grad_rows.astype(jnp.float32)).astype(
        jnp.bfloat16
    )
    hidden_grad = lax.dot_general(
        scaled, down_matrix, (((1,), (1,)), ((), ())), preferred_element_type=jnp.float32
    )
    pre_grad = (hidden_grad * gelu_slope(pre_act)).astype(jnp.bfloat16)
    feat_grad = lax.dot_general(
        pre_grad, up_matrix, (((1,), (1,)), ((), ())), preferred_element_type=jnp.float32
    ).astype(jnp.bfloat16)
    return (feat_grad, gate_grad, hidden, scaled, pre_grad)


def per_device(tokens, out_grad, gate_prob, expert_id, up_weight, down_weight):
    up_matrix = up_weight[0]
    down_matrix = down_weight[0]
    feat_width = tokens.shape[1]
    local_count = tokens.shape[0]
    experts = lax.axis_size("expert") * up_weight.shape[0]
    capacity = 2 * local_count // experts
    one_hot = (expert_id[:, None] == jnp.arange(experts, dtype=jnp.int32)[None, :]).astype(
        jnp.int32
    )
    running = jnp.cumsum(one_hot, axis=0)
    position = jnp.sum((running - one_hot) * one_hot, axis=1)
    slot_index = expert_id * capacity + position
    token_of_slot = (
        jnp.full((experts * capacity,), local_count, jnp.int32)
        .at[slot_index]
        .set(jnp.arange(local_count, dtype=jnp.int32))
    )
    feat_slots = jnp.take(tokens, token_of_slot, axis=0, mode="fill", fill_value=0).reshape(
        experts, capacity, feat_width
    )
    grad_slots = jnp.take(out_grad, token_of_slot, axis=0, mode="fill", fill_value=0).reshape(
        experts, capacity, feat_width
    )
    gate_slots = jnp.take(gate_prob, token_of_slot, axis=0, mode="fill", fill_value=0).reshape(
        experts, capacity
    )
    feat_recv, grad_recv, gate_recv = (
        lax.all_to_all(feat_slots, "expert", split_axis=0, concat_axis=0, tiled=True),
        lax.all_to_all(grad_slots, "expert", split_axis=0, concat_axis=0, tiled=True),
        lax.all_to_all(gate_slots, "expert", split_axis=0, concat_axis=0, tiled=True),
    )
    sources = gate_recv.shape[0]
    feat_rows = feat_recv.reshape(-1, feat_width)
    feat_grad, gate_grad, hidden, scaled, pre_grad = expert_rows(
        feat_rows, grad_recv.reshape(-1, feat_width), gate_recv.reshape(-1), up_matrix, down_matrix
    )
    feat_back, gate_back = (
        lax.all_to_all(
            feat_grad.reshape(sources, capacity, feat_width),
            "expert",
            split_axis=0,
            concat_axis=0,
            tiled=True,
        ),
        lax.all_to_all(
            gate_grad.reshape(sources, capacity), "expert", split_axis=0, concat_axis=0, tiled=True
        ),
    )
    divisor = 1.0 / lax.axis_size("dp")
    up_sum, down_sum = (
        lax.psum_scatter(
            contract_rows(feat_rows, pre_grad).astype(jnp.bfloat16),
            "dp",
            scatter_dimension=0,
            tiled=True,
        ).astype(jnp.float32),
        lax.psum_scatter(
            contract_rows(hidden, scaled).astype(jnp.bfloat16),
            "dp",
            scatter_dimension=0,
            tiled=True,
        ).astype(jnp.float32),
    )
    tokens_grad = feat_back.reshape(experts * capacity, feat_width)[slot_index]
    gate_result = gate_back.reshape(experts * capacity)[slot_index]
    return (tokens_grad, gate_result, (up_sum * divisor)[None], (down_sum * divisor)[None])


def solution(mesh):
    return jax.shard_map(
        per_device,
        mesh=mesh,
        in_specs=(
            P(("dp", "expert"), None),
            P(("dp", "expert"), None),
            P(("dp", "expert")),
            P(("dp", "expert")),
            P("expert", None, None),
            P("expert", None, None),
        ),
        out_specs=(
            P(("dp", "expert"), None),
            P(("dp", "expert")),
            P("expert", "dp", None),
            P("expert", "dp", None),
        ),
        check_vma=False,
    )
```

profile of v0, /device:TPU:0, one launch (start us, length us, event | category | flops | bytes accessed | tf_op | source)
XLA Modules:
  0.0 264.1 jit_solution(13411268086748777658)
XLA Ops:
  7.2 0.7 compare_convert_fusion
  7.9 1.2 reduce-window.6
  9.5 0.7 fusion.26
  10.2 0.7 compare_select_fusion.1
  10.9 1.4 scatter_custom_fusion
  12.3 3.5 %gather_fusion = bf16[512]{0:T(512)(128)(2,1)S(1)} fusion(bf16[256]{0:T(256)(128)(2,1)} %param.10, s32[1024]{0:T(1024)S(1)} %pad_clamp_fusion.1), kind=kCustom, calls=%fused_computation.2 | custom fusion | bytes 4096 | tf_op jit(solution)/shard_map/jit(_take)/gather | solution.py:67
  15.8 0.6 copy.19
  16.4 4.2 %all-to-all-start = ((bf16[4,1,128]{2,1,0:T(2,128)(2,1)}), bf16[4,1,128]{2,1,0:T(2,128)(2,1)S(1)}, u32[]{:S(2)}, u32[]{:S(2)}) async-start(bf16[4,1,128]{2,1,0:T(2,128)(2,1)} %copy.19), calls=%async_computation | async-start | bytes 4096 | tf_op jit(solution)/shard_map/all_to_all | solution.py:73
  20.6 2.1 gather_fusion.3
  22.7 2.1 gather_fusion.4
  24.8 1.5 broadcast_select_fusion.1
  26.3 18.0 %all_to_all.27 = bf16[4,128,1024]{2,1,0:T(8,128)(2,1)S(1)} all-to-all(bf16[4,128,1024]{2,1,0:T(8,128)(2,1)} %bitcast.74), channel_id=1, replica_groups=mesh['dp'=8,'expert'=4] {'expert'}, dimensions={0} | all-to-all | bytes 2097152 | tf_op jit(solution)/shard_map/all_to_all | solution.py:71
  44.2 3.5 %all-to-all-start.1 = ((bf16[4,128,1024]{2,1,0:T(8,128)(2,1)}), bf16[4,128,1024]{2,1,0:T(8,128)(2,1)S(1)}, u32[]{:S(2)}, u32[]{:S(2)}) async-start(bf16[4,128,1024]{2,1,0:T(8,128)(2,1)} %bitcast.73), calls=%async_computation.1 | async-start | bytes 2097152 | tf_op jit(solution)/shard_map/all_to_all | solution.py:72
  47.8 6.7 %multiply_convert_fusion = (bf16[512,2048]{1,0:T(8,128)(2,1)}, f32[512,2048]{1,0:T(8,128)}) fusion(bf16[512,1024]{1,0:T(8,128)(2,1)S(1)} %bitcast.76, bf16[1,1024,2048]{2,1,0:T(8,128)(2,1)} %param.12), kind=kOutput, calls=%fused_computation.21 | convolution fusion | flops 2152726528 | bytes 11534336 | tf_op jit(solution)/shard_map/dot_general | solution.py:26
  54.5 7.7 %all-to-all-done.1 = bf16[4,128,1024]{2,1,0:T(8,128)(2,1)S(1)} async-done(((bf16[4,128,1024]{2,1,0:T(8,128)(2,1)}), bf16[4,128,1024]{2,1,0:T(8,128)(2,1)S(1)}, u32[]{:S(2)}, u32[]{:S(2)}) %all-to-all-start.1) | async-done | bytes 1048608 | tf_op jit(solution)/shard_map/all_to_all | solution.py:72
  62.4 6.3 %fusion.5 = bf16[512,2048]{1,0:T(8,128)(2,1)S(1)} fusion(f32[512,2048]{1,0:T(8,128)} %get-tuple-element.10, bf16[512,1024]{1,0:T(8,128)(2,1)S(1)} %bitcast.75, bf16[1,2048,1024]{2,1,0:T(8,128)(2,1)} %param.13), kind=kOutput, calls=%fused_computation.12 | convolution fusion | flops 2157969408 | bytes 11534336 | tf_op jit(solution)/shard_map/dot_general | solution.py:33
  68.8 1.3 copy-done.2
  70.1 4.3 %convolution_convert_fusion.1 = bf16[1024,2048]{1,0:T(8,128)(2,1)} fusion(bf16[512,1024]{1,0:T(8,128)(2,1)S(1)} %bitcast.77, bf16[512,2048]{1,0:T(8,128)(2,1)S(1)} %fusion.5), kind=kOutput, calls=%fused_computation.24 | convolution fusion | flops 2149580800 | bytes 7340032 | tf_op jit(solution)/shard_map/dot_general | solution.py:20
  74.6 0.2 fusion.18
  74.9 5.9 %convolution_convert_fusion = bf16[2048,1024]{1,0:T(8,128)(2,1)} fusion(bf16[512,2048]{1,0:T(8,128)(2,1)} %get-tuple-element.9, bf16[512,1024]{1,0:T(8,128)(2,1)S(1)} %fusion.18), kind=kOutput, calls=%fused_computation.23 | convolution fusion | flops 2149580800 | bytes 7340032 | tf_op jit(solution)/shard_map/dot_general | solution.py:20
  80.8 5.6 %fusion.17 = bf16[512]{0:T(512)(128)(2,1)S(1)} fusion(bf16[4,128,1024]{2,1,0:T(8,128)(2,1)S(1)} %all-to-all-done.1, bf16[512,2048]{1,0:T(8,128)(2,1)} %get-tuple-element.9, bf16[1,2048,1024]{2,1,0:T(8,128)(2,1)} %param.13), kind=kOutput, calls=%fused_computation.29 | convolution fusion | flops 2149056000 | bytes 7341056 | tf_op jit(solution)/shard_map/dot_general | solution.py:28
  86.4 0.6 copy.20
  87.0 3.2 %all-to-all-start.4 = ((bf16[4,1,128]{2,1,0:T(2,128)(2,1)}), bf16[4,1,128]{2,1,0:T(2,128)(2,1)S(1)}, u32[]{:S(2)}, u32[]{:S(2)}) async-start(bf16[4,1,128]{2,1,0:T(2,128)(2,1)} %copy.20), calls=%async_computation.4 | async-start | bytes 4096 | tf_op jit(solution)/shard_map/all_to_all | solution.py:88
  90.3 6.2 %fusion.21 = bf16[512,1024]{1,0:T(8,128)(2,1)} fusion(bf16[512,2048]{1,0:T(8,128)(2,1)} %copy-done.2, bf16[1,1024,2048]{2,1,0:T(8,128)(2,1)} %param.12), kind=kOutput, calls=%fused_computation.31 | convolution fusion | flops 2148007936 | bytes 7340032 | tf_op jit(solution)/shard_map/dot_general | solution.py:37
  96.5 3.5 %all-to-all-start.3 = ((bf16[4,128,1024]{2,1,0:T(8,128)(2,1)}), bf16[4,128,1024]{2,1,0:T(8,128)(2,1)S(1)}, u32[]{:S(2)}, u32[]{:S(2)}) async-start(bf16[4,128,1024]{2,1,0:T(8,128)(2,1)} %bitcast.11), calls=%async_computation.3 | async-start | bytes 2097152 | tf_op jit(solution)/shard_map/all_to_all | solution.py:81
  100.0 2.4 gather_fusion.2
  102.5 11.9 %all-to-all-done.3 = bf16[4,128,1024]{2,1,0:T(8,128)(2,1)S(1)} async-done(((bf16[4,128,1024]{2,1,0:T(8,128)(2,1)}), bf16[4,128,1024]{2,1,0:T(8,128)(2,1)S(1)}, u32[]{:S(2)}, u32[]{:S(2)}) %all-to-all-start.3) | async-done | bytes 1048608 | tf_op jit(solution)/shard_map/all_to_all | solution.py:81
  114.4 2.0 gather_fusion.1
  116.4 46.9 %reduce-scatter.3.cloned.1.call-done = bf16[128,2048]{1,0:T(8,128)(2,1)} async-done(((bf16[1024,2048]{1,0:T(8,128)(2,1)}), bf16[128,2048]{1,0:T(8,128)(2,1)}) %reduce-scatter.3.cloned.1.call-update) | async-done | bytes 524304 | tf_op jit(solution)/shard_map/reduce_scatter | solution.py:94
  163.3 2.1 multiply_bitcast_fusion.1
  165.4 89.8 %reduce-scatter.5.cloned.1.call-done = bf16[256,1024]{1,0:T(8,128)(2,1)} async-done(((bf16[2048,1024]{1,0:T(8,128)(2,1)}), bf16[256,1024]{1,0:T(8,128)(2,1)}) %reduce-scatter.5.cloned.1.call-update) | async-done | bytes 524304 | tf_op jit(solution)/shard_map/reduce_scatter | solution.py:100
  255.2 2.1 multiply_bitcast_fusion
  (25 shorter events, 1.0 us)
Async XLA Ops:
  7.2 13.4 %copy-start = (bf16[256,1024]{1,0:T(8,128)(2,1)S(1)}, bf16[256,1024]{1,0:T(8,128)(2,1)}, u32[]{:S(2)}) copy-start(bf16[256,1024]{1,0:T(8,128)(2,1)} %param.9) | copy-start | bytes 1572868
  16.4 9.9 %all-to-all-start = ((bf16[4,1,128]{2,1,0:T(2,128)(2,1)}), bf16[4,1,128]{2,1,0:T(2,128)(2,1)S(1)}, u32[]{:S(2)}, u32[]{:S(2)}) async-start(bf16[4,1,128]{2,1,0:T(2,128)(2,1)} %copy.19), calls=%async_computation | async-start | bytes 4096 | tf_op jit(solution)/shard_map/all_to_all | solution.py:73
  20.6 2.1 copy-start.1
  44.2 18.0 %all-to-all-start.1 = ((bf16[4,128,1024]{2,1,0:T(8,128)(2,1)}), bf16[4,128,1024]{2,1,0:T(8,128)(2,1)S(1)}, u32[]{:S(2)}, u32[]{:S(2)}) async-start(bf16[4,128,1024]{2,1,0:T(8,128)(2,1)} %bitcast.73), calls=%async_computation.1 | async-start | bytes 2097152 | tf_op jit(solution)/shard_map/all_to_all | solution.py:72
  47.8 115.5 %reduce-scatter.3.cloned.1.call-start = ((), (), s32[]{:S(2)}) async-start(), calls=%async_computation.7 | async-start | bytes 4718592 | tf_op jit(solution)/shard_map/reduce_scatter | solution.py:94
  68.8 1.3 copy-start.2
  74.4 180.8 %reduce-scatter.5.cloned.1.call-start = ((), (), s32[]{:S(2)}) async-start(), calls=%async_computation.8 | async-start | bytes 4718592 | tf_op jit(solution)/shard_map/reduce_scatter | solution.py:100
  87.0 9.4 %all-to-all-start.4 = ((bf16[4,1,128]{2,1,0:T(2,128)(2,1)}), bf16[4,1,128]{2,1,0:T(2,128)(2,1)S(1)}, u32[]{:S(2)}, u32[]{:S(2)}) async-start(bf16[4,1,128]{2,1,0:T(2,128)(2,1)} %copy.20), calls=%async_computation.4 | async-start | bytes 4096 | tf_op jit(solution)/shard_map/all_to_all | solution.py:88
  96.5 18.0 %all-to-all-start.3 = ((bf16[4,128,1024]{2,1,0:T(8,128)(2,1)}), bf16[4,128,1024]{2,1,0:T(8,128)(2,1)S(1)}, u32[]{:S(2)}, u32[]{:S(2)}) async-start(bf16[4,128,1024]{2,1,0:T(8,128)(2,1)} %bitcast.11), calls=%async_computation.3 | async-start | bytes 2097152 | tf_op jit(solution)/shard_map/all_to_all | solution.py:81
Sparse Core Ops, SparseCore 0:
  74.5 88.6 reduce-scatter.2
  167.3 87.7 reduce-scatter.4
where the time goes:
time: 265 us; the launch traced here: 264 us
  waiting for transfers between devices  156 us (59%)
  matrix products  35 us (13%)
  blocking collectives  18 us (7%)
  local copies, waits for them, and re-layouts  16.1 us (6%)
  starting transfers between devices  14.7 us (6%)
  between operations  14.2 us (5%)
  other arithmetic  9.74 us (4%)
    reduce_scatter x1, waiting for transfers between devices, per_device(): lax.psum_scatter(contract_rows(hidden, scaled).astype(jnp.bfloat16), 'dp'...  89.8 us
    reduce_scatter x1, waiting for transfers between devices, per_device(): lax.psum_scatter(contract_rows(feat_rows, pre_grad).astype(jnp.bfloat16),...  46.9 us
    all_to_all x1, blocking collectives, per_device(): lax.all_to_all(feat_slots, 'expert', split_axis=0, concat_axis=0, tiled=T...  18 us
    all_to_all x1, waiting for transfers between devices, per_device(): lax.all_to_all(feat_grad.reshape(sources, capacity, feat_width), 'expert'...  11.9 us
    dot_general x2, matrix products, contract_rows(): lax.dot_general(left, right, (((0,), (0,)), ((), ())), preferred_element_...  10.3 us
    all_to_all x1, waiting for transfers between devices, per_device(): lax.all_to_all(grad_slots, 'expert', split_axis=0, concat_axis=0, tiled=T...  7.72 us
    dot_general x1, matrix products, expert_rows(): pre_act = jnp.dot(feat_rows, up_matrix, preferred_element_type=jnp.float32)  6.65 us
    dot_general x1, matrix products, expert_rows(): lax.dot_general(scaled, down_matrix, (((1,), (1,)), ((), ())), preferred_...  6.31 us
  transfers between devices with their start and end apart: 6, of which 4 were waited for; matrix products, arithmetic and copies ran while one was open for 14% of the time, Pallas kernels for 0%

commit v1 on v0

v1 whole, which is shorter than its diff:
```python
import functools

import jax
import jax.numpy as jnp
from jax import lax
from jax.experimental import pallas as pl
from jax.experimental.pallas import tpu as pltpu
from jax.sharding import PartitionSpec as P

SQRT_HALF = 0.7071067811865476
INV_ROOT_TAU = 0.3989422804014327
LANES = 128
VMEM_LIMIT = 40 * 1024 * 1024
F32 = jnp.float32
BF16 = jnp.bfloat16
WHOLE = pl.BlockSpec(memory_space=pltpu.VMEM)


def params(*semantics):
    return pltpu.CompilerParams(
        vmem_limit_bytes=VMEM_LIMIT, dimension_semantics=semantics or None
    )


def dot(left, right, left_dim, right_dim):
    return lax.dot_general(
        left, right, (((left_dim,), (right_dim,)), ((), ())), preferred_element_type=F32
    )


def slot_row(id_row, experts, capacity, me):
    count = id_row.shape[1]
    expert = lax.broadcasted_iota(jnp.int32, (max(experts, 8), count), 0)
    chosen = expert == id_row
    earlier = lax.broadcasted_iota(jnp.int32, (count, count), 0) < lax.broadcasted_iota(
        jnp.int32, (count, count), 1
    )
    before = dot(
        jnp.where(chosen, 1.0, 0.0).astype(BF16), jnp.where(earlier, 1.0, 0.0).astype(BF16), 1, 0
    )
    position = jnp.sum(jnp.where(chosen, before, 0.0), axis=0, keepdims=True).astype(jnp.int32)
    return (id_row ^ me) * capacity + position


def feat_pack_kernel(experts, capacity, me_ref, id_ref, tokens_ref, slot_ref, *outs):
    slot = slot_row(id_ref[...], experts, capacity, me_ref[0])
    slot_ref[...] = slot
    count = slot.shape[1]
    for block, out in enumerate(outs):
        row = lax.broadcasted_iota(jnp.int32, (capacity, count), 0) + block * capacity
        pick = jnp.where(row == slot, 1.0, 0.0).astype(BF16)
        out[...] = dot(pick, tokens_ref[...], 1, 0).astype(BF16)


def grad_pack_kernel(capacity, slot_ref, gate_ref, grad_ref, *outs):
    slot = slot_ref[...]
    gate = gate_ref[...].astype(F32)
    count = slot.shape[1]
    for block, out in enumerate(outs):
        row = lax.broadcasted_iota(jnp.int32, (capacity, count), 0) + block * capacity
        pick = jnp.where(row == slot, gate, 0.0).astype(BF16)
        out[...] = dot(pick, grad_ref[...], 1, 0).astype(BF16)


def unpack_kernel(capacity, width, slot_ref, *refs):
    blocks, (feat_ref, gate_ref) = refs[:-2], refs[-2:]
    slot = slot_ref[...]
    count = slot.shape[1]
    total = None
    for block, ref in enumerate(blocks):
        row = lax.broadcasted_iota(jnp.int32, (capacity, count), 0) + block * capacity
        pick = jnp.where(row == slot, 1.0, 0.0).astype(BF16)
        part = dot(pick, ref[...], 0, 0)
        total = part if total is None else total + part
    feat_ref[...] = total[:, :width].astype(BF16)
    gate_ref[...] = total[:, width:]


def hidden_kernel(*refs):
    *blocks, up_ref, flip_feat_ref, hidden_ref, flip_hidden_ref, slope_ref, feat_ref = refs

    @pl.when(pl.program_id(0) == 0)
    def _():
        feat_ref[...] = jnp.concatenate([ref[...] for ref in blocks], axis=0)
        flip_feat_ref[...] = feat_ref[...].T

    pre_act = dot(feat_ref[...], up_ref[0], 1, 0)
    cdf = 0.5 * (1.0 + lax.erf(pre_act * SQRT_HALF))
    hidden = (pre_act * cdf).astype(BF16)
    hidden_ref[...] = hidden
    flip_hidden_ref[...] = hidden.T
    slope = cdf + pre_act * jnp.exp(-0.5 * pre_act * pre_act) * INV_ROOT_TAU
    slope_ref[...] = slope.astype(BF16)


def pre_grad_kernel(*refs):
    *blocks, down_ref, hidden_ref, slope_ref, pre_ref, sum_ref = refs
    scaled = jnp.concatenate([ref[...] for ref in blocks], axis=0)
    hidden_grad = dot(scaled, down_ref[0], 1, 1)
    pre_ref[...] = (hidden_grad * slope_ref[...].astype(F32)).astype(BF16)
    part = jnp.sum(hidden_grad * hidden_ref[...].astype(F32), axis=1, keepdims=True)

    @pl.when(pl.program_id(0) == 0)
    def _():
        sum_ref[...] = jnp.zeros_like(sum_ref)

    sum_ref[...] += jnp.broadcast_to(part, sum_ref.shape)


def feat_grad_kernel(pre_ref, up_ref, sum_ref, out_ref):
    width = up_ref.shape[1]
    out_ref[:, :width] = dot(pre_ref[...], up_ref[0], 1, 1).astype(BF16)
    total = sum_ref[...]
    high = total.astype(BF16)
    low = (total - high.astype(F32)).astype(BF16)
    lane = lax.broadcasted_iota(jnp.int32, total.shape, 1)
    out_ref[:, width:] = jnp.where(lane == 0, high.astype(F32), low.astype(F32)).astype(BF16)


def feat_grad(pre_grad, up_weight, sums, block, capacity):
    _, width, inner = up_weight.shape
    return pl.pallas_call(
        feat_grad_kernel,
        grid=(1,),
        in_specs=[
            pl.BlockSpec((capacity, inner), lambda i: (block, 0)),
            pl.BlockSpec((1, width, inner), lambda i: (0, 0, 0)),
            pl.BlockSpec((capacity, LANES), lambda i: (block, 0)),
        ],
        out_specs=pl.BlockSpec((capacity, width + LANES), lambda i: (0, 0)),
        out_shape=jax.ShapeDtypeStruct((capacity, width + LANES), BF16),
        compiler_params=params(),
        name="feat_grad",
    )(pre_grad, up_weight, sums)


def ring_index(position, count):
    half = count // 2
    return jnp.where(position < half, 2 * position, 2 * (count - 1 - position) + 1)


def ring_position(index, count):
    return jnp.where(index % 2 == 0, index // 2, count - 1 - index // 2)


def ring_pairs(count):
    half = count // 2
    ring = [2 * p if p < half else 2 * (count - 1 - p) + 1 for p in range(count)]
    return [(ring[p], ring[(p + 1) % count]) for p in range(count)]


def down_kernel(scale, order_ref, fore_ref, back_ref, *refs):
    *blocks, fore_in, back_in = refs[: -1 if scale else -2]
    scaled = jnp.concatenate([ref[...] for ref in blocks], axis=0)
    half = scaled.shape[1] // 2
    fore = dot(fore_ref[...], scaled[:, :half], 1, 0) + fore_in[...].astype(F32)
    back = dot(back_ref[...], scaled[:, half:], 1, 0) + back_in[...].astype(F32)
    if scale:
        refs[-1][0, :, :half] = fore * scale
        refs[-1][0, :, half:] = back * scale
    else:
        refs[-2][...] = fore.astype(BF16)
        refs[-1][...] = back.astype(BF16)


def down_first_kernel(order_ref, fore_ref, back_ref, *refs):
    *blocks, fore_out, back_out = refs
    scaled = jnp.concatenate([ref[...] for ref in blocks], axis=0)
    half = scaled.shape[1] // 2
    fore_out[...] = dot(fore_ref[...], scaled[:, :half], 1, 0).astype(BF16)
    back_out[...] = dot(back_ref[...], scaled[:, half:], 1, 0).astype(BF16)


def up_kernel(scale, order_ref, fore_ref, back_ref, pre_ref, fore_in, back_in, *outs):
    half = pre_ref.shape[1] // 2
    fore = dot(fore_ref[...], pre_ref[:, :half], 1, 0) + fore_in[...].astype(F32)
    back = dot(back_ref[...], pre_ref[:, half:], 1, 0) + back_in[...].astype(F32)
    if scale:
        outs[0][0, :, :half] = fore * scale
        outs[0][0, :, half:] = back * scale
    else:
        outs[0][...] = fore.astype(BF16)
        outs[1][...] = back.astype(BF16)


def up_first_kernel(order_ref, fore_ref, back_ref, pre_ref, fore_out, back_out):
    half = pre_ref.shape[1] // 2
    fore_out[...] = dot(fore_ref[...], pre_ref[:, :half], 1, 0).astype(BF16)
    back_out[...] = dot(back_ref[...], pre_ref[:, half:], 1, 0).astype(BF16)


def ring_step(kernels, name, order, step, count, lefts, rights, arrived):
    first, later = kernels
    rows = lefts.shape[0] // count
    tokens = lefts.shape[1]
    width = rights[0].shape[1]
    last = step == count
    if arrived is None:
        body, arrived = first, ()
    else:
        body = functools.partial(later, 1.0 / count if last else None)
    if last:
        out_specs = pl.BlockSpec((1, rows, width), lambda i, o: (0, 0, 0))
        out_shape = jax.ShapeDtypeStruct((1, rows, width), F32)
    else:
        out_specs = [pl.BlockSpec((rows, width // 2), lambda i, o: (0, 0))] * 2
        out_shape = [jax.ShapeDtypeStruct((rows, width // 2), BF16)] * 2
    full = [pl.BlockSpec(a.shape, lambda i, o: (0, 0)) for a in (*rights, *arrived)]
    return pl.pallas_call(
        body,
        grid_spec=pltpu.PrefetchScalarGridSpec(
            num_scalar_prefetch=1,
            grid=(1,),
            in_specs=[
                pl.BlockSpec((rows, tokens), lambda i, o: (o[0, step - 1], 0)),
                pl.BlockSpec((rows, tokens), lambda i, o: (o[1, step - 1], 0)),
                *full,
            ],
            out_specs=out_specs,
        ),
        out_shape=out_shape,
        compiler_params=params(),
        name=name,
    )(order, lefts, lefts, *rights, *arrived)


def per_device(tokens, out_grad, gate_prob, expert_id, up_weight, down_weight):
    count, width = tokens.shape
    inner = up_weight.shape[2]
    peers = lax.axis_size("expert")
    experts = peers * up_weight.shape[0]
    capacity = 2 * count // experts
    rows = peers * capacity
    ring = lax.axis_size("dp")
    me = lax.axis_index("expert")
    sources = [[(i, i ^ k) for i in range(peers)] for k in range(peers)]
    forward = ring_pairs(ring)
    backward = [(b, a) for a, b in forward]
    place = ring_position(lax.axis_index("dp"), ring)
    steps = jnp.arange(1, ring + 1, dtype=jnp.int32)
    order = ring_index(
        jnp.stack([(place - steps) % ring, (place + steps) % ring]), ring
    ).astype(jnp.int32)

    slot, *feat_out = pl.pallas_call(
        functools.partial(feat_pack_kernel, experts, capacity),
        in_specs=[pl.BlockSpec(memory_space=pltpu.SMEM), WHOLE, WHOLE],
        out_specs=[WHOLE] * (1 + peers),
        out_shape=[jax.ShapeDtypeStruct((1, count), jnp.int32)]
        + [jax.ShapeDtypeStruct((capacity, width), BF16)] * peers,
        compiler_params=params(),
        name="feat_pack",
    )(me.reshape(1), expert_id.reshape(1, count), tokens)
    feat_in = [feat_out[0]] + [
        lax.ppermute(feat_out[k], "expert", sources[k]) for k in reversed(range(1, peers))
    ][::-1]

    grad_out = pl.pallas_call(
        functools.partial(grad_pack_kernel, capacity),
        in_specs=[WHOLE] * 3,
        out_specs=[WHOLE] * peers,
        out_shape=[jax.ShapeDtypeStruct((capacity, width), BF16)] * peers,
        compiler_params=params(),
        name="grad_pack",
    )(slot, gate_prob.reshape(1, count), out_grad)
    grad_in = [grad_out[0]] + [
        lax.ppermute(grad_out[k], "expert", sources[k]) for k in reversed(range(1, peers))
    ][::-1]

    tile = inner // 8
    flip_feat, hidden, flip_hidden, slope = pl.pallas_call(
        hidden_kernel,
        grid=(inner // tile,),
        in_specs=[pl.BlockSpec((capacity, width), lambda i: (0, 0))] * peers
        + [pl.BlockSpec((1, width, tile), lambda i: (0, 0, i))],
        out_specs=[
            pl.BlockSpec((width, rows), lambda i: (0, 0)),
            pl.BlockSpec((rows, tile), lambda i: (0, i)),
            pl.BlockSpec((tile, rows), lambda i: (i, 0)),
            pl.BlockSpec((rows, tile), lambda i: (0, i)),
        ],
        out_shape=[
            jax.ShapeDtypeStruct((width, rows), BF16),
            jax.ShapeDtypeStruct((rows, inner), BF16),
            jax.ShapeDtypeStruct((inner, rows), BF16),
            jax.ShapeDtypeStruct((rows, inner), BF16),
        ],
        scratch_shapes=[pltpu.VMEM((rows, width), BF16)],
        compiler_params=params("arbitrary"),
        name="hidden",
    )(*feat_in, up_weight)

    pre_grad, sums = pl.pallas_call(
        pre_grad_kernel,
        grid=(inner // tile,),
        in_specs=[pl.BlockSpec((capacity, width), lambda i: (0, 0))] * peers
        + [
            pl.BlockSpec((1, tile, width), lambda i: (0, i, 0)),
            pl.BlockSpec((rows, tile), lambda i: (0, i)),
            pl.BlockSpec((rows, tile), lambda i: (0, i)),
        ],
        out_specs=[
            pl.BlockSpec((rows, tile), lambda i: (0, i)),
            pl.BlockSpec((rows, LANES), lambda i: (0, 0)),
        ],
        out_shape=[
            jax.ShapeDtypeStruct((rows, inner), BF16),
            jax.ShapeDtypeStruct((rows, LANES), F32),
        ],
        compiler_params=params("arbitrary"),
        name="pre_grad",
    )(*grad_in, down_weight, hidden, slope)

    down_kernels = (down_first_kernel, down_kernel)
    up_kernels = (up_first_kernel, up_kernel)
    down_arrived = up_arrived = None
    for step in range(1, ring + 1):
        down = ring_step(
            down_kernels, "down_step", order, step, ring, flip_hidden, grad_in, down_arrived
        )
        up = ring_step(
            up_kernels, "up_step", order, step, ring, flip_feat, [pre_grad], up_arrived
        )
        if step < ring:
            down_arrived = (
                lax.ppermute(down[0], "dp", forward),
                lax.ppermute(down[1], "dp", backward),
            )
            up_arrived = (
                lax.ppermute(up[0], "dp", forward),
                lax.ppermute(up[1], "dp", backward),
            )

    feat_back = [feat_grad(pre_grad, up_weight, sums, k, capacity) for k in range(peers)]
    feat_back = [feat_back[0]] + [
        lax.ppermute(feat_back[k], "expert", sources[k]) for k in range(1, peers)
    ]
    tokens_grad, gate_sums = pl.pallas_call(
        functools.partial(unpack_kernel, capacity, width),
        in_specs=[WHOLE] * (1 + peers),
        out_specs=[WHOLE] * 2,
        out_shape=[
            jax.ShapeDtypeStruct((count, width), BF16),
            jax.ShapeDtypeStruct((count, LANES), F32),
        ],
        compiler_params=params(),
        name="unpack",
    )(slot, *feat_back)
    gate_result = ((gate_sums[:, 0] + gate_sums[:, 1]) / gate_prob.astype(F32)).astype(BF16)
    return (tokens_grad, gate_result, up, down)


def solution(mesh):
    return jax.shard_map(
        per_device,
        mesh=mesh,
        in_specs=(
            P(("dp", "expert"), None),
            P(("dp", "expert"), None),
            P(("dp", "expert")),
            P(("dp", "expert")),
            P("expert", None, None),
            P("expert", None, None),
        ),
        out_specs=(
            P(("dp", "expert"), None),
            P(("dp", "expert")),
            P("expert", "dp", None),
            P("expert", "dp", None),
        ),
        check_vma=False,
    )
```

time: 265 us -> 123 us (0.46)
  waiting for transfers between devices: 156 us -> 40.5 us
  Pallas kernels: 0 us -> 38.4 us
  matrix products: 35 us -> 0 us
  starting transfers between devices: 14.7 us -> 36.3 us
  blocking collectives: 18 us -> 0 us
  between operations: 14.2 us -> 0.91 us
  local copies, waits for them, and re-layouts: 16.1 us -> 5.61 us
  other arithmetic: 9.74 us -> 0.73 us
    reduce_scatter x2 -> x0, waiting for transfers between devices: 137 us -> none  [the longest x1 89.8 us: per_device(): lax.psum_scatter(contract_rows(hidden, scaled).astype(jnp.bfloat16), 'dp'...]
    ppermute x0 -> x37, waiting for transfers between devices: none -> 40.5 us  [the longest x7 13 us: per_device(): lax.ppermute(up[0], 'dp', forward)]
    pallas_call x0 -> x25, Pallas kernels: none -> 38.4 us  [the longest x16 17.9 us: ring_step(): pl.pallas_call(body, grid_spec=pltpu.PrefetchScalarGridSpec(num_scalar_pr...]
    ppermute x0 -> x37, starting transfers between devices: none -> 36.3 us  [the longest x7 9.52 us: per_device(): lax.ppermute(up[1], 'dp', backward)]
    dot_general x6 -> x0, matrix products: 35 us -> none  [the longest x2 10.3 us: contract_rows(): lax.dot_general(left, right, (((0,), (0,)), ((), ())), preferred_element_...]
    all_to_all x4 -> x0, waiting for transfers between devices: 19.7 us -> none  [the longest x1 11.9 us: per_device(): lax.all_to_all(feat_grad.reshape(sources, capacity, feat_width), 'expert'...]
    all_to_all x1 -> x0, blocking collectives: 18 us -> none  [per_device(): lax.all_to_all(feat_slots, 'expert', split_axis=0, concat_axis=0, tiled=T...]
    all_to_all x4 -> x0, starting transfers between devices: 14.5 us -> none  [the longest x1 4.21 us: per_device(): lax.all_to_all(gate_slots, 'expert', split_axis=0, concat_axis=0, tiled=T...]
  transfers between devices with their start and end apart: 6 -> 37, of which waited for: 4 -> 20; matrix products, arithmetic and copies ran while one was open for 14% -> 1% of each run, Pallas kernels for 0% -> 28%
where the time goes in v1:
time: 123 us; the launch traced here: 122 us
  waiting for transfers between devices  40.5 us (33%)
  Pallas kernels  38.4 us (31%)
  starting transfers between devices  36.3 us (30%)
  local copies, waits for them, and re-layouts  5.61 us (5%)
    pallas_call x16, Pallas kernels, ring_step(): pl.pallas_call(body, grid_spec=pltpu.PrefetchScalarGridSpec(num_scalar_pr...  17.9 us
    ppermute x7, waiting for transfers between devices, per_device(): lax.ppermute(up[0], 'dp', forward)  13 us
    ppermute x7, waiting for transfers between devices, per_device(): lax.ppermute(down[0], 'dp', forward)  9.84 us
    ppermute x7, starting transfers between devices, per_device(): lax.ppermute(up[1], 'dp', backward)  9.52 us
    ppermute x3, waiting for transfers between devices, per_device(): lax.ppermute(feat_out[k], 'expert', sources[k])  7.86 us
    ppermute x7, starting transfers between devices, per_device(): lax.ppermute(down[0], 'dp', forward)  7.64 us
    ppermute x7, starting transfers between devices, per_device(): lax.ppermute(down[1], 'dp', backward)  6.85 us
    pallas_call x1, Pallas kernels, per_device(): pl.pallas_call(hidden_kernel, grid=(inner // tile,), in_specs=[pl.BlockSp...  6.45 us
  transfers between devices with their start and end apart: 37, of which 20 were waited for; matrix products, arithmetic and copies ran while one was open for 1% of the time, Pallas kernels for 28%

profile of v1, /device:TPU:0, one launch (start us, length us, event | category | flops | bytes accessed | tf_op | source)
XLA Modules:
  0.0 122.5 jit_solution(5573307164532456105)
XLA Ops:
  3.5 2.6 %collective-permute-start.4 = (bf16[128,1024]{1,0:T(8,128)(2,1)S(1)}, bf16[128,1024]{1,0:T(8,128)(2,1)S(1)}, u32[]{:S(2)}, u32[]{:S(2)}) collective-permute-start(bf16[128,1024]{1,0:T(8,128)(2,1)S(1)} %get-tuple-element.56), channel_id=1, source_target_pairs={{0,2},{1,3},{2,0},{3,1},{4,6},{5,7},{6,4},{7,5},{8,10},{9,11},{10,... | collective-permute-start | bytes 786440 | tf_op jit(solution)/shard_map/ppermute | solution.py:255
  8.5 1.9 %collective-permute-start.1 = (bf16[128,1024]{1,0:T(8,128)(2,1)S(1)}, bf16[128,1024]{1,0:T(8,128)(2,1)S(1)}, u32[]{:S(2)}, u32[]{:S(2)}) collective-permute-start(bf16[128,1024]{1,0:T(8,128)(2,1)S(1)} %get-tuple-element.52), channel_id=1, source_target_pairs={{0,2},{1,3},{2,0},{3,1},{4,6},{5,7},{6,4},{7,5},{8,10},{9,11},{10,... | collective-permute-start | bytes 786440 | tf_op jit(solution)/shard_map/ppermute | solution.py:267
  10.4 2.8 %collective-permute-done.4.refs_2_ = bf16[128,1024]{1,0:T(8,128)(2,1)S(1)} collective-permute-done((bf16[128,1024]{1,0:T(8,128)(2,1)S(1)}, bf16[128,1024]{1,0:T(8,128)(2,1)S(1)}, u32[]{:S(2)}, u32[]{:S(2)}) %collective-permute-start.4) | collective-permute-done | bytes 262176 | tf_op jit(solution)/shard_map/ppermute | solution.py:255
  13.2 5.1 %collective-permute-done.5.refs_3_ = bf16[128,1024]{1,0:T(8,128)(2,1)S(1)} collective-permute-done((bf16[128,1024]{1,0:T(8,128)(2,1)S(1)}, bf16[128,1024]{1,0:T(8,128)(2,1)S(1)}, u32[]{:S(2)}, u32[]{:S(2)}) %collective-permute-start.5) | collective-permute-done | bytes 262176 | tf_op jit(solution)/shard_map/ppermute | solution.py:255
  18.3 2.2 %copy-done = bf16[1,1024,2048]{2,1,0:T(8,128)(2,1)S(1)} copy-done((bf16[1,1024,2048]{2,1,0:T(8,128)(2,1)S(1)}, bf16[1,1024,2048]{2,1,0:T(8,128)(2,1)}, u32[]{:S(2)}) %copy-start) | copy-done | bytes 4194328
  20.5 6.4 %hidden.1 = (bf16[1024,512]{1,0:T(8,128)(2,1)S(1)}, bf16[512,2048]{1,0:T(8,128)(2,1)S(1)}, bf16[2048,512]{1,0:T(8,128)(2,1)S(1)}, bf16[512,2048]{1,0:T(8,128)(2,1)S(1)}) custom-call(bf16[128,1024]{1,0:T(8,128)(2,1)S(1)} %get-tuple-element.54.refs_0_, bf16[128,1024]{1,0:T(8,128)(2,1)S(1)} %collective-permute-done.3.refs_1_, ...), custom_call_target="tpu_custom_call" | custom-call | tf_op jit(solution)/shard_map/hidden/pallas_call | solution.py:271
  27.0 2.6 %collective-permute-done.2.refs_3_ = bf16[128,1024]{1,0:T(8,128)(2,1)S(1)} collective-permute-done((bf16[128,1024]{1,0:T(8,128)(2,1)S(1)}, bf16[128,1024]{1,0:T(8,128)(2,1)S(1)}, u32[]{:S(2)}, u32[]{:S(2)}) %collective-permute-start.2) | collective-permute-done | bytes 262176 | tf_op jit(solution)/shard_map/ppermute | solution.py:267
  30.5 1.7 %collective-permute-start.23 = (bf16[256,512]{1,0:T(8,128)(2,1)S(1)}, bf16[256,512]{1,0:T(8,128)(2,1)S(1)}, u32[]{:S(2)}, u32[]{:S(2)}) collective-permute-start(bf16[256,512]{1,0:T(8,128)(2,1)S(1)} %get-tuple-element.80), channel_id=1, source_target_pairs={{0,8},{8,16},{16,24},{24,28},{28,20},{20,12},{12,4},{4,0},{1,9},{9... | collective-permute-start | bytes 786440 | tf_op jit(solution)/shard_map/ppermute | solution.py:326
  32.6 5.5 %pre_grad.1 = (bf16[512,2048]{1,0:T(8,128)(2,1)S(1)}, f32[512,128]{1,0:T(8,128)S(1)}) custom-call(bf16[128,1024]{1,0:T(8,128)(2,1)S(1)} %get-tuple-element.50.refs_0_, bf16[128,1024]{1,0:T(8,128)(2,1)S(1)} %collective-permute-done.refs_1_, bf16[128,1024]{1,0:T(8,128)(2,1)S(1)} %collective-permute-done.1.refs_2_, ...), custom_call_target="tpu_custom_call" | custom-call | tf_op jit(solution)/shard_map/pre_grad/pallas_call | solution.py:293
  39.1 1.6 %collective-permute-start.10 = (bf16[128,1024]{1,0:T(8,128)(2,1)S(1)}, bf16[128,1024]{1,0:T(8,128)(2,1)S(1)}, u32[]{:S(2)}, u32[]{:S(2)}) collective-permute-start(bf16[128,1024]{1,0:T(8,128)(2,1)S(1)} %get-tuple-element.66), channel_id=1, source_target_pairs={{8,0},{16,8},{24,16},{28,24},{20,28},{12,20},{4,12},{0,4},{9,1},{1... | collective-permute-start | bytes 786440 | tf_op jit(solution)/shard_map/ppermute | solution.py:331
  42.2 1.7 %collective-permute-start.25 = (bf16[256,512]{1,0:T(8,128)(2,1)S(1)}, bf16[256,512]{1,0:T(8,128)(2,1)S(1)}, u32[]{:S(2)}, u32[]{:S(2)}) collective-permute-start(bf16[256,512]{1,0:T(8,128)(2,1)S(1)} %get-tuple-element.82), channel_id=1, source_target_pairs={{0,8},{8,16},{16,24},{24,28},{28,20},{20,12},{12,4},{4,0},{1,9},{9... | collective-permute-start | bytes 786440 | tf_op jit(solution)/shard_map/ppermute | solution.py:326
  44.3 4.1 %collective-permute-done.10.back_in = bf16[128,1024]{1,0:T(8,128)(2,1)S(1)} collective-permute-done((bf16[128,1024]{1,0:T(8,128)(2,1)S(1)}, bf16[128,1024]{1,0:T(8,128)(2,1)S(1)}, u32[]{:S(2)}, u32[]{:S(2)}) %collective-permute-start.10) | collective-permute-done | bytes 262176 | tf_op jit(solution)/shard_map/ppermute | solution.py:331
  48.4 1.6 %collective-permute-done.9.fore_in = bf16[128,1024]{1,0:T(8,128)(2,1)S(1)} collective-permute-done((bf16[128,1024]{1,0:T(8,128)(2,1)S(1)}, bf16[128,1024]{1,0:T(8,128)(2,1)S(1)}, u32[]{:S(2)}, u32[]{:S(2)}) %collective-permute-start.9) | collective-permute-done | bytes 262176 | tf_op jit(solution)/shard_map/ppermute | solution.py:330
  51.5 1.6 %collective-permute-start.12 = (bf16[128,1024]{1,0:T(8,128)(2,1)S(1)}, bf16[128,1024]{1,0:T(8,128)(2,1)S(1)}, u32[]{:S(2)}, u32[]{:S(2)}) collective-permute-start(bf16[128,1024]{1,0:T(8,128)(2,1)S(1)} %get-tuple-element.68), channel_id=1, source_target_pairs={{8,0},{16,8},{24,16},{28,24},{20,28},{12,20},{4,12},{0,4},{9,1},{1... | collective-permute-start | bytes 786440 | tf_op jit(solution)/shard_map/ppermute | solution.py:331
  53.1 2.5 %collective-permute-done.25.refs_4_ = bf16[256,512]{1,0:T(8,128)(2,1)S(1)} collective-permute-done((bf16[256,512]{1,0:T(8,128)(2,1)S(1)}, bf16[256,512]{1,0:T(8,128)(2,1)S(1)}, u32[]{:S(2)}, u32[]{:S(2)}) %collective-permute-start.25) | collective-permute-done | bytes 262176 | tf_op jit(solution)/shard_map/ppermute | solution.py:326
  57.1 1.6 %collective-permute-start.28 = (bf16[256,512]{1,0:T(8,128)(2,1)S(1)}, bf16[256,512]{1,0:T(8,128)(2,1)S(1)}, u32[]{:S(2)}, u32[]{:S(2)}) collective-permute-start(bf16[256,512]{1,0:T(8,128)(2,1)S(1)} %get-tuple-element.85), channel_id=1, source_target_pairs={{8,0},{16,8},{24,16},{28,24},{20,28},{12,20},{4,12},{0,4},{9,1},{1... | collective-permute-start | bytes 786440 | tf_op jit(solution)/shard_map/ppermute | solution.py:327
  58.7 2.5 %collective-permute-done.11.fore_in = bf16[128,1024]{1,0:T(8,128)(2,1)S(1)} collective-permute-done((bf16[128,1024]{1,0:T(8,128)(2,1)S(1)}, bf16[128,1024]{1,0:T(8,128)(2,1)S(1)}, u32[]{:S(2)}, u32[]{:S(2)}) %collective-permute-start.11) | collective-permute-done | bytes 262176 | tf_op jit(solution)/shard_map/ppermute | solution.py:330
  62.8 1.6 %collective-permute-start.14 = (bf16[128,1024]{1,0:T(8,128)(2,1)S(1)}, bf16[128,1024]{1,0:T(8,128)(2,1)S(1)}, u32[]{:S(2)}, u32[]{:S(2)}) collective-permute-start(bf16[128,1024]{1,0:T(8,128)(2,1)S(1)} %get-tuple-element.70), channel_id=1, source_target_pairs={{8,0},{16,8},{24,16},{28,24},{20,28},{12,20},{4,12},{0,4},{9,1},{1... | collective-permute-start | bytes 786440 | tf_op jit(solution)/shard_map/ppermute | solution.py:331
  64.3 2.5 %collective-permute-done.27.refs_4_ = bf16[256,512]{1,0:T(8,128)(2,1)S(1)} collective-permute-done((bf16[256,512]{1,0:T(8,128)(2,1)S(1)}, bf16[256,512]{1,0:T(8,128)(2,1)S(1)}, u32[]{:S(2)}, u32[]{:S(2)}) %collective-permute-start.27) | collective-permute-done | bytes 262176 | tf_op jit(solution)/shard_map/ppermute | solution.py:326
  69.9 2.5 %collective-permute-done.13.fore_in = bf16[128,1024]{1,0:T(8,128)(2,1)S(1)} collective-permute-done((bf16[128,1024]{1,0:T(8,128)(2,1)S(1)}, bf16[128,1024]{1,0:T(8,128)(2,1)S(1)}, u32[]{:S(2)}, u32[]{:S(2)}) %collective-permute-start.13) | collective-permute-done | bytes 262176 | tf_op jit(solution)/shard_map/ppermute | solution.py:330
  75.6 2.5 %collective-permute-done.29.refs_4_ = bf16[256,512]{1,0:T(8,128)(2,1)S(1)} collective-permute-done((bf16[256,512]{1,0:T(8,128)(2,1)S(1)}, bf16[256,512]{1,0:T(8,128)(2,1)S(1)}, u32[]{:S(2)}, u32[]{:S(2)}) %collective-permute-start.29) | collective-permute-done | bytes 262176 | tf_op jit(solution)/shard_map/ppermute | solution.py:326
  82.7 1.5 %feat_grad.6 = bf16[128,1152]{1,0:T(8,128)(2,1)S(1)} custom-call(bf16[512,2048]{1,0:T(8,128)(2,1)S(1)} %get-tuple-element.60.pre_ref, bf16[1,1024,2048]{2,1,0:T(8,128)(2,1)S(1)} %copy-done.1, f32[512,128]{1,0:T(8,128)S(1)} %get-tuple-element.61.sum_ref), custom_call_target="tpu_custom_call" | custom-call | tf_op jit(solution)/shard_map/feat_grad/pallas_call | solution.py:122
  84.3 1.5 %collective-permute-start.7 = (bf16[128,1152]{1,0:T(8,128)(2,1)S(1)}, bf16[128,1152]{1,0:T(8,128)(2,1)S(1)}, u32[]{:S(2)}, u32[]{:S(2)}) collective-permute-start(bf16[128,1152]{1,0:T(8,128)(2,1)S(1)} %feat_grad.6), channel_id=1, source_target_pairs={{0,2},{1,3},{2,0},{3,1},{4,6},{5,7},{6,4},{7,5},{8,10},{9,11},{10,... | collective-permute-start | bytes 884744 | tf_op jit(solution)/shard_map/ppermute | solution.py:336
  87.7 1.6 %collective-permute-start.18 = (bf16[128,1024]{1,0:T(8,128)(2,1)S(1)}, bf16[128,1024]{1,0:T(8,128)(2,1)S(1)}, u32[]{:S(2)}, u32[]{:S(2)}) collective-permute-start(bf16[128,1024]{1,0:T(8,128)(2,1)S(1)} %get-tuple-element.74), channel_id=1, source_target_pairs={{8,0},{16,8},{24,16},{28,24},{20,28},{12,20},{4,12},{0,4},{9,1},{1... | collective-permute-start | bytes 786440 | tf_op jit(solution)/shard_map/ppermute | solution.py:331
  89.3 1.5 %feat_grad.5 = bf16[128,1152]{1,0:T(8,128)(2,1)S(1)} custom-call(bf16[512,2048]{1,0:T(8,128)(2,1)S(1)} %get-tuple-element.60.pre_ref, bf16[1,1024,2048]{2,1,0:T(8,128)(2,1)S(1)} %copy-done.1, f32[512,128]{1,0:T(8,128)S(1)} %get-tuple-element.61.sum_ref), custom_call_target="tpu_custom_call" | custom-call | tf_op jit(solution)/shard_map/feat_grad/pallas_call | solution.py:122
  91.9 3.6 %collective-permute-done.17.fore_in = bf16[128,1024]{1,0:T(8,128)(2,1)S(1)} collective-permute-done((bf16[128,1024]{1,0:T(8,128)(2,1)S(1)}, bf16[128,1024]{1,0:T(8,128)(2,1)S(1)}, u32[]{:S(2)}, u32[]{:S(2)}) %collective-permute-start.17) | collective-permute-done | bytes 262176 | tf_op jit(solution)/shard_map/ppermute | solution.py:330
  102.1 1.6 %unpack.1 = (bf16[256,1024]{1,0:T(8,128)(2,1)}, f32[256,128]{1,0:T(8,128)S(1)}) custom-call(s32[1,256]{1,0:T(1,128)S(1)} %get-tuple-element.49.slot_ref, bf16[128,1152]{1,0:T(8,128)(2,1)S(1)} %feat_grad.4.refs_0_, bf16[128,1152]{1,0:T(8,128)(2,1)S(1)} %collective-permute-done.6.refs_1_, bf16[128,1152]{1,0:T(8,128)(2,1)S(1)} %collective-permute-done.7.refs_2_, ...), custom_call_target="tpu_custom_call" | custom-call | tf_op jit(solution)/shard_map/unpack/pallas_call | solution.py:338
  106.4 1.6 %collective-permute-start.35 = (bf16[256,512]{1,0:T(8,128)(2,1)S(1)}, bf16[256,512]{1,0:T(8,128)(2,1)S(1)}, u32[]{:S(2)}, u32[]{:S(2)}) collective-permute-start(bf16[256,512]{1,0:T(8,128)(2,1)S(1)} %get-tuple-element.92), channel_id=1, source_target_pairs={{0,8},{8,16},{16,24},{24,28},{28,20},{20,12},{12,4},{4,0},{1,9},{9... | collective-permute-start | bytes 786440 | tf_op jit(solution)/shard_map/ppermute | solution.py:326
  108.5 1.8 %collective-permute-done.19.fore_in = bf16[128,1024]{1,0:T(8,128)(2,1)S(1)} collective-permute-done((bf16[128,1024]{1,0:T(8,128)(2,1)S(1)}, bf16[128,1024]{1,0:T(8,128)(2,1)S(1)}, u32[]{:S(2)}, u32[]{:S(2)}) %collective-permute-start.19) | collective-permute-done | bytes 262176 | tf_op jit(solution)/shard_map/ppermute | solution.py:330
  112.0 1.6 %collective-permute-start.21 = (bf16[128,1024]{1,0:T(8,128)(2,1)S(1)}, bf16[128,1024]{1,0:T(8,128)(2,1)S(1)}, u32[]{:S(2)}, u32[]{:S(2)}) collective-permute-start(bf16[128,1024]{1,0:T(8,128)(2,1)S(1)} %get-tuple-element.77), channel_id=1, source_target_pairs={{0,8},{8,16},{16,24},{24,28},{28,20},{20,12},{12,4},{4,0},{1,9},{9... | collective-permute-start | bytes 786440 | tf_op jit(solution)/shard_map/ppermute | solution.py:330
  117.2 2.0 %down_step.15 = f32[1,256,1024]{2,1,0:T(8,128)} custom-call(s32[2,8]{1,0:T(2,128)S(1)} %compare_select_fusion.4.order_ref, bf16[2048,512]{1,0:T(8,128)(2,1)S(1)} %get-tuple-element.79.fore_ref.back_ref, bf16[2048,512]{1,0:T(8,128)(2,1)S(1)} %get-tuple-element.79.fore_ref.back_ref, bf16[128,1024]{1,0:T(8,128)(2,1)S(1)} %get-tuple-element.50.refs_0_, ...), custom_call_target="tpu_custom_call" | custom-call | tf_op jit(solution)/shard_map/down_step/pallas_call | solution.py:209
  120.5 2.0 %up_step.15 = f32[1,128,2048]{2,1,0:T(8,128)} custom-call(s32[2,8]{1,0:T(2,128)S(1)} %compare_select_fusion.4.order_ref, bf16[1024,512]{1,0:T(8,128)(2,1)S(1)} %get-tuple-element.64.fore_ref.back_ref, bf16[1024,512]{1,0:T(8,128)(2,1)S(1)} %get-tuple-element.64.fore_ref.back_ref, bf16[512,2048]{1,0:T(8,128)(2,1)S(1)} %get-tuple-element.60.pre_ref, ...), custom_call_target="tpu_custom_call" | custom-call | tf_op jit(solution)/shard_map/up_step/pallas_call | solution.py:209
  (86 shorter events, 44.1 us)
Async XLA Ops:
  3.5 9.7 %collective-permute-start.4 = (bf16[128,1024]{1,0:T(8,128)(2,1)S(1)}, bf16[128,1024]{1,0:T(8,128)(2,1)S(1)}, u32[]{:S(2)}, u32[]{:S(2)}) collective-permute-start(bf16[128,1024]{1,0:T(8,128)(2,1)S(1)} %get-tuple-element.56), channel_id=1, source_target_pairs={{0,2},{1,3},{2,0},{3,1},{4,6},{5,7},{6,4},{7,5},{8,10},{9,11},{10,... | collective-permute-start | bytes 786440 | tf_op jit(solution)/shard_map/ppermute | solution.py:255
  6.0 12.3 %collective-permute-start.5 = (bf16[128,1024]{1,0:T(8,128)(2,1)S(1)}, bf16[128,1024]{1,0:T(8,128)(2,1)S(1)}, u32[]{:S(2)}, u32[]{:S(2)}) collective-permute-start(bf16[128,1024]{1,0:T(8,128)(2,1)S(1)} %get-tuple-element.57), channel_id=1, source_target_pairs={{0,3},{1,2},{2,1},{3,0},{4,7},{5,6},{6,5},{7,4},{8,11},{9,10},{10,... | collective-permute-start | bytes 786440 | tf_op jit(solution)/shard_map/ppermute | solution.py:255
  8.3 18.7 %collective-permute-start = (bf16[128,1024]{1,0:T(8,128)(2,1)S(1)}, bf16[128,1024]{1,0:T(8,128)(2,1)S(1)}, u32[]{:S(2)}, u32[]{:S(2)}) collective-permute-start(bf16[128,1024]{1,0:T(8,128)(2,1)S(1)} %get-tuple-element.51), channel_id=1, source_target_pairs={{0,1},{1,0},{2,3},{3,2},{4,5},{5,4},{6,7},{7,6},{8,9},{9,8},{10,11... | collective-permute-start | bytes 786440 | tf_op jit(solution)/shard_map/ppermute | solution.py:267
  8.5 18.5 %collective-permute-start.1 = (bf16[128,1024]{1,0:T(8,128)(2,1)S(1)}, bf16[128,1024]{1,0:T(8,128)(2,1)S(1)}, u32[]{:S(2)}, u32[]{:S(2)}) collective-permute-start(bf16[128,1024]{1,0:T(8,128)(2,1)S(1)} %get-tuple-element.52), channel_id=1, source_target_pairs={{0,2},{1,3},{2,0},{3,1},{4,6},{5,7},{6,4},{7,5},{8,10},{9,11},{10,... | collective-permute-start | bytes 786440 | tf_op jit(solution)/shard_map/ppermute | solution.py:267
  10.4 19.1 %collective-permute-start.2 = (bf16[128,1024]{1,0:T(8,128)(2,1)S(1)}, bf16[128,1024]{1,0:T(8,128)(2,1)S(1)}, u32[]{:S(2)}, u32[]{:S(2)}) collective-permute-start(bf16[128,1024]{1,0:T(8,128)(2,1)S(1)} %get-tuple-element.53), channel_id=1, source_target_pairs={{0,3},{1,2},{2,1},{3,0},{4,7},{5,6},{6,5},{7,4},{8,11},{9,10},{10,... | collective-permute-start | bytes 786440 | tf_op jit(solution)/shard_map/ppermute | solution.py:267
  30.5 10.7 %collective-permute-start.23 = (bf16[256,512]{1,0:T(8,128)(2,1)S(1)}, bf16[256,512]{1,0:T(8,128)(2,1)S(1)}, u32[]{:S(2)}, u32[]{:S(2)}) collective-permute-start(bf16[256,512]{1,0:T(8,128)(2,1)S(1)} %get-tuple-element.80), channel_id=1, source_target_pairs={{0,8},{8,16},{16,24},{24,28},{28,20},{20,12},{12,4},{4,0},{1,9},{9... | collective-permute-start | bytes 786440 | tf_op jit(solution)/shard_map/ppermute | solution.py:326
  32.2 9.0 %collective-permute-start.24 = (bf16[256,512]{1,0:T(8,128)(2,1)S(1)}, bf16[256,512]{1,0:T(8,128)(2,1)S(1)}, u32[]{:S(2)}, u32[]{:S(2)}) collective-permute-start(bf16[256,512]{1,0:T(8,128)(2,1)S(1)} %get-tuple-element.81), channel_id=1, source_target_pairs={{8,0},{16,8},{24,16},{28,24},{20,28},{12,20},{4,12},{0,4},{9,1},{1... | collective-permute-start | bytes 786440 | tf_op jit(solution)/shard_map/ppermute | solution.py:327
  39.1 9.3 %collective-permute-start.10 = (bf16[128,1024]{1,0:T(8,128)(2,1)S(1)}, bf16[128,1024]{1,0:T(8,128)(2,1)S(1)}, u32[]{:S(2)}, u32[]{:S(2)}) collective-permute-start(bf16[128,1024]{1,0:T(8,128)(2,1)S(1)} %get-tuple-element.66), channel_id=1, source_target_pairs={{8,0},{16,8},{24,16},{28,24},{20,28},{12,20},{4,12},{0,4},{9,1},{1... | collective-permute-start | bytes 786440 | tf_op jit(solution)/shard_map/ppermute | solution.py:331
  40.8 9.2 %collective-permute-start.9 = (bf16[128,1024]{1,0:T(8,128)(2,1)S(1)}, bf16[128,1024]{1,0:T(8,128)(2,1)S(1)}, u32[]{:S(2)}, u32[]{:S(2)}) collective-permute-start(bf16[128,1024]{1,0:T(8,128)(2,1)S(1)} %get-tuple-element.65), channel_id=1, source_target_pairs={{0,8},{8,16},{16,24},{24,28},{28,20},{20,12},{12,4},{4,0},{1,9},{9... | collective-permute-start | bytes 786440 | tf_op jit(solution)/shard_map/ppermute | solution.py:330
  42.2 13.4 %collective-permute-start.25 = (bf16[256,512]{1,0:T(8,128)(2,1)S(1)}, bf16[256,512]{1,0:T(8,128)(2,1)S(1)}, u32[]{:S(2)}, u32[]{:S(2)}) collective-permute-start(bf16[256,512]{1,0:T(8,128)(2,1)S(1)} %get-tuple-element.82), channel_id=1, source_target_pairs={{0,8},{8,16},{16,24},{24,28},{28,20},{20,12},{12,4},{4,0},{1,9},{9... | collective-permute-start | bytes 786440 | tf_op jit(solution)/shard_map/ppermute | solution.py:326
  43.9 11.7 %collective-permute-start.26 = (bf16[256,512]{1,0:T(8,128)(2,1)S(1)}, bf16[256,512]{1,0:T(8,128)(2,1)S(1)}, u32[]{:S(2)}, u32[]{:S(2)}) collective-permute-start(bf16[256,512]{1,0:T(8,128)(2,1)S(1)} %get-tuple-element.83), channel_id=1, source_target_pairs={{8,0},{16,8},{24,16},{28,24},{20,28},{12,20},{4,12},{0,4},{9,1},{1... | collective-permute-start | bytes 786440 | tf_op jit(solution)/shard_map/ppermute | solution.py:327
  51.0 10.2 %collective-permute-start.11 = (bf16[128,1024]{1,0:T(8,128)(2,1)S(1)}, bf16[128,1024]{1,0:T(8,128)(2,1)S(1)}, u32[]{:S(2)}, u32[]{:S(2)}) collective-permute-start(bf16[128,1024]{1,0:T(8,128)(2,1)S(1)} %get-tuple-element.67), channel_id=1, source_target_pairs={{0,8},{8,16},{16,24},{24,28},{28,20},{20,12},{12,4},{4,0},{1,9},{9... | collective-permute-start | bytes 786440 | tf_op jit(solution)/shard_map/ppermute | solution.py:330
  51.5 9.7 %collective-permute-start.12 = (bf16[128,1024]{1,0:T(8,128)(2,1)S(1)}, bf16[128,1024]{1,0:T(8,128)(2,1)S(1)}, u32[]{:S(2)}, u32[]{:S(2)}) collective-permute-start(bf16[128,1024]{1,0:T(8,128)(2,1)S(1)} %get-tuple-element.68), channel_id=1, source_target_pairs={{8,0},{16,8},{24,16},{28,24},{20,28},{12,20},{4,12},{0,4},{9,1},{1... | collective-permute-start | bytes 786440 | tf_op jit(solution)/shard_map/ppermute | solution.py:331
  56.6 10.2 %collective-permute-start.27 = (bf16[256,512]{1,0:T(8,128)(2,1)S(1)}, bf16[256,512]{1,0:T(8,128)(2,1)S(1)}, u32[]{:S(2)}, u32[]{:S(2)}) collective-permute-start(bf16[256,512]{1,0:T(8,128)(2,1)S(1)} %get-tuple-element.84), channel_id=1, source_target_pairs={{0,8},{8,16},{16,24},{24,28},{28,20},{20,12},{12,4},{4,0},{1,9},{9... | collective-permute-start | bytes 786440 | tf_op jit(solution)/shard_map/ppermute | solution.py:326
  57.1 9.8 %collective-permute-start.28 = (bf16[256,512]{1,0:T(8,128)(2,1)S(1)}, bf16[256,512]{1,0:T(8,128)(2,1)S(1)}, u32[]{:S(2)}, u32[]{:S(2)}) collective-permute-start(bf16[256,512]{1,0:T(8,128)(2,1)S(1)} %get-tuple-element.85), channel_id=1, source_target_pairs={{8,0},{16,8},{24,16},{28,24},{20,28},{12,20},{4,12},{0,4},{9,1},{1... | collective-permute-start | bytes 786440 | tf_op jit(solution)/shard_map/ppermute | solution.py:327
  62.2 10.2 %collective-permute-start.13 = (bf16[128,1024]{1,0:T(8,128)(2,1)S(1)}, bf16[128,1024]{1,0:T(8,128)(2,1)S(1)}, u32[]{:S(2)}, u32[]{:S(2)}) collective-permute-start(bf16[128,1024]{1,0:T(8,128)(2,1)S(1)} %get-tuple-element.69), channel_id=1, source_target_pairs={{0,8},{8,16},{16,24},{24,28},{28,20},{20,12},{12,4},{4,0},{1,9},{9... | collective-permute-start | bytes 786440 | tf_op jit(solution)/shard_map/ppermute | solution.py:330
  62.8 9.7 %collective-permute-start.14 = (bf16[128,1024]{1,0:T(8,128)(2,1)S(1)}, bf16[128,1024]{1,0:T(8,128)(2,1)S(1)}, u32[]{:S(2)}, u32[]{:S(2)}) collective-permute-start(bf16[128,1024]{1,0:T(8,128)(2,1)S(1)} %get-tuple-element.70), channel_id=1, source_target_pairs={{8,0},{16,8},{24,16},{28,24},{20,28},{12,20},{4,12},{0,4},{9,1},{1... | collective-permute-start | bytes 786440 | tf_op jit(solution)/shard_map/ppermute | solution.py:331
  67.9 10.2 %collective-permute-start.29 = (bf16[256,512]{1,0:T(8,128)(2,1)S(1)}, bf16[256,512]{1,0:T(8,128)(2,1)S(1)}, u32[]{:S(2)}, u32[]{:S(2)}) collective-permute-start(bf16[256,512]{1,0:T(8,128)(2,1)S(1)} %get-tuple-element.86), channel_id=1, source_target_pairs={{0,8},{8,16},{16,24},{24,28},{28,20},{20,12},{12,4},{4,0},{1,9},{9... | collective-permute-start | bytes 786440 | tf_op jit(solution)/shard_map/ppermute | solution.py:326
  68.6 9.5 %collective-permute-start.30 = (bf16[256,512]{1,0:T(8,128)(2,1)S(1)}, bf16[256,512]{1,0:T(8,128)(2,1)S(1)}, u32[]{:S(2)}, u32[]{:S(2)}) collective-permute-start(bf16[256,512]{1,0:T(8,128)(2,1)S(1)} %get-tuple-element.87), channel_id=1, source_target_pairs={{8,0},{16,8},{24,16},{28,24},{20,28},{12,20},{4,12},{0,4},{9,1},{1... | collective-permute-start | bytes 786440 | tf_op jit(solution)/shard_map/ppermute | solution.py:327
  73.5 10.8 %collective-permute-start.15 = (bf16[128,1024]{1,0:T(8,128)(2,1)S(1)}, bf16[128,1024]{1,0:T(8,128)(2,1)S(1)}, u32[]{:S(2)}, u32[]{:S(2)}) collective-permute-start(bf16[128,1024]{1,0:T(8,128)(2,1)S(1)} %get-tuple-element.71), channel_id=1, source_target_pairs={{0,8},{8,16},{16,24},{24,28},{28,20},{20,12},{12,4},{4,0},{1,9},{9... | collective-permute-start | bytes 786440 | tf_op jit(solution)/shard_map/ppermute | solution.py:330
  74.2 11.6 %collective-permute-start.16 = (bf16[128,1024]{1,0:T(8,128)(2,1)S(1)}, bf16[128,1024]{1,0:T(8,128)(2,1)S(1)}, u32[]{:S(2)}, u32[]{:S(2)}) collective-permute-start(bf16[128,1024]{1,0:T(8,128)(2,1)S(1)} %get-tuple-element.72), channel_id=1, source_target_pairs={{8,0},{16,8},{24,16},{28,24},{20,28},{12,20},{4,12},{0,4},{9,1},{1... | collective-permute-start | bytes 786440 | tf_op jit(solution)/shard_map/ppermute | solution.py:331
  79.8 11.0 %collective-permute-start.32 = (bf16[256,512]{1,0:T(8,128)(2,1)S(1)}, bf16[256,512]{1,0:T(8,128)(2,1)S(1)}, u32[]{:S(2)}, u32[]{:S(2)}) collective-permute-start(bf16[256,512]{1,0:T(8,128)(2,1)S(1)} %get-tuple-element.89), channel_id=1, source_target_pairs={{8,0},{16,8},{24,16},{28,24},{20,28},{12,20},{4,12},{0,4},{9,1},{1... | collective-permute-start | bytes 786440 | tf_op jit(solution)/shard_map/ppermute | solution.py:327
  82.7 15.8 %collective-permute-start.8 = (bf16[128,1152]{1,0:T(8,128)(2,1)S(1)}, bf16[128,1152]{1,0:T(8,128)(2,1)S(1)}, u32[]{:S(2)}, u32[]{:S(2)}) collective-permute-start(bf16[128,1152]{1,0:T(8,128)(2,1)S(1)} %feat_grad.7), channel_id=1, source_target_pairs={{0,3},{1,2},{2,1},{3,0},{4,7},{5,6},{6,5},{7,4},{8,11},{9,10},{10,... | collective-permute-start | bytes 884744 | tf_op jit(solution)/shard_map/ppermute | solution.py:336
  84.3 15.0 %collective-permute-start.7 = (bf16[128,1152]{1,0:T(8,128)(2,1)S(1)}, bf16[128,1152]{1,0:T(8,128)(2,1)S(1)}, u32[]{:S(2)}, u32[]{:S(2)}) collective-permute-start(bf16[128,1152]{1,0:T(8,128)(2,1)S(1)} %feat_grad.6), channel_id=1, source_target_pairs={{0,2},{1,3},{2,0},{3,1},{4,6},{5,7},{6,4},{7,5},{8,10},{9,11},{10,... | collective-permute-start | bytes 884744 | tf_op jit(solution)/shard_map/ppermute | solution.py:336
  86.8 8.6 %collective-permute-start.17 = (bf16[128,1024]{1,0:T(8,128)(2,1)S(1)}, bf16[128,1024]{1,0:T(8,128)(2,1)S(1)}, u32[]{:S(2)}, u32[]{:S(2)}) collective-permute-start(bf16[128,1024]{1,0:T(8,128)(2,1)S(1)} %get-tuple-element.73), channel_id=1, source_target_pairs={{0,8},{8,16},{16,24},{24,28},{28,20},{20,12},{12,4},{4,0},{1,9},{9... | collective-permute-start | bytes 786440 | tf_op jit(solution)/shard_map/ppermute | solution.py:330
  90.8 11.3 %collective-permute-start.6 = (bf16[128,1152]{1,0:T(8,128)(2,1)S(1)}, bf16[128,1152]{1,0:T(8,128)(2,1)S(1)}, u32[]{:S(2)}, u32[]{:S(2)}) collective-permute-start(bf16[128,1152]{1,0:T(8,128)(2,1)S(1)} %feat_grad.5), channel_id=1, source_target_pairs={{0,1},{1,0},{2,3},{3,2},{4,5},{5,4},{6,7},{7,6},{8,9},{9,8},{10,11... | collective-permute-start | bytes 884744 | tf_op jit(solution)/shard_map/ppermute | solution.py:336
  95.5 9.2 %collective-permute-start.33 = (bf16[256,512]{1,0:T(8,128)(2,1)S(1)}, bf16[256,512]{1,0:T(8,128)(2,1)S(1)}, u32[]{:S(2)}, u32[]{:S(2)}) collective-permute-start(bf16[256,512]{1,0:T(8,128)(2,1)S(1)} %get-tuple-element.90), channel_id=1, source_target_pairs={{0,8},{8,16},{16,24},{24,28},{28,20},{20,12},{12,4},{4,0},{1,9},{9... | collective-permute-start | bytes 786440 | tf_op jit(solution)/shard_map/ppermute | solution.py:326
  96.1 9.2 %collective-permute-start.34 = (bf16[256,512]{1,0:T(8,128)(2,1)S(1)}, bf16[256,512]{1,0:T(8,128)(2,1)S(1)}, u32[]{:S(2)}, u32[]{:S(2)}) collective-permute-start(bf16[256,512]{1,0:T(8,128)(2,1)S(1)} %get-tuple-element.91), channel_id=1, source_target_pairs={{8,0},{16,8},{24,16},{28,24},{20,28},{12,20},{4,12},{0,4},{9,1},{1... | collective-permute-start | bytes 786440 | tf_op jit(solution)/shard_map/ppermute | solution.py:327
  98.5 11.8 %collective-permute-start.19 = (bf16[128,1024]{1,0:T(8,128)(2,1)S(1)}, bf16[128,1024]{1,0:T(8,128)(2,1)S(1)}, u32[]{:S(2)}, u32[]{:S(2)}) collective-permute-start(bf16[128,1024]{1,0:T(8,128)(2,1)S(1)} %get-tuple-element.75), channel_id=1, source_target_pairs={{0,8},{8,16},{16,24},{24,28},{28,20},{20,12},{12,4},{4,0},{1,9},{9... | collective-permute-start | bytes 786440 | tf_op jit(solution)/shard_map/ppermute | solution.py:330
  99.2 11.8 %collective-permute-start.20 = (bf16[128,1024]{1,0:T(8,128)(2,1)S(1)}, bf16[128,1024]{1,0:T(8,128)(2,1)S(1)}, u32[]{:S(2)}, u32[]{:S(2)}) collective-permute-start(bf16[128,1024]{1,0:T(8,128)(2,1)S(1)} %get-tuple-element.76), channel_id=1, source_target_pairs={{8,0},{16,8},{24,16},{28,24},{20,28},{12,20},{4,12},{0,4},{9,1},{1... | collective-permute-start | bytes 786440 | tf_op jit(solution)/shard_map/ppermute | solution.py:331
  106.4 9.5 %collective-permute-start.35 = (bf16[256,512]{1,0:T(8,128)(2,1)S(1)}, bf16[256,512]{1,0:T(8,128)(2,1)S(1)}, u32[]{:S(2)}, u32[]{:S(2)}) collective-permute-start(bf16[256,512]{1,0:T(8,128)(2,1)S(1)} %get-tuple-element.92), channel_id=1, source_target_pairs={{0,8},{8,16},{16,24},{24,28},{28,20},{20,12},{12,4},{4,0},{1,9},{9... | collective-permute-start | bytes 786440 | tf_op jit(solution)/shard_map/ppermute | solution.py:326
  108.0 9.2 %collective-permute-start.36 = (bf16[256,512]{1,0:T(8,128)(2,1)S(1)}, bf16[256,512]{1,0:T(8,128)(2,1)S(1)}, u32[]{:S(2)}, u32[]{:S(2)}) collective-permute-start(bf16[256,512]{1,0:T(8,128)(2,1)S(1)} %get-tuple-element.93), channel_id=1, source_target_pairs={{8,0},{16,8},{24,16},{28,24},{20,28},{12,20},{4,12},{0,4},{9,1},{1... | collective-permute-start | bytes 786440 | tf_op jit(solution)/shard_map/ppermute | solution.py:327
  (12 other events, 60.7 us)

commit v2 on v0

v2 whole, which is shorter than its diff:
```python
import functools

import jax
import jax.numpy as jnp
from jax import lax
from jax.experimental import pallas as pl
from jax.experimental.pallas import tpu as pltpu
from jax.sharding import PartitionSpec as P

SQRT_HALF = 0.7071067811865476
INV_ROOT_TAU = 0.3989422804014327
LANES = 128
VMEM_LIMIT = 40 * 1024 * 1024
F32 = jnp.float32
BF16 = jnp.bfloat16
WHOLE = pl.BlockSpec(memory_space=pltpu.VMEM)
LATER = pl.BlockSpec(memory_space=pl.ANY)


def in_hbm(array):
    return pltpu.with_memory_space_constraint(array, pltpu.HBM)


def params(*semantics):
    return pltpu.CompilerParams(
        vmem_limit_bytes=VMEM_LIMIT, dimension_semantics=semantics or None
    )


def dot(left, right, left_dim, right_dim):
    return lax.dot_general(
        left, right, (((left_dim,), (right_dim,)), ((), ())), preferred_element_type=F32
    )


def slot_row(id_row, experts, capacity, me):
    count = id_row.shape[1]
    expert = lax.broadcasted_iota(jnp.int32, (max(experts, 8), count), 0)
    chosen = expert == id_row
    earlier = lax.broadcasted_iota(jnp.int32, (count, count), 0) < lax.broadcasted_iota(
        jnp.int32, (count, count), 1
    )
    before = dot(
        jnp.where(chosen, 1.0, 0.0).astype(BF16), jnp.where(earlier, 1.0, 0.0).astype(BF16), 1, 0
    )
    position = jnp.sum(jnp.where(chosen, before, 0.0), axis=0, keepdims=True).astype(jnp.int32)
    return (id_row ^ me) * capacity + position


def pack_kernel(experts, capacity, me_ref, *refs):
    sources, refs = refs[:4], refs[4:]
    slot_ref, outs = refs[0], refs[1:-5]
    held, sems = refs[-5:-1], refs[-1]
    copies = [
        pltpu.make_async_copy(source, target, sems.at[i])
        for i, (source, target) in enumerate(zip(sources, held))
    ]
    for copy in copies:
        copy.start()
    id_ref, tokens_ref, gate_ref, grad_ref = held
    copies[0].wait()
    count = id_ref.shape[0]
    slot = slot_row(id_ref[...].reshape(1, count), experts, capacity, me_ref[0])
    slot_ref[...] = slot
    peers = len(outs) // 2
    copies[1].wait()
    for block in range(peers):
        row = lax.broadcasted_iota(jnp.int32, (capacity, count), 0) + block * capacity
        pick = jnp.where(row == slot, 1.0, 0.0).astype(BF16)
        outs[block][...] = dot(pick, tokens_ref[...], 1, 0).astype(BF16)
    copies[2].wait()
    copies[3].wait()
    gate = gate_ref[...].astype(F32).reshape(1, count)
    for block in range(peers):
        row = lax.broadcasted_iota(jnp.int32, (capacity, count), 0) + block * capacity
        pick = jnp.where(row == slot, gate, 0.0).astype(BF16)
        outs[peers + block][...] = dot(pick, grad_ref[...], 1, 0).astype(BF16)


def unpack_kernel(capacity, width, peers, slot_ref, *refs):
    blocks, (feat_ref, gate_ref) = refs[:peers], refs[-2:]
    slot = slot_ref[...]
    count = slot.shape[1]
    total = None
    for block, ref in enumerate(blocks):
        row = lax.broadcasted_iota(jnp.int32, (capacity, count), 0) + block * capacity
        pick = jnp.where(row == slot, 1.0, 0.0).astype(BF16)
        part = dot(pick, ref[...], 0, 0)
        total = part if total is None else total + part
    feat_ref[...] = total[:, :width].astype(BF16)
    gate_ref[...] = total[:, width:]


def call(body, inputs, out_shape, name, after=()):
    return pl.pallas_call(
        body,
        in_specs=[WHOLE] * len(inputs) + [LATER] * len(after),
        out_specs=[WHOLE] * len(out_shape),
        out_shape=[jax.ShapeDtypeStruct(*s) for s in out_shape],
        compiler_params=params(),
        name=name,
    )(*inputs, *after)


def hidden_kernel(peers, tiles, *refs):
    blocks, up_ref = refs[:peers], refs[peers]
    flip_feat_ref, hidden_ref, flip_hidden_ref, slope_ref = refs[-4:]
    feat = jnp.concatenate([ref[...] for ref in blocks], axis=0)
    flip_feat_ref[...] = feat.T
    tile = up_ref.shape[2] // tiles
    for i in range(tiles):
        part = slice(i * tile, (i + 1) * tile)
        pre_act = dot(feat, up_ref[0, :, part], 1, 0)
        cdf = 0.5 * (1.0 + lax.erf(pre_act * SQRT_HALF))
        hidden = (pre_act * cdf).astype(BF16)
        hidden_ref[:, part] = hidden
        flip_hidden_ref[part, :] = hidden.T
        slope = cdf + pre_act * jnp.exp(-0.5 * pre_act * pre_act) * INV_ROOT_TAU
        slope_ref[:, part] = slope.astype(BF16)


def hidden_call(blocks, up_weight, after=()):
    _, width, inner = up_weight.shape
    rows = len(blocks) * blocks[0].shape[0]
    return call(
        functools.partial(hidden_kernel, len(blocks), 8),
        [*blocks, up_weight],
        [
            ((width, rows), BF16),
            ((rows, inner), BF16),
            ((inner, rows), BF16),
            ((rows, inner), BF16),
        ],
        "hidden",
        after,
    )


def pre_grad_kernel(peers, tiles, *refs):
    blocks = refs[:peers]
    down_ref, hidden_ref, slope_ref = refs[peers : peers + 3]
    pre_ref, sum_ref = refs[-2:]
    scaled = jnp.concatenate([ref[...] for ref in blocks], axis=0)
    tile = down_ref.shape[1] // tiles
    total = 0.0
    for i in range(tiles):
        part = slice(i * tile, (i + 1) * tile)
        hidden_grad = dot(scaled, down_ref[0, part, :], 1, 1)
        pre_ref[:, part] = (hidden_grad * slope_ref[:, part].astype(F32)).astype(BF16)
        product = hidden_grad * hidden_ref[:, part].astype(F32)
        for j in range(tile // LANES):
            total += product[:, j * LANES : (j + 1) * LANES]
    sum_ref[...] = jnp.broadcast_to(jnp.sum(total, axis=1, keepdims=True), sum_ref.shape)


def pre_grad_call(blocks, down_weight, hidden, slope, after=()):
    _, inner, width = down_weight.shape
    rows = len(blocks) * blocks[0].shape[0]
    return call(
        functools.partial(pre_grad_kernel, len(blocks), 8),
        [*blocks, down_weight, hidden, slope],
        [((rows, inner), BF16), ((rows, LANES), F32)],
        "pre_grad",
        after,
    )


def feat_grad_kernel(block, pre_ref, up_ref, sum_ref, *refs):
    out = refs[-1]
    capacity = out.shape[0]
    part = slice(block * capacity, (block + 1) * capacity)
    width = up_ref.shape[1]
    out[:, :width] = dot(pre_ref[part, :], up_ref[0], 1, 1).astype(BF16)
    total = sum_ref[part, :]
    high = total.astype(BF16).astype(F32)
    lane = lax.broadcasted_iota(jnp.int32, total.shape, 1)
    out[:, width:] = jnp.where(lane == 0, high, total - high).astype(BF16)


def feat_grad_call(pre_grad, up_weight, sums, block, capacity, after=()):
    shape = (capacity, up_weight.shape[1] + LANES)
    return call(
        functools.partial(feat_grad_kernel, block),
        [pre_grad, up_weight, sums],
        [(shape, BF16)],
        "feat_grad",
        after,
    )[0]


def ring_index(position, count):
    half = count // 2
    return jnp.where(position < half, 2 * position, 2 * (count - 1 - position) + 1)


def ring_position(index, count):
    return jnp.where(index % 2 == 0, index // 2, count - 1 - index // 2)


def ring_pairs(count):
    half = count // 2
    ring = [2 * p if p < half else 2 * (count - 1 - p) + 1 for p in range(count)]
    return [(ring[p], ring[(p + 1) % count]) for p in range(count)]


def step_kernel(parts, arrivals, step, count, order_ref, *refs):
    groups = len(parts)
    lefts, refs = refs[:groups], refs[groups:]
    last = step == count
    if last:
        out, held, sems = refs[-3:]
    else:
        outs = refs[-2:]
    half = refs[0].shape[1] // 2
    rows = lefts[0].shape[0] // count
    totals = [ref[...].astype(F32) for ref in refs[sum(parts) : sum(parts) + arrivals]] or [0.0] * 2
    for left, blocks in zip(lefts, parts):
        right = [ref[...] for ref in refs[:blocks]]
        right = right[0] if blocks == 1 else jnp.concatenate(right, axis=0)
        refs = refs[blocks:]
        for way in range(2):
            start = pl.multiple_of(order_ref[way, step - 1] * rows, rows)
            totals[way] += dot(
                left[pl.ds(start, rows), :], right[:, way * half : (way + 1) * half], 1, 0
            )
    copies = []
    for way in range(2):
        if last:
            held[way] = totals[way] * (1.0 / count)
            target = out.at[0, :, way * half : (way + 1) * half]
            copies.append(pltpu.make_async_copy(held.at[way], target, sems.at[way]))
            copies[-1].start()
        else:
            outs[way][...] = totals[way].astype(BF16)
    for copy in copies:
        copy.wait()


def ring_step(name, order, step, count, lefts, rights, arrived, after=()):
    rows = lefts[0].shape[0] // count
    width = rights[0][0].shape[1]
    if step == count:
        out_specs = [pl.BlockSpec(memory_space=pltpu.HBM)]
        out_shape = [pltpu.HBM((1, rows, width), F32)]
        scratch = [pltpu.VMEM((2, rows, width // 2), F32), pltpu.SemaphoreType.DMA((2,))]
    else:
        out_specs = [WHOLE] * 2
        out_shape = [jax.ShapeDtypeStruct((rows, width // 2), BF16)] * 2
        scratch = []
    blocks = [block for group in rights for block in group]
    inputs = [*lefts, *blocks, *arrived]
    return pl.pallas_call(
        functools.partial(
            step_kernel, [len(group) for group in rights], len(arrived), step, count
        ),
        in_specs=[pl.BlockSpec(memory_space=pltpu.SMEM)]
        + [WHOLE] * len(inputs)
        + [LATER] * len(after),
        out_specs=out_specs,
        out_shape=out_shape,
        scratch_shapes=scratch,
        compiler_params=params(),
        name=name,
    )(order, *inputs, *after)


def per_device(tokens, out_grad, gate_prob, expert_id, up_weight, down_weight):
    count, width = tokens.shape
    inner = up_weight.shape[2]
    peers = lax.axis_size("expert")
    experts = peers * up_weight.shape[0]
    capacity = 2 * count // experts
    ring = lax.axis_size("dp")
    me = lax.axis_index("expert")
    sources = [[(i, i ^ k) for i in range(peers)] for k in range(peers)]
    forward = ring_pairs(ring)
    backward = [(b, a) for a, b in forward]
    place = ring_position(lax.axis_index("dp"), ring)
    steps = jnp.arange(1, ring + 1, dtype=jnp.int32)
    order = ring_index(
        jnp.stack([(place - steps) % ring, (place + steps) % ring]), ring
    ).astype(jnp.int32)

    def exchange(outs, reach):
        return {k: lax.ppermute(outs[k], "expert", sources[k]) for k in reach}

    near, far = range(1, peers // 2), range(peers // 2, peers)
    hbm = pl.BlockSpec(memory_space=pltpu.HBM)
    slot, *packed = pl.pallas_call(
        functools.partial(pack_kernel, experts, capacity),
        in_specs=[pl.BlockSpec(memory_space=pltpu.SMEM)] + [hbm] * 4,
        out_specs=[WHOLE] * (1 + 2 * peers),
        out_shape=[jax.ShapeDtypeStruct((1, count), jnp.int32)]
        + [jax.ShapeDtypeStruct((capacity, width), BF16)] * (2 * peers),
        scratch_shapes=[
            pltpu.VMEM((count,), jnp.int32),
            pltpu.VMEM((count, width), BF16),
            pltpu.VMEM((count,), BF16),
            pltpu.VMEM((count, width), BF16),
            pltpu.SemaphoreType.DMA((4,)),
        ],
        compiler_params=params(),
        name="pack",
    )(me.reshape(1), *(in_hbm(a) for a in (expert_id, tokens, gate_prob, out_grad)))
    feat_out, grad_out = packed[:peers], packed[peers:]
    feat_in = {0: feat_out[0], **exchange(feat_out, far), **exchange(feat_out, near)}
    grad_in = {0: grad_out[0], **exchange(grad_out, far), **exchange(grad_out, near)}

    groups = [[0, *near], [*far]]
    feats = [[feat_in[k] for k in group] for group in groups]
    scaleds = [[grad_in[k] for k in group] for group in groups]
    near_hidden = hidden_call(feats[0], up_weight)
    near_pre = pre_grad_call(scaleds[0], down_weight, near_hidden[1], near_hidden[3])
    far_hidden = hidden_call(feats[1], up_weight, [near_pre[1]])
    flip_feats = [near_hidden[0], far_hidden[0]]
    flip_hiddens = [near_hidden[2], far_hidden[2]]

    def send(pair):
        return [lax.ppermute(pair[0], "dp", forward), lax.ppermute(pair[1], "dp", backward)]

    turn = 1 if ring < 8 else 2
    span = min(4, ring - turn)
    returns = [*far, *near, 0]
    feat_back = {}
    down_in, up_in, after, landed = [], [], [], []
    for step in range(1, ring + 1):
        down = ring_step("down_step", order, step, ring, flip_hiddens, scaleds, down_in, after)
        if step < ring:
            down_in = send(down)
            after = [down[0]]
        else:
            after = []
        if step == 1:
            far_pre = pre_grad_call(scaleds[1], down_weight, far_hidden[1], far_hidden[3], after)
            pre_grads = [[near_pre[0]], [far_pre[0]]]
            after = [far_pre[1]]
        up = ring_step("up_step", order, step, ring, flip_feats, pre_grads, up_in, after)
        if step < ring:
            up_in = send(up)
            after = [up[0]]
        after = after + landed
        landed = []
        first = (step - turn) * len(returns) // span
        stop = (step - turn + 1) * len(returns) // span
        for k in returns[max(first, 0) : max(stop, 0)]:
            group = int(k in far)
            block = feat_grad_call(
                pre_grads[group][0],
                up_weight,
                (near_pre, far_pre)[group][1],
                groups[group].index(k),
                capacity,
                after,
            )
            after = [block]
            feat_back[k] = lax.ppermute(block, "expert", sources[k]) if k else block
            landed.append(feat_back[k])
        if step == ring - 1:
            tokens_grad, gate_sums = pl.pallas_call(
                functools.partial(unpack_kernel, capacity, width, peers),
                in_specs=[WHOLE] * (1 + peers) + [LATER] * len(after),
                out_specs=[WHOLE] * 2,
                out_shape=[
                    jax.ShapeDtypeStruct((count, width), BF16),
                    jax.ShapeDtypeStruct((count, LANES), F32),
                ],
                compiler_params=params(),
                name="unpack",
            )(slot, *(feat_back[k] for k in range(peers)), *after)
            after = [gate_sums]
    gate_result = ((gate_sums[:, 0] + gate_sums[:, 1]) / gate_prob.astype(F32)).astype(BF16)
    return (tokens_grad, gate_result, up[0], down[0])


def solution(mesh):
    return jax.shard_map(
        per_device,
        mesh=mesh,
        in_specs=(
            P(("dp", "expert"), None),
            P(("dp", "expert"), None),
            P(("dp", "expert")),
            P(("dp", "expert")),
            P("expert", None, None),
            P("expert", None, None),
        ),
        out_specs=(
            P(("dp", "expert"), None),
            P(("dp", "expert")),
            P("expert", "dp", None),
            P("expert", "dp", None),
        ),
        check_vma=False,
    )
```

time: 265 us -> 117 us (0.44)
  waiting for transfers between devices: 156 us -> 41.7 us
  matrix products: 35 us -> 0 us
  Pallas kernels: 0 us -> 34.3 us
  starting transfers between devices: 14.7 us -> 36.2 us
  blocking collectives: 18 us -> 0 us
  local copies, waits for them, and re-layouts: 16.1 us -> 2.34 us
  between operations: 14.2 us -> 1.03 us
  other arithmetic: 9.74 us -> 0.73 us
    reduce_scatter x2 -> x0, waiting for transfers between devices: 137 us -> none  [the longest x1 89.8 us: per_device(): lax.psum_scatter(contract_rows(hidden, scaled).astype(jnp.bfloat16), 'dp'...]
    ppermute x0 -> x37, waiting for transfers between devices: none -> 41.7 us  [the longest x14 15.6 us: send(): lax.ppermute(pair[1], 'dp', backward)]
    ppermute x0 -> x37, starting transfers between devices: none -> 36.2 us  [the longest x14 19.7 us: send(): lax.ppermute(pair[0], 'dp', forward)]
    dot_general x6 -> x0, matrix products: 35 us -> none  [the longest x2 10.3 us: contract_rows(): lax.dot_general(left, right, (((0,), (0,)), ((), ())), preferred_element_...]
    pallas_call x0 -> x26, Pallas kernels: none -> 34.3 us  [the longest x16 17.7 us: ring_step(): pl.pallas_call(functools.partial(step_kernel, [len(group) for group in ri...]
    all_to_all x4 -> x0, waiting for transfers between devices: 19.7 us -> none  [the longest x1 11.9 us: per_device(): lax.all_to_all(feat_grad.reshape(sources, capacity, feat_width), 'expert'...]
    all_to_all x1 -> x0, blocking collectives: 18 us -> none  [per_device(): lax.all_to_all(feat_slots, 'expert', split_axis=0, concat_axis=0, tiled=T...]
    all_to_all x4 -> x0, starting transfers between devices: 14.5 us -> none  [the longest x1 4.21 us: per_device(): lax.all_to_all(gate_slots, 'expert', split_axis=0, concat_axis=0, tiled=T...]
  transfers between devices with their start and end apart: 6 -> 37, of which waited for: 4 -> 27; matrix products, arithmetic and copies ran while one was open for 14% -> 1% of each run, Pallas kernels for 0% -> 25%
where the time goes in v2:
time: 117 us; the launch traced here: 116 us
  waiting for transfers between devices  41.7 us (36%)
  starting transfers between devices  36.2 us (31%)
  Pallas kernels  34.3 us (29%)
  local copies, waits for them, and re-layouts  2.34 us (2%)
    ppermute x14, starting transfers between devices, send(): lax.ppermute(pair[0], 'dp', forward)  19.7 us
    pallas_call x16, Pallas kernels, ring_step(): pl.pallas_call(functools.partial(step_kernel, [len(group) for group in ri...  17.7 us
    ppermute x14, waiting for transfers between devices, send(): lax.ppermute(pair[1], 'dp', backward)  15.6 us
    ppermute x6, waiting for transfers between devices, exchange(): return {k: lax.ppermute(outs[k], 'expert', sources[k]) for k in reach}  13.1 us
    pallas_call x8, Pallas kernels, call(): pl.pallas_call(body, in_specs=[WHOLE] * len(inputs) + [LATER] * len(after...  13 us
    ppermute x14, waiting for transfers between devices, send(): lax.ppermute(pair[0], 'dp', forward)  12.3 us
    ppermute x14, starting transfers between devices, send(): lax.ppermute(pair[1], 'dp', backward)  9.41 us
    ppermute x6, starting transfers between devices, exchange(): return {k: lax.ppermute(outs[k], 'expert', sources[k]) for k in reach}  5.3 us
  transfers between devices with their start and end apart: 37, of which 27 were waited for; matrix products, arithmetic and copies ran while one was open for 1% of the time, Pallas kernels for 25%

profile of v2, /device:TPU:0, one launch (start us, length us, event | category | flops | bytes accessed | tf_op | source)
XLA Modules:
  0.0 116.4 jit_solution(13437570077854863928)
XLA Ops:
  0.6 2.0 %pack.1 = (s32[1,256]{1,0:T(1,128)S(1)}, bf16[128,1024]{1,0:T(8,128)(2,1)S(1)}, bf16[128,1024]{1,0:T(8,128)(2,1)S(1)}, bf16[128,1024]{1,0:T(8,128)(2,1)S(1)}, bf...) custom-call(s32[1]{0:T(128)} %bitcast.me_ref, ...), custom_call_target="tpu_custom_call" | custom-call | tf_op jit(solution)/shard_map/pack/pallas_call | solution.py:289
  3.3 2.9 %collective-permute-start.2 = (bf16[128,1024]{1,0:T(8,128)(2,1)S(1)}, bf16[128,1024]{1,0:T(8,128)(2,1)S(1)}, u32[]{:S(2)}, u32[]{:S(2)}) collective-permute-start(bf16[128,1024]{1,0:T(8,128)(2,1)S(1)} %get-tuple-element.65), channel_id=1, source_target_pairs={{0,2},{1,3},{2,0},{3,1},{4,6},{5,7},{6,4},{7,5},{8,10},{9,11},{10,... | collective-permute-start | bytes 786440 | tf_op jit(solution)/shard_map/ppermute | solution.py:285
  8.0 2.2 %copy-done = bf16[1,1024,2048]{2,1,0:T(8,128)(2,1)S(1)} copy-done((bf16[1,1024,2048]{2,1,0:T(8,128)(2,1)S(1)}, bf16[1,1024,2048]{2,1,0:T(8,128)(2,1)}, u32[]{:S(2)}) %copy-start) | copy-done | bytes 4194328
  10.2 2.0 %hidden.2 = (bf16[1024,256]{1,0:T(8,128)(2,1)S(1)}, bf16[256,2048]{1,0:T(8,128)(2,1)S(1)}, bf16[2048,256]{1,0:T(8,128)(2,1)S(1)}, bf16[256,2048]{1,0:T(8,128)(2,1)S(1)}) custom-call(bf16[128,1024]{1,0:T(8,128)(2,1)S(1)} %get-tuple-element.58.refs_0_, bf16[128,1024]{1,0:T(8,128)(2,1)S(1)} %collective-permute-done.1.refs_1_, bf16[1,1024,2048]{2,1,0:T(8,128)(2,1)S(1)} %copy-done), custom_call_target="tpu_custom_call" | custom-call | tf_op jit(solution)/shard_map/hidden/pallas_call | solution.py:95
  12.4 1.5 %pre_grad.2 = (bf16[256,2048]{1,0:T(8,128)(2,1)S(1)}, f32[256,128]{1,0:T(8,128)S(1)}) custom-call(bf16[128,1024]{1,0:T(8,128)(2,1)S(1)} %get-tuple-element.56.refs_0_.refs_2_, bf16[128,1024]{1,0:T(8,128)(2,1)S(1)} %collective-permute-done.refs_1_.refs_3_, bf16[1,2048,1024]{2,1,0:T(8,128)(2,1)S(1)} %copy-done.2, ...), custom_call_target="tpu_custom_call" | custom-call | tf_op jit(solution)/shard_map/pre_grad/pallas_call | solution.py:95
  13.9 4.6 %collective-permute-done.3.refs_1_ = bf16[128,1024]{1,0:T(8,128)(2,1)S(1)} collective-permute-done((bf16[128,1024]{1,0:T(8,128)(2,1)S(1)}, bf16[128,1024]{1,0:T(8,128)(2,1)S(1)}, u32[]{:S(2)}, u32[]{:S(2)}) %collective-permute-start.3) | collective-permute-done | bytes 262176 | tf_op jit(solution)/shard_map/ppermute | solution.py:285
  18.5 2.0 %hidden.3 = (bf16[1024,256]{1,0:T(8,128)(2,1)S(1)}, bf16[256,2048]{1,0:T(8,128)(2,1)S(1)}, bf16[2048,256]{1,0:T(8,128)(2,1)S(1)}, bf16[256,2048]{1,0:T(8,128)(2,1)S(1)}) custom-call(bf16[128,1024]{1,0:T(8,128)(2,1)S(1)} %collective-permute-done.2.refs_0_, bf16[128,1024]{1,0:T(8,128)(2,1)S(1)} %collective-permute-done.3.refs_1_, ...), custom_call_target="tpu_custom_call" | custom-call | tf_op jit(solution)/shard_map/hidden/pallas_call | solution.py:95
  20.5 4.0 %collective-permute-done.4.refs_4_.refs_0_ = bf16[128,1024]{1,0:T(8,128)(2,1)S(1)} collective-permute-done((bf16[128,1024]{1,0:T(8,128)(2,1)S(1)}, bf16[128,1024]{1,0:T(8,128)(2,1)S(1)}, u32[]{:S(2)}, u32[]{:S(2)}) %collective-permute-start.4) | collective-permute-done | bytes 262176 | tf_op jit(solution)/shard_map/ppermute | solution.py:285
  24.5 4.5 %collective-permute-done.5.refs_5_.refs_1_ = bf16[128,1024]{1,0:T(8,128)(2,1)S(1)} collective-permute-done((bf16[128,1024]{1,0:T(8,128)(2,1)S(1)}, bf16[128,1024]{1,0:T(8,128)(2,1)S(1)}, u32[]{:S(2)}, u32[]{:S(2)}) %collective-permute-start.5) | collective-permute-done | bytes 262176 | tf_op jit(solution)/shard_map/ppermute | solution.py:285
  30.0 1.6 %collective-permute-start.8 = (bf16[256,512]{1,0:T(8,128)(2,1)S(1)}, bf16[256,512]{1,0:T(8,128)(2,1)S(1)}, u32[]{:S(2)}, u32[]{:S(2)}) collective-permute-start(bf16[256,512]{1,0:T(8,128)(2,1)S(1)} %get-tuple-element.74.refs_5_), channel_id=1, source_target_pairs={{0,8},{8,16},{16,24},{24,28},{28,20},{20,12},{12,4},{4,0},{1,9},{9... | collective-permute-start | bytes 786440 | tf_op jit(solution)/shard_map/ppermute | solution.py:319
  32.1 1.5 %pre_grad.3 = (bf16[256,2048]{1,0:T(8,128)(2,1)S(1)}, f32[256,128]{1,0:T(8,128)S(1)}) custom-call(bf16[128,1024]{1,0:T(8,128)(2,1)S(1)} %collective-permute-done.4.refs_4_.refs_0_, bf16[128,1024]{1,0:T(8,128)(2,1)S(1)} %collective-permute-done.5.refs_5_.refs_1_, bf16[1,2048,1024]{2,1,0:T(8,128)(2,1)S(1)} %copy-done.2, ...), custom_call_target="tpu_custom_call" | custom-call | tf_op jit(solution)/shard_map/pre_grad/pallas_call | solution.py:95
  34.6 1.5 %collective-permute-start.6 = (bf16[128,1024]{1,0:T(8,128)(2,1)S(1)}, bf16[128,1024]{1,0:T(8,128)(2,1)S(1)}, u32[]{:S(2)}, u32[]{:S(2)}) collective-permute-start(bf16[128,1024]{1,0:T(8,128)(2,1)S(1)} %get-tuple-element.77.refs_8_), channel_id=1, source_target_pairs={{0,8},{8,16},{16,24},{24,28},{28,20},{20,12},{12,4},{4,0},{1,9},{9... | collective-permute-start | bytes 786440 | tf_op jit(solution)/shard_map/ppermute | solution.py:319
  36.7 2.5 %collective-permute-done.8.refs_6_ = bf16[256,512]{1,0:T(8,128)(2,1)S(1)} collective-permute-done((bf16[256,512]{1,0:T(8,128)(2,1)S(1)}, bf16[256,512]{1,0:T(8,128)(2,1)S(1)}, u32[]{:S(2)}, u32[]{:S(2)}) %collective-permute-start.8) | collective-permute-done | bytes 262176 | tf_op jit(solution)/shard_map/ppermute | solution.py:319
  39.2 1.5 %collective-permute-done.9.refs_7_ = bf16[256,512]{1,0:T(8,128)(2,1)S(1)} collective-permute-done((bf16[256,512]{1,0:T(8,128)(2,1)S(1)}, bf16[256,512]{1,0:T(8,128)(2,1)S(1)}, u32[]{:S(2)}, u32[]{:S(2)}) %collective-permute-start.9) | collective-permute-done | bytes 262176 | tf_op jit(solution)/shard_map/ppermute | solution.py:319
  41.7 1.6 %collective-permute-start.12 = (bf16[256,512]{1,0:T(8,128)(2,1)S(1)}, bf16[256,512]{1,0:T(8,128)(2,1)S(1)}, u32[]{:S(2)}, u32[]{:S(2)}) collective-permute-start(bf16[256,512]{1,0:T(8,128)(2,1)S(1)} %get-tuple-element.80.refs_6_), channel_id=1, source_target_pairs={{0,8},{8,16},{16,24},{24,28},{28,20},{20,12},{12,4},{4,0},{1,9},{9... | collective-permute-start | bytes 786440 | tf_op jit(solution)/shard_map/ppermute | solution.py:319
  44.8 1.5 %collective-permute-done.7.refs_5_ = bf16[128,1024]{1,0:T(8,128)(2,1)S(1)} collective-permute-done((bf16[128,1024]{1,0:T(8,128)(2,1)S(1)}, bf16[128,1024]{1,0:T(8,128)(2,1)S(1)}, u32[]{:S(2)}, u32[]{:S(2)}) %collective-permute-start.7) | collective-permute-done | bytes 262176 | tf_op jit(solution)/shard_map/ppermute | solution.py:319
  47.3 1.6 %collective-permute-start.10 = (bf16[128,1024]{1,0:T(8,128)(2,1)S(1)}, bf16[128,1024]{1,0:T(8,128)(2,1)S(1)}, u32[]{:S(2)}, u32[]{:S(2)}) collective-permute-start(bf16[128,1024]{1,0:T(8,128)(2,1)S(1)} %get-tuple-element.81.refs_0_), channel_id=1, source_target_pairs={{0,8},{8,16},{16,24},{24,28},{28,20},{20,12},{12,4},{4,0},{1,9},{9... | collective-permute-start | bytes 786440 | tf_op jit(solution)/shard_map/ppermute | solution.py:319
  49.4 1.5 %feat_grad.4.refs_8_ = bf16[128,1152]{1,0:T(8,128)(2,1)S(1)} custom-call(bf16[256,2048]{1,0:T(8,128)(2,1)S(1)} %get-tuple-element.75.refs_3_.pre_ref, bf16[1,1024,2048]{2,1,0:T(8,128)(2,1)S(1)} %copy-done.1, f32[256,128]{1,0:T(8,128)S(1)} %get-tuple-element.76.refs_4_.sum_ref, bf16[128,1024]{1,0:T(8,128)(2,1)S(1)} %get-tuple-element.81.refs_0_), custom_call_target="tpu_custom_call" | custom-call | tf_op jit(solution)/shard_map/feat_grad/pallas_call | solution.py:95
  50.9 1.5 %collective-permute-start.18 = (bf16[128,1152]{1,0:T(8,128)(2,1)S(1)}, bf16[128,1152]{1,0:T(8,128)(2,1)S(1)}, u32[]{:S(2)}, u32[]{:S(2)}) collective-permute-start(bf16[128,1152]{1,0:T(8,128)(2,1)S(1)} %feat_grad.4.refs_8_), channel_id=1, source_target_pairs={{0,2},{1,3},{2,0},{3,1},{4,6},{5,7},{6,4},{7,5},{8,10},{9,11},{10,... | collective-permute-start | bytes 884744 | tf_op jit(solution)/shard_map/ppermute | solution.py:356
  53.4 1.6 %collective-permute-start.16 = (bf16[256,512]{1,0:T(8,128)(2,1)S(1)}, bf16[256,512]{1,0:T(8,128)(2,1)S(1)}, u32[]{:S(2)}, u32[]{:S(2)}) collective-permute-start(bf16[256,512]{1,0:T(8,128)(2,1)S(1)} %get-tuple-element.84.refs_6_), channel_id=1, source_target_pairs={{0,8},{8,16},{16,24},{24,28},{28,20},{20,12},{12,4},{4,0},{1,9},{9... | collective-permute-start | bytes 786440 | tf_op jit(solution)/shard_map/ppermute | solution.py:319
  56.6 1.6 %collective-permute-done.11.refs_5_ = bf16[128,1024]{1,0:T(8,128)(2,1)S(1)} collective-permute-done((bf16[128,1024]{1,0:T(8,128)(2,1)S(1)}, bf16[128,1024]{1,0:T(8,128)(2,1)S(1)}, u32[]{:S(2)}, u32[]{:S(2)}) %collective-permute-start.11) | collective-permute-done | bytes 262176 | tf_op jit(solution)/shard_map/ppermute | solution.py:319
  59.2 1.6 %collective-permute-start.14 = (bf16[128,1024]{1,0:T(8,128)(2,1)S(1)}, bf16[128,1024]{1,0:T(8,128)(2,1)S(1)}, u32[]{:S(2)}, u32[]{:S(2)}) collective-permute-start(bf16[128,1024]{1,0:T(8,128)(2,1)S(1)} %get-tuple-element.85.refs_0_), channel_id=1, source_target_pairs={{0,8},{8,16},{16,24},{24,28},{28,20},{20,12},{12,4},{4,0},{1,9},{9... | collective-permute-start | bytes 786440 | tf_op jit(solution)/shard_map/ppermute | solution.py:319
  61.3 1.5 %feat_grad.5.refs_8_ = bf16[128,1152]{1,0:T(8,128)(2,1)S(1)} custom-call(bf16[256,2048]{1,0:T(8,128)(2,1)S(1)} %get-tuple-element.75.refs_3_.pre_ref, bf16[1,1024,2048]{2,1,0:T(8,128)(2,1)S(1)} %copy-done.1, f32[256,128]{1,0:T(8,128)S(1)} %get-tuple-element.76.refs_4_.sum_ref, bf16[128,1024]{1,0:T(8,128)(2,1)S(1)} %get-tuple-element.85.refs_0_, ...), custom_call_target="tpu_custom_call" | custom-call | tf_op jit(solution)/shard_map/feat_grad/pallas_call | solution.py:95
  69.3 1.6 %collective-permute-start.19 = (bf16[128,1024]{1,0:T(8,128)(2,1)S(1)}, bf16[128,1024]{1,0:T(8,128)(2,1)S(1)}, u32[]{:S(2)}, u32[]{:S(2)}) collective-permute-start(bf16[128,1024]{1,0:T(8,128)(2,1)S(1)} %get-tuple-element.89.refs_0_), channel_id=1, source_target_pairs={{0,8},{8,16},{16,24},{24,28},{28,20},{20,12},{12,4},{4,0},{1,9},{9... | collective-permute-start | bytes 786440 | tf_op jit(solution)/shard_map/ppermute | solution.py:319
  72.1 1.5 %feat_grad.6.refs_8_ = bf16[128,1152]{1,0:T(8,128)(2,1)S(1)} custom-call(bf16[256,2048]{1,0:T(8,128)(2,1)S(1)} %get-tuple-element.62.refs_2_.pre_ref, bf16[1,1024,2048]{2,1,0:T(8,128)(2,1)S(1)} %copy-done.1, f32[256,128]{1,0:T(8,128)S(1)} %get-tuple-element.63.refs_3_.sum_ref, bf16[128,1024]{1,0:T(8,128)(2,1)S(1)} %get-tuple-element.89.refs_0_, ...), custom_call_target="tpu_custom_call" | custom-call | tf_op jit(solution)/shard_map/feat_grad/pallas_call | solution.py:95
  82.3 1.5 %collective-permute-start.25 = (bf16[128,1024]{1,0:T(8,128)(2,1)S(1)}, bf16[128,1024]{1,0:T(8,128)(2,1)S(1)}, u32[]{:S(2)}, u32[]{:S(2)}) collective-permute-start(bf16[128,1024]{1,0:T(8,128)(2,1)S(1)} %get-tuple-element.93.refs_0_), channel_id=1, source_target_pairs={{0,8},{8,16},{16,24},{24,28},{28,20},{20,12},{12,4},{4,0},{1,9},{9... | collective-permute-start | bytes 786440 | tf_op jit(solution)/shard_map/ppermute | solution.py:319
  84.3 1.5 %feat_grad.7.refs_8_.refs_9_.refs_0_ = bf16[128,1152]{1,0:T(8,128)(2,1)S(1)} custom-call(bf16[256,2048]{1,0:T(8,128)(2,1)S(1)} %get-tuple-element.62.refs_2_.pre_ref, bf16[1,1024,2048]{2,1,0:T(8,128)(2,1)S(1)} %copy-done.1, f32[256,128]{1,0:T(8,128)S(1)} %get-tuple-element.63.refs_3_.sum_ref, bf16[128,1024]{1,0:T(8,128)(2,1)S(1)} %get-tuple-element.93.refs_0_, ...), custom_call_target="tpu_custom_call" | custom-call | tf_op jit(solution)/shard_map/feat_grad/pallas_call | solution.py:95
  96.1 1.6 %collective-permute-done.31.refs_6_ = bf16[256,512]{1,0:T(8,128)(2,1)S(1)} collective-permute-done((bf16[256,512]{1,0:T(8,128)(2,1)S(1)}, bf16[256,512]{1,0:T(8,128)(2,1)S(1)}, u32[]{:S(2)}, u32[]{:S(2)}) %collective-permute-start.31) | collective-permute-done | bytes 262176 | tf_op jit(solution)/shard_map/ppermute | solution.py:319
  101.7 1.6 %collective-permute-done.29.refs_4_ = bf16[128,1024]{1,0:T(8,128)(2,1)S(1)} collective-permute-done((bf16[128,1024]{1,0:T(8,128)(2,1)S(1)}, bf16[128,1024]{1,0:T(8,128)(2,1)S(1)}, u32[]{:S(2)}, u32[]{:S(2)}) %collective-permute-start.29) | collective-permute-done | bytes 262176 | tf_op jit(solution)/shard_map/ppermute | solution.py:319
  107.4 1.6 %unpack.1 = (bf16[256,1024]{1,0:T(8,128)(2,1)}, f32[256,128]{1,0:T(8,128)S(1)}) custom-call(s32[1,256]{1,0:T(1,128)S(1)} %get-tuple-element.55.slot_ref, bf16[128,1152]{1,0:T(8,128)(2,1)S(1)} %feat_grad.7.refs_8_.refs_9_.refs_0_, bf16[128,1152]{1,0:T(8,128)(2,1)S(1)} %collective-permute-done.24.refs_1_, ...), custom_call_target="tpu_custom_call" | custom-call | tf_op jit(solution)/shard_map/unpack/pallas_call | solution.py:359
  110.0 1.9 %down_step.15 = f32[1,256,1024]{2,1,0:T(8,128)} custom-call(s32[2,8]{1,0:T(2,128)S(1)} %compare_select_fusion.4.order_ref, bf16[2048,256]{1,0:T(8,128)(2,1)S(1)} %get-tuple-element.72.refs_0_, bf16[2048,256]{1,0:T(8,128)(2,1)S(1)} %get-tuple-element.73.refs_1_, bf16[128,1024]{1,0:T(8,128)(2,1)S(1)} %get-tuple-element.56.refs_0_.refs_2_, ...), custom_call_target="tpu_custom_call" | custom-call | tf_op jit(solution)/shard_map/down_step/pallas_call | solution.py:252
  114.3 1.9 %up_step.15 = f32[1,128,2048]{2,1,0:T(8,128)} custom-call(s32[2,8]{1,0:T(2,128)S(1)} %compare_select_fusion.4.order_ref, bf16[1024,256]{1,0:T(8,128)(2,1)S(1)} %get-tuple-element.64.refs_0_, bf16[1024,256]{1,0:T(8,128)(2,1)S(1)} %get-tuple-element.67.refs_1_, bf16[256,2048]{1,0:T(8,128)(2,1)S(1)} %get-tuple-element.62.refs_2_.pre_ref, ...), custom_call_target="tpu_custom_call" | custom-call | tf_op jit(solution)/shard_map/up_step/pallas_call | solution.py:252
  (80 shorter events, 52.1 us)
Async XLA Ops:
  3.2 9.0 %collective-permute-start = (bf16[128,1024]{1,0:T(8,128)(2,1)S(1)}, bf16[128,1024]{1,0:T(8,128)(2,1)S(1)}, u32[]{:S(2)}, u32[]{:S(2)}) collective-permute-start(bf16[128,1024]{1,0:T(8,128)(2,1)S(1)} %get-tuple-element.57), channel_id=1, source_target_pairs={{0,1},{1,0},{2,3},{3,2},{4,5},{5,4},{6,7},{7,6},{8,9},{9,8},{10,11... | collective-permute-start | bytes 786440 | tf_op jit(solution)/shard_map/ppermute | solution.py:285
  3.3 10.6 %collective-permute-start.2 = (bf16[128,1024]{1,0:T(8,128)(2,1)S(1)}, bf16[128,1024]{1,0:T(8,128)(2,1)S(1)}, u32[]{:S(2)}, u32[]{:S(2)}) collective-permute-start(bf16[128,1024]{1,0:T(8,128)(2,1)S(1)} %get-tuple-element.65), channel_id=1, source_target_pairs={{0,2},{1,3},{2,0},{3,1},{4,6},{5,7},{6,4},{7,5},{8,10},{9,11},{10,... | collective-permute-start | bytes 786440 | tf_op jit(solution)/shard_map/ppermute | solution.py:285
  6.2 12.3 %collective-permute-start.3 = (bf16[128,1024]{1,0:T(8,128)(2,1)S(1)}, bf16[128,1024]{1,0:T(8,128)(2,1)S(1)}, u32[]{:S(2)}, u32[]{:S(2)}) collective-permute-start(bf16[128,1024]{1,0:T(8,128)(2,1)S(1)} %get-tuple-element.66), channel_id=1, source_target_pairs={{0,3},{1,2},{2,1},{3,0},{4,7},{5,6},{6,5},{7,4},{8,11},{9,10},{10,... | collective-permute-start | bytes 786440 | tf_op jit(solution)/shard_map/ppermute | solution.py:285
  6.2 18.3 %collective-permute-start.4 = (bf16[128,1024]{1,0:T(8,128)(2,1)S(1)}, bf16[128,1024]{1,0:T(8,128)(2,1)S(1)}, u32[]{:S(2)}, u32[]{:S(2)}) collective-permute-start(bf16[128,1024]{1,0:T(8,128)(2,1)S(1)} %get-tuple-element.68), channel_id=1, source_target_pairs={{0,2},{1,3},{2,0},{3,1},{4,6},{5,7},{6,4},{7,5},{8,10},{9,11},{10,... | collective-permute-start | bytes 786440 | tf_op jit(solution)/shard_map/ppermute | solution.py:285
  7.6 21.4 %collective-permute-start.5 = (bf16[128,1024]{1,0:T(8,128)(2,1)S(1)}, bf16[128,1024]{1,0:T(8,128)(2,1)S(1)}, u32[]{:S(2)}, u32[]{:S(2)}) collective-permute-start(bf16[128,1024]{1,0:T(8,128)(2,1)S(1)} %get-tuple-element.69), channel_id=1, source_target_pairs={{0,3},{1,2},{2,1},{3,0},{4,7},{5,6},{6,5},{7,4},{8,11},{9,10},{10,... | collective-permute-start | bytes 786440 | tf_op jit(solution)/shard_map/ppermute | solution.py:285
  30.0 9.2 %collective-permute-start.8 = (bf16[256,512]{1,0:T(8,128)(2,1)S(1)}, bf16[256,512]{1,0:T(8,128)(2,1)S(1)}, u32[]{:S(2)}, u32[]{:S(2)}) collective-permute-start(bf16[256,512]{1,0:T(8,128)(2,1)S(1)} %get-tuple-element.74.refs_5_), channel_id=1, source_target_pairs={{0,8},{8,16},{16,24},{24,28},{28,20},{20,12},{12,4},{4,0},{1,9},{9... | collective-permute-start | bytes 786440 | tf_op jit(solution)/shard_map/ppermute | solution.py:319
  31.6 9.1 %collective-permute-start.9 = (bf16[256,512]{1,0:T(8,128)(2,1)S(1)}, bf16[256,512]{1,0:T(8,128)(2,1)S(1)}, u32[]{:S(2)}, u32[]{:S(2)}) collective-permute-start(bf16[256,512]{1,0:T(8,128)(2,1)S(1)} %get-tuple-element.79), channel_id=1, source_target_pairs={{8,0},{16,8},{24,16},{28,24},{20,28},{12,20},{4,12},{0,4},{9,1},{1... | collective-permute-start | bytes 786440 | tf_op jit(solution)/shard_map/ppermute | solution.py:319
  34.6 10.2 %collective-permute-start.6 = (bf16[128,1024]{1,0:T(8,128)(2,1)S(1)}, bf16[128,1024]{1,0:T(8,128)(2,1)S(1)}, u32[]{:S(2)}, u32[]{:S(2)}) collective-permute-start(bf16[128,1024]{1,0:T(8,128)(2,1)S(1)} %get-tuple-element.77.refs_8_), channel_id=1, source_target_pairs={{0,8},{8,16},{16,24},{24,28},{28,20},{20,12},{12,4},{4,0},{1,9},{9... | collective-permute-start | bytes 786440 | tf_op jit(solution)/shard_map/ppermute | solution.py:319
  36.2 10.2 %collective-permute-start.7 = (bf16[128,1024]{1,0:T(8,128)(2,1)S(1)}, bf16[128,1024]{1,0:T(8,128)(2,1)S(1)}, u32[]{:S(2)}, u32[]{:S(2)}) collective-permute-start(bf16[128,1024]{1,0:T(8,128)(2,1)S(1)} %get-tuple-element.78), channel_id=1, source_target_pairs={{8,0},{16,8},{24,16},{28,24},{20,28},{12,20},{4,12},{0,4},{9,1},{1... | collective-permute-start | bytes 786440 | tf_op jit(solution)/shard_map/ppermute | solution.py:319
  41.7 10.8 %collective-permute-start.12 = (bf16[256,512]{1,0:T(8,128)(2,1)S(1)}, bf16[256,512]{1,0:T(8,128)(2,1)S(1)}, u32[]{:S(2)}, u32[]{:S(2)}) collective-permute-start(bf16[256,512]{1,0:T(8,128)(2,1)S(1)} %get-tuple-element.80.refs_6_), channel_id=1, source_target_pairs={{0,8},{8,16},{16,24},{24,28},{28,20},{20,12},{12,4},{4,0},{1,9},{9... | collective-permute-start | bytes 786440 | tf_op jit(solution)/shard_map/ppermute | solution.py:319
  43.3 9.1 %collective-permute-start.13 = (bf16[256,512]{1,0:T(8,128)(2,1)S(1)}, bf16[256,512]{1,0:T(8,128)(2,1)S(1)}, u32[]{:S(2)}, u32[]{:S(2)}) collective-permute-start(bf16[256,512]{1,0:T(8,128)(2,1)S(1)} %get-tuple-element.83), channel_id=1, source_target_pairs={{8,0},{16,8},{24,16},{28,24},{20,28},{12,20},{4,12},{0,4},{9,1},{1... | collective-permute-start | bytes 786440 | tf_op jit(solution)/shard_map/ppermute | solution.py:319
  47.3 9.3 %collective-permute-start.10 = (bf16[128,1024]{1,0:T(8,128)(2,1)S(1)}, bf16[128,1024]{1,0:T(8,128)(2,1)S(1)}, u32[]{:S(2)}, u32[]{:S(2)}) collective-permute-start(bf16[128,1024]{1,0:T(8,128)(2,1)S(1)} %get-tuple-element.81.refs_0_), channel_id=1, source_target_pairs={{0,8},{8,16},{16,24},{24,28},{28,20},{20,12},{12,4},{4,0},{1,9},{9... | collective-permute-start | bytes 786440 | tf_op jit(solution)/shard_map/ppermute | solution.py:319
  48.9 9.2 %collective-permute-start.11 = (bf16[128,1024]{1,0:T(8,128)(2,1)S(1)}, bf16[128,1024]{1,0:T(8,128)(2,1)S(1)}, u32[]{:S(2)}, u32[]{:S(2)}) collective-permute-start(bf16[128,1024]{1,0:T(8,128)(2,1)S(1)} %get-tuple-element.82), channel_id=1, source_target_pairs={{8,0},{16,8},{24,16},{28,24},{20,28},{12,20},{4,12},{0,4},{9,1},{1... | collective-permute-start | bytes 786440 | tf_op jit(solution)/shard_map/ppermute | solution.py:319
  50.9 10.4 %collective-permute-start.18 = (bf16[128,1152]{1,0:T(8,128)(2,1)S(1)}, bf16[128,1152]{1,0:T(8,128)(2,1)S(1)}, u32[]{:S(2)}, u32[]{:S(2)}) collective-permute-start(bf16[128,1152]{1,0:T(8,128)(2,1)S(1)} %feat_grad.4.refs_8_), channel_id=1, source_target_pairs={{0,2},{1,3},{2,0},{3,1},{4,6},{5,7},{6,4},{7,5},{8,10},{9,11},{10,... | collective-permute-start | bytes 884744 | tf_op jit(solution)/shard_map/ppermute | solution.py:356
  53.4 9.4 %collective-permute-start.16 = (bf16[256,512]{1,0:T(8,128)(2,1)S(1)}, bf16[256,512]{1,0:T(8,128)(2,1)S(1)}, u32[]{:S(2)}, u32[]{:S(2)}) collective-permute-start(bf16[256,512]{1,0:T(8,128)(2,1)S(1)} %get-tuple-element.84.refs_6_), channel_id=1, source_target_pairs={{0,8},{8,16},{16,24},{24,28},{28,20},{20,12},{12,4},{4,0},{1,9},{9... | collective-permute-start | bytes 786440 | tf_op jit(solution)/shard_map/ppermute | solution.py:319
  55.1 9.2 %collective-permute-start.17 = (bf16[256,512]{1,0:T(8,128)(2,1)S(1)}, bf16[256,512]{1,0:T(8,128)(2,1)S(1)}, u32[]{:S(2)}, u32[]{:S(2)}) collective-permute-start(bf16[256,512]{1,0:T(8,128)(2,1)S(1)} %get-tuple-element.87), channel_id=1, source_target_pairs={{8,0},{16,8},{24,16},{28,24},{20,28},{12,20},{4,12},{0,4},{9,1},{1... | collective-permute-start | bytes 786440 | tf_op jit(solution)/shard_map/ppermute | solution.py:319
  62.8 9.3 %collective-permute-start.23 = (bf16[128,1152]{1,0:T(8,128)(2,1)S(1)}, bf16[128,1152]{1,0:T(8,128)(2,1)S(1)}, u32[]{:S(2)}, u32[]{:S(2)}) collective-permute-start(bf16[128,1152]{1,0:T(8,128)(2,1)S(1)} %feat_grad.5.refs_8_), channel_id=1, source_target_pairs={{0,3},{1,2},{2,1},{3,0},{4,7},{5,6},{6,5},{7,4},{8,11},{9,10},{10,... | collective-permute-start | bytes 884744 | tf_op jit(solution)/shard_map/ppermute | solution.py:356
  65.3 9.2 %collective-permute-start.21 = (bf16[256,512]{1,0:T(8,128)(2,1)S(1)}, bf16[256,512]{1,0:T(8,128)(2,1)S(1)}, u32[]{:S(2)}, u32[]{:S(2)}) collective-permute-start(bf16[256,512]{1,0:T(8,128)(2,1)S(1)} %get-tuple-element.88.refs_6_), channel_id=1, source_target_pairs={{0,8},{8,16},{16,24},{24,28},{28,20},{20,12},{12,4},{4,0},{1,9},{9... | collective-permute-start | bytes 786440 | tf_op jit(solution)/shard_map/ppermute | solution.py:319
  66.5 9.1 %collective-permute-start.22 = (bf16[256,512]{1,0:T(8,128)(2,1)S(1)}, bf16[256,512]{1,0:T(8,128)(2,1)S(1)}, u32[]{:S(2)}, u32[]{:S(2)}) collective-permute-start(bf16[256,512]{1,0:T(8,128)(2,1)S(1)} %get-tuple-element.91), channel_id=1, source_target_pairs={{8,0},{16,8},{24,16},{28,24},{20,28},{12,20},{4,12},{0,4},{9,1},{1... | collective-permute-start | bytes 786440 | tf_op jit(solution)/shard_map/ppermute | solution.py:319
  69.3 10.8 %collective-permute-start.19 = (bf16[128,1024]{1,0:T(8,128)(2,1)S(1)}, bf16[128,1024]{1,0:T(8,128)(2,1)S(1)}, u32[]{:S(2)}, u32[]{:S(2)}) collective-permute-start(bf16[128,1024]{1,0:T(8,128)(2,1)S(1)} %get-tuple-element.89.refs_0_), channel_id=1, source_target_pairs={{0,8},{8,16},{16,24},{24,28},{28,20},{20,12},{12,4},{4,0},{1,9},{9... | collective-permute-start | bytes 786440 | tf_op jit(solution)/shard_map/ppermute | solution.py:319
  70.9 10.3 %collective-permute-start.20 = (bf16[128,1024]{1,0:T(8,128)(2,1)S(1)}, bf16[128,1024]{1,0:T(8,128)(2,1)S(1)}, u32[]{:S(2)}, u32[]{:S(2)}) collective-permute-start(bf16[128,1024]{1,0:T(8,128)(2,1)S(1)} %get-tuple-element.90), channel_id=1, source_target_pairs={{8,0},{16,8},{24,16},{28,24},{20,28},{12,20},{4,12},{0,4},{9,1},{1... | collective-permute-start | bytes 786440 | tf_op jit(solution)/shard_map/ppermute | solution.py:319
  73.6 10.7 %collective-permute-start.24 = (bf16[128,1152]{1,0:T(8,128)(2,1)S(1)}, bf16[128,1152]{1,0:T(8,128)(2,1)S(1)}, u32[]{:S(2)}, u32[]{:S(2)}) collective-permute-start(bf16[128,1152]{1,0:T(8,128)(2,1)S(1)} %feat_grad.6.refs_8_), channel_id=1, source_target_pairs={{0,1},{1,0},{2,3},{3,2},{4,5},{5,4},{6,7},{7,6},{8,9},{9,8},{10,11... | collective-permute-start | bytes 884744 | tf_op jit(solution)/shard_map/ppermute | solution.py:356
  76.6 9.3 %collective-permute-start.27 = (bf16[256,512]{1,0:T(8,128)(2,1)S(1)}, bf16[256,512]{1,0:T(8,128)(2,1)S(1)}, u32[]{:S(2)}, u32[]{:S(2)}) collective-permute-start(bf16[256,512]{1,0:T(8,128)(2,1)S(1)} %get-tuple-element.92.refs_6_), channel_id=1, source_target_pairs={{0,8},{8,16},{16,24},{24,28},{28,20},{20,12},{12,4},{4,0},{1,9},{9... | collective-permute-start | bytes 786440 | tf_op jit(solution)/shard_map/ppermute | solution.py:319
  78.1 9.2 %collective-permute-start.28 = (bf16[256,512]{1,0:T(8,128)(2,1)S(1)}, bf16[256,512]{1,0:T(8,128)(2,1)S(1)}, u32[]{:S(2)}, u32[]{:S(2)}) collective-permute-start(bf16[256,512]{1,0:T(8,128)(2,1)S(1)} %get-tuple-element.95), channel_id=1, source_target_pairs={{8,0},{16,8},{24,16},{28,24},{20,28},{12,20},{4,12},{0,4},{9,1},{1... | collective-permute-start | bytes 786440 | tf_op jit(solution)/shard_map/ppermute | solution.py:319
  82.3 9.3 %collective-permute-start.25 = (bf16[128,1024]{1,0:T(8,128)(2,1)S(1)}, bf16[128,1024]{1,0:T(8,128)(2,1)S(1)}, u32[]{:S(2)}, u32[]{:S(2)}) collective-permute-start(bf16[128,1024]{1,0:T(8,128)(2,1)S(1)} %get-tuple-element.93.refs_0_), channel_id=1, source_target_pairs={{0,8},{8,16},{16,24},{24,28},{28,20},{20,12},{12,4},{4,0},{1,9},{9... | collective-permute-start | bytes 786440 | tf_op jit(solution)/shard_map/ppermute | solution.py:319
  83.7 9.2 %collective-permute-start.26 = (bf16[128,1024]{1,0:T(8,128)(2,1)S(1)}, bf16[128,1024]{1,0:T(8,128)(2,1)S(1)}, u32[]{:S(2)}, u32[]{:S(2)}) collective-permute-start(bf16[128,1024]{1,0:T(8,128)(2,1)S(1)} %get-tuple-element.94), channel_id=1, source_target_pairs={{8,0},{16,8},{24,16},{28,24},{20,28},{12,20},{4,12},{0,4},{9,1},{1... | collective-permute-start | bytes 786440 | tf_op jit(solution)/shard_map/ppermute | solution.py:319
  88.3 9.3 %collective-permute-start.31 = (bf16[256,512]{1,0:T(8,128)(2,1)S(1)}, bf16[256,512]{1,0:T(8,128)(2,1)S(1)}, u32[]{:S(2)}, u32[]{:S(2)}) collective-permute-start(bf16[256,512]{1,0:T(8,128)(2,1)S(1)} %get-tuple-element.96.refs_6_), channel_id=1, source_target_pairs={{0,8},{8,16},{16,24},{24,28},{28,20},{20,12},{12,4},{4,0},{1,9},{9... | collective-permute-start | bytes 786440 | tf_op jit(solution)/shard_map/ppermute | solution.py:319
  89.3 9.2 %collective-permute-start.32 = (bf16[256,512]{1,0:T(8,128)(2,1)S(1)}, bf16[256,512]{1,0:T(8,128)(2,1)S(1)}, u32[]{:S(2)}, u32[]{:S(2)}) collective-permute-start(bf16[256,512]{1,0:T(8,128)(2,1)S(1)} %get-tuple-element.99), channel_id=1, source_target_pairs={{8,0},{16,8},{24,16},{28,24},{20,28},{12,20},{4,12},{0,4},{9,1},{1... | collective-permute-start | bytes 786440 | tf_op jit(solution)/shard_map/ppermute | solution.py:319
  94.0 9.3 %collective-permute-start.29 = (bf16[128,1024]{1,0:T(8,128)(2,1)S(1)}, bf16[128,1024]{1,0:T(8,128)(2,1)S(1)}, u32[]{:S(2)}, u32[]{:S(2)}) collective-permute-start(bf16[128,1024]{1,0:T(8,128)(2,1)S(1)} %get-tuple-element.97.refs_8_), channel_id=1, source_target_pairs={{0,8},{8,16},{16,24},{24,28},{28,20},{20,12},{12,4},{4,0},{1,9},{9... | collective-permute-start | bytes 786440 | tf_op jit(solution)/shard_map/ppermute | solution.py:319
  95.1 9.2 %collective-permute-start.30 = (bf16[128,1024]{1,0:T(8,128)(2,1)S(1)}, bf16[128,1024]{1,0:T(8,128)(2,1)S(1)}, u32[]{:S(2)}, u32[]{:S(2)}) collective-permute-start(bf16[128,1024]{1,0:T(8,128)(2,1)S(1)} %get-tuple-element.98), channel_id=1, source_target_pairs={{8,0},{16,8},{24,16},{28,24},{20,28},{12,20},{4,12},{0,4},{9,1},{1... | collective-permute-start | bytes 786440 | tf_op jit(solution)/shard_map/ppermute | solution.py:319
  99.6 10.2 %collective-permute-start.35 = (bf16[256,512]{1,0:T(8,128)(2,1)S(1)}, bf16[256,512]{1,0:T(8,128)(2,1)S(1)}, u32[]{:S(2)}, u32[]{:S(2)}) collective-permute-start(bf16[256,512]{1,0:T(8,128)(2,1)S(1)} %get-tuple-element.100.refs_6_), channel_id=1, source_target_pairs={{0,8},{8,16},{16,24},{24,28},{28,20},{20,12},{12,4},{4,0},{1,9},{9... | collective-permute-start | bytes 786440 | tf_op jit(solution)/shard_map/ppermute | solution.py:319
  100.7 9.3 %collective-permute-start.36 = (bf16[256,512]{1,0:T(8,128)(2,1)S(1)}, bf16[256,512]{1,0:T(8,128)(2,1)S(1)}, u32[]{:S(2)}, u32[]{:S(2)}) collective-permute-start(bf16[256,512]{1,0:T(8,128)(2,1)S(1)} %get-tuple-element.105), channel_id=1, source_target_pairs={{8,0},{16,8},{24,16},{28,24},{20,28},{12,20},{4,12},{0,4},{9,1},{1... | collective-permute-start | bytes 786440 | tf_op jit(solution)/shard_map/ppermute | solution.py:319
  (9 other events, 61.1 us)

commit v3 on v2

--- a/solution.py
+++ b/solution.py
@@ -10,7 +10,7 @@
 SQRT_HALF = 0.7071067811865476
 INV_ROOT_TAU = 0.3989422804014327
 LANES = 128
-VMEM_LIMIT = 40 * 1024 * 1024
+VMEM_LIMIT = 16 * 1024 * 1024
 F32 = jnp.float32
 BF16 = jnp.bfloat16
 WHOLE = pl.BlockSpec(memory_space=pltpu.VMEM)
@@ -47,7 +47,12 @@
     return (id_row ^ me) * capacity + position
 
 
-def pack_kernel(experts, capacity, me_ref, *refs):
+def pick_rows(slot, block, capacity, value):
+    row = lax.broadcasted_iota(jnp.int32, (capacity, slot.shape[1]), 0) + block * capacity
+    return jnp.where(row == slot, value, 0.0).astype(BF16)
+
+
+def pack_kernel(experts, capacity, near, *refs):
     sources, refs = refs[:4], refs[4:]
     slot_ref, outs = refs[0], refs[1:-5]
     held, sems = refs[-5:-1], refs[-1]
@@ -57,24 +62,24 @@
     ]
     for copy in copies:
         copy.start()
-    id_ref, tokens_ref, gate_ref, grad_ref = held
+    id_ref, gate_ref, grad_ref, tokens_ref = held
     copies[0].wait()
     count = id_ref.shape[0]
-    slot = slot_row(id_ref[...].reshape(1, count), experts, capacity, me_ref[0])
+    slot = slot_row(id_ref[...].reshape(1, count), experts, capacity, lax.axis_index("expert"))
     slot_ref[...] = slot
-    peers = len(outs) // 2
-    copies[1].wait()
-    for block in range(peers):
-        row = lax.broadcasted_iota(jnp.int32, (capacity, count), 0) + block * capacity
-        pick = jnp.where(row == slot, 1.0, 0.0).astype(BF16)
-        outs[block][...] = dot(pick, tokens_ref[...], 1, 0).astype(BF16)
-    copies[2].wait()
-    copies[3].wait()
+    for copy in copies[1:]:
+        copy.wait()
     gate = gate_ref[...].astype(F32).reshape(1, count)
-    for block in range(peers):
-        row = lax.broadcasted_iota(jnp.int32, (capacity, count), 0) + block * capacity
-        pick = jnp.where(row == slot, gate, 0.0).astype(BF16)
-        outs[peers + block][...] = dot(pick, grad_ref[...], 1, 0).astype(BF16)
+    for block, out in enumerate(outs[near:]):
+        out[...] = dot(pick_rows(slot, block, capacity, gate), grad_ref[...], 1, 0).astype(BF16)
+    for block, out in enumerate(outs[:near]):
+        out[...] = dot(pick_rows(slot, block, capacity, 1.0), tokens_ref[...], 1, 0).astype(BF16)
+
+
+def repack_kernel(experts, capacity, id_ref, tokens_ref, _, *outs):
+    slot = slot_row(id_ref[...], experts, capacity, lax.axis_index("expert"))
+    for block, out in enumerate(outs):
+        out[...] = dot(pick_rows(slot, block, capacity, 1.0), tokens_ref[...], 1, 0).astype(BF16)
 
 
 def unpack_kernel(capacity, width, peers, slot_ref, *refs):
@@ -188,13 +193,16 @@
     )[0]
 
 
-def ring_index(position, count):
-    half = count // 2
-    return jnp.where(position < half, 2 * position, 2 * (count - 1 - position) + 1)
-
-
-def ring_position(index, count):
-    return jnp.where(index % 2 == 0, index // 2, count - 1 - index // 2)
+def ring_chunk(step, count):
+    index = lax.axis_index("dp")
+    half = lax.div(index, 2)
+    place = jnp.where(lax.rem(index, 2) == 0, half, count - 1 - half)
+    chunks = []
+    for move in (count - step, step):
+        position = lax.rem(place + move, count)
+        mirror = 2 * (count - 1 - position) + 1
+        chunks.append(jnp.where(position < count // 2, 2 * position, mirror))
+    return chunks
 
 
 def ring_pairs(count):
@@ -203,65 +211,65 @@
     return [(ring[p], ring[(p + 1) % count]) for p in range(count)]
 
 
-def step_kernel(parts, arrivals, step, count, order_ref, *refs):
+def step_kernel(parts, arrivals, step, count, last, *refs):
     groups = len(parts)
     lefts, refs = refs[:groups], refs[groups:]
-    last = step == count
-    if last:
-        out, held, sems = refs[-3:]
-    else:
-        outs = refs[-2:]
-    half = refs[0].shape[1] // 2
-    rows = lefts[0].shape[0] // count
-    totals = [ref[...].astype(F32) for ref in refs[sum(parts) : sum(parts) + arrivals]] or [0.0] * 2
+    rights, refs = refs[: sum(parts)], refs[sum(parts) :]
+    totals = [0.0, 0.0]
+    chunks = ring_chunk(step, count) if groups else None
+    for i, ref in enumerate(refs[:arrivals]):
+        totals[i % 2] += ref[...].astype(F32)
     for left, blocks in zip(lefts, parts):
-        right = [ref[...] for ref in refs[:blocks]]
+        right = [ref[...] for ref in rights[:blocks]]
         right = right[0] if blocks == 1 else jnp.concatenate(right, axis=0)
-        refs = refs[blocks:]
+        rights = rights[blocks:]
+        half = right.shape[1] // 2
+        rows = left.shape[0] // count
         for way in range(2):
-            start = pl.multiple_of(order_ref[way, step - 1] * rows, rows)
+            start = pl.multiple_of(chunks[way] * rows, rows)
             totals[way] += dot(
                 left[pl.ds(start, rows), :], right[:, way * half : (way + 1) * half], 1, 0
             )
+    if not last:
+        for way, out in enumerate(refs[-2:]):
+            out[...] = totals[way].astype(out.dtype)
+        return
+    out, held, sems = refs[-3:]
+    half = held.shape[2]
     copies = []
     for way in range(2):
-        if last:
-            held[way] = totals[way] * (1.0 / count)
-            target = out.at[0, :, way * half : (way + 1) * half]
-            copies.append(pltpu.make_async_copy(held.at[way], target, sems.at[way]))
-            copies[-1].start()
-        else:
-            outs[way][...] = totals[way].astype(BF16)
+        held[way] = totals[way] * (1.0 / count)
+        target = out.at[0, :, way * half : (way + 1) * half]
+        copies.append(pltpu.make_async_copy(held.at[way], target, sems.at[way]))
+        copies[-1].start()
     for copy in copies:
         copy.wait()
 
 
-def ring_step(name, order, step, count, lefts, rights, arrived, after=()):
-    rows = lefts[0].shape[0] // count
-    width = rights[0][0].shape[1]
-    if step == count:
+def ring_step(name, step, count, shape, lefts, rights, arrived, after=(), dtype=BF16):
+    rows, half = shape
+    last = dtype is None
+    if last:
         out_specs = [pl.BlockSpec(memory_space=pltpu.HBM)]
-        out_shape = [pltpu.HBM((1, rows, width), F32)]
-        scratch = [pltpu.VMEM((2, rows, width // 2), F32), pltpu.SemaphoreType.DMA((2,))]
+        out_shape = [pltpu.HBM((1, rows, 2 * half), F32)]
+        scratch = [pltpu.VMEM((2, rows, half), F32), pltpu.SemaphoreType.DMA((2,))]
     else:
         out_specs = [WHOLE] * 2
-        out_shape = [jax.ShapeDtypeStruct((rows, width // 2), BF16)] * 2
+        out_shape = [jax.ShapeDtypeStruct(shape, dtype)] * 2
         scratch = []
     blocks = [block for group in rights for block in group]
     inputs = [*lefts, *blocks, *arrived]
     return pl.pallas_call(
         functools.partial(
-            step_kernel, [len(group) for group in rights], len(arrived), step, count
+            step_kernel, [len(group) for group in rights], len(arrived), step, count, last
         ),
-        in_specs=[pl.BlockSpec(memory_space=pltpu.SMEM)]
-        + [WHOLE] * len(inputs)
-        + [LATER] * len(after),
+        in_specs=[WHOLE] * len(inputs) + [LATER] * len(after),
         out_specs=out_specs,
         out_shape=out_shape,
         scratch_shapes=scratch,
         compiler_params=params(),
         name=name,
-    )(order, *inputs, *after)
+    )(*inputs, *after)
 
 
 def per_device(tokens, out_grad, gate_prob, expert_id, up_weight, down_weight):
@@ -271,49 +279,86 @@
     experts = peers * up_weight.shape[0]
     capacity = 2 * count // experts
     ring = lax.axis_size("dp")
-    me = lax.axis_index("expert")
     sources = [[(i, i ^ k) for i in range(peers)] for k in range(peers)]
     forward = ring_pairs(ring)
     backward = [(b, a) for a, b in forward]
-    place = ring_position(lax.axis_index("dp"), ring)
-    steps = jnp.arange(1, ring + 1, dtype=jnp.int32)
-    order = ring_index(
-        jnp.stack([(place - steps) % ring, (place + steps) % ring]), ring
-    ).astype(jnp.int32)
 
     def exchange(outs, reach):
         return {k: lax.ppermute(outs[k], "expert", sources[k]) for k in reach}
 
     near, far = range(1, peers // 2), range(peers // 2, peers)
     hbm = pl.BlockSpec(memory_space=pltpu.HBM)
+    across = [(i, i ^ peers // 2) for i in range(peers)]
+    tokens_across = lax.ppermute(tokens, "expert", across)
+    id_across = lax.ppermute(expert_id.reshape(1, count), "expert", across)
+
+    block_shape = jax.ShapeDtypeStruct((capacity, width), BF16)
     slot, *packed = pl.pallas_call(
-        functools.partial(pack_kernel, experts, capacity),
-        in_specs=[pl.BlockSpec(memory_space=pltpu.SMEM)] + [hbm] * 4,
-        out_specs=[WHOLE] * (1 + 2 * peers),
+        functools.partial(pack_kernel, experts, capacity, peers // 2),
+        in_specs=[hbm] * 4,
+        out_specs=[WHOLE] * (1 + peers // 2 + peers),
         out_shape=[jax.ShapeDtypeStruct((1, count), jnp.int32)]
-        + [jax.ShapeDtypeStruct((capacity, width), BF16)] * (2 * peers),
+        + [block_shape] * (peers // 2 + peers),
         scratch_shapes=[
             pltpu.VMEM((count,), jnp.int32),
+            pltpu.VMEM((count,), BF16),
             pltpu.VMEM((count, width), BF16),
-            pltpu.VMEM((count,), BF16),
             pltpu.VMEM((count, width), BF16),
             pltpu.SemaphoreType.DMA((4,)),
         ],
         compiler_params=params(),
         name="pack",
-    )(me.reshape(1), *(in_hbm(a) for a in (expert_id, tokens, gate_prob, out_grad)))
-    feat_out, grad_out = packed[:peers], packed[peers:]
-    feat_in = {0: feat_out[0], **exchange(feat_out, far), **exchange(feat_out, near)}
+    )(*(in_hbm(a) for a in (expert_id, gate_prob, out_grad, tokens)))
+    feat_out, grad_out = packed[: peers // 2], packed[peers // 2 :]
     grad_in = {0: grad_out[0], **exchange(grad_out, far), **exchange(grad_out, near)}
-
-    groups = [[0, *near], [*far]]
-    feats = [[feat_in[k] for k in group] for group in groups]
+    feat_in = {0: feat_out[0], **exchange(feat_out, near)}
+    groups = [[0, *near], [peers // 2], [*far][1:]]
+    groups = [group for group in groups if group]
     scaleds = [[grad_in[k] for k in group] for group in groups]
-    near_hidden = hidden_call(feats[0], up_weight)
-    near_pre = pre_grad_call(scaleds[0], down_weight, near_hidden[1], near_hidden[3])
-    far_hidden = hidden_call(feats[1], up_weight, [near_pre[1]])
-    flip_feats = [near_hidden[0], far_hidden[0]]
-    flip_hiddens = [near_hidden[2], far_hidden[2]]
+    hiddens, pre_grads, sums = [], [], []
+
+    def add_hidden(blocks, after=()):
+        hiddens.append(hidden_call(blocks, up_weight, after))
+        return [hiddens[-1][1]]
+
+    def add_pre_grad(after=()):
+        group = len(pre_grads)
+        _, hidden, _, slope = hiddens[group]
+        pre, total = pre_grad_call(scaleds[group], down_weight, hidden, slope, after)
+        pre_grads.append([pre])
+        sums.append(total)
+        return [total]
+
+    add_hidden([feat_in[k] for k in groups[0]])
+    after = add_pre_grad()
+    across_out = pl.pallas_call(
+        functools.partial(repack_kernel, experts, capacity),
+        in_specs=[WHOLE, WHOLE, LATER],
+        out_specs=[WHOLE] * (peers // 2),
+        out_shape=[block_shape] * (peers // 2),
+        compiler_params=params(),
+        name="repack",
+    )(id_across, tokens_across, *after)
+    across_in = exchange(across_out, near)
+    after = add_hidden(across_out[:1])
+    if len(groups) > 2:
+        after = add_pre_grad(after)
+        after = add_hidden([across_in[k] for k in near], after)
+    flip_feats = [part[0] for part in hiddens]
+    flip_hiddens = [part[2] for part in hiddens]
+    down_shape = (inner // ring, width // 2)
+    up_shape = (width // ring, inner // 2)
+    down_in = ring_step(
+        "down_early",
+        1,
+        ring,
+        down_shape,
+        flip_hiddens[:-1],
+        scaleds[:-1],
+        [],
+        after,
+        F32,
+    )
 
     def send(pair):
         return [lax.ppermute(pair[0], "dp", forward), lax.ppermute(pair[1], "dp", backward)]
@@ -322,32 +367,37 @@
     span = min(4, ring - turn)
     returns = [*far, *near, 0]
     feat_back = {}
-    down_in, up_in, after, landed = [], [], [], []
-    for step in range(1, ring + 1):
-        down = ring_step("down_step", order, step, ring, flip_hiddens, scaleds, down_in, after)
-        if step < ring:
-            down_in = send(down)
-            after = [down[0]]
-        else:
-            after = []
+    up_in, after, landed = [], [], []
+    for step in range(1, ring):
+        late = slice(-1, None) if step == 1 else slice(None)
+        down = ring_step(
+            "down_step",
+                step,
+            ring,
+            down_shape,
+            flip_hiddens[late],
+            scaleds[late],
+            down_in,
+            after,
+        )
+        down_in = send(down)
+        after = [*down]
         if step == 1:
-            far_pre = pre_grad_call(scaleds[1], down_weight, far_hidden[1], far_hidden[3], after)
-            pre_grads = [[near_pre[0]], [far_pre[0]]]
-            after = [far_pre[1]]
-        up = ring_step("up_step", order, step, ring, flip_feats, pre_grads, up_in, after)
-        if step < ring:
-            up_in = send(up)
-            after = [up[0]]
-        after = after + landed
+            after = add_pre_grad(after)
+        up = ring_step(
+            "up_step", step, ring, up_shape, flip_feats, pre_grads, up_in, after
+        )
+        up_in = send(up)
+        after = [*up] + landed
         landed = []
         first = (step - turn) * len(returns) // span
         stop = (step - turn + 1) * len(returns) // span
         for k in returns[max(first, 0) : max(stop, 0)]:
-            group = int(k in far)
+            group = [k in members for members in groups].index(True)
             block = feat_grad_call(
                 pre_grads[group][0],
                 up_weight,
-                (near_pre, far_pre)[group][1],
+                sums[group],
                 groups[group].index(k),
                 capacity,
                 after,
@@ -355,19 +405,48 @@
             after = [block]
             feat_back[k] = lax.ppermute(block, "expert", sources[k]) if k else block
             landed.append(feat_back[k])
-        if step == ring - 1:
-            tokens_grad, gate_sums = pl.pallas_call(
-                functools.partial(unpack_kernel, capacity, width, peers),
-                in_specs=[WHOLE] * (1 + peers) + [LATER] * len(after),
-                out_specs=[WHOLE] * 2,
-                out_shape=[
-                    jax.ShapeDtypeStruct((count, width), BF16),
-                    jax.ShapeDtypeStruct((count, LANES), F32),
-                ],
-                compiler_params=params(),
-                name="unpack",
-            )(slot, *(feat_back[k] for k in range(peers)), *after)
-            after = [gate_sums]
+        if step == max(ring - 2, 1):
+            down_last = ring_step(
+                "down_own",
+                        ring,
+                ring,
+                down_shape,
+                flip_hiddens,
+                scaleds,
+                [],
+                after,
+                F32,
+            )
+            up_last = ring_step(
+                "up_own",
+                        ring,
+                ring,
+                up_shape,
+                flip_feats,
+                pre_grads,
+                [],
+                down_last[:1],
+                F32,
+            )
+            after = up_last[:1]
+    down = ring_step(
+        "down_last", ring, ring, down_shape, [], [], [*down_in, *down_last], [], None
+    )
+    after_down = [in_hbm(down[0])]
+    up = ring_step(
+        "up_last", ring, ring, up_shape, [], [], [*up_in, *up_last], after_down, None
+    )
+    tokens_grad, gate_sums = pl.pallas_call(
+        functools.partial(unpack_kernel, capacity, width, peers),
+        in_specs=[WHOLE] * (1 + peers) + [LATER] * len(after),
+        out_specs=[WHOLE] * 2,
+        out_shape=[
+            jax.ShapeDtypeStruct((count, width), BF16),
+            jax.ShapeDtypeStruct((count, LANES), F32),
+        ],
+        compiler_params=params(),
+        name="unpack",
+    )(slot, *(feat_back[k] for k in range(peers)), *after)
     gate_result = ((gate_sums[:, 0] + gate_sums[:, 1]) / gate_prob.astype(F32)).astype(BF16)
     return (tokens_grad, gate_result, up[0], down[0])
 

time: 117 us -> 111 us (0.949)
  Pallas kernels: 34.3 us -> 30.2 us
  waiting for transfers between devices: 41.7 us -> 38.1 us
  starting transfers between devices: 36.2 us -> 38.8 us
    ppermute x6 -> x5, waiting for transfers between devices: 13.1 us -> 2.74 us  [exchange(): return {k: lax.ppermute(outs[k], 'expert', sources[k]) for k in reach}]
    pallas_call x16 -> x19, Pallas kernels: 17.7 us -> 11.4 us  [ring_step(): pl.pallas_call(functools.partial(step_kernel, [len(group) for group in ri...]
    ppermute x14, waiting for transfers between devices: 15.6 us -> 19.2 us  [send(): lax.ppermute(pair[1], 'dp', backward)]
    ppermute x0 -> x2, starting transfers between devices: none -> 3.02 us  [the longest x1 3 us: per_device(): tokens_across = lax.ppermute(tokens, 'expert', across)]
    ppermute x0 -> x2, waiting for transfers between devices: none -> 2.65 us  [the longest x1 2.65 us: per_device(): id_across = lax.ppermute(expert_id.reshape(1, count), 'expert', across)]
    ppermute x14, starting transfers between devices: 9.41 us -> 7.01 us  [send(): lax.ppermute(pair[1], 'dp', backward)]
    ppermute x14, starting transfers between devices: 19.7 us -> 22.1 us  [send(): lax.ppermute(pair[0], 'dp', forward)]
    pallas_call x8 -> x10, Pallas kernels: 13 us -> 14.9 us  [call(): pl.pallas_call(body, in_specs=[WHOLE] * len(inputs) + [LATER] * len(after...]
  transfers between devices with their start and end apart: 37 -> 38, of which waited for: 27 -> 29; matrix products, arithmetic and copies ran while one was open for 1% -> 1% of each run, Pallas kernels for 25% -> 26%
where the time goes in v3:
time: 111 us
  starting transfers between devices  38.8 us (35%)
  waiting for transfers between devices  38.1 us (34%)
  Pallas kernels  30.2 us (27%)
  local copies, waits for them, and re-layouts  2.34 us (2%)
    ppermute x14, starting transfers between devices, send(): lax.ppermute(pair[0], 'dp', forward)  22.1 us
    ppermute x14, waiting for transfers between devices, send(): lax.ppermute(pair[1], 'dp', backward)  19.2 us
    pallas_call x10, Pallas kernels, call(): pl.pallas_call(body, in_specs=[WHOLE] * len(inputs) + [LATER] * len(after...  14.9 us
    ppermute x14, waiting for transfers between devices, send(): lax.ppermute(pair[0], 'dp', forward)  13.1 us
    pallas_call x19, Pallas kernels, ring_step(): pl.pallas_call(functools.partial(step_kernel, [len(group) for group in ri...  11.4 us
    ppermute x14, starting transfers between devices, send(): lax.ppermute(pair[1], 'dp', backward)  7.01 us
    ppermute x5, starting transfers between devices, exchange(): return {k: lax.ppermute(outs[k], 'expert', sources[k]) for k in reach}  4.83 us
    ppermute x1, starting transfers between devices, per_device(): tokens_across = lax.ppermute(tokens, 'expert', across)  3 us
  transfers between devices with their start and end apart: 38, of which 29 were waited for; matrix products, arithmetic and copies ran while one was open for 1% of the time, Pallas kernels for 26%

profile of v3, /device:TPU:0, one launch (start us, length us, event | category | flops | bytes accessed | tf_op | source)
XLA Modules:
  0.0 111.2 jit_solution(9315525964963073204)
XLA Ops:
  0.6 3.0 %collective-permute-start.3 = (bf16[256,1024]{1,0:T(8,128)(2,1)}, bf16[256,1024]{1,0:T(8,128)(2,1)S(1)}, u32[]{:S(2)}, u32[]{:S(2)}) collective-permute-start(bf16[256,1024]{1,0:T(8,128)(2,1)} %refs_3_.1), channel_id=1, source_target_pairs={{0,2},{1,3},{2,0},{3,1},{4,6},{5,7},{6,4},{7,5},{8,10},{9,11},{10,... | collective-permute-start | bytes 1572872 | tf_op jit(solution)/shard_map/ppermute | solution.py:292
  3.6 1.9 %pack.1 = (s32[1,256]{1,0:T(1,128)S(1)}, bf16[128,1024]{1,0:T(8,128)(2,1)S(1)}, bf16[128,1024]{1,0:T(8,128)(2,1)S(1)}, bf16[128,1024]{1,0:T(8,128)(2,1)S(1)}, bf...) custom-call(s32[256]{0:T(256)} %refs_0_.1, bf16[256]{0:T(256)(128)(2,1)} %refs_1_.5, ...), custom_call_target="tpu_custom_call" | custom-call | tf_op jit(solution)/shard_map/pack/pallas_call | solution.py:296
  6.1 2.0 %collective-permute-start.5 = (bf16[128,1024]{1,0:T(8,128)(2,1)S(1)}, bf16[128,1024]{1,0:T(8,128)(2,1)S(1)}, u32[]{:S(2)}, u32[]{:S(2)}) collective-permute-start(bf16[128,1024]{1,0:T(8,128)(2,1)S(1)} %get-tuple-element.80), channel_id=1, source_target_pairs={{0,2},{1,3},{2,0},{3,1},{4,6},{5,7},{6,4},{7,5},{8,10},{9,11},{10,... | collective-permute-start | bytes 786440 | tf_op jit(solution)/shard_map/ppermute | solution.py:287
  8.1 2.2 %copy-done = bf16[1,1024,2048]{2,1,0:T(8,128)(2,1)S(1)} copy-done((bf16[1,1024,2048]{2,1,0:T(8,128)(2,1)S(1)}, bf16[1,1024,2048]{2,1,0:T(8,128)(2,1)}, u32[]{:S(2)}) %copy-start) | copy-done | bytes 4194328
  10.3 2.0 %hidden.3 = (bf16[1024,256]{1,0:T(8,128)(2,1)S(1)}, bf16[256,2048]{1,0:T(8,128)(2,1)S(1)}, bf16[2048,256]{1,0:T(8,128)(2,1)S(1)}, bf16[256,2048]{1,0:T(8,128)(2,1)S(1)}) custom-call(bf16[128,1024]{1,0:T(8,128)(2,1)S(1)} %get-tuple-element.70.refs_0_, bf16[128,1024]{1,0:T(8,128)(2,1)S(1)} %collective-permute-done.1.refs_1_, bf16[1,1024,2048]{2,1,0:T(8,128)(2,1)S(1)} %copy-done), custom_call_target="tpu_custom_call" | custom-call | tf_op jit(solution)/shard_map/hidden/pallas_call | solution.py:100
  14.0 2.7 %collective-permute-done.2.id_ref = s32[1,256]{1,0:T(1,128)S(1)} collective-permute-done((s32[1,256]{1,0:T(1,128)}, s32[1,256]{1,0:T(1,128)S(1)}, u32[]{:S(2)}, u32[]{:S(2)}) %collective-permute-start.2) | collective-permute-done | bytes 1056 | tf_op jit(solution)/shard_map/ppermute | solution.py:293
  17.2 2.2 %collective-permute-start.6 = (bf16[128,1024]{1,0:T(8,128)(2,1)S(1)}, bf16[128,1024]{1,0:T(8,128)(2,1)S(1)}, u32[]{:S(2)}, u32[]{:S(2)}) collective-permute-start(bf16[128,1024]{1,0:T(8,128)(2,1)S(1)} %get-tuple-element.86), channel_id=1, source_target_pairs={{0,3},{1,2},{2,1},{3,0},{4,7},{5,6},{6,5},{7,4},{8,11},{9,10},{10,... | collective-permute-start | bytes 786440 | tf_op jit(solution)/shard_map/ppermute | solution.py:287
  20.4 1.7 %collective-permute-done.5.refs_0_.refs_4_.refs_5_ = bf16[128,1024]{1,0:T(8,128)(2,1)S(1)} collective-permute-done((bf16[128,1024]{1,0:T(8,128)(2,1)S(1)}, bf16[128,1024]{1,0:T(8,128)(2,1)S(1)}, u32[]{:S(2)}, u32[]{:S(2)}) %collective-permute-start.5) | collective-permute-done | bytes 262176 | tf_op jit(solution)/shard_map/ppermute | solution.py:287
  22.1 1.6 %pre_grad.4 = (bf16[128,2048]{1,0:T(8,128)(2,1)S(1)}, f32[128,128]{1,0:T(8,128)S(1)}) custom-call(bf16[128,1024]{1,0:T(8,128)(2,1)S(1)} %collective-permute-done.5.refs_0_.refs_4_.refs_5_, bf16[1,2048,1024]{2,1,0:T(8,128)(2,1)S(1)} %copy-done.2, bf16[128,2048]{1,0:T(8,128)(2,1)S(1)} %get-tuple-element.81.refs_2_.refs_4_, ...), custom_call_target="tpu_custom_call" | custom-call | tf_op jit(solution)/shard_map/pre_grad/pallas_call | solution.py:100
  26.6 1.8 %collective-permute-start.9 = (bf16[256,512]{1,0:T(8,128)(2,1)S(1)}, bf16[256,512]{1,0:T(8,128)(2,1)S(1)}, u32[]{:S(2)}, u32[]{:S(2)}) collective-permute-start(bf16[256,512]{1,0:T(8,128)(2,1)S(1)} %get-tuple-element.94.refs_4_), channel_id=1, source_target_pairs={{0,8},{8,16},{16,24},{24,28},{28,20},{20,12},{12,4},{4,0},{1,9},{9... | collective-permute-start | bytes 786440 | tf_op jit(solution)/shard_map/ppermute | solution.py:364
  28.7 1.6 %pre_grad.5 = (bf16[128,2048]{1,0:T(8,128)(2,1)S(1)}, f32[128,128]{1,0:T(8,128)S(1)}) custom-call(bf16[128,1024]{1,0:T(8,128)(2,1)S(1)} %collective-permute-done.6.refs_1_.refs_0_.refs_6_, bf16[1,2048,1024]{2,1,0:T(8,128)(2,1)S(1)} %copy-done.2, bf16[128,2048]{1,0:T(8,128)(2,1)S(1)} %get-tuple-element.87.refs_5_.refs_2_, ...), custom_call_target="tpu_custom_call" | custom-call | tf_op jit(solution)/shard_map/pre_grad/pallas_call | solution.py:100
  30.9 1.8 %collective-permute-start.7 = (bf16[128,1024]{1,0:T(8,128)(2,1)S(1)}, bf16[128,1024]{1,0:T(8,128)(2,1)S(1)}, u32[]{:S(2)}, u32[]{:S(2)}) collective-permute-start(bf16[128,1024]{1,0:T(8,128)(2,1)S(1)} %get-tuple-element.98.refs_9_), channel_id=1, source_target_pairs={{0,8},{8,16},{16,24},{24,28},{28,20},{20,12},{12,4},{4,0},{1,9},{9... | collective-permute-start | bytes 786440 | tf_op jit(solution)/shard_map/ppermute | solution.py:364
  32.9 2.8 %collective-permute-done.9.refs_7_ = bf16[256,512]{1,0:T(8,128)(2,1)S(1)} collective-permute-done((bf16[256,512]{1,0:T(8,128)(2,1)S(1)}, bf16[256,512]{1,0:T(8,128)(2,1)S(1)}, u32[]{:S(2)}, u32[]{:S(2)}) %collective-permute-start.9) | collective-permute-done | bytes 262176 | tf_op jit(solution)/shard_map/ppermute | solution.py:364
  35.7 1.8 %collective-permute-done.10.refs_8_ = bf16[256,512]{1,0:T(8,128)(2,1)S(1)} collective-permute-done((bf16[256,512]{1,0:T(8,128)(2,1)S(1)}, bf16[256,512]{1,0:T(8,128)(2,1)S(1)}, u32[]{:S(2)}, u32[]{:S(2)}) %collective-permute-start.10) | collective-permute-done | bytes 262176 | tf_op jit(solution)/shard_map/ppermute | solution.py:364
  38.1 1.6 %collective-permute-start.13 = (bf16[256,512]{1,0:T(8,128)(2,1)S(1)}, bf16[256,512]{1,0:T(8,128)(2,1)S(1)}, u32[]{:S(2)}, u32[]{:S(2)}) collective-permute-start(bf16[256,512]{1,0:T(8,128)(2,1)S(1)} %get-tuple-element.100.refs_8_), channel_id=1, source_target_pairs={{0,8},{8,16},{16,24},{24,28},{28,20},{20,12},{12,4},{4,0},{1,9},{9... | collective-permute-start | bytes 786440 | tf_op jit(solution)/shard_map/ppermute | solution.py:364
  41.3 1.8 %collective-permute-done.8.refs_7_ = bf16[128,1024]{1,0:T(8,128)(2,1)S(1)} collective-permute-done((bf16[128,1024]{1,0:T(8,128)(2,1)S(1)}, bf16[128,1024]{1,0:T(8,128)(2,1)S(1)}, u32[]{:S(2)}, u32[]{:S(2)}) %collective-permute-start.8) | collective-permute-done | bytes 262176 | tf_op jit(solution)/shard_map/ppermute | solution.py:364
  43.8 1.6 %collective-permute-start.11 = (bf16[128,1024]{1,0:T(8,128)(2,1)S(1)}, bf16[128,1024]{1,0:T(8,128)(2,1)S(1)}, u32[]{:S(2)}, u32[]{:S(2)}) collective-permute-start(bf16[128,1024]{1,0:T(8,128)(2,1)S(1)} %get-tuple-element.102.refs_0_), channel_id=1, source_target_pairs={{0,8},{8,16},{16,24},{24,28},{28,20},{20,12},{12,4},{4,0},{1,9},{9... | collective-permute-start | bytes 786440 | tf_op jit(solution)/shard_map/ppermute | solution.py:364
  47.4 1.5 %collective-permute-start.19 = (bf16[128,1152]{1,0:T(8,128)(2,1)S(1)}, bf16[128,1152]{1,0:T(8,128)(2,1)S(1)}, u32[]{:S(2)}, u32[]{:S(2)}) collective-permute-start(bf16[128,1152]{1,0:T(8,128)(2,1)S(1)} %feat_grad.4.refs_9_), channel_id=1, source_target_pairs={{0,2},{1,3},{2,0},{3,1},{4,6},{5,7},{6,4},{7,5},{8,10},{9,11},{10,... | collective-permute-start | bytes 884744 | tf_op jit(solution)/shard_map/ppermute | solution.py:406
  49.6 1.6 %collective-permute-start.17 = (bf16[256,512]{1,0:T(8,128)(2,1)S(1)}, bf16[256,512]{1,0:T(8,128)(2,1)S(1)}, u32[]{:S(2)}, u32[]{:S(2)}) collective-permute-start(bf16[256,512]{1,0:T(8,128)(2,1)S(1)} %get-tuple-element.104.refs_8_), channel_id=1, source_target_pairs={{0,8},{8,16},{16,24},{24,28},{28,20},{20,12},{12,4},{4,0},{1,9},{9... | collective-permute-start | bytes 786440 | tf_op jit(solution)/shard_map/ppermute | solution.py:364
  53.0 1.6 %collective-permute-done.12.refs_7_ = bf16[128,1024]{1,0:T(8,128)(2,1)S(1)} collective-permute-done((bf16[128,1024]{1,0:T(8,128)(2,1)S(1)}, bf16[128,1024]{1,0:T(8,128)(2,1)S(1)}, u32[]{:S(2)}, u32[]{:S(2)}) %collective-permute-start.12) | collective-permute-done | bytes 262176 | tf_op jit(solution)/shard_map/ppermute | solution.py:364
  55.2 1.6 %collective-permute-start.15 = (bf16[128,1024]{1,0:T(8,128)(2,1)S(1)}, bf16[128,1024]{1,0:T(8,128)(2,1)S(1)}, u32[]{:S(2)}, u32[]{:S(2)}) collective-permute-start(bf16[128,1024]{1,0:T(8,128)(2,1)S(1)} %get-tuple-element.106.refs_0_), channel_id=1, source_target_pairs={{0,8},{8,16},{16,24},{24,28},{28,20},{20,12},{12,4},{4,0},{1,9},{9... | collective-permute-start | bytes 786440 | tf_op jit(solution)/shard_map/ppermute | solution.py:364
  58.9 1.6 %collective-permute-done.18.refs_8_ = bf16[256,512]{1,0:T(8,128)(2,1)S(1)} collective-permute-done((bf16[256,512]{1,0:T(8,128)(2,1)S(1)}, bf16[256,512]{1,0:T(8,128)(2,1)S(1)}, u32[]{:S(2)}, u32[]{:S(2)}) %collective-permute-start.18) | collective-permute-done | bytes 262176 | tf_op jit(solution)/shard_map/ppermute | solution.py:364
  61.0 1.6 %collective-permute-start.22 = (bf16[256,512]{1,0:T(8,128)(2,1)S(1)}, bf16[256,512]{1,0:T(8,128)(2,1)S(1)}, u32[]{:S(2)}, u32[]{:S(2)}) collective-permute-start(bf16[256,512]{1,0:T(8,128)(2,1)S(1)} %get-tuple-element.108.refs_8_), channel_id=1, source_target_pairs={{0,8},{8,16},{16,24},{24,28},{28,20},{20,12},{12,4},{4,0},{1,9},{9... | collective-permute-start | bytes 786440 | tf_op jit(solution)/shard_map/ppermute | solution.py:364
  63.5 1.5 %collective-permute-done.16.refs_7_ = bf16[128,1024]{1,0:T(8,128)(2,1)S(1)} collective-permute-done((bf16[128,1024]{1,0:T(8,128)(2,1)S(1)}, bf16[128,1024]{1,0:T(8,128)(2,1)S(1)}, u32[]{:S(2)}, u32[]{:S(2)}) %collective-permute-start.16) | collective-permute-done | bytes 262176 | tf_op jit(solution)/shard_map/ppermute | solution.py:364
  65.6 1.6 %collective-permute-start.20 = (bf16[128,1024]{1,0:T(8,128)(2,1)S(1)}, bf16[128,1024]{1,0:T(8,128)(2,1)S(1)}, u32[]{:S(2)}, u32[]{:S(2)}) collective-permute-start(bf16[128,1024]{1,0:T(8,128)(2,1)S(1)} %get-tuple-element.110.refs_0_), channel_id=1, source_target_pairs={{0,8},{8,16},{16,24},{24,28},{28,20},{20,12},{12,4},{4,0},{1,9},{9... | collective-permute-start | bytes 786440 | tf_op jit(solution)/shard_map/ppermute | solution.py:364
  70.3 1.6 %collective-permute-done.23.refs_8_ = bf16[256,512]{1,0:T(8,128)(2,1)S(1)} collective-permute-done((bf16[256,512]{1,0:T(8,128)(2,1)S(1)}, bf16[256,512]{1,0:T(8,128)(2,1)S(1)}, u32[]{:S(2)}, u32[]{:S(2)}) %collective-permute-start.23) | collective-permute-done | bytes 262176 | tf_op jit(solution)/shard_map/ppermute | solution.py:364
  72.4 1.5 %collective-permute-start.28 = (bf16[256,512]{1,0:T(8,128)(2,1)S(1)}, bf16[256,512]{1,0:T(8,128)(2,1)S(1)}, u32[]{:S(2)}, u32[]{:S(2)}) collective-permute-start(bf16[256,512]{1,0:T(8,128)(2,1)S(1)} %get-tuple-element.112.refs_8_), channel_id=1, source_target_pairs={{0,8},{8,16},{16,24},{24,28},{28,20},{20,12},{12,4},{4,0},{1,9},{9... | collective-permute-start | bytes 786440 | tf_op jit(solution)/shard_map/ppermute | solution.py:364
  75.9 1.6 %collective-permute-done.21.refs_7_ = bf16[128,1024]{1,0:T(8,128)(2,1)S(1)} collective-permute-done((bf16[128,1024]{1,0:T(8,128)(2,1)S(1)}, bf16[128,1024]{1,0:T(8,128)(2,1)S(1)}, u32[]{:S(2)}, u32[]{:S(2)}) %collective-permute-start.21) | collective-permute-done | bytes 262176 | tf_op jit(solution)/shard_map/ppermute | solution.py:364
  78.0 1.5 %collective-permute-start.26 = (bf16[128,1024]{1,0:T(8,128)(2,1)S(1)}, bf16[128,1024]{1,0:T(8,128)(2,1)S(1)}, u32[]{:S(2)}, u32[]{:S(2)}) collective-permute-start(bf16[128,1024]{1,0:T(8,128)(2,1)S(1)} %get-tuple-element.114.refs_0_), channel_id=1, source_target_pairs={{0,8},{8,16},{16,24},{24,28},{28,20},{20,12},{12,4},{4,0},{1,9},{9... | collective-permute-start | bytes 786440 | tf_op jit(solution)/shard_map/ppermute | solution.py:364
  97.0 1.6 %collective-permute-done.30.refs_6_ = bf16[128,1024]{1,0:T(8,128)(2,1)S(1)} collective-permute-done((bf16[128,1024]{1,0:T(8,128)(2,1)S(1)}, bf16[128,1024]{1,0:T(8,128)(2,1)S(1)}, u32[]{:S(2)}, u32[]{:S(2)}) %collective-permute-start.30) | collective-permute-done | bytes 262176 | tf_op jit(solution)/shard_map/ppermute | solution.py:364
  102.7 1.6 %unpack.1 = (bf16[256,1024]{1,0:T(8,128)(2,1)}, f32[256,128]{1,0:T(8,128)S(1)}) custom-call(s32[1,256]{1,0:T(1,128)S(1)} %get-tuple-element.67.slot_ref, bf16[128,1152]{1,0:T(8,128)(2,1)S(1)} %feat_grad.7.refs_9_.refs_0_, bf16[128,1152]{1,0:T(8,128)(2,1)S(1)} %collective-permute-done.25.refs_2_.refs_1_, ...), custom_call_target="tpu_custom_call" | custom-call | tf_op jit(solution)/shard_map/unpack/pallas_call | solution.py:439
  106.7 2.0 %collective-permute-done.34.refs_0_ = bf16[128,1024]{1,0:T(8,128)(2,1)S(1)} collective-permute-done((bf16[128,1024]{1,0:T(8,128)(2,1)S(1)}, bf16[128,1024]{1,0:T(8,128)(2,1)S(1)}, u32[]{:S(2)}, u32[]{:S(2)}) %collective-permute-start.34) | collective-permute-done | bytes 262176 | tf_op jit(solution)/shard_map/ppermute | solution.py:364
  (86 shorter events, 51.9 us)
Async XLA Ops:
  0.6 16.0 %collective-permute-start.3 = (bf16[256,1024]{1,0:T(8,128)(2,1)}, bf16[256,1024]{1,0:T(8,128)(2,1)S(1)}, u32[]{:S(2)}, u32[]{:S(2)}) collective-permute-start(bf16[256,1024]{1,0:T(8,128)(2,1)} %refs_3_.1), channel_id=1, source_target_pairs={{0,2},{1,3},{2,0},{3,1},{4,6},{5,7},{6,4},{7,5},{8,10},{9,11},{10,... | collective-permute-start | bytes 1572872 | tf_op jit(solution)/shard_map/ppermute | solution.py:292
  6.1 10.6 %collective-permute-start.2 = (s32[1,256]{1,0:T(1,128)}, s32[1,256]{1,0:T(1,128)S(1)}, u32[]{:S(2)}, u32[]{:S(2)}) collective-permute-start(s32[1,256]{1,0:T(1,128)} %bitcast.1), channel_id=1, source_target_pairs={{0,2},{1,3},{2,0},{3,1},{4,6},{5,7},{6,4},{7,5},{8,10},{9,11},{10,... | collective-permute-start | bytes 3080 | tf_op jit(solution)/shard_map/ppermute | solution.py:293
  6.1 16.0 %collective-permute-start.5 = (bf16[128,1024]{1,0:T(8,128)(2,1)S(1)}, bf16[128,1024]{1,0:T(8,128)(2,1)S(1)}, u32[]{:S(2)}, u32[]{:S(2)}) collective-permute-start(bf16[128,1024]{1,0:T(8,128)(2,1)S(1)} %get-tuple-element.80), channel_id=1, source_target_pairs={{0,2},{1,3},{2,0},{3,1},{4,6},{5,7},{6,4},{7,5},{8,10},{9,11},{10,... | collective-permute-start | bytes 786440 | tf_op jit(solution)/shard_map/ppermute | solution.py:287
  17.2 9.1 %collective-permute-start.6 = (bf16[128,1024]{1,0:T(8,128)(2,1)S(1)}, bf16[128,1024]{1,0:T(8,128)(2,1)S(1)}, u32[]{:S(2)}, u32[]{:S(2)}) collective-permute-start(bf16[128,1024]{1,0:T(8,128)(2,1)S(1)} %get-tuple-element.86), channel_id=1, source_target_pairs={{0,3},{1,2},{2,1},{3,0},{4,7},{5,6},{6,5},{7,4},{8,11},{9,10},{10,... | collective-permute-start | bytes 786440 | tf_op jit(solution)/shard_map/ppermute | solution.py:287
  26.6 9.1 %collective-permute-start.9 = (bf16[256,512]{1,0:T(8,128)(2,1)S(1)}, bf16[256,512]{1,0:T(8,128)(2,1)S(1)}, u32[]{:S(2)}, u32[]{:S(2)}) collective-permute-start(bf16[256,512]{1,0:T(8,128)(2,1)S(1)} %get-tuple-element.94.refs_4_), channel_id=1, source_target_pairs={{0,8},{8,16},{16,24},{24,28},{28,20},{20,12},{12,4},{4,0},{1,9},{9... | collective-permute-start | bytes 786440 | tf_op jit(solution)/shard_map/ppermute | solution.py:364
  28.4 9.1 %collective-permute-start.10 = (bf16[256,512]{1,0:T(8,128)(2,1)S(1)}, bf16[256,512]{1,0:T(8,128)(2,1)S(1)}, u32[]{:S(2)}, u32[]{:S(2)}) collective-permute-start(bf16[256,512]{1,0:T(8,128)(2,1)S(1)} %get-tuple-element.95.refs_5_), channel_id=1, source_target_pairs={{8,0},{16,8},{24,16},{28,24},{20,28},{12,20},{4,12},{0,4},{9,1},{1... | collective-permute-start | bytes 786440 | tf_op jit(solution)/shard_map/ppermute | solution.py:364
  30.9 10.5 %collective-permute-start.7 = (bf16[128,1024]{1,0:T(8,128)(2,1)S(1)}, bf16[128,1024]{1,0:T(8,128)(2,1)S(1)}, u32[]{:S(2)}, u32[]{:S(2)}) collective-permute-start(bf16[128,1024]{1,0:T(8,128)(2,1)S(1)} %get-tuple-element.98.refs_9_), channel_id=1, source_target_pairs={{0,8},{8,16},{16,24},{24,28},{28,20},{20,12},{12,4},{4,0},{1,9},{9... | collective-permute-start | bytes 786440 | tf_op jit(solution)/shard_map/ppermute | solution.py:364
  32.7 10.5 %collective-permute-start.8 = (bf16[128,1024]{1,0:T(8,128)(2,1)S(1)}, bf16[128,1024]{1,0:T(8,128)(2,1)S(1)}, u32[]{:S(2)}, u32[]{:S(2)}) collective-permute-start(bf16[128,1024]{1,0:T(8,128)(2,1)S(1)} %get-tuple-element.99.refs_10_), channel_id=1, source_target_pairs={{8,0},{16,8},{24,16},{28,24},{20,28},{12,20},{4,12},{0,4},{9,1},{1... | collective-permute-start | bytes 786440 | tf_op jit(solution)/shard_map/ppermute | solution.py:364
  38.1 10.8 %collective-permute-start.13 = (bf16[256,512]{1,0:T(8,128)(2,1)S(1)}, bf16[256,512]{1,0:T(8,128)(2,1)S(1)}, u32[]{:S(2)}, u32[]{:S(2)}) collective-permute-start(bf16[256,512]{1,0:T(8,128)(2,1)S(1)} %get-tuple-element.100.refs_8_), channel_id=1, source_target_pairs={{0,8},{8,16},{16,24},{24,28},{28,20},{20,12},{12,4},{4,0},{1,9},{9... | collective-permute-start | bytes 786440 | tf_op jit(solution)/shard_map/ppermute | solution.py:364
  39.8 9.2 %collective-permute-start.14 = (bf16[256,512]{1,0:T(8,128)(2,1)S(1)}, bf16[256,512]{1,0:T(8,128)(2,1)S(1)}, u32[]{:S(2)}, u32[]{:S(2)}) collective-permute-start(bf16[256,512]{1,0:T(8,128)(2,1)S(1)} %get-tuple-element.101.refs_9_), channel_id=1, source_target_pairs={{8,0},{16,8},{24,16},{28,24},{20,28},{12,20},{4,12},{0,4},{9,1},{1... | collective-permute-start | bytes 786440 | tf_op jit(solution)/shard_map/ppermute | solution.py:364
  43.8 9.3 %collective-permute-start.11 = (bf16[128,1024]{1,0:T(8,128)(2,1)S(1)}, bf16[128,1024]{1,0:T(8,128)(2,1)S(1)}, u32[]{:S(2)}, u32[]{:S(2)}) collective-permute-start(bf16[128,1024]{1,0:T(8,128)(2,1)S(1)} %get-tuple-element.102.refs_0_), channel_id=1, source_target_pairs={{0,8},{8,16},{16,24},{24,28},{28,20},{20,12},{12,4},{4,0},{1,9},{9... | collective-permute-start | bytes 786440 | tf_op jit(solution)/shard_map/ppermute | solution.py:364
  45.4 9.2 %collective-permute-start.12 = (bf16[128,1024]{1,0:T(8,128)(2,1)S(1)}, bf16[128,1024]{1,0:T(8,128)(2,1)S(1)}, u32[]{:S(2)}, u32[]{:S(2)}) collective-permute-start(bf16[128,1024]{1,0:T(8,128)(2,1)S(1)} %get-tuple-element.103.refs_1_), channel_id=1, source_target_pairs={{8,0},{16,8},{24,16},{28,24},{20,28},{12,20},{4,12},{0,4},{9,1},{1... | collective-permute-start | bytes 786440 | tf_op jit(solution)/shard_map/ppermute | solution.py:364
  47.4 9.9 %collective-permute-start.19 = (bf16[128,1152]{1,0:T(8,128)(2,1)S(1)}, bf16[128,1152]{1,0:T(8,128)(2,1)S(1)}, u32[]{:S(2)}, u32[]{:S(2)}) collective-permute-start(bf16[128,1152]{1,0:T(8,128)(2,1)S(1)} %feat_grad.4.refs_9_), channel_id=1, source_target_pairs={{0,2},{1,3},{2,0},{3,1},{4,6},{5,7},{6,4},{7,5},{8,10},{9,11},{10,... | collective-permute-start | bytes 884744 | tf_op jit(solution)/shard_map/ppermute | solution.py:406
  49.6 9.3 %collective-permute-start.17 = (bf16[256,512]{1,0:T(8,128)(2,1)S(1)}, bf16[256,512]{1,0:T(8,128)(2,1)S(1)}, u32[]{:S(2)}, u32[]{:S(2)}) collective-permute-start(bf16[256,512]{1,0:T(8,128)(2,1)S(1)} %get-tuple-element.104.refs_8_), channel_id=1, source_target_pairs={{0,8},{8,16},{16,24},{24,28},{28,20},{20,12},{12,4},{4,0},{1,9},{9... | collective-permute-start | bytes 786440 | tf_op jit(solution)/shard_map/ppermute | solution.py:364
  51.2 9.2 %collective-permute-start.18 = (bf16[256,512]{1,0:T(8,128)(2,1)S(1)}, bf16[256,512]{1,0:T(8,128)(2,1)S(1)}, u32[]{:S(2)}, u32[]{:S(2)}) collective-permute-start(bf16[256,512]{1,0:T(8,128)(2,1)S(1)} %get-tuple-element.105.refs_9_), channel_id=1, source_target_pairs={{8,0},{16,8},{24,16},{28,24},{20,28},{12,20},{4,12},{0,4},{9,1},{1... | collective-permute-start | bytes 786440 | tf_op jit(solution)/shard_map/ppermute | solution.py:364
  55.2 8.3 %collective-permute-start.15 = (bf16[128,1024]{1,0:T(8,128)(2,1)S(1)}, bf16[128,1024]{1,0:T(8,128)(2,1)S(1)}, u32[]{:S(2)}, u32[]{:S(2)}) collective-permute-start(bf16[128,1024]{1,0:T(8,128)(2,1)S(1)} %get-tuple-element.106.refs_0_), channel_id=1, source_target_pairs={{0,8},{8,16},{16,24},{24,28},{28,20},{20,12},{12,4},{4,0},{1,9},{9... | collective-permute-start | bytes 786440 | tf_op jit(solution)/shard_map/ppermute | solution.py:364
  58.8 9.3 %collective-permute-start.24 = (bf16[128,1152]{1,0:T(8,128)(2,1)S(1)}, bf16[128,1152]{1,0:T(8,128)(2,1)S(1)}, u32[]{:S(2)}, u32[]{:S(2)}) collective-permute-start(bf16[128,1152]{1,0:T(8,128)(2,1)S(1)} %feat_grad.5.refs_9_), channel_id=1, source_target_pairs={{0,3},{1,2},{2,1},{3,0},{4,7},{5,6},{6,5},{7,4},{8,11},{9,10},{10,... | collective-permute-start | bytes 884744 | tf_op jit(solution)/shard_map/ppermute | solution.py:406
  61.0 9.2 %collective-permute-start.22 = (bf16[256,512]{1,0:T(8,128)(2,1)S(1)}, bf16[256,512]{1,0:T(8,128)(2,1)S(1)}, u32[]{:S(2)}, u32[]{:S(2)}) collective-permute-start(bf16[256,512]{1,0:T(8,128)(2,1)S(1)} %get-tuple-element.108.refs_8_), channel_id=1, source_target_pairs={{0,8},{8,16},{16,24},{24,28},{28,20},{20,12},{12,4},{4,0},{1,9},{9... | collective-permute-start | bytes 786440 | tf_op jit(solution)/shard_map/ppermute | solution.py:364
  62.6 9.2 %collective-permute-start.23 = (bf16[256,512]{1,0:T(8,128)(2,1)S(1)}, bf16[256,512]{1,0:T(8,128)(2,1)S(1)}, u32[]{:S(2)}, u32[]{:S(2)}) collective-permute-start(bf16[256,512]{1,0:T(8,128)(2,1)S(1)} %get-tuple-element.109.refs_9_), channel_id=1, source_target_pairs={{8,0},{16,8},{24,16},{28,24},{20,28},{12,20},{4,12},{0,4},{9,1},{1... | collective-permute-start | bytes 786440 | tf_op jit(solution)/shard_map/ppermute | solution.py:364
  65.6 10.3 %collective-permute-start.20 = (bf16[128,1024]{1,0:T(8,128)(2,1)S(1)}, bf16[128,1024]{1,0:T(8,128)(2,1)S(1)}, u32[]{:S(2)}, u32[]{:S(2)}) collective-permute-start(bf16[128,1024]{1,0:T(8,128)(2,1)S(1)} %get-tuple-element.110.refs_0_), channel_id=1, source_target_pairs={{0,8},{8,16},{16,24},{24,28},{28,20},{20,12},{12,4},{4,0},{1,9},{9... | collective-permute-start | bytes 786440 | tf_op jit(solution)/shard_map/ppermute | solution.py:364
  67.3 10.2 %collective-permute-start.21 = (bf16[128,1024]{1,0:T(8,128)(2,1)S(1)}, bf16[128,1024]{1,0:T(8,128)(2,1)S(1)}, u32[]{:S(2)}, u32[]{:S(2)}) collective-permute-start(bf16[128,1024]{1,0:T(8,128)(2,1)S(1)} %get-tuple-element.111.refs_1_), channel_id=1, source_target_pairs={{8,0},{16,8},{24,16},{28,24},{20,28},{12,20},{4,12},{0,4},{9,1},{1... | collective-permute-start | bytes 786440 | tf_op jit(solution)/shard_map/ppermute | solution.py:364
  69.6 10.5 %collective-permute-start.25 = (bf16[128,1152]{1,0:T(8,128)(2,1)S(1)}, bf16[128,1152]{1,0:T(8,128)(2,1)S(1)}, u32[]{:S(2)}, u32[]{:S(2)}) collective-permute-start(bf16[128,1152]{1,0:T(8,128)(2,1)S(1)} %feat_grad.6.refs_9_), channel_id=1, source_target_pairs={{0,1},{1,0},{2,3},{3,2},{4,5},{5,4},{6,7},{7,6},{8,9},{9,8},{10,11... | collective-permute-start | bytes 884744 | tf_op jit(solution)/shard_map/ppermute | solution.py:406
  72.4 9.3 %collective-permute-start.28 = (bf16[256,512]{1,0:T(8,128)(2,1)S(1)}, bf16[256,512]{1,0:T(8,128)(2,1)S(1)}, u32[]{:S(2)}, u32[]{:S(2)}) collective-permute-start(bf16[256,512]{1,0:T(8,128)(2,1)S(1)} %get-tuple-element.112.refs_8_), channel_id=1, source_target_pairs={{0,8},{8,16},{16,24},{24,28},{28,20},{20,12},{12,4},{4,0},{1,9},{9... | collective-permute-start | bytes 786440 | tf_op jit(solution)/shard_map/ppermute | solution.py:364
  73.9 9.2 %collective-permute-start.29 = (bf16[256,512]{1,0:T(8,128)(2,1)S(1)}, bf16[256,512]{1,0:T(8,128)(2,1)S(1)}, u32[]{:S(2)}, u32[]{:S(2)}) collective-permute-start(bf16[256,512]{1,0:T(8,128)(2,1)S(1)} %get-tuple-element.113.refs_9_), channel_id=1, source_target_pairs={{8,0},{16,8},{24,16},{28,24},{20,28},{12,20},{4,12},{0,4},{9,1},{1... | collective-permute-start | bytes 786440 | tf_op jit(solution)/shard_map/ppermute | solution.py:364
  78.0 9.3 %collective-permute-start.26 = (bf16[128,1024]{1,0:T(8,128)(2,1)S(1)}, bf16[128,1024]{1,0:T(8,128)(2,1)S(1)}, u32[]{:S(2)}, u32[]{:S(2)}) collective-permute-start(bf16[128,1024]{1,0:T(8,128)(2,1)S(1)} %get-tuple-element.114.refs_0_), channel_id=1, source_target_pairs={{0,8},{8,16},{16,24},{24,28},{28,20},{20,12},{12,4},{4,0},{1,9},{9... | collective-permute-start | bytes 786440 | tf_op jit(solution)/shard_map/ppermute | solution.py:364
  79.5 9.2 %collective-permute-start.27 = (bf16[128,1024]{1,0:T(8,128)(2,1)S(1)}, bf16[128,1024]{1,0:T(8,128)(2,1)S(1)}, u32[]{:S(2)}, u32[]{:S(2)}) collective-permute-start(bf16[128,1024]{1,0:T(8,128)(2,1)S(1)} %get-tuple-element.115.refs_1_), channel_id=1, source_target_pairs={{8,0},{16,8},{24,16},{28,24},{20,28},{12,20},{4,12},{0,4},{9,1},{1... | collective-permute-start | bytes 786440 | tf_op jit(solution)/shard_map/ppermute | solution.py:364
  83.7 9.3 %collective-permute-start.32 = (bf16[256,512]{1,0:T(8,128)(2,1)S(1)}, bf16[256,512]{1,0:T(8,128)(2,1)S(1)}, u32[]{:S(2)}, u32[]{:S(2)}) collective-permute-start(bf16[256,512]{1,0:T(8,128)(2,1)S(1)} %get-tuple-element.116.refs_8_), channel_id=1, source_target_pairs={{0,8},{8,16},{16,24},{24,28},{28,20},{20,12},{12,4},{4,0},{1,9},{9... | collective-permute-start | bytes 786440 | tf_op jit(solution)/shard_map/ppermute | solution.py:364
  85.1 9.2 %collective-permute-start.33 = (bf16[256,512]{1,0:T(8,128)(2,1)S(1)}, bf16[256,512]{1,0:T(8,128)(2,1)S(1)}, u32[]{:S(2)}, u32[]{:S(2)}) collective-permute-start(bf16[256,512]{1,0:T(8,128)(2,1)S(1)} %get-tuple-element.117.refs_9_), channel_id=1, source_target_pairs={{8,0},{16,8},{24,16},{28,24},{20,28},{12,20},{4,12},{0,4},{9,1},{1... | collective-permute-start | bytes 786440 | tf_op jit(solution)/shard_map/ppermute | solution.py:364
  89.4 9.3 %collective-permute-start.30 = (bf16[128,1024]{1,0:T(8,128)(2,1)S(1)}, bf16[128,1024]{1,0:T(8,128)(2,1)S(1)}, u32[]{:S(2)}, u32[]{:S(2)}) collective-permute-start(bf16[128,1024]{1,0:T(8,128)(2,1)S(1)} %get-tuple-element.118.refs_7_), channel_id=1, source_target_pairs={{0,8},{8,16},{16,24},{24,28},{28,20},{20,12},{12,4},{4,0},{1,9},{9... | collective-permute-start | bytes 786440 | tf_op jit(solution)/shard_map/ppermute | solution.py:364
  90.8 9.2 %collective-permute-start.31 = (bf16[128,1024]{1,0:T(8,128)(2,1)S(1)}, bf16[128,1024]{1,0:T(8,128)(2,1)S(1)}, u32[]{:S(2)}, u32[]{:S(2)}) collective-permute-start(bf16[128,1024]{1,0:T(8,128)(2,1)S(1)} %get-tuple-element.119.refs_8_), channel_id=1, source_target_pairs={{8,0},{16,8},{24,16},{28,24},{20,28},{12,20},{4,12},{0,4},{9,1},{1... | collective-permute-start | bytes 786440 | tf_op jit(solution)/shard_map/ppermute | solution.py:364
  95.0 10.0 %collective-permute-start.36 = (bf16[256,512]{1,0:T(8,128)(2,1)S(1)}, bf16[256,512]{1,0:T(8,128)(2,1)S(1)}, u32[]{:S(2)}, u32[]{:S(2)}) collective-permute-start(bf16[256,512]{1,0:T(8,128)(2,1)S(1)} %get-tuple-element.122.refs_8_), channel_id=1, source_target_pairs={{0,8},{8,16},{16,24},{24,28},{28,20},{20,12},{12,4},{4,0},{1,9},{9... | collective-permute-start | bytes 786440 | tf_op jit(solution)/shard_map/ppermute | solution.py:364
  96.4 9.2 %collective-permute-start.37 = (bf16[256,512]{1,0:T(8,128)(2,1)S(1)}, bf16[256,512]{1,0:T(8,128)(2,1)S(1)}, u32[]{:S(2)}, u32[]{:S(2)}) collective-permute-start(bf16[256,512]{1,0:T(8,128)(2,1)S(1)} %get-tuple-element.123.refs_9_), channel_id=1, source_target_pairs={{8,0},{16,8},{24,16},{28,24},{20,28},{12,20},{4,12},{0,4},{9,1},{1... | collective-permute-start | bytes 786440 | tf_op jit(solution)/shard_map/ppermute | solution.py:364
  (10 other events, 61.7 us)

commit v4 on v3

--- a/solution.py
+++ b/solution.py
@@ -193,16 +193,23 @@
     )[0]
 
 
-def ring_chunk(step, count):
+def ring_chunk(offset, count):
     index = lax.axis_index("dp")
     half = lax.div(index, 2)
     place = jnp.where(lax.rem(index, 2) == 0, half, count - 1 - half)
-    chunks = []
-    for move in (count - step, step):
-        position = lax.rem(place + move, count)
-        mirror = 2 * (count - 1 - position) + 1
-        chunks.append(jnp.where(position < count // 2, 2 * position, mirror))
-    return chunks
+    position = lax.rem(place + (offset + count), count)
+    mirror = 2 * (count - 1 - position) + 1
+    return jnp.where(position < count // 2, 2 * position, mirror)
+
+
+def ring_targets(step, count):
+    targets = []
+    for way, sign in ((0, 1), (1, -1)):
+        for side in range(2):
+            offset = count // 2 - step + (side == way)
+            if offset > 0:
+                targets.append(((way, side), sign * offset))
+    return targets
 
 
 def ring_pairs(count):
@@ -211,65 +218,88 @@
     return [(ring[p], ring[(p + 1) % count]) for p in range(count)]
 
 
-def step_kernel(parts, arrivals, step, count, last, *refs):
+def step_kernel(parts, arrivals, targets, count, half, *refs):
     groups = len(parts)
     lefts, refs = refs[:groups], refs[groups:]
     rights, refs = refs[: sum(parts)], refs[sum(parts) :]
-    totals = [0.0, 0.0]
-    chunks = ring_chunk(step, count) if groups else None
-    for i, ref in enumerate(refs[:arrivals]):
-        totals[i % 2] += ref[...].astype(F32)
+    totals = {key: 0.0 for key, _ in targets}
+    for ref, (way, sides) in zip(refs, arrivals):
+        for i, side in enumerate(sides):
+            if (way, side) in totals:
+                totals[way, side] += ref[:, i * half : (i + 1) * half].astype(F32)
     for left, blocks in zip(lefts, parts):
-        right = [ref[...] for ref in rights[:blocks]]
-        right = right[0] if blocks == 1 else jnp.concatenate(right, axis=0)
+        rows = left.shape[0] // count
+        for side in range(2):
+            wanted = [(key, offset) for key, offset in targets if key[1] == side]
+            if not wanted:
+                continue
+            right = [
+                ref[...] if ref.shape[1] == half else ref[:, side * half : (side + 1) * half]
+                for ref in rights[:blocks]
+            ]
+            right = right[0] if blocks == 1 else jnp.concatenate(right, axis=0)
+            picked = []
+            for _, offset in wanted:
+                start = pl.multiple_of(ring_chunk(offset, count) * rows, rows)
+                picked.append(left[pl.ds(start, rows), :])
+            picked = picked[0] if len(picked) == 1 else jnp.concatenate(picked, axis=0)
+            product = dot(picked, right, 1, 0)
+            for i, (key, _) in enumerate(wanted):
+                totals[key] += product[i * rows : (i + 1) * rows]
         rights = rights[blocks:]
-        half = right.shape[1] // 2
-        rows = left.shape[0] // count
-        for way in range(2):
-            start = pl.multiple_of(chunks[way] * rows, rows)
-            totals[way] += dot(
-                left[pl.ds(start, rows), :], right[:, way * half : (way + 1) * half], 1, 0
-            )
-    if not last:
-        for way, out in enumerate(refs[-2:]):
-            out[...] = totals[way].astype(out.dtype)
-        return
-    out, held, sems = refs[-3:]
+    ways = sorted({way for way, _ in totals})
+    for way, out in zip(ways, refs[-len(ways) :]):
+        for i, key in enumerate(sorted(key for key in totals if key[0] == way)):
+            out[:, i * half : (i + 1) * half] = totals[key].astype(out.dtype)
+
+
+def ring_step(name, targets, count, shape, lefts, rights, arrived, after=(), dtype=BF16):
+    rows, half = shape
+    held = {}
+    for way, side in sorted(key for key, _ in targets):
+        held.setdefault(way, []).append(side)
+    blocks = [block for group in rights for block in group]
+    outs = call(
+        functools.partial(
+            step_kernel,
+            [len(group) for group in rights],
+            [(way, sides) for _, way, sides in arrived],
+            targets,
+            count,
+            half,
+        ),
+        [*lefts, *blocks, *(array for array, _, _ in arrived)],
+        [((rows, half * len(sides)), dtype) for sides in held.values()],
+        name,
+        after,
+    )
+    return [(out, way, tuple(sides)) for out, (way, sides) in zip(outs, held.items())]
+
+
+def last_kernel(count, own_ref, *refs):
+    arrived, (out, held, sems) = refs[:2], refs[-3:]
     half = held.shape[2]
     copies = []
-    for way in range(2):
-        held[way] = totals[way] * (1.0 / count)
-        target = out.at[0, :, way * half : (way + 1) * half]
-        copies.append(pltpu.make_async_copy(held.at[way], target, sems.at[way]))
+    for side, ref in enumerate(arrived):
+        part = slice(side * half, (side + 1) * half)
+        held[side] = (own_ref[:, part] + ref[...].astype(F32)) * (1.0 / count)
+        copies.append(pltpu.make_async_copy(held.at[side], out.at[0, :, part], sems.at[side]))
         copies[-1].start()
     for copy in copies:
         copy.wait()
 
 
-def ring_step(name, step, count, shape, lefts, rights, arrived, after=(), dtype=BF16):
-    rows, half = shape
-    last = dtype is None
-    if last:
-        out_specs = [pl.BlockSpec(memory_space=pltpu.HBM)]
-        out_shape = [pltpu.HBM((1, rows, 2 * half), F32)]
-        scratch = [pltpu.VMEM((2, rows, half), F32), pltpu.SemaphoreType.DMA((2,))]
-    else:
-        out_specs = [WHOLE] * 2
-        out_shape = [jax.ShapeDtypeStruct(shape, dtype)] * 2
-        scratch = []
-    blocks = [block for group in rights for block in group]
-    inputs = [*lefts, *blocks, *arrived]
+def last_call(name, count, own, arrived, after):
+    rows, width = own.shape
     return pl.pallas_call(
-        functools.partial(
-            step_kernel, [len(group) for group in rights], len(arrived), step, count, last
-        ),
-        in_specs=[WHOLE] * len(inputs) + [LATER] * len(after),
-        out_specs=out_specs,
-        out_shape=out_shape,
-        scratch_shapes=scratch,
+        functools.partial(last_kernel, count),
+        in_specs=[WHOLE] * 3 + [LATER] * len(after),
+        out_specs=pl.BlockSpec(memory_space=pltpu.HBM),
+        out_shape=pltpu.HBM((1, rows, width), F32),
+        scratch_shapes=[pltpu.VMEM((2, rows, width // 2), F32), pltpu.SemaphoreType.DMA((2,))],
         compiler_params=params(),
         name=name,
-    )(*inputs, *after)
+    )(own, *arrived, *after)
 
 
 def per_device(tokens, out_grad, gate_prob, expert_id, up_weight, down_weight):
@@ -348,9 +378,9 @@
     flip_hiddens = [part[2] for part in hiddens]
     down_shape = (inner // ring, width // 2)
     up_shape = (width // ring, inner // 2)
-    down_in = ring_step(
+    early = ring_step(
         "down_early",
-        1,
+        ring_targets(1, ring),
         ring,
         down_shape,
         flip_hiddens[:-1],
@@ -359,40 +389,24 @@
         after,
         F32,
     )
-
-    def send(pair):
-        return [lax.ppermute(pair[0], "dp", forward), lax.ppermute(pair[1], "dp", backward)]
-
-    turn = 1 if ring < 8 else 2
-    span = min(4, ring - turn)
+    after = [early[0][0]]
+
+    def send(messages):
+        ways = (forward, backward)
+        return [(lax.ppermute(a, "dp", ways[way]), way, sides) for a, way, sides in messages]
+
+    hops = ring // 2
     returns = [*far, *near, 0]
-    feat_back = {}
-    up_in, after, landed = [], [], []
-    for step in range(1, ring):
-        late = slice(-1, None) if step == 1 else slice(None)
-        down = ring_step(
-            "down_step",
-                step,
-            ring,
-            down_shape,
-            flip_hiddens[late],
-            scaleds[late],
-            down_in,
-            after,
-        )
-        down_in = send(down)
-        after = [*down]
-        if step == 1:
-            after = add_pre_grad(after)
-        up = ring_step(
-            "up_step", step, ring, up_shape, flip_feats, pre_grads, up_in, after
-        )
-        up_in = send(up)
-        after = [*up] + landed
-        landed = []
-        first = (step - turn) * len(returns) // span
-        stop = (step - turn + 1) * len(returns) // span
-        for k in returns[max(first, 0) : max(stop, 0)]:
+    spread = max(min(4, 2 * hops - 2), 1)
+    feat_back, landed, slots = {}, [], []
+
+    def give_back(after):
+        slots.append(0)
+        first = (len(slots) - 1) * len(returns) // spread
+        stop = len(slots) * len(returns) // spread
+        after = [*after, *landed]
+        landed.clear()
+        for k in returns[first:stop]:
             group = [k in members for members in groups].index(True)
             block = feat_grad_call(
                 pre_grads[group][0],
@@ -405,37 +419,57 @@
             after = [block]
             feat_back[k] = lax.ppermute(block, "expert", sources[k]) if k else block
             landed.append(feat_back[k])
-        if step == max(ring - 2, 1):
-            down_last = ring_step(
-                "down_own",
-                        ring,
+        return after
+
+    def own(name, shape, lefts, rights, arrived, after):
+        done = [
+            (a, 0, tuple(None if side == way else side for side in sides))
+            for a, way, sides in arrived
+        ]
+        targets = [((0, 0), 0), ((0, 1), 0)]
+        return ring_step(name, targets, ring, shape, lefts, rights, done, after, F32)[0][0]
+
+    down_in, up_in = [], []
+    for step in range(1, hops + 1):
+        targets = ring_targets(step, ring)
+        if step == 1:
+            messages = ring_step(
+                "down_step",
+                targets,
                 ring,
                 down_shape,
-                flip_hiddens,
-                scaleds,
-                [],
+                flip_hiddens[-1:],
+                scaleds[-1:],
+                early,
                 after,
-                F32,
             )
-            up_last = ring_step(
-                "up_own",
-                        ring,
-                ring,
-                up_shape,
-                flip_feats,
-                pre_grads,
-                [],
-                down_last[:1],
-                F32,
+            down_in = send(messages)
+            after = add_pre_grad([a for a, _, _ in messages])
+        else:
+            messages = ring_step(
+                "down_step", targets, ring, down_shape, flip_hiddens, scaleds, down_in, after
             )
-            after = up_last[:1]
-    down = ring_step(
-        "down_last", ring, ring, down_shape, [], [], [*down_in, *down_last], [], None
-    )
-    after_down = [in_hbm(down[0])]
-    up = ring_step(
-        "up_last", ring, ring, up_shape, [], [], [*up_in, *up_last], after_down, None
-    )
+            after = [a for a, _, _ in messages]
+            if step == hops:
+                down_own = own(
+                    "down_own", down_shape, flip_hiddens, scaleds, down_in, after
+                )
+                after = [down_own]
+            else:
+                after = give_back(after)
+            down_in = send(messages)
+        messages = ring_step(
+            "up_step", targets, ring, up_shape, flip_feats, pre_grads, up_in, after
+        )
+        after = [a for a, _, _ in messages]
+        if step == hops:
+            up_own = own("up_own", up_shape, flip_feats, pre_grads, up_in, after)
+            after = [up_own]
+        else:
+            after = give_back(after)
+        up_in = send(messages)
+    while len(feat_back) < peers:
+        after = give_back(after)
     tokens_grad, gate_sums = pl.pallas_call(
         functools.partial(unpack_kernel, capacity, width, peers),
         in_specs=[WHOLE] * (1 + peers) + [LATER] * len(after),
@@ -447,8 +481,10 @@
         compiler_params=params(),
         name="unpack",
     )(slot, *(feat_back[k] for k in range(peers)), *after)
+    down = last_call("down_last", ring, down_own, [a for a, _, _ in down_in], [up_own])
+    up = last_call("up_last", ring, up_own, [a for a, _, _ in up_in], [in_hbm(down)])
     gate_result = ((gate_sums[:, 0] + gate_sums[:, 1]) / gate_prob.astype(F32)).astype(BF16)
-    return (tokens_grad, gate_result, up[0], down[0])
+    return (tokens_grad, gate_result, up, down)
 
 
 def solution(mesh):

time: 111 us -> 112 us (level)
  waiting for transfers between devices: 38.1 us -> 51.6 us
  starting transfers between devices: 38.8 us -> 26.4 us
    ppermute x31 -> x19, waiting for transfers between devices: 32.7 us -> 46.5 us  [the longest x16 46.5 us: send(): lax.ppermute(a, 'dp', ways[way])]
    ppermute x31 -> x19, starting transfers between devices: 30.9 us -> 18.5 us  [the longest x16 16.6 us: send(): lax.ppermute(a, 'dp', ways[way])]
    pallas_call x19 -> x2, Pallas kernels: 11.4 us -> 2.07 us  [last_call(): pl.pallas_call(functools.partial(last_kernel, count), in_specs=[WHOLE] *...]
    pallas_call x10 -> x21, Pallas kernels: 14.9 us -> 23.2 us  [call(): pl.pallas_call(body, in_specs=[WHOLE] * len(inputs) + [LATER] * len(after...]
  transfers between devices with their start and end apart: 38 -> 26, of which waited for: 29 -> 17; matrix products, arithmetic and copies ran while one was open for 1% -> 1% of each run, Pallas kernels for 26% -> 25%
where the time goes in v4:
time: 112 us; the launch traced here: 111 us
  waiting for transfers between devices  51.6 us (46%)
  Pallas kernels  29.2 us (26%)
  starting transfers between devices  26.4 us (24%)
  local copies, waits for them, and re-layouts  2.35 us (2%)
    ppermute x16, waiting for transfers between devices, send(): lax.ppermute(a, 'dp', ways[way])  46.5 us
    pallas_call x21, Pallas kernels, call(): pl.pallas_call(body, in_specs=[WHOLE] * len(inputs) + [LATER] * len(after...  23.2 us
    ppermute x16, starting transfers between devices, send(): lax.ppermute(a, 'dp', ways[way])  16.6 us
    ppermute x5, starting transfers between devices, exchange(): return {k: lax.ppermute(outs[k], 'expert', sources[k]) for k in reach}  4.83 us
    ppermute x1, starting transfers between devices, per_device(): tokens_across = lax.ppermute(tokens, 'expert', across)  3 us
    ppermute x1, waiting for transfers between devices, per_device(): id_across = lax.ppermute(expert_id.reshape(1, count), 'expert', across)  2.65 us
    ppermute x5, waiting for transfers between devices, exchange(): return {k: lax.ppermute(outs[k], 'expert', sources[k]) for k in reach}  2.46 us
    unnamed x8, local copies, waits for them, and re-layouts  2.35 us
  transfers between devices with their start and end apart: 26, of which 17 were waited for; matrix products, arithmetic and copies ran while one was open for 1% of the time, Pallas kernels for 25%

profile of v4, /device:TPU:0, one launch (start us, length us, event | category | flops | bytes accessed | tf_op | source)
XLA Modules:
  0.0 111.3 jit_solution(3875775579688353496)
XLA Ops:
  0.6 3.0 %collective-permute-start.3 = (bf16[256,1024]{1,0:T(8,128)(2,1)}, bf16[256,1024]{1,0:T(8,128)(2,1)S(1)}, u32[]{:S(2)}, u32[]{:S(2)}) collective-permute-start(bf16[256,1024]{1,0:T(8,128)(2,1)} %refs_3_.1), channel_id=1, source_target_pairs={{0,2},{1,3},{2,0},{3,1},{4,6},{5,7},{6,4},{7,5},{8,10},{9,11},{10,... | collective-permute-start | bytes 1572872 | tf_op jit(solution)/shard_map/ppermute | solution.py:322
  3.6 1.9 %pack.1 = (s32[1,256]{1,0:T(1,128)S(1)}, bf16[128,1024]{1,0:T(8,128)(2,1)S(1)}, bf16[128,1024]{1,0:T(8,128)(2,1)S(1)}, bf16[128,1024]{1,0:T(8,128)(2,1)S(1)}, bf...) custom-call(s32[256]{0:T(256)} %refs_0_.1, bf16[256]{0:T(256)(128)(2,1)} %refs_1_.5, ...), custom_call_target="tpu_custom_call" | custom-call | tf_op jit(solution)/shard_map/pack/pallas_call | solution.py:326
  6.1 2.0 %collective-permute-start.5 = (bf16[128,1024]{1,0:T(8,128)(2,1)S(1)}, bf16[128,1024]{1,0:T(8,128)(2,1)S(1)}, u32[]{:S(2)}, u32[]{:S(2)}) collective-permute-start(bf16[128,1024]{1,0:T(8,128)(2,1)S(1)} %get-tuple-element.64), channel_id=1, source_target_pairs={{0,2},{1,3},{2,0},{3,1},{4,6},{5,7},{6,4},{7,5},{8,10},{9,11},{10,... | collective-permute-start | bytes 786440 | tf_op jit(solution)/shard_map/ppermute | solution.py:317
  8.1 2.2 %copy-done = bf16[1,1024,2048]{2,1,0:T(8,128)(2,1)S(1)} copy-done((bf16[1,1024,2048]{2,1,0:T(8,128)(2,1)S(1)}, bf16[1,1024,2048]{2,1,0:T(8,128)(2,1)}, u32[]{:S(2)}) %copy-start) | copy-done | bytes 4194328
  10.3 2.0 %hidden.3 = (bf16[1024,256]{1,0:T(8,128)(2,1)S(1)}, bf16[256,2048]{1,0:T(8,128)(2,1)S(1)}, bf16[2048,256]{1,0:T(8,128)(2,1)S(1)}, bf16[256,2048]{1,0:T(8,128)(2,1)S(1)}) custom-call(bf16[128,1024]{1,0:T(8,128)(2,1)S(1)} %get-tuple-element.54.refs_0_, bf16[128,1024]{1,0:T(8,128)(2,1)S(1)} %collective-permute-done.1.refs_1_, bf16[1,1024,2048]{2,1,0:T(8,128)(2,1)S(1)} %copy-done), custom_call_target="tpu_custom_call" | custom-call | tf_op jit(solution)/shard_map/hidden/pallas_call | solution.py:100
  14.0 2.7 %collective-permute-done.2.id_ref = s32[1,256]{1,0:T(1,128)S(1)} collective-permute-done((s32[1,256]{1,0:T(1,128)}, s32[1,256]{1,0:T(1,128)S(1)}, u32[]{:S(2)}, u32[]{:S(2)}) %collective-permute-start.2) | collective-permute-done | bytes 1056 | tf_op jit(solution)/shard_map/ppermute | solution.py:323
  17.2 2.2 %collective-permute-start.6 = (bf16[128,1024]{1,0:T(8,128)(2,1)S(1)}, bf16[128,1024]{1,0:T(8,128)(2,1)S(1)}, u32[]{:S(2)}, u32[]{:S(2)}) collective-permute-start(bf16[128,1024]{1,0:T(8,128)(2,1)S(1)} %get-tuple-element.69), channel_id=1, source_target_pairs={{0,3},{1,2},{2,1},{3,0},{4,7},{5,6},{6,5},{7,4},{8,11},{9,10},{10,... | collective-permute-start | bytes 786440 | tf_op jit(solution)/shard_map/ppermute | solution.py:317
  20.4 1.7 %collective-permute-done.5.refs_0_.refs_4_.refs_5_ = bf16[128,1024]{1,0:T(8,128)(2,1)S(1)} collective-permute-done((bf16[128,1024]{1,0:T(8,128)(2,1)S(1)}, bf16[128,1024]{1,0:T(8,128)(2,1)S(1)}, u32[]{:S(2)}, u32[]{:S(2)}) %collective-permute-start.5) | collective-permute-done | bytes 262176 | tf_op jit(solution)/shard_map/ppermute | solution.py:317
  22.1 1.6 %pre_grad.4 = (bf16[128,2048]{1,0:T(8,128)(2,1)S(1)}, f32[128,128]{1,0:T(8,128)S(1)}) custom-call(bf16[128,1024]{1,0:T(8,128)(2,1)S(1)} %collective-permute-done.5.refs_0_.refs_4_.refs_5_, bf16[1,2048,1024]{2,1,0:T(8,128)(2,1)S(1)} %copy-done.2, bf16[128,2048]{1,0:T(8,128)(2,1)S(1)} %get-tuple-element.65.refs_2_.refs_4_, ...), custom_call_target="tpu_custom_call" | custom-call | tf_op jit(solution)/shard_map/pre_grad/pallas_call | solution.py:100
  26.7 1.8 %collective-permute-start.7 = (bf16[256,1024]{1,0:T(8,128)(2,1)S(1)}, bf16[256,1024]{1,0:T(8,128)(2,1)S(1)}, u32[]{:S(2)}, u32[]{:S(2)}) collective-permute-start(bf16[256,1024]{1,0:T(8,128)(2,1)S(1)} %get-tuple-element.73.refs_4_), channel_id=1, source_target_pairs={{0,8},{8,16},{16,24},{24,28},{28,20},{20,12},{12,4},{4,0},{1,9},{9... | collective-permute-start | bytes 1572872 | tf_op jit(solution)/shard_map/ppermute | solution.py:396
  28.8 1.6 %pre_grad.5 = (bf16[128,2048]{1,0:T(8,128)(2,1)S(1)}, f32[128,128]{1,0:T(8,128)S(1)}) custom-call(bf16[128,1024]{1,0:T(8,128)(2,1)S(1)} %collective-permute-done.6.refs_1_.refs_0_.refs_6_, bf16[1,2048,1024]{2,1,0:T(8,128)(2,1)S(1)} %copy-done.2, bf16[128,2048]{1,0:T(8,128)(2,1)S(1)} %get-tuple-element.70.refs_5_.refs_2_, ...), custom_call_target="tpu_custom_call" | custom-call | tf_op jit(solution)/shard_map/pre_grad/pallas_call | solution.py:100
  31.4 1.8 %collective-permute-start.11 = (bf16[128,2048]{1,0:T(8,128)(2,1)S(1)}, bf16[128,2048]{1,0:T(8,128)(2,1)S(1)}, u32[]{:S(2)}, u32[]{:S(2)}) collective-permute-start(bf16[128,2048]{1,0:T(8,128)(2,1)S(1)} %get-tuple-element.82.refs_0_), channel_id=1, source_target_pairs={{0,8},{8,16},{16,24},{24,28},{28,20},{20,12},{12,4},{4,0},{1,9},{9... | collective-permute-start | bytes 1572872 | tf_op jit(solution)/shard_map/ppermute | solution.py:396
  35.0 1.7 %collective-permute-start.13 = (bf16[128,1152]{1,0:T(8,128)(2,1)S(1)}, bf16[128,1152]{1,0:T(8,128)(2,1)S(1)}, u32[]{:S(2)}, u32[]{:S(2)}) collective-permute-start(bf16[128,1152]{1,0:T(8,128)(2,1)S(1)} %feat_grad.4.refs_9_), channel_id=1, source_target_pairs={{0,2},{1,3},{2,0},{3,1},{4,6},{5,7},{6,4},{7,5},{8,10},{9,11},{10,... | collective-permute-start | bytes 884744 | tf_op jit(solution)/shard_map/ppermute | solution.py:420
  36.8 4.7 %collective-permute-done.7.refs_7_ = bf16[256,1024]{1,0:T(8,128)(2,1)S(1)} collective-permute-done((bf16[256,1024]{1,0:T(8,128)(2,1)S(1)}, bf16[256,1024]{1,0:T(8,128)(2,1)S(1)}, u32[]{:S(2)}, u32[]{:S(2)}) %collective-permute-start.7) | collective-permute-done | bytes 524320 | tf_op jit(solution)/shard_map/ppermute | solution.py:396
  41.5 1.8 %collective-permute-done.8.refs_8_ = bf16[256,1024]{1,0:T(8,128)(2,1)S(1)} collective-permute-done((bf16[256,1024]{1,0:T(8,128)(2,1)S(1)}, bf16[256,1024]{1,0:T(8,128)(2,1)S(1)}, u32[]{:S(2)}, u32[]{:S(2)}) %collective-permute-start.8) | collective-permute-done | bytes 524320 | tf_op jit(solution)/shard_map/ppermute | solution.py:396
  45.9 1.6 %collective-permute-start.9 = (bf16[256,1024]{1,0:T(8,128)(2,1)S(1)}, bf16[256,1024]{1,0:T(8,128)(2,1)S(1)}, u32[]{:S(2)}, u32[]{:S(2)}) collective-permute-start(bf16[256,1024]{1,0:T(8,128)(2,1)S(1)} %get-tuple-element.84.refs_0_), channel_id=1, source_target_pairs={{0,8},{8,16},{16,24},{24,28},{28,20},{20,12},{12,4},{4,0},{1,9},{9... | collective-permute-start | bytes 1572872 | tf_op jit(solution)/shard_map/ppermute | solution.py:396
  48.0 4.7 %collective-permute-done.11.refs_6_ = bf16[128,2048]{1,0:T(8,128)(2,1)S(1)} collective-permute-done((bf16[128,2048]{1,0:T(8,128)(2,1)S(1)}, bf16[128,2048]{1,0:T(8,128)(2,1)S(1)}, u32[]{:S(2)}, u32[]{:S(2)}) %collective-permute-start.11) | collective-permute-done | bytes 524320 | tf_op jit(solution)/shard_map/ppermute | solution.py:396
  52.7 1.8 %collective-permute-done.12.refs_7_ = bf16[128,2048]{1,0:T(8,128)(2,1)S(1)} collective-permute-done((bf16[128,2048]{1,0:T(8,128)(2,1)S(1)}, bf16[128,2048]{1,0:T(8,128)(2,1)S(1)}, u32[]{:S(2)}, u32[]{:S(2)}) %collective-permute-start.12) | collective-permute-done | bytes 524320 | tf_op jit(solution)/shard_map/ppermute | solution.py:396
  55.5 1.6 %collective-permute-start.16 = (bf16[128,2048]{1,0:T(8,128)(2,1)S(1)}, bf16[128,2048]{1,0:T(8,128)(2,1)S(1)}, u32[]{:S(2)}, u32[]{:S(2)}) collective-permute-start(bf16[128,2048]{1,0:T(8,128)(2,1)S(1)} %get-tuple-element.86.refs_0_), channel_id=1, source_target_pairs={{0,8},{8,16},{16,24},{24,28},{28,20},{20,12},{12,4},{4,0},{1,9},{9... | collective-permute-start | bytes 1572872 | tf_op jit(solution)/shard_map/ppermute | solution.py:396
  59.2 4.7 %collective-permute-done.9.refs_7_ = bf16[256,1024]{1,0:T(8,128)(2,1)S(1)} collective-permute-done((bf16[256,1024]{1,0:T(8,128)(2,1)S(1)}, bf16[256,1024]{1,0:T(8,128)(2,1)S(1)}, u32[]{:S(2)}, u32[]{:S(2)}) %collective-permute-start.9) | collective-permute-done | bytes 524320 | tf_op jit(solution)/shard_map/ppermute | solution.py:396
  63.9 1.8 %collective-permute-done.10.refs_8_ = bf16[256,1024]{1,0:T(8,128)(2,1)S(1)} collective-permute-done((bf16[256,1024]{1,0:T(8,128)(2,1)S(1)}, bf16[256,1024]{1,0:T(8,128)(2,1)S(1)}, u32[]{:S(2)}, u32[]{:S(2)}) %collective-permute-start.10) | collective-permute-done | bytes 524320 | tf_op jit(solution)/shard_map/ppermute | solution.py:396
  66.8 1.6 %collective-permute-start.20 = (bf16[256,1024]{1,0:T(8,128)(2,1)S(1)}, bf16[256,1024]{1,0:T(8,128)(2,1)S(1)}, u32[]{:S(2)}, u32[]{:S(2)}) collective-permute-start(bf16[256,1024]{1,0:T(8,128)(2,1)S(1)} %get-tuple-element.88.refs_0_), channel_id=1, source_target_pairs={{0,8},{8,16},{16,24},{24,28},{28,20},{20,12},{12,4},{4,0},{1,9},{9... | collective-permute-start | bytes 1572872 | tf_op jit(solution)/shard_map/ppermute | solution.py:396
  70.4 4.8 %collective-permute-done.16.refs_6_ = bf16[128,2048]{1,0:T(8,128)(2,1)S(1)} collective-permute-done((bf16[128,2048]{1,0:T(8,128)(2,1)S(1)}, bf16[128,2048]{1,0:T(8,128)(2,1)S(1)}, u32[]{:S(2)}, u32[]{:S(2)}) %collective-permute-start.16) | collective-permute-done | bytes 524320 | tf_op jit(solution)/shard_map/ppermute | solution.py:396
  75.2 1.8 %collective-permute-done.17.refs_7_ = bf16[128,2048]{1,0:T(8,128)(2,1)S(1)} collective-permute-done((bf16[128,2048]{1,0:T(8,128)(2,1)S(1)}, bf16[128,2048]{1,0:T(8,128)(2,1)S(1)}, u32[]{:S(2)}, u32[]{:S(2)}) %collective-permute-start.17) | collective-permute-done | bytes 524320 | tf_op jit(solution)/shard_map/ppermute | solution.py:396
  78.0 1.6 %collective-permute-start.18 = (bf16[128,2048]{1,0:T(8,128)(2,1)S(1)}, bf16[128,2048]{1,0:T(8,128)(2,1)S(1)}, u32[]{:S(2)}, u32[]{:S(2)}) collective-permute-start(bf16[128,2048]{1,0:T(8,128)(2,1)S(1)} %get-tuple-element.90.refs_9_), channel_id=1, source_target_pairs={{0,8},{8,16},{16,24},{24,28},{28,20},{20,12},{12,4},{4,0},{1,9},{9... | collective-permute-start | bytes 1572872 | tf_op jit(solution)/shard_map/ppermute | solution.py:396
  80.1 6.3 %collective-permute-done.20.refs_7_ = bf16[256,1024]{1,0:T(8,128)(2,1)S(1)} collective-permute-done((bf16[256,1024]{1,0:T(8,128)(2,1)S(1)}, bf16[256,1024]{1,0:T(8,128)(2,1)S(1)}, u32[]{:S(2)}, u32[]{:S(2)}) %collective-permute-start.20) | collective-permute-done | bytes 524320 | tf_op jit(solution)/shard_map/ppermute | solution.py:396
  86.4 1.8 %collective-permute-done.21.refs_8_ = bf16[256,1024]{1,0:T(8,128)(2,1)S(1)} collective-permute-done((bf16[256,1024]{1,0:T(8,128)(2,1)S(1)}, bf16[256,1024]{1,0:T(8,128)(2,1)S(1)}, u32[]{:S(2)}, u32[]{:S(2)}) %collective-permute-start.21) | collective-permute-done | bytes 524320 | tf_op jit(solution)/shard_map/ppermute | solution.py:396
  88.8 1.6 %collective-permute-start.24 = (bf16[256,512]{1,0:T(8,128)(2,1)S(1)}, bf16[256,512]{1,0:T(8,128)(2,1)S(1)}, u32[]{:S(2)}, u32[]{:S(2)}) collective-permute-start(bf16[256,512]{1,0:T(8,128)(2,1)S(1)} %get-tuple-element.92.refs_9_), channel_id=1, source_target_pairs={{0,8},{8,16},{16,24},{24,28},{28,20},{20,12},{12,4},{4,0},{1,9},{9... | collective-permute-start | bytes 786440 | tf_op jit(solution)/shard_map/ppermute | solution.py:396
  91.5 6.2 %collective-permute-done.18.refs_6_ = bf16[128,2048]{1,0:T(8,128)(2,1)S(1)} collective-permute-done((bf16[128,2048]{1,0:T(8,128)(2,1)S(1)}, bf16[128,2048]{1,0:T(8,128)(2,1)S(1)}, u32[]{:S(2)}, u32[]{:S(2)}) %collective-permute-start.18) | collective-permute-done | bytes 524320 | tf_op jit(solution)/shard_map/ppermute | solution.py:396
  97.6 1.8 %collective-permute-done.19.refs_7_ = bf16[128,2048]{1,0:T(8,128)(2,1)S(1)} collective-permute-done((bf16[128,2048]{1,0:T(8,128)(2,1)S(1)}, bf16[128,2048]{1,0:T(8,128)(2,1)S(1)}, u32[]{:S(2)}, u32[]{:S(2)}) %collective-permute-start.19) | collective-permute-done | bytes 524320 | tf_op jit(solution)/shard_map/ppermute | solution.py:396
  100.1 1.6 %collective-permute-start.22 = (bf16[128,1024]{1,0:T(8,128)(2,1)S(1)}, bf16[128,1024]{1,0:T(8,128)(2,1)S(1)}, u32[]{:S(2)}, u32[]{:S(2)}) collective-permute-start(bf16[128,1024]{1,0:T(8,128)(2,1)S(1)} %get-tuple-element.94.refs_8_), channel_id=1, source_target_pairs={{0,8},{8,16},{16,24},{24,28},{28,20},{20,12},{12,4},{4,0},{1,9},{9... | collective-permute-start | bytes 786440 | tf_op jit(solution)/shard_map/ppermute | solution.py:396
  106.1 2.4 %collective-permute-done.22.refs_0_ = bf16[128,1024]{1,0:T(8,128)(2,1)S(1)} collective-permute-done((bf16[128,1024]{1,0:T(8,128)(2,1)S(1)}, bf16[128,1024]{1,0:T(8,128)(2,1)S(1)}, u32[]{:S(2)}, u32[]{:S(2)}) %collective-permute-start.22) | collective-permute-done | bytes 262176 | tf_op jit(solution)/shard_map/ppermute | solution.py:396
  (56 shorter events, 29.2 us)
Async XLA Ops:
  0.6 16.0 %collective-permute-start.3 = (bf16[256,1024]{1,0:T(8,128)(2,1)}, bf16[256,1024]{1,0:T(8,128)(2,1)S(1)}, u32[]{:S(2)}, u32[]{:S(2)}) collective-permute-start(bf16[256,1024]{1,0:T(8,128)(2,1)} %refs_3_.1), channel_id=1, source_target_pairs={{0,2},{1,3},{2,0},{3,1},{4,6},{5,7},{6,4},{7,5},{8,10},{9,11},{10,... | collective-permute-start | bytes 1572872 | tf_op jit(solution)/shard_map/ppermute | solution.py:322
  5.5 2.6 %collective-permute-start.1 = (bf16[128,1024]{1,0:T(8,128)(2,1)S(1)}, bf16[128,1024]{1,0:T(8,128)(2,1)S(1)}, u32[]{:S(2)}, u32[]{:S(2)}) collective-permute-start(bf16[128,1024]{1,0:T(8,128)(2,1)S(1)} %get-tuple-element.55), channel_id=1, source_target_pairs={{0,1},{1,0},{2,3},{3,2},{4,5},{5,4},{6,7},{7,6},{8,9},{9,8},{10,11... | collective-permute-start | bytes 786440 | tf_op jit(solution)/shard_map/ppermute | solution.py:317
  5.6 6.8 %collective-permute-start = (bf16[128,1024]{1,0:T(8,128)(2,1)S(1)}, bf16[128,1024]{1,0:T(8,128)(2,1)S(1)}, u32[]{:S(2)}, u32[]{:S(2)}) collective-permute-start(bf16[128,1024]{1,0:T(8,128)(2,1)S(1)} %get-tuple-element.53), channel_id=1, source_target_pairs={{0,1},{1,0},{2,3},{3,2},{4,5},{5,4},{6,7},{7,6},{8,9},{9,8},{10,11... | collective-permute-start | bytes 786440 | tf_op jit(solution)/shard_map/ppermute | solution.py:317
  6.1 10.6 %collective-permute-start.2 = (s32[1,256]{1,0:T(1,128)}, s32[1,256]{1,0:T(1,128)S(1)}, u32[]{:S(2)}, u32[]{:S(2)}) collective-permute-start(s32[1,256]{1,0:T(1,128)} %bitcast.1), channel_id=1, source_target_pairs={{0,2},{1,3},{2,0},{3,1},{4,6},{5,7},{6,4},{7,5},{8,10},{9,11},{10,... | collective-permute-start | bytes 3080 | tf_op jit(solution)/shard_map/ppermute | solution.py:323
  6.1 16.0 %collective-permute-start.5 = (bf16[128,1024]{1,0:T(8,128)(2,1)S(1)}, bf16[128,1024]{1,0:T(8,128)(2,1)S(1)}, u32[]{:S(2)}, u32[]{:S(2)}) collective-permute-start(bf16[128,1024]{1,0:T(8,128)(2,1)S(1)} %get-tuple-element.64), channel_id=1, source_target_pairs={{0,2},{1,3},{2,0},{3,1},{4,6},{5,7},{6,4},{7,5},{8,10},{9,11},{10,... | collective-permute-start | bytes 786440 | tf_op jit(solution)/shard_map/ppermute | solution.py:317
  8.1 2.2 %copy-start = (bf16[1,1024,2048]{2,1,0:T(8,128)(2,1)S(1)}, bf16[1,1024,2048]{2,1,0:T(8,128)(2,1)}, u32[]{:S(2)}) copy-start(bf16[1,1024,2048]{2,1,0:T(8,128)(2,1)} %up_ref.7) | copy-start | bytes 12582916
  10.3 2.2 %copy-start.2 = (bf16[1,2048,1024]{2,1,0:T(8,128)(2,1)S(1)}, bf16[1,2048,1024]{2,1,0:T(8,128)(2,1)}, u32[]{:S(2)}) copy-start(bf16[1,2048,1024]{2,1,0:T(8,128)(2,1)} %refs_1_.9) | copy-start | bytes 12582916
  12.3 7.0 %copy-start.1 = (bf16[1,1024,2048]{2,1,0:T(8,128)(2,1)S(1)}, bf16[1,1024,2048]{2,1,0:T(8,128)(2,1)}, u32[]{:S(2)}) copy-start(bf16[1,1024,2048]{2,1,0:T(8,128)(2,1)} %up_ref.7) | copy-start | bytes 12582916
  17.1 6.7 %collective-permute-start.4 = (bf16[128,1024]{1,0:T(8,128)(2,1)S(1)}, bf16[128,1024]{1,0:T(8,128)(2,1)S(1)}, u32[]{:S(2)}, u32[]{:S(2)}) collective-permute-start(bf16[128,1024]{1,0:T(8,128)(2,1)S(1)} %get-tuple-element.63), channel_id=1, source_target_pairs={{0,1},{1,0},{2,3},{3,2},{4,5},{5,4},{6,7},{7,6},{8,9},{9,8},{10,11... | collective-permute-start | bytes 786440 | tf_op jit(solution)/shard_map/ppermute | solution.py:317
  17.2 9.1 %collective-permute-start.6 = (bf16[128,1024]{1,0:T(8,128)(2,1)S(1)}, bf16[128,1024]{1,0:T(8,128)(2,1)S(1)}, u32[]{:S(2)}, u32[]{:S(2)}) collective-permute-start(bf16[128,1024]{1,0:T(8,128)(2,1)S(1)} %get-tuple-element.69), channel_id=1, source_target_pairs={{0,3},{1,2},{2,1},{3,0},{4,7},{5,6},{6,5},{7,4},{8,11},{9,10},{10,... | collective-permute-start | bytes 786440 | tf_op jit(solution)/shard_map/ppermute | solution.py:317
  26.7 14.8 %collective-permute-start.7 = (bf16[256,1024]{1,0:T(8,128)(2,1)S(1)}, bf16[256,1024]{1,0:T(8,128)(2,1)S(1)}, u32[]{:S(2)}, u32[]{:S(2)}) collective-permute-start(bf16[256,1024]{1,0:T(8,128)(2,1)S(1)} %get-tuple-element.73.refs_4_), channel_id=1, source_target_pairs={{0,8},{8,16},{16,24},{24,28},{28,20},{20,12},{12,4},{4,0},{1,9},{9... | collective-permute-start | bytes 1572872 | tf_op jit(solution)/shard_map/ppermute | solution.py:396
  28.6 14.7 %collective-permute-start.8 = (bf16[256,1024]{1,0:T(8,128)(2,1)S(1)}, bf16[256,1024]{1,0:T(8,128)(2,1)S(1)}, u32[]{:S(2)}, u32[]{:S(2)}) collective-permute-start(bf16[256,1024]{1,0:T(8,128)(2,1)S(1)} %get-tuple-element.74.refs_5_), channel_id=1, source_target_pairs={{8,0},{16,8},{24,16},{28,24},{20,28},{12,20},{4,12},{0,4},{9,1},{1... | collective-permute-start | bytes 1572872 | tf_op jit(solution)/shard_map/ppermute | solution.py:396
  31.4 21.3 %collective-permute-start.11 = (bf16[128,2048]{1,0:T(8,128)(2,1)S(1)}, bf16[128,2048]{1,0:T(8,128)(2,1)S(1)}, u32[]{:S(2)}, u32[]{:S(2)}) collective-permute-start(bf16[128,2048]{1,0:T(8,128)(2,1)S(1)} %get-tuple-element.82.refs_0_), channel_id=1, source_target_pairs={{0,8},{8,16},{16,24},{24,28},{28,20},{20,12},{12,4},{4,0},{1,9},{9... | collective-permute-start | bytes 1572872 | tf_op jit(solution)/shard_map/ppermute | solution.py:396
  33.2 21.3 %collective-permute-start.12 = (bf16[128,2048]{1,0:T(8,128)(2,1)S(1)}, bf16[128,2048]{1,0:T(8,128)(2,1)S(1)}, u32[]{:S(2)}, u32[]{:S(2)}) collective-permute-start(bf16[128,2048]{1,0:T(8,128)(2,1)S(1)} %get-tuple-element.83.refs_1_), channel_id=1, source_target_pairs={{8,0},{16,8},{24,16},{28,24},{20,28},{12,20},{4,12},{0,4},{9,1},{1... | collective-permute-start | bytes 1572872 | tf_op jit(solution)/shard_map/ppermute | solution.py:396
  35.0 9.3 %collective-permute-start.13 = (bf16[128,1152]{1,0:T(8,128)(2,1)S(1)}, bf16[128,1152]{1,0:T(8,128)(2,1)S(1)}, u32[]{:S(2)}, u32[]{:S(2)}) collective-permute-start(bf16[128,1152]{1,0:T(8,128)(2,1)S(1)} %feat_grad.4.refs_9_), channel_id=1, source_target_pairs={{0,2},{1,3},{2,0},{3,1},{4,6},{5,7},{6,4},{7,5},{8,10},{9,11},{10,... | collective-permute-start | bytes 884744 | tf_op jit(solution)/shard_map/ppermute | solution.py:420
  45.8 11.8 %collective-permute-start.14 = (bf16[128,1152]{1,0:T(8,128)(2,1)S(1)}, bf16[128,1152]{1,0:T(8,128)(2,1)S(1)}, u32[]{:S(2)}, u32[]{:S(2)}) collective-permute-start(bf16[128,1152]{1,0:T(8,128)(2,1)S(1)} %feat_grad.5.refs_8_), channel_id=1, source_target_pairs={{0,3},{1,2},{2,1},{3,0},{4,7},{5,6},{6,5},{7,4},{8,11},{9,10},{10,... | collective-permute-start | bytes 884744 | tf_op jit(solution)/shard_map/ppermute | solution.py:420
  45.9 18.1 %collective-permute-start.9 = (bf16[256,1024]{1,0:T(8,128)(2,1)S(1)}, bf16[256,1024]{1,0:T(8,128)(2,1)S(1)}, u32[]{:S(2)}, u32[]{:S(2)}) collective-permute-start(bf16[256,1024]{1,0:T(8,128)(2,1)S(1)} %get-tuple-element.84.refs_0_), channel_id=1, source_target_pairs={{0,8},{8,16},{16,24},{24,28},{28,20},{20,12},{12,4},{4,0},{1,9},{9... | collective-permute-start | bytes 1572872 | tf_op jit(solution)/shard_map/ppermute | solution.py:396
  47.5 18.3 %collective-permute-start.10 = (bf16[256,1024]{1,0:T(8,128)(2,1)S(1)}, bf16[256,1024]{1,0:T(8,128)(2,1)S(1)}, u32[]{:S(2)}, u32[]{:S(2)}) collective-permute-start(bf16[256,1024]{1,0:T(8,128)(2,1)S(1)} %get-tuple-element.85.refs_1_), channel_id=1, source_target_pairs={{8,0},{16,8},{24,16},{28,24},{20,28},{12,20},{4,12},{0,4},{9,1},{1... | collective-permute-start | bytes 1572872 | tf_op jit(solution)/shard_map/ppermute | solution.py:396
  55.5 19.6 %collective-permute-start.16 = (bf16[128,2048]{1,0:T(8,128)(2,1)S(1)}, bf16[128,2048]{1,0:T(8,128)(2,1)S(1)}, u32[]{:S(2)}, u32[]{:S(2)}) collective-permute-start(bf16[128,2048]{1,0:T(8,128)(2,1)S(1)} %get-tuple-element.86.refs_0_), channel_id=1, source_target_pairs={{0,8},{8,16},{16,24},{24,28},{28,20},{20,12},{12,4},{4,0},{1,9},{9... | collective-permute-start | bytes 1572872 | tf_op jit(solution)/shard_map/ppermute | solution.py:396
  57.2 19.9 %collective-permute-start.17 = (bf16[128,2048]{1,0:T(8,128)(2,1)S(1)}, bf16[128,2048]{1,0:T(8,128)(2,1)S(1)}, u32[]{:S(2)}, u32[]{:S(2)}) collective-permute-start(bf16[128,2048]{1,0:T(8,128)(2,1)S(1)} %get-tuple-element.87.refs_1_), channel_id=1, source_target_pairs={{8,0},{16,8},{24,16},{28,24},{20,28},{12,20},{4,12},{0,4},{9,1},{1... | collective-permute-start | bytes 1572872 | tf_op jit(solution)/shard_map/ppermute | solution.py:396
  59.1 9.7 %collective-permute-start.15 = (bf16[128,1152]{1,0:T(8,128)(2,1)S(1)}, bf16[128,1152]{1,0:T(8,128)(2,1)S(1)}, u32[]{:S(2)}, u32[]{:S(2)}) collective-permute-start(bf16[128,1152]{1,0:T(8,128)(2,1)S(1)} %feat_grad.6.refs_9_), channel_id=1, source_target_pairs={{0,1},{1,0},{2,3},{3,2},{4,5},{5,4},{6,7},{7,6},{8,9},{9,8},{10,11... | collective-permute-start | bytes 884744 | tf_op jit(solution)/shard_map/ppermute | solution.py:420
  66.8 19.7 %collective-permute-start.20 = (bf16[256,1024]{1,0:T(8,128)(2,1)S(1)}, bf16[256,1024]{1,0:T(8,128)(2,1)S(1)}, u32[]{:S(2)}, u32[]{:S(2)}) collective-permute-start(bf16[256,1024]{1,0:T(8,128)(2,1)S(1)} %get-tuple-element.88.refs_0_), channel_id=1, source_target_pairs={{0,8},{8,16},{16,24},{24,28},{28,20},{20,12},{12,4},{4,0},{1,9},{9... | collective-permute-start | bytes 1572872 | tf_op jit(solution)/shard_map/ppermute | solution.py:396
  68.4 19.9 %collective-permute-start.21 = (bf16[256,1024]{1,0:T(8,128)(2,1)S(1)}, bf16[256,1024]{1,0:T(8,128)(2,1)S(1)}, u32[]{:S(2)}, u32[]{:S(2)}) collective-permute-start(bf16[256,1024]{1,0:T(8,128)(2,1)S(1)} %get-tuple-element.89.refs_1_), channel_id=1, source_target_pairs={{8,0},{16,8},{24,16},{28,24},{20,28},{12,20},{4,12},{0,4},{9,1},{1... | collective-permute-start | bytes 1572872 | tf_op jit(solution)/shard_map/ppermute | solution.py:396
  78.0 19.6 %collective-permute-start.18 = (bf16[128,2048]{1,0:T(8,128)(2,1)S(1)}, bf16[128,2048]{1,0:T(8,128)(2,1)S(1)}, u32[]{:S(2)}, u32[]{:S(2)}) collective-permute-start(bf16[128,2048]{1,0:T(8,128)(2,1)S(1)} %get-tuple-element.90.refs_9_), channel_id=1, source_target_pairs={{0,8},{8,16},{16,24},{24,28},{28,20},{20,12},{12,4},{4,0},{1,9},{9... | collective-permute-start | bytes 1572872 | tf_op jit(solution)/shard_map/ppermute | solution.py:396
  79.6 19.9 %collective-permute-start.19 = (bf16[128,2048]{1,0:T(8,128)(2,1)S(1)}, bf16[128,2048]{1,0:T(8,128)(2,1)S(1)}, u32[]{:S(2)}, u32[]{:S(2)}) collective-permute-start(bf16[128,2048]{1,0:T(8,128)(2,1)S(1)} %get-tuple-element.91.refs_10_), channel_id=1, source_target_pairs={{8,0},{16,8},{24,16},{28,24},{20,28},{12,20},{4,12},{0,4},{9,1},{1... | collective-permute-start | bytes 1572872 | tf_op jit(solution)/shard_map/ppermute | solution.py:396
  88.8 16.2 %collective-permute-start.24 = (bf16[256,512]{1,0:T(8,128)(2,1)S(1)}, bf16[256,512]{1,0:T(8,128)(2,1)S(1)}, u32[]{:S(2)}, u32[]{:S(2)}) collective-permute-start(bf16[256,512]{1,0:T(8,128)(2,1)S(1)} %get-tuple-element.92.refs_9_), channel_id=1, source_target_pairs={{0,8},{8,16},{16,24},{24,28},{28,20},{20,12},{12,4},{4,0},{1,9},{9... | collective-permute-start | bytes 786440 | tf_op jit(solution)/shard_map/ppermute | solution.py:396
  90.5 14.6 %collective-permute-start.25 = (bf16[256,512]{1,0:T(8,128)(2,1)S(1)}, bf16[256,512]{1,0:T(8,128)(2,1)S(1)}, u32[]{:S(2)}, u32[]{:S(2)}) collective-permute-start(bf16[256,512]{1,0:T(8,128)(2,1)S(1)} %get-tuple-element.93.refs_10_), channel_id=1, source_target_pairs={{8,0},{16,8},{24,16},{28,24},{20,28},{12,20},{4,12},{0,4},{9,1},{1... | collective-permute-start | bytes 786440 | tf_op jit(solution)/shard_map/ppermute | solution.py:396
  100.1 4.5 %copy-start.3 = (bf16[256]{0:T(256)(128)(2,1)S(1)}, bf16[256]{0:T(256)(128)(2,1)}, u32[]{:S(2)}) copy-start(bf16[256]{0:T(256)(128)(2,1)} %refs_1_.5) | copy-start | bytes 1540
  100.1 8.5 %collective-permute-start.22 = (bf16[128,1024]{1,0:T(8,128)(2,1)S(1)}, bf16[128,1024]{1,0:T(8,128)(2,1)S(1)}, u32[]{:S(2)}, u32[]{:S(2)}) collective-permute-start(bf16[128,1024]{1,0:T(8,128)(2,1)S(1)} %get-tuple-element.94.refs_8_), channel_id=1, source_target_pairs={{0,8},{8,16},{16,24},{24,28},{28,20},{20,12},{12,4},{4,0},{1,9},{9... | collective-permute-start | bytes 786440 | tf_op jit(solution)/shard_map/ppermute | solution.py:396
  101.7 8.4 %collective-permute-start.23 = (bf16[128,1024]{1,0:T(8,128)(2,1)S(1)}, bf16[128,1024]{1,0:T(8,128)(2,1)S(1)}, u32[]{:S(2)}, u32[]{:S(2)}) collective-permute-start(bf16[128,1024]{1,0:T(8,128)(2,1)S(1)} %get-tuple-element.95.refs_9_), channel_id=1, source_target_pairs={{8,0},{16,8},{24,16},{28,24},{20,28},{12,20},{4,12},{0,4},{9,1},{1... | collective-permute-start | bytes 786440 | tf_op jit(solution)/shard_map/ppermute | solution.py:396

commit v5 on v3

--- a/solution.py
+++ b/solution.py
@@ -211,7 +211,7 @@
     return [(ring[p], ring[(p + 1) % count]) for p in range(count)]
 
 
-def step_kernel(parts, arrivals, step, count, last, *refs):
+def step_kernel(parts, arrivals, step, count, *refs):
     groups = len(parts)
     lefts, refs = refs[:groups], refs[groups:]
     rights, refs = refs[: sum(parts)], refs[sum(parts) :]
@@ -230,43 +230,49 @@
             totals[way] += dot(
                 left[pl.ds(start, rows), :], right[:, way * half : (way + 1) * half], 1, 0
             )
-    if not last:
-        for way, out in enumerate(refs[-2:]):
-            out[...] = totals[way].astype(out.dtype)
-        return
-    out, held, sems = refs[-3:]
-    half = held.shape[2]
-    copies = []
+    for way, out in enumerate(refs[-2:]):
+        out[...] = totals[way].astype(out.dtype)
+
+
+def last_kernel(way, count, arrived_ref, own_ref, *refs):
+    out, held, sem = refs[-3:]
+    half = held.shape[1]
+    held[...] = (own_ref[...] + arrived_ref[...].astype(F32)) * (1.0 / count)
+    copy = pltpu.make_async_copy(held, out.at[0, :, way * half : (way + 1) * half], sem)
+    copy.start()
+    copy.wait()
+
+
+def last_call(name, count, arrived, own, after):
+    rows, half = own[0].shape
+    out = []
     for way in range(2):
-        held[way] = totals[way] * (1.0 / count)
-        target = out.at[0, :, way * half : (way + 1) * half]
-        copies.append(pltpu.make_async_copy(held.at[way], target, sems.at[way]))
-        copies[-1].start()
-    for copy in copies:
-        copy.wait()
+        out = [
+            pl.pallas_call(
+                functools.partial(last_kernel, way, count),
+                in_specs=[WHOLE] * 2
+                + [pl.BlockSpec(memory_space=pltpu.HBM)] * len(out)
+                + [LATER] * len(after),
+                out_specs=pl.BlockSpec(memory_space=pltpu.HBM),
+                out_shape=pltpu.HBM((1, rows, 2 * half), F32),
+                input_output_aliases={2: 0} if out else {},
+                scratch_shapes=[pltpu.VMEM((rows, half), F32), pltpu.SemaphoreType.DMA],
+                compiler_params=params(),
+                name=name,
+            )(arrived[way], own[way], *(in_hbm(a) for a in out), *after)
+        ]
+        after = []
+    return out[0]
 
 
 def ring_step(name, step, count, shape, lefts, rights, arrived, after=(), dtype=BF16):
-    rows, half = shape
-    last = dtype is None
-    if last:
-        out_specs = [pl.BlockSpec(memory_space=pltpu.HBM)]
-        out_shape = [pltpu.HBM((1, rows, 2 * half), F32)]
-        scratch = [pltpu.VMEM((2, rows, half), F32), pltpu.SemaphoreType.DMA((2,))]
-    else:
-        out_specs = [WHOLE] * 2
-        out_shape = [jax.ShapeDtypeStruct(shape, dtype)] * 2
-        scratch = []
     blocks = [block for group in rights for block in group]
     inputs = [*lefts, *blocks, *arrived]
     return pl.pallas_call(
-        functools.partial(
-            step_kernel, [len(group) for group in rights], len(arrived), step, count, last
-        ),
+        functools.partial(step_kernel, [len(group) for group in rights], len(arrived), step, count),
         in_specs=[WHOLE] * len(inputs) + [LATER] * len(after),
-        out_specs=out_specs,
-        out_shape=out_shape,
-        scratch_shapes=scratch,
+        out_specs=[WHOLE] * 2,
+        out_shape=[jax.ShapeDtypeStruct(shape, dtype)] * 2,
         compiler_params=params(),
         name=name,
     )(*inputs, *after)
@@ -429,13 +435,8 @@
                 F32,
             )
             after = up_last[:1]
-    down = ring_step(
-        "down_last", ring, ring, down_shape, [], [], [*down_in, *down_last], [], None
-    )
-    after_down = [in_hbm(down[0])]
-    up = ring_step(
-        "up_last", ring, ring, up_shape, [], [], [*up_in, *up_last], after_down, None
-    )
+    down = last_call("down_last", ring, down_in, down_last, [])
+    up = last_call("up_last", ring, up_in, up_last, [in_hbm(down)])
     tokens_grad, gate_sums = pl.pallas_call(
         functools.partial(unpack_kernel, capacity, width, peers),
         in_specs=[WHOLE] * (1 + peers) + [LATER] * len(after),
@@ -448,7 +449,7 @@
         name="unpack",
     )(slot, *(feat_back[k] for k in range(peers)), *after)
     gate_result = ((gate_sums[:, 0] + gate_sums[:, 1]) / gate_prob.astype(F32)).astype(BF16)
-    return (tokens_grad, gate_result, up[0], down[0])
+    return (tokens_grad, gate_result, up, down)
 
 
 def solution(mesh):

time: 111 us -> 111 us (level)
  waiting for transfers between devices: 38.1 us -> 36.5 us
  Pallas kernels: 30.2 us -> 31.6 us
    pallas_call x0 -> x4, Pallas kernels: none -> 3.44 us  [last_call(): pl.pallas_call(functools.partial(last_kernel, way, count), in_specs=[WHOL...]
    pallas_call x19 -> x17, Pallas kernels: 11.4 us -> 9.32 us  [ring_step(): pl.pallas_call(functools.partial(step_kernel, [len(group) for group in ri...]
    ppermute x14, waiting for transfers between devices: 19.2 us -> 17.7 us  [send(): lax.ppermute(pair[1], 'dp', backward)]
  transfers between devices with their start and end apart: 38 -> 38, of which waited for: 29 -> 28; matrix products, arithmetic and copies ran while one was open for 1% -> 1% of each run, Pallas kernels for 26% -> 27%
where the time goes in v5:
time: 111 us
  starting transfers between devices  38.8 us (35%)
  waiting for transfers between devices  36.5 us (33%)
  Pallas kernels  31.6 us (28%)
  local copies, waits for them, and re-layouts  2.35 us (2%)
    ppermute x14, starting transfers between devices, send(): lax.ppermute(pair[0], 'dp', forward)  22.1 us
    ppermute x14, waiting for transfers between devices, send(): lax.ppermute(pair[1], 'dp', backward)  17.7 us
    pallas_call x10, Pallas kernels, call(): pl.pallas_call(body, in_specs=[WHOLE] * len(inputs) + [LATER] * len(after...  14.9 us
    ppermute x14, waiting for transfers between devices, send(): lax.ppermute(pair[0], 'dp', forward)  13 us
    pallas_call x17, Pallas kernels, ring_step(): pl.pallas_call(functools.partial(step_kernel, [len(group) for group in ri...  9.32 us
    ppermute x14, starting transfers between devices, send(): lax.ppermute(pair[1], 'dp', backward)  7 us
    ppermute x5, starting transfers between devices, exchange(): return {k: lax.ppermute(outs[k], 'expert', sources[k]) for k in reach}  4.82 us
    pallas_call x4, Pallas kernels, last_call(): pl.pallas_call(functools.partial(last_kernel, way, count), in_specs=[WHOL...  3.44 us
  transfers between devices with their start and end apart: 38, of which 28 were waited for; matrix products, arithmetic and copies ran while one was open for 1% of the time, Pallas kernels for 27%

profile of v5, /device:TPU:0, one launch (start us, length us, event | category | flops | bytes accessed | tf_op | source)
XLA Modules:
  0.0 111.0 jit_solution(16845779842795540656)
XLA Ops:
  0.6 3.0 %collective-permute-start.3 = (bf16[256,1024]{1,0:T(8,128)(2,1)}, bf16[256,1024]{1,0:T(8,128)(2,1)S(1)}, u32[]{:S(2)}, u32[]{:S(2)}) collective-permute-start(bf16[256,1024]{1,0:T(8,128)(2,1)} %refs_3_.1), channel_id=1, source_target_pairs={{0,2},{1,3},{2,0},{3,1},{4,6},{5,7},{6,4},{7,5},{8,10},{9,11},{10,... | collective-permute-start | bytes 1572872 | tf_op jit(solution)/shard_map/ppermute | solution.py:298
  3.6 1.9 %pack.1 = (s32[1,256]{1,0:T(1,128)S(1)}, bf16[128,1024]{1,0:T(8,128)(2,1)S(1)}, bf16[128,1024]{1,0:T(8,128)(2,1)S(1)}, bf16[128,1024]{1,0:T(8,128)(2,1)S(1)}, bf...) custom-call(s32[256]{0:T(256)} %refs_0_.1, bf16[256]{0:T(256)(128)(2,1)} %refs_1_.5, ...), custom_call_target="tpu_custom_call" | custom-call | tf_op jit(solution)/shard_map/pack/pallas_call | solution.py:302
  6.1 2.0 %collective-permute-start.5 = (bf16[128,1024]{1,0:T(8,128)(2,1)S(1)}, bf16[128,1024]{1,0:T(8,128)(2,1)S(1)}, u32[]{:S(2)}, u32[]{:S(2)}) collective-permute-start(bf16[128,1024]{1,0:T(8,128)(2,1)S(1)} %get-tuple-element.80), channel_id=1, source_target_pairs={{0,2},{1,3},{2,0},{3,1},{4,6},{5,7},{6,4},{7,5},{8,10},{9,11},{10,... | collective-permute-start | bytes 786440 | tf_op jit(solution)/shard_map/ppermute | solution.py:293
  8.1 2.2 %copy-done = bf16[1,1024,2048]{2,1,0:T(8,128)(2,1)S(1)} copy-done((bf16[1,1024,2048]{2,1,0:T(8,128)(2,1)S(1)}, bf16[1,1024,2048]{2,1,0:T(8,128)(2,1)}, u32[]{:S(2)}) %copy-start) | copy-done | bytes 4194328
  10.3 2.0 %hidden.3 = (bf16[1024,256]{1,0:T(8,128)(2,1)S(1)}, bf16[256,2048]{1,0:T(8,128)(2,1)S(1)}, bf16[2048,256]{1,0:T(8,128)(2,1)S(1)}, bf16[256,2048]{1,0:T(8,128)(2,1)S(1)}) custom-call(bf16[128,1024]{1,0:T(8,128)(2,1)S(1)} %get-tuple-element.70.refs_0_, bf16[128,1024]{1,0:T(8,128)(2,1)S(1)} %collective-permute-done.1.refs_1_, bf16[1,1024,2048]{2,1,0:T(8,128)(2,1)S(1)} %copy-done), custom_call_target="tpu_custom_call" | custom-call | tf_op jit(solution)/shard_map/hidden/pallas_call | solution.py:100
  14.0 2.7 %collective-permute-done.2.id_ref = s32[1,256]{1,0:T(1,128)S(1)} collective-permute-done((s32[1,256]{1,0:T(1,128)}, s32[1,256]{1,0:T(1,128)S(1)}, u32[]{:S(2)}, u32[]{:S(2)}) %collective-permute-start.2) | collective-permute-done | bytes 1056 | tf_op jit(solution)/shard_map/ppermute | solution.py:299
  17.2 2.2 %collective-permute-start.6 = (bf16[128,1024]{1,0:T(8,128)(2,1)S(1)}, bf16[128,1024]{1,0:T(8,128)(2,1)S(1)}, u32[]{:S(2)}, u32[]{:S(2)}) collective-permute-start(bf16[128,1024]{1,0:T(8,128)(2,1)S(1)} %get-tuple-element.86), channel_id=1, source_target_pairs={{0,3},{1,2},{2,1},{3,0},{4,7},{5,6},{6,5},{7,4},{8,11},{9,10},{10,... | collective-permute-start | bytes 786440 | tf_op jit(solution)/shard_map/ppermute | solution.py:293
  20.4 1.7 %collective-permute-done.5.refs_0_.refs_4_.refs_5_ = bf16[128,1024]{1,0:T(8,128)(2,1)S(1)} collective-permute-done((bf16[128,1024]{1,0:T(8,128)(2,1)S(1)}, bf16[128,1024]{1,0:T(8,128)(2,1)S(1)}, u32[]{:S(2)}, u32[]{:S(2)}) %collective-permute-start.5) | collective-permute-done | bytes 262176 | tf_op jit(solution)/shard_map/ppermute | solution.py:293
  22.1 1.6 %pre_grad.4 = (bf16[128,2048]{1,0:T(8,128)(2,1)S(1)}, f32[128,128]{1,0:T(8,128)S(1)}) custom-call(bf16[128,1024]{1,0:T(8,128)(2,1)S(1)} %collective-permute-done.5.refs_0_.refs_4_.refs_5_, bf16[1,2048,1024]{2,1,0:T(8,128)(2,1)S(1)} %copy-done.2, bf16[128,2048]{1,0:T(8,128)(2,1)S(1)} %get-tuple-element.81.refs_2_.refs_4_, ...), custom_call_target="tpu_custom_call" | custom-call | tf_op jit(solution)/shard_map/pre_grad/pallas_call | solution.py:100
  26.6 1.8 %collective-permute-start.9 = (bf16[256,512]{1,0:T(8,128)(2,1)S(1)}, bf16[256,512]{1,0:T(8,128)(2,1)S(1)}, u32[]{:S(2)}, u32[]{:S(2)}) collective-permute-start(bf16[256,512]{1,0:T(8,128)(2,1)S(1)} %get-tuple-element.94.refs_4_), channel_id=1, source_target_pairs={{0,8},{8,16},{16,24},{24,28},{28,20},{20,12},{12,4},{4,0},{1,9},{9... | collective-permute-start | bytes 786440 | tf_op jit(solution)/shard_map/ppermute | solution.py:370
  28.7 1.6 %pre_grad.5 = (bf16[128,2048]{1,0:T(8,128)(2,1)S(1)}, f32[128,128]{1,0:T(8,128)S(1)}) custom-call(bf16[128,1024]{1,0:T(8,128)(2,1)S(1)} %collective-permute-done.6.refs_1_.refs_0_.refs_6_, bf16[1,2048,1024]{2,1,0:T(8,128)(2,1)S(1)} %copy-done.2, bf16[128,2048]{1,0:T(8,128)(2,1)S(1)} %get-tuple-element.87.refs_5_.refs_2_, ...), custom_call_target="tpu_custom_call" | custom-call | tf_op jit(solution)/shard_map/pre_grad/pallas_call | solution.py:100
  30.9 1.8 %collective-permute-start.7 = (bf16[128,1024]{1,0:T(8,128)(2,1)S(1)}, bf16[128,1024]{1,0:T(8,128)(2,1)S(1)}, u32[]{:S(2)}, u32[]{:S(2)}) collective-permute-start(bf16[128,1024]{1,0:T(8,128)(2,1)S(1)} %get-tuple-element.98.refs_9_), channel_id=1, source_target_pairs={{0,8},{8,16},{16,24},{24,28},{28,20},{20,12},{12,4},{4,0},{1,9},{9... | collective-permute-start | bytes 786440 | tf_op jit(solution)/shard_map/ppermute | solution.py:370
  33.0 2.8 %collective-permute-done.9.refs_7_ = bf16[256,512]{1,0:T(8,128)(2,1)S(1)} collective-permute-done((bf16[256,512]{1,0:T(8,128)(2,1)S(1)}, bf16[256,512]{1,0:T(8,128)(2,1)S(1)}, u32[]{:S(2)}, u32[]{:S(2)}) %collective-permute-start.9) | collective-permute-done | bytes 262176 | tf_op jit(solution)/shard_map/ppermute | solution.py:370
  35.7 1.8 %collective-permute-done.10.refs_8_ = bf16[256,512]{1,0:T(8,128)(2,1)S(1)} collective-permute-done((bf16[256,512]{1,0:T(8,128)(2,1)S(1)}, bf16[256,512]{1,0:T(8,128)(2,1)S(1)}, u32[]{:S(2)}, u32[]{:S(2)}) %collective-permute-start.10) | collective-permute-done | bytes 262176 | tf_op jit(solution)/shard_map/ppermute | solution.py:370
  38.1 1.6 %collective-permute-start.13 = (bf16[256,512]{1,0:T(8,128)(2,1)S(1)}, bf16[256,512]{1,0:T(8,128)(2,1)S(1)}, u32[]{:S(2)}, u32[]{:S(2)}) collective-permute-start(bf16[256,512]{1,0:T(8,128)(2,1)S(1)} %get-tuple-element.100.refs_8_), channel_id=1, source_target_pairs={{0,8},{8,16},{16,24},{24,28},{28,20},{20,12},{12,4},{4,0},{1,9},{9... | collective-permute-start | bytes 786440 | tf_op jit(solution)/shard_map/ppermute | solution.py:370
  41.3 1.8 %collective-permute-done.8.refs_7_ = bf16[128,1024]{1,0:T(8,128)(2,1)S(1)} collective-permute-done((bf16[128,1024]{1,0:T(8,128)(2,1)S(1)}, bf16[128,1024]{1,0:T(8,128)(2,1)S(1)}, u32[]{:S(2)}, u32[]{:S(2)}) %collective-permute-start.8) | collective-permute-done | bytes 262176 | tf_op jit(solution)/shard_map/ppermute | solution.py:370
  43.8 1.6 %collective-permute-start.11 = (bf16[128,1024]{1,0:T(8,128)(2,1)S(1)}, bf16[128,1024]{1,0:T(8,128)(2,1)S(1)}, u32[]{:S(2)}, u32[]{:S(2)}) collective-permute-start(bf16[128,1024]{1,0:T(8,128)(2,1)S(1)} %get-tuple-element.102.refs_0_), channel_id=1, source_target_pairs={{0,8},{8,16},{16,24},{24,28},{28,20},{20,12},{12,4},{4,0},{1,9},{9... | collective-permute-start | bytes 786440 | tf_op jit(solution)/shard_map/ppermute | solution.py:370
  47.3 1.6 %collective-permute-start.19 = (bf16[128,1152]{1,0:T(8,128)(2,1)S(1)}, bf16[128,1152]{1,0:T(8,128)(2,1)S(1)}, u32[]{:S(2)}, u32[]{:S(2)}) collective-permute-start(bf16[128,1152]{1,0:T(8,128)(2,1)S(1)} %feat_grad.4.refs_9_), channel_id=1, source_target_pairs={{0,2},{1,3},{2,0},{3,1},{4,6},{5,7},{6,4},{7,5},{8,10},{9,11},{10,... | collective-permute-start | bytes 884744 | tf_op jit(solution)/shard_map/ppermute | solution.py:412
  49.6 1.6 %collective-permute-start.17 = (bf16[256,512]{1,0:T(8,128)(2,1)S(1)}, bf16[256,512]{1,0:T(8,128)(2,1)S(1)}, u32[]{:S(2)}, u32[]{:S(2)}) collective-permute-start(bf16[256,512]{1,0:T(8,128)(2,1)S(1)} %get-tuple-element.104.refs_8_), channel_id=1, source_target_pairs={{0,8},{8,16},{16,24},{24,28},{28,20},{20,12},{12,4},{4,0},{1,9},{9... | collective-permute-start | bytes 786440 | tf_op jit(solution)/shard_map/ppermute | solution.py:370
  53.0 1.6 %collective-permute-done.12.refs_7_ = bf16[128,1024]{1,0:T(8,128)(2,1)S(1)} collective-permute-done((bf16[128,1024]{1,0:T(8,128)(2,1)S(1)}, bf16[128,1024]{1,0:T(8,128)(2,1)S(1)}, u32[]{:S(2)}, u32[]{:S(2)}) %collective-permute-start.12) | collective-permute-done | bytes 262176 | tf_op jit(solution)/shard_map/ppermute | solution.py:370
  55.2 1.6 %collective-permute-start.15 = (bf16[128,1024]{1,0:T(8,128)(2,1)S(1)}, bf16[128,1024]{1,0:T(8,128)(2,1)S(1)}, u32[]{:S(2)}, u32[]{:S(2)}) collective-permute-start(bf16[128,1024]{1,0:T(8,128)(2,1)S(1)} %get-tuple-element.106.refs_0_), channel_id=1, source_target_pairs={{0,8},{8,16},{16,24},{24,28},{28,20},{20,12},{12,4},{4,0},{1,9},{9... | collective-permute-start | bytes 786440 | tf_op jit(solution)/shard_map/ppermute | solution.py:370
  58.9 1.6 %collective-permute-done.18.refs_8_ = bf16[256,512]{1,0:T(8,128)(2,1)S(1)} collective-permute-done((bf16[256,512]{1,0:T(8,128)(2,1)S(1)}, bf16[256,512]{1,0:T(8,128)(2,1)S(1)}, u32[]{:S(2)}, u32[]{:S(2)}) %collective-permute-start.18) | collective-permute-done | bytes 262176 | tf_op jit(solution)/shard_map/ppermute | solution.py:370
  61.0 1.6 %collective-permute-start.22 = (bf16[256,512]{1,0:T(8,128)(2,1)S(1)}, bf16[256,512]{1,0:T(8,128)(2,1)S(1)}, u32[]{:S(2)}, u32[]{:S(2)}) collective-permute-start(bf16[256,512]{1,0:T(8,128)(2,1)S(1)} %get-tuple-element.108.refs_8_), channel_id=1, source_target_pairs={{0,8},{8,16},{16,24},{24,28},{28,20},{20,12},{12,4},{4,0},{1,9},{9... | collective-permute-start | bytes 786440 | tf_op jit(solution)/shard_map/ppermute | solution.py:370
  63.5 1.5 %collective-permute-done.16.refs_7_ = bf16[128,1024]{1,0:T(8,128)(2,1)S(1)} collective-permute-done((bf16[128,1024]{1,0:T(8,128)(2,1)S(1)}, bf16[128,1024]{1,0:T(8,128)(2,1)S(1)}, u32[]{:S(2)}, u32[]{:S(2)}) %collective-permute-start.16) | collective-permute-done | bytes 262176 | tf_op jit(solution)/shard_map/ppermute | solution.py:370
  65.6 1.6 %collective-permute-start.20 = (bf16[128,1024]{1,0:T(8,128)(2,1)S(1)}, bf16[128,1024]{1,0:T(8,128)(2,1)S(1)}, u32[]{:S(2)}, u32[]{:S(2)}) collective-permute-start(bf16[128,1024]{1,0:T(8,128)(2,1)S(1)} %get-tuple-element.110.refs_0_), channel_id=1, source_target_pairs={{0,8},{8,16},{16,24},{24,28},{28,20},{20,12},{12,4},{4,0},{1,9},{9... | collective-permute-start | bytes 786440 | tf_op jit(solution)/shard_map/ppermute | solution.py:370
  70.3 1.6 %collective-permute-done.23.refs_8_ = bf16[256,512]{1,0:T(8,128)(2,1)S(1)} collective-permute-done((bf16[256,512]{1,0:T(8,128)(2,1)S(1)}, bf16[256,512]{1,0:T(8,128)(2,1)S(1)}, u32[]{:S(2)}, u32[]{:S(2)}) %collective-permute-start.23) | collective-permute-done | bytes 262176 | tf_op jit(solution)/shard_map/ppermute | solution.py:370
  72.4 1.5 %collective-permute-start.28 = (bf16[256,512]{1,0:T(8,128)(2,1)S(1)}, bf16[256,512]{1,0:T(8,128)(2,1)S(1)}, u32[]{:S(2)}, u32[]{:S(2)}) collective-permute-start(bf16[256,512]{1,0:T(8,128)(2,1)S(1)} %get-tuple-element.112.refs_8_), channel_id=1, source_target_pairs={{0,8},{8,16},{16,24},{24,28},{28,20},{20,12},{12,4},{4,0},{1,9},{9... | collective-permute-start | bytes 786440 | tf_op jit(solution)/shard_map/ppermute | solution.py:370
  75.9 1.6 %collective-permute-done.21.refs_7_ = bf16[128,1024]{1,0:T(8,128)(2,1)S(1)} collective-permute-done((bf16[128,1024]{1,0:T(8,128)(2,1)S(1)}, bf16[128,1024]{1,0:T(8,128)(2,1)S(1)}, u32[]{:S(2)}, u32[]{:S(2)}) %collective-permute-start.21) | collective-permute-done | bytes 262176 | tf_op jit(solution)/shard_map/ppermute | solution.py:370
  78.0 1.5 %collective-permute-start.26 = (bf16[128,1024]{1,0:T(8,128)(2,1)S(1)}, bf16[128,1024]{1,0:T(8,128)(2,1)S(1)}, u32[]{:S(2)}, u32[]{:S(2)}) collective-permute-start(bf16[128,1024]{1,0:T(8,128)(2,1)S(1)} %get-tuple-element.114.refs_0_), channel_id=1, source_target_pairs={{0,8},{8,16},{16,24},{24,28},{28,20},{20,12},{12,4},{4,0},{1,9},{9... | collective-permute-start | bytes 786440 | tf_op jit(solution)/shard_map/ppermute | solution.py:370
  97.1 1.6 %collective-permute-done.30.refs_6_ = bf16[128,1024]{1,0:T(8,128)(2,1)S(1)} collective-permute-done((bf16[128,1024]{1,0:T(8,128)(2,1)S(1)}, bf16[128,1024]{1,0:T(8,128)(2,1)S(1)}, u32[]{:S(2)}, u32[]{:S(2)}) %collective-permute-start.30) | collective-permute-done | bytes 262176 | tf_op jit(solution)/shard_map/ppermute | solution.py:370
  102.7 1.6 %unpack.1 = (bf16[256,1024]{1,0:T(8,128)(2,1)}, f32[256,128]{1,0:T(8,128)S(1)}) custom-call(s32[1,256]{1,0:T(1,128)S(1)} %get-tuple-element.67.slot_ref, bf16[128,1152]{1,0:T(8,128)(2,1)S(1)} %feat_grad.7.refs_9_.refs_0_, bf16[128,1152]{1,0:T(8,128)(2,1)S(1)} %collective-permute-done.25.refs_2_.refs_1_, ...), custom_call_target="tpu_custom_call" | custom-call | tf_op jit(solution)/shard_map/unpack/pallas_call | solution.py:440
  106.7 1.9 %collective-permute-done.35.arrived_ref = bf16[128,1024]{1,0:T(8,128)(2,1)S(1)} collective-permute-done((bf16[128,1024]{1,0:T(8,128)(2,1)S(1)}, bf16[128,1024]{1,0:T(8,128)(2,1)S(1)}, u32[]{:S(2)}, u32[]{:S(2)}) %collective-permute-start.35) | collective-permute-done | bytes 262176 | tf_op jit(solution)/shard_map/ppermute | solution.py:370
  (88 shorter events, 51.7 us)
Async XLA Ops:
  0.6 16.0 %collective-permute-start.3 = (bf16[256,1024]{1,0:T(8,128)(2,1)}, bf16[256,1024]{1,0:T(8,128)(2,1)S(1)}, u32[]{:S(2)}, u32[]{:S(2)}) collective-permute-start(bf16[256,1024]{1,0:T(8,128)(2,1)} %refs_3_.1), channel_id=1, source_target_pairs={{0,2},{1,3},{2,0},{3,1},{4,6},{5,7},{6,4},{7,5},{8,10},{9,11},{10,... | collective-permute-start | bytes 1572872 | tf_op jit(solution)/shard_map/ppermute | solution.py:298
  6.1 10.6 %collective-permute-start.2 = (s32[1,256]{1,0:T(1,128)}, s32[1,256]{1,0:T(1,128)S(1)}, u32[]{:S(2)}, u32[]{:S(2)}) collective-permute-start(s32[1,256]{1,0:T(1,128)} %bitcast.1), channel_id=1, source_target_pairs={{0,2},{1,3},{2,0},{3,1},{4,6},{5,7},{6,4},{7,5},{8,10},{9,11},{10,... | collective-permute-start | bytes 3080 | tf_op jit(solution)/shard_map/ppermute | solution.py:299
  6.1 16.0 %collective-permute-start.5 = (bf16[128,1024]{1,0:T(8,128)(2,1)S(1)}, bf16[128,1024]{1,0:T(8,128)(2,1)S(1)}, u32[]{:S(2)}, u32[]{:S(2)}) collective-permute-start(bf16[128,1024]{1,0:T(8,128)(2,1)S(1)} %get-tuple-element.80), channel_id=1, source_target_pairs={{0,2},{1,3},{2,0},{3,1},{4,6},{5,7},{6,4},{7,5},{8,10},{9,11},{10,... | collective-permute-start | bytes 786440 | tf_op jit(solution)/shard_map/ppermute | solution.py:293
  17.2 9.1 %collective-permute-start.6 = (bf16[128,1024]{1,0:T(8,128)(2,1)S(1)}, bf16[128,1024]{1,0:T(8,128)(2,1)S(1)}, u32[]{:S(2)}, u32[]{:S(2)}) collective-permute-start(bf16[128,1024]{1,0:T(8,128)(2,1)S(1)} %get-tuple-element.86), channel_id=1, source_target_pairs={{0,3},{1,2},{2,1},{3,0},{4,7},{5,6},{6,5},{7,4},{8,11},{9,10},{10,... | collective-permute-start | bytes 786440 | tf_op jit(solution)/shard_map/ppermute | solution.py:293
  26.6 9.1 %collective-permute-start.9 = (bf16[256,512]{1,0:T(8,128)(2,1)S(1)}, bf16[256,512]{1,0:T(8,128)(2,1)S(1)}, u32[]{:S(2)}, u32[]{:S(2)}) collective-permute-start(bf16[256,512]{1,0:T(8,128)(2,1)S(1)} %get-tuple-element.94.refs_4_), channel_id=1, source_target_pairs={{0,8},{8,16},{16,24},{24,28},{28,20},{20,12},{12,4},{4,0},{1,9},{9... | collective-permute-start | bytes 786440 | tf_op jit(solution)/shard_map/ppermute | solution.py:370
  28.4 9.1 %collective-permute-start.10 = (bf16[256,512]{1,0:T(8,128)(2,1)S(1)}, bf16[256,512]{1,0:T(8,128)(2,1)S(1)}, u32[]{:S(2)}, u32[]{:S(2)}) collective-permute-start(bf16[256,512]{1,0:T(8,128)(2,1)S(1)} %get-tuple-element.95.refs_5_), channel_id=1, source_target_pairs={{8,0},{16,8},{24,16},{28,24},{20,28},{12,20},{4,12},{0,4},{9,1},{1... | collective-permute-start | bytes 786440 | tf_op jit(solution)/shard_map/ppermute | solution.py:370
  30.9 10.5 %collective-permute-start.7 = (bf16[128,1024]{1,0:T(8,128)(2,1)S(1)}, bf16[128,1024]{1,0:T(8,128)(2,1)S(1)}, u32[]{:S(2)}, u32[]{:S(2)}) collective-permute-start(bf16[128,1024]{1,0:T(8,128)(2,1)S(1)} %get-tuple-element.98.refs_9_), channel_id=1, source_target_pairs={{0,8},{8,16},{16,24},{24,28},{28,20},{20,12},{12,4},{4,0},{1,9},{9... | collective-permute-start | bytes 786440 | tf_op jit(solution)/shard_map/ppermute | solution.py:370
  32.7 10.5 %collective-permute-start.8 = (bf16[128,1024]{1,0:T(8,128)(2,1)S(1)}, bf16[128,1024]{1,0:T(8,128)(2,1)S(1)}, u32[]{:S(2)}, u32[]{:S(2)}) collective-permute-start(bf16[128,1024]{1,0:T(8,128)(2,1)S(1)} %get-tuple-element.99.refs_10_), channel_id=1, source_target_pairs={{8,0},{16,8},{24,16},{28,24},{20,28},{12,20},{4,12},{0,4},{9,1},{1... | collective-permute-start | bytes 786440 | tf_op jit(solution)/shard_map/ppermute | solution.py:370
  38.1 10.8 %collective-permute-start.13 = (bf16[256,512]{1,0:T(8,128)(2,1)S(1)}, bf16[256,512]{1,0:T(8,128)(2,1)S(1)}, u32[]{:S(2)}, u32[]{:S(2)}) collective-permute-start(bf16[256,512]{1,0:T(8,128)(2,1)S(1)} %get-tuple-element.100.refs_8_), channel_id=1, source_target_pairs={{0,8},{8,16},{16,24},{24,28},{28,20},{20,12},{12,4},{4,0},{1,9},{9... | collective-permute-start | bytes 786440 | tf_op jit(solution)/shard_map/ppermute | solution.py:370
  39.8 9.2 %collective-permute-start.14 = (bf16[256,512]{1,0:T(8,128)(2,1)S(1)}, bf16[256,512]{1,0:T(8,128)(2,1)S(1)}, u32[]{:S(2)}, u32[]{:S(2)}) collective-permute-start(bf16[256,512]{1,0:T(8,128)(2,1)S(1)} %get-tuple-element.101.refs_9_), channel_id=1, source_target_pairs={{8,0},{16,8},{24,16},{28,24},{20,28},{12,20},{4,12},{0,4},{9,1},{1... | collective-permute-start | bytes 786440 | tf_op jit(solution)/shard_map/ppermute | solution.py:370
  43.8 9.3 %collective-permute-start.11 = (bf16[128,1024]{1,0:T(8,128)(2,1)S(1)}, bf16[128,1024]{1,0:T(8,128)(2,1)S(1)}, u32[]{:S(2)}, u32[]{:S(2)}) collective-permute-start(bf16[128,1024]{1,0:T(8,128)(2,1)S(1)} %get-tuple-element.102.refs_0_), channel_id=1, source_target_pairs={{0,8},{8,16},{16,24},{24,28},{28,20},{20,12},{12,4},{4,0},{1,9},{9... | collective-permute-start | bytes 786440 | tf_op jit(solution)/shard_map/ppermute | solution.py:370
  45.4 9.2 %collective-permute-start.12 = (bf16[128,1024]{1,0:T(8,128)(2,1)S(1)}, bf16[128,1024]{1,0:T(8,128)(2,1)S(1)}, u32[]{:S(2)}, u32[]{:S(2)}) collective-permute-start(bf16[128,1024]{1,0:T(8,128)(2,1)S(1)} %get-tuple-element.103.refs_1_), channel_id=1, source_target_pairs={{8,0},{16,8},{24,16},{28,24},{20,28},{12,20},{4,12},{0,4},{9,1},{1... | collective-permute-start | bytes 786440 | tf_op jit(solution)/shard_map/ppermute | solution.py:370
  47.3 10.0 %collective-permute-start.19 = (bf16[128,1152]{1,0:T(8,128)(2,1)S(1)}, bf16[128,1152]{1,0:T(8,128)(2,1)S(1)}, u32[]{:S(2)}, u32[]{:S(2)}) collective-permute-start(bf16[128,1152]{1,0:T(8,128)(2,1)S(1)} %feat_grad.4.refs_9_), channel_id=1, source_target_pairs={{0,2},{1,3},{2,0},{3,1},{4,6},{5,7},{6,4},{7,5},{8,10},{9,11},{10,... | collective-permute-start | bytes 884744 | tf_op jit(solution)/shard_map/ppermute | solution.py:412
  49.6 9.3 %collective-permute-start.17 = (bf16[256,512]{1,0:T(8,128)(2,1)S(1)}, bf16[256,512]{1,0:T(8,128)(2,1)S(1)}, u32[]{:S(2)}, u32[]{:S(2)}) collective-permute-start(bf16[256,512]{1,0:T(8,128)(2,1)S(1)} %get-tuple-element.104.refs_8_), channel_id=1, source_target_pairs={{0,8},{8,16},{16,24},{24,28},{28,20},{20,12},{12,4},{4,0},{1,9},{9... | collective-permute-start | bytes 786440 | tf_op jit(solution)/shard_map/ppermute | solution.py:370
  51.2 9.2 %collective-permute-start.18 = (bf16[256,512]{1,0:T(8,128)(2,1)S(1)}, bf16[256,512]{1,0:T(8,128)(2,1)S(1)}, u32[]{:S(2)}, u32[]{:S(2)}) collective-permute-start(bf16[256,512]{1,0:T(8,128)(2,1)S(1)} %get-tuple-element.105.refs_9_), channel_id=1, source_target_pairs={{8,0},{16,8},{24,16},{28,24},{20,28},{12,20},{4,12},{0,4},{9,1},{1... | collective-permute-start | bytes 786440 | tf_op jit(solution)/shard_map/ppermute | solution.py:370
  55.2 8.3 %collective-permute-start.15 = (bf16[128,1024]{1,0:T(8,128)(2,1)S(1)}, bf16[128,1024]{1,0:T(8,128)(2,1)S(1)}, u32[]{:S(2)}, u32[]{:S(2)}) collective-permute-start(bf16[128,1024]{1,0:T(8,128)(2,1)S(1)} %get-tuple-element.106.refs_0_), channel_id=1, source_target_pairs={{0,8},{8,16},{16,24},{24,28},{28,20},{20,12},{12,4},{4,0},{1,9},{9... | collective-permute-start | bytes 786440 | tf_op jit(solution)/shard_map/ppermute | solution.py:370
  58.8 9.3 %collective-permute-start.24 = (bf16[128,1152]{1,0:T(8,128)(2,1)S(1)}, bf16[128,1152]{1,0:T(8,128)(2,1)S(1)}, u32[]{:S(2)}, u32[]{:S(2)}) collective-permute-start(bf16[128,1152]{1,0:T(8,128)(2,1)S(1)} %feat_grad.5.refs_9_), channel_id=1, source_target_pairs={{0,3},{1,2},{2,1},{3,0},{4,7},{5,6},{6,5},{7,4},{8,11},{9,10},{10,... | collective-permute-start | bytes 884744 | tf_op jit(solution)/shard_map/ppermute | solution.py:412
  61.0 9.2 %collective-permute-start.22 = (bf16[256,512]{1,0:T(8,128)(2,1)S(1)}, bf16[256,512]{1,0:T(8,128)(2,1)S(1)}, u32[]{:S(2)}, u32[]{:S(2)}) collective-permute-start(bf16[256,512]{1,0:T(8,128)(2,1)S(1)} %get-tuple-element.108.refs_8_), channel_id=1, source_target_pairs={{0,8},{8,16},{16,24},{24,28},{28,20},{20,12},{12,4},{4,0},{1,9},{9... | collective-permute-start | bytes 786440 | tf_op jit(solution)/shard_map/ppermute | solution.py:370
  62.6 9.2 %collective-permute-start.23 = (bf16[256,512]{1,0:T(8,128)(2,1)S(1)}, bf16[256,512]{1,0:T(8,128)(2,1)S(1)}, u32[]{:S(2)}, u32[]{:S(2)}) collective-permute-start(bf16[256,512]{1,0:T(8,128)(2,1)S(1)} %get-tuple-element.109.refs_9_), channel_id=1, source_target_pairs={{8,0},{16,8},{24,16},{28,24},{20,28},{12,20},{4,12},{0,4},{9,1},{1... | collective-permute-start | bytes 786440 | tf_op jit(solution)/shard_map/ppermute | solution.py:370
  65.6 10.3 %collective-permute-start.20 = (bf16[128,1024]{1,0:T(8,128)(2,1)S(1)}, bf16[128,1024]{1,0:T(8,128)(2,1)S(1)}, u32[]{:S(2)}, u32[]{:S(2)}) collective-permute-start(bf16[128,1024]{1,0:T(8,128)(2,1)S(1)} %get-tuple-element.110.refs_0_), channel_id=1, source_target_pairs={{0,8},{8,16},{16,24},{24,28},{28,20},{20,12},{12,4},{4,0},{1,9},{9... | collective-permute-start | bytes 786440 | tf_op jit(solution)/shard_map/ppermute | solution.py:370
  67.3 10.2 %collective-permute-start.21 = (bf16[128,1024]{1,0:T(8,128)(2,1)S(1)}, bf16[128,1024]{1,0:T(8,128)(2,1)S(1)}, u32[]{:S(2)}, u32[]{:S(2)}) collective-permute-start(bf16[128,1024]{1,0:T(8,128)(2,1)S(1)} %get-tuple-element.111.refs_1_), channel_id=1, source_target_pairs={{8,0},{16,8},{24,16},{28,24},{20,28},{12,20},{4,12},{0,4},{9,1},{1... | collective-permute-start | bytes 786440 | tf_op jit(solution)/shard_map/ppermute | solution.py:370
  69.6 10.5 %collective-permute-start.25 = (bf16[128,1152]{1,0:T(8,128)(2,1)S(1)}, bf16[128,1152]{1,0:T(8,128)(2,1)S(1)}, u32[]{:S(2)}, u32[]{:S(2)}) collective-permute-start(bf16[128,1152]{1,0:T(8,128)(2,1)S(1)} %feat_grad.6.refs_9_), channel_id=1, source_target_pairs={{0,1},{1,0},{2,3},{3,2},{4,5},{5,4},{6,7},{7,6},{8,9},{9,8},{10,11... | collective-permute-start | bytes 884744 | tf_op jit(solution)/shard_map/ppermute | solution.py:412
  72.4 9.3 %collective-permute-start.28 = (bf16[256,512]{1,0:T(8,128)(2,1)S(1)}, bf16[256,512]{1,0:T(8,128)(2,1)S(1)}, u32[]{:S(2)}, u32[]{:S(2)}) collective-permute-start(bf16[256,512]{1,0:T(8,128)(2,1)S(1)} %get-tuple-element.112.refs_8_), channel_id=1, source_target_pairs={{0,8},{8,16},{16,24},{24,28},{28,20},{20,12},{12,4},{4,0},{1,9},{9... | collective-permute-start | bytes 786440 | tf_op jit(solution)/shard_map/ppermute | solution.py:370
  73.9 9.2 %collective-permute-start.29 = (bf16[256,512]{1,0:T(8,128)(2,1)S(1)}, bf16[256,512]{1,0:T(8,128)(2,1)S(1)}, u32[]{:S(2)}, u32[]{:S(2)}) collective-permute-start(bf16[256,512]{1,0:T(8,128)(2,1)S(1)} %get-tuple-element.113.refs_9_), channel_id=1, source_target_pairs={{8,0},{16,8},{24,16},{28,24},{20,28},{12,20},{4,12},{0,4},{9,1},{1... | collective-permute-start | bytes 786440 | tf_op jit(solution)/shard_map/ppermute | solution.py:370
  78.0 9.3 %collective-permute-start.26 = (bf16[128,1024]{1,0:T(8,128)(2,1)S(1)}, bf16[128,1024]{1,0:T(8,128)(2,1)S(1)}, u32[]{:S(2)}, u32[]{:S(2)}) collective-permute-start(bf16[128,1024]{1,0:T(8,128)(2,1)S(1)} %get-tuple-element.114.refs_0_), channel_id=1, source_target_pairs={{0,8},{8,16},{16,24},{24,28},{28,20},{20,12},{12,4},{4,0},{1,9},{9... | collective-permute-start | bytes 786440 | tf_op jit(solution)/shard_map/ppermute | solution.py:370
  79.5 9.2 %collective-permute-start.27 = (bf16[128,1024]{1,0:T(8,128)(2,1)S(1)}, bf16[128,1024]{1,0:T(8,128)(2,1)S(1)}, u32[]{:S(2)}, u32[]{:S(2)}) collective-permute-start(bf16[128,1024]{1,0:T(8,128)(2,1)S(1)} %get-tuple-element.115.refs_1_), channel_id=1, source_target_pairs={{8,0},{16,8},{24,16},{28,24},{20,28},{12,20},{4,12},{0,4},{9,1},{1... | collective-permute-start | bytes 786440 | tf_op jit(solution)/shard_map/ppermute | solution.py:370
  83.7 9.3 %collective-permute-start.32 = (bf16[256,512]{1,0:T(8,128)(2,1)S(1)}, bf16[256,512]{1,0:T(8,128)(2,1)S(1)}, u32[]{:S(2)}, u32[]{:S(2)}) collective-permute-start(bf16[256,512]{1,0:T(8,128)(2,1)S(1)} %get-tuple-element.116.refs_8_), channel_id=1, source_target_pairs={{0,8},{8,16},{16,24},{24,28},{28,20},{20,12},{12,4},{4,0},{1,9},{9... | collective-permute-start | bytes 786440 | tf_op jit(solution)/shard_map/ppermute | solution.py:370
  85.2 9.2 %collective-permute-start.33 = (bf16[256,512]{1,0:T(8,128)(2,1)S(1)}, bf16[256,512]{1,0:T(8,128)(2,1)S(1)}, u32[]{:S(2)}, u32[]{:S(2)}) collective-permute-start(bf16[256,512]{1,0:T(8,128)(2,1)S(1)} %get-tuple-element.117.refs_9_), channel_id=1, source_target_pairs={{8,0},{16,8},{24,16},{28,24},{20,28},{12,20},{4,12},{0,4},{9,1},{1... | collective-permute-start | bytes 786440 | tf_op jit(solution)/shard_map/ppermute | solution.py:370
  89.4 9.3 %collective-permute-start.30 = (bf16[128,1024]{1,0:T(8,128)(2,1)S(1)}, bf16[128,1024]{1,0:T(8,128)(2,1)S(1)}, u32[]{:S(2)}, u32[]{:S(2)}) collective-permute-start(bf16[128,1024]{1,0:T(8,128)(2,1)S(1)} %get-tuple-element.118.refs_7_), channel_id=1, source_target_pairs={{0,8},{8,16},{16,24},{24,28},{28,20},{20,12},{12,4},{4,0},{1,9},{9... | collective-permute-start | bytes 786440 | tf_op jit(solution)/shard_map/ppermute | solution.py:370
  90.8 9.2 %collective-permute-start.31 = (bf16[128,1024]{1,0:T(8,128)(2,1)S(1)}, bf16[128,1024]{1,0:T(8,128)(2,1)S(1)}, u32[]{:S(2)}, u32[]{:S(2)}) collective-permute-start(bf16[128,1024]{1,0:T(8,128)(2,1)S(1)} %get-tuple-element.119.refs_8_), channel_id=1, source_target_pairs={{8,0},{16,8},{24,16},{28,24},{20,28},{12,20},{4,12},{0,4},{9,1},{1... | collective-permute-start | bytes 786440 | tf_op jit(solution)/shard_map/ppermute | solution.py:370
  95.0 10.0 %collective-permute-start.37 = (bf16[256,512]{1,0:T(8,128)(2,1)S(1)}, bf16[256,512]{1,0:T(8,128)(2,1)S(1)}, u32[]{:S(2)}, u32[]{:S(2)}) collective-permute-start(bf16[256,512]{1,0:T(8,128)(2,1)S(1)} %get-tuple-element.122.refs_8_), channel_id=1, source_target_pairs={{0,8},{8,16},{16,24},{24,28},{28,20},{20,12},{12,4},{4,0},{1,9},{9... | collective-permute-start | bytes 786440 | tf_op jit(solution)/shard_map/ppermute | solution.py:370
  96.4 9.5 %collective-permute-start.36 = (bf16[256,512]{1,0:T(8,128)(2,1)S(1)}, bf16[256,512]{1,0:T(8,128)(2,1)S(1)}, u32[]{:S(2)}, u32[]{:S(2)}) collective-permute-start(bf16[256,512]{1,0:T(8,128)(2,1)S(1)} %get-tuple-element.123.refs_9_), channel_id=1, source_target_pairs={{8,0},{16,8},{24,16},{28,24},{20,28},{12,20},{4,12},{0,4},{9,1},{1... | collective-permute-start | bytes 786440 | tf_op jit(solution)/shard_map/ppermute | solution.py:370
  (10 other events, 61.7 us)

commit v6 on v4

--- a/solution.py
+++ b/solution.py
@@ -276,30 +276,36 @@
     return [(out, way, tuple(sides)) for out, (way, sides) in zip(outs, held.items())]
 
 
-def last_kernel(count, own_ref, *refs):
-    arrived, (out, held, sems) = refs[:2], refs[-3:]
-    half = held.shape[2]
-    copies = []
-    for side, ref in enumerate(arrived):
-        part = slice(side * half, (side + 1) * half)
-        held[side] = (own_ref[:, part] + ref[...].astype(F32)) * (1.0 / count)
-        copies.append(pltpu.make_async_copy(held.at[side], out.at[0, :, part], sems.at[side]))
-        copies[-1].start()
-    for copy in copies:
-        copy.wait()
-
-
-def last_call(name, count, own, arrived, after):
-    rows, width = own.shape
-    return pl.pallas_call(
-        functools.partial(last_kernel, count),
-        in_specs=[WHOLE] * 3 + [LATER] * len(after),
-        out_specs=pl.BlockSpec(memory_space=pltpu.HBM),
-        out_shape=pltpu.HBM((1, rows, width), F32),
-        scratch_shapes=[pltpu.VMEM((2, rows, width // 2), F32), pltpu.SemaphoreType.DMA((2,))],
-        compiler_params=params(),
-        name=name,
-    )(own, *arrived, *after)
+def last_kernel(way, count, arrived_ref, own_ref, *refs):
+    out, held, sem = refs[-3:]
+    half = held.shape[1]
+    own = own_ref[:, way * half : (way + 1) * half]
+    held[...] = (own + arrived_ref[...].astype(F32)) * (1.0 / count)
+    copy = pltpu.make_async_copy(held, out.at[0, :, way * half : (way + 1) * half], sem)
+    copy.start()
+    copy.wait()
+
+
+def last_call(name, count, arrived, own, after):
+    rows, half = own.shape[0], own.shape[1] // 2
+    out = []
+    for way in range(2):
+        out = [
+            pl.pallas_call(
+                functools.partial(last_kernel, way, count),
+                in_specs=[WHOLE] * 2
+                + [pl.BlockSpec(memory_space=pltpu.HBM)] * len(out)
+                + [LATER] * len(after),
+                out_specs=pl.BlockSpec(memory_space=pltpu.HBM),
+                out_shape=pltpu.HBM((1, rows, 2 * half), F32),
+                input_output_aliases={2: 0} if out else {},
+                scratch_shapes=[pltpu.VMEM((rows, half), F32), pltpu.SemaphoreType.DMA],
+                compiler_params=params(),
+                name=name,
+            )(arrived[way], own, *(in_hbm(a) for a in out), *after)
+        ]
+        after = []
+    return out[0]
 
 
 def per_device(tokens, out_grad, gate_prob, expert_id, up_weight, down_weight):
@@ -481,8 +487,8 @@
         compiler_params=params(),
         name="unpack",
     )(slot, *(feat_back[k] for k in range(peers)), *after)
-    down = last_call("down_last", ring, down_own, [a for a, _, _ in down_in], [up_own])
-    up = last_call("up_last", ring, up_own, [a for a, _, _ in up_in], [in_hbm(down)])
+    down = last_call("down_last", ring, [a for a, _, _ in down_in], down_own, [up_own])
+    up = last_call("up_last", ring, [a for a, _, _ in up_in], up_own, [in_hbm(down)])
     gate_result = ((gate_sums[:, 0] + gate_sums[:, 1]) / gate_prob.astype(F32)).astype(BF16)
     return (tokens_grad, gate_result, up, down)
 

time: 112 us -> 111 us (level)
  waiting for transfers between devices: 51.6 us -> 50.1 us
  Pallas kernels: 29.2 us -> 30.6 us
    ppermute x16, waiting for transfers between devices: 46.5 us -> 44.9 us  [send(): lax.ppermute(a, 'dp', ways[way])]
    pallas_call x2 -> x4, Pallas kernels: 2.07 us -> 3.42 us  [last_call(): pl.pallas_call(functools.partial(last_kernel, way, count), in_specs=[WHOL...]
  transfers between devices with their start and end apart: 26 -> 26, of which waited for: 17 -> 17; matrix products, arithmetic and copies ran while one was open for 1% -> 1% of each run, Pallas kernels for 25% -> 26%
where the time goes in v6:
time: 111 us
  waiting for transfers between devices  50.1 us (45%)
  Pallas kernels  30.6 us (28%)
  starting transfers between devices  26.4 us (24%)
  local copies, waits for them, and re-layouts  2.35 us (2%)
    ppermute x16, waiting for transfers between devices, send(): lax.ppermute(a, 'dp', ways[way])  44.9 us
    pallas_call x21, Pallas kernels, call(): pl.pallas_call(body, in_specs=[WHOLE] * len(inputs) + [LATER] * len(after...  23.2 us
    ppermute x16, starting transfers between devices, send(): lax.ppermute(a, 'dp', ways[way])  16.6 us
    ppermute x5, starting transfers between devices, exchange(): return {k: lax.ppermute(outs[k], 'expert', sources[k]) for k in reach}  4.82 us
    pallas_call x4, Pallas kernels, last_call(): pl.pallas_call(functools.partial(last_kernel, way, count), in_specs=[WHOL...  3.42 us
    ppermute x1, starting transfers between devices, per_device(): tokens_across = lax.ppermute(tokens, 'expert', across)  3 us
    ppermute x1, waiting for transfers between devices, per_device(): id_across = lax.ppermute(expert_id.reshape(1, count), 'expert', across)  2.65 us
    ppermute x5, waiting for transfers between devices, exchange(): return {k: lax.ppermute(outs[k], 'expert', sources[k]) for k in reach}  2.46 us
  transfers between devices with their start and end apart: 26, of which 17 were waited for; matrix products, arithmetic and copies ran while one was open for 1% of the time, Pallas kernels for 26%

profile of v6, /device:TPU:0, one launch (start us, length us, event | category | flops | bytes accessed | tf_op | source)
XLA Modules:
  0.0 111.1 jit_solution(15613580469824652110)
XLA Ops:
  0.6 3.0 %collective-permute-start.3 = (bf16[256,1024]{1,0:T(8,128)(2,1)}, bf16[256,1024]{1,0:T(8,128)(2,1)S(1)}, u32[]{:S(2)}, u32[]{:S(2)}) collective-permute-start(bf16[256,1024]{1,0:T(8,128)(2,1)} %refs_3_.1), channel_id=1, source_target_pairs={{0,2},{1,3},{2,0},{3,1},{4,6},{5,7},{6,4},{7,5},{8,10},{9,11},{10,... | collective-permute-start | bytes 1572872 | tf_op jit(solution)/shard_map/ppermute | solution.py:328
  3.6 1.9 %pack.1 = (s32[1,256]{1,0:T(1,128)S(1)}, bf16[128,1024]{1,0:T(8,128)(2,1)S(1)}, bf16[128,1024]{1,0:T(8,128)(2,1)S(1)}, bf16[128,1024]{1,0:T(8,128)(2,1)S(1)}, bf...) custom-call(s32[256]{0:T(256)} %refs_0_.1, bf16[256]{0:T(256)(128)(2,1)} %refs_1_.5, ...), custom_call_target="tpu_custom_call" | custom-call | tf_op jit(solution)/shard_map/pack/pallas_call | solution.py:332
  6.1 2.0 %collective-permute-start.5 = (bf16[128,1024]{1,0:T(8,128)(2,1)S(1)}, bf16[128,1024]{1,0:T(8,128)(2,1)S(1)}, u32[]{:S(2)}, u32[]{:S(2)}) collective-permute-start(bf16[128,1024]{1,0:T(8,128)(2,1)S(1)} %get-tuple-element.64), channel_id=1, source_target_pairs={{0,2},{1,3},{2,0},{3,1},{4,6},{5,7},{6,4},{7,5},{8,10},{9,11},{10,... | collective-permute-start | bytes 786440 | tf_op jit(solution)/shard_map/ppermute | solution.py:323
  8.1 2.2 %copy-done = bf16[1,1024,2048]{2,1,0:T(8,128)(2,1)S(1)} copy-done((bf16[1,1024,2048]{2,1,0:T(8,128)(2,1)S(1)}, bf16[1,1024,2048]{2,1,0:T(8,128)(2,1)}, u32[]{:S(2)}) %copy-start) | copy-done | bytes 4194328
  10.3 2.0 %hidden.3 = (bf16[1024,256]{1,0:T(8,128)(2,1)S(1)}, bf16[256,2048]{1,0:T(8,128)(2,1)S(1)}, bf16[2048,256]{1,0:T(8,128)(2,1)S(1)}, bf16[256,2048]{1,0:T(8,128)(2,1)S(1)}) custom-call(bf16[128,1024]{1,0:T(8,128)(2,1)S(1)} %get-tuple-element.54.refs_0_, bf16[128,1024]{1,0:T(8,128)(2,1)S(1)} %collective-permute-done.1.refs_1_, bf16[1,1024,2048]{2,1,0:T(8,128)(2,1)S(1)} %copy-done), custom_call_target="tpu_custom_call" | custom-call | tf_op jit(solution)/shard_map/hidden/pallas_call | solution.py:100
  14.0 2.7 %collective-permute-done.2.id_ref = s32[1,256]{1,0:T(1,128)S(1)} collective-permute-done((s32[1,256]{1,0:T(1,128)}, s32[1,256]{1,0:T(1,128)S(1)}, u32[]{:S(2)}, u32[]{:S(2)}) %collective-permute-start.2) | collective-permute-done | bytes 1056 | tf_op jit(solution)/shard_map/ppermute | solution.py:329
  17.2 2.2 %collective-permute-start.6 = (bf16[128,1024]{1,0:T(8,128)(2,1)S(1)}, bf16[128,1024]{1,0:T(8,128)(2,1)S(1)}, u32[]{:S(2)}, u32[]{:S(2)}) collective-permute-start(bf16[128,1024]{1,0:T(8,128)(2,1)S(1)} %get-tuple-element.69), channel_id=1, source_target_pairs={{0,3},{1,2},{2,1},{3,0},{4,7},{5,6},{6,5},{7,4},{8,11},{9,10},{10,... | collective-permute-start | bytes 786440 | tf_op jit(solution)/shard_map/ppermute | solution.py:323
  20.4 1.7 %collective-permute-done.5.refs_0_.refs_4_.refs_5_ = bf16[128,1024]{1,0:T(8,128)(2,1)S(1)} collective-permute-done((bf16[128,1024]{1,0:T(8,128)(2,1)S(1)}, bf16[128,1024]{1,0:T(8,128)(2,1)S(1)}, u32[]{:S(2)}, u32[]{:S(2)}) %collective-permute-start.5) | collective-permute-done | bytes 262176 | tf_op jit(solution)/shard_map/ppermute | solution.py:323
  22.1 1.6 %pre_grad.4 = (bf16[128,2048]{1,0:T(8,128)(2,1)S(1)}, f32[128,128]{1,0:T(8,128)S(1)}) custom-call(bf16[128,1024]{1,0:T(8,128)(2,1)S(1)} %collective-permute-done.5.refs_0_.refs_4_.refs_5_, bf16[1,2048,1024]{2,1,0:T(8,128)(2,1)S(1)} %copy-done.2, bf16[128,2048]{1,0:T(8,128)(2,1)S(1)} %get-tuple-element.65.refs_2_.refs_4_, ...), custom_call_target="tpu_custom_call" | custom-call | tf_op jit(solution)/shard_map/pre_grad/pallas_call | solution.py:100
  26.7 1.8 %collective-permute-start.7 = (bf16[256,1024]{1,0:T(8,128)(2,1)S(1)}, bf16[256,1024]{1,0:T(8,128)(2,1)S(1)}, u32[]{:S(2)}, u32[]{:S(2)}) collective-permute-start(bf16[256,1024]{1,0:T(8,128)(2,1)S(1)} %get-tuple-element.73.refs_4_), channel_id=1, source_target_pairs={{0,8},{8,16},{16,24},{24,28},{28,20},{20,12},{12,4},{4,0},{1,9},{9... | collective-permute-start | bytes 1572872 | tf_op jit(solution)/shard_map/ppermute | solution.py:402
  28.8 1.6 %pre_grad.5 = (bf16[128,2048]{1,0:T(8,128)(2,1)S(1)}, f32[128,128]{1,0:T(8,128)S(1)}) custom-call(bf16[128,1024]{1,0:T(8,128)(2,1)S(1)} %collective-permute-done.6.refs_1_.refs_0_.refs_6_, bf16[1,2048,1024]{2,1,0:T(8,128)(2,1)S(1)} %copy-done.2, bf16[128,2048]{1,0:T(8,128)(2,1)S(1)} %get-tuple-element.70.refs_5_.refs_2_, ...), custom_call_target="tpu_custom_call" | custom-call | tf_op jit(solution)/shard_map/pre_grad/pallas_call | solution.py:100
  31.4 1.8 %collective-permute-start.11 = (bf16[128,2048]{1,0:T(8,128)(2,1)S(1)}, bf16[128,2048]{1,0:T(8,128)(2,1)S(1)}, u32[]{:S(2)}, u32[]{:S(2)}) collective-permute-start(bf16[128,2048]{1,0:T(8,128)(2,1)S(1)} %get-tuple-element.82.refs_0_), channel_id=1, source_target_pairs={{0,8},{8,16},{16,24},{24,28},{28,20},{20,12},{12,4},{4,0},{1,9},{9... | collective-permute-start | bytes 1572872 | tf_op jit(solution)/shard_map/ppermute | solution.py:402
  35.0 1.8 %collective-permute-start.13 = (bf16[128,1152]{1,0:T(8,128)(2,1)S(1)}, bf16[128,1152]{1,0:T(8,128)(2,1)S(1)}, u32[]{:S(2)}, u32[]{:S(2)}) collective-permute-start(bf16[128,1152]{1,0:T(8,128)(2,1)S(1)} %feat_grad.4.refs_9_), channel_id=1, source_target_pairs={{0,2},{1,3},{2,0},{3,1},{4,6},{5,7},{6,4},{7,5},{8,10},{9,11},{10,... | collective-permute-start | bytes 884744 | tf_op jit(solution)/shard_map/ppermute | solution.py:426
  36.8 4.7 %collective-permute-done.7.refs_7_ = bf16[256,1024]{1,0:T(8,128)(2,1)S(1)} collective-permute-done((bf16[256,1024]{1,0:T(8,128)(2,1)S(1)}, bf16[256,1024]{1,0:T(8,128)(2,1)S(1)}, u32[]{:S(2)}, u32[]{:S(2)}) %collective-permute-start.7) | collective-permute-done | bytes 524320 | tf_op jit(solution)/shard_map/ppermute | solution.py:402
  41.5 1.8 %collective-permute-done.8.refs_8_ = bf16[256,1024]{1,0:T(8,128)(2,1)S(1)} collective-permute-done((bf16[256,1024]{1,0:T(8,128)(2,1)S(1)}, bf16[256,1024]{1,0:T(8,128)(2,1)S(1)}, u32[]{:S(2)}, u32[]{:S(2)}) %collective-permute-start.8) | collective-permute-done | bytes 524320 | tf_op jit(solution)/shard_map/ppermute | solution.py:402
  45.9 1.6 %collective-permute-start.9 = (bf16[256,1024]{1,0:T(8,128)(2,1)S(1)}, bf16[256,1024]{1,0:T(8,128)(2,1)S(1)}, u32[]{:S(2)}, u32[]{:S(2)}) collective-permute-start(bf16[256,1024]{1,0:T(8,128)(2,1)S(1)} %get-tuple-element.84.refs_0_), channel_id=1, source_target_pairs={{0,8},{8,16},{16,24},{24,28},{28,20},{20,12},{12,4},{4,0},{1,9},{9... | collective-permute-start | bytes 1572872 | tf_op jit(solution)/shard_map/ppermute | solution.py:402
  48.0 4.7 %collective-permute-done.11.refs_6_ = bf16[128,2048]{1,0:T(8,128)(2,1)S(1)} collective-permute-done((bf16[128,2048]{1,0:T(8,128)(2,1)S(1)}, bf16[128,2048]{1,0:T(8,128)(2,1)S(1)}, u32[]{:S(2)}, u32[]{:S(2)}) %collective-permute-start.11) | collective-permute-done | bytes 524320 | tf_op jit(solution)/shard_map/ppermute | solution.py:402
  52.7 1.8 %collective-permute-done.12.refs_7_ = bf16[128,2048]{1,0:T(8,128)(2,1)S(1)} collective-permute-done((bf16[128,2048]{1,0:T(8,128)(2,1)S(1)}, bf16[128,2048]{1,0:T(8,128)(2,1)S(1)}, u32[]{:S(2)}, u32[]{:S(2)}) %collective-permute-start.12) | collective-permute-done | bytes 524320 | tf_op jit(solution)/shard_map/ppermute | solution.py:402
  55.5 1.6 %collective-permute-start.16 = (bf16[128,2048]{1,0:T(8,128)(2,1)S(1)}, bf16[128,2048]{1,0:T(8,128)(2,1)S(1)}, u32[]{:S(2)}, u32[]{:S(2)}) collective-permute-start(bf16[128,2048]{1,0:T(8,128)(2,1)S(1)} %get-tuple-element.86.refs_0_), channel_id=1, source_target_pairs={{0,8},{8,16},{16,24},{24,28},{28,20},{20,12},{12,4},{4,0},{1,9},{9... | collective-permute-start | bytes 1572872 | tf_op jit(solution)/shard_map/ppermute | solution.py:402
  59.2 4.7 %collective-permute-done.9.refs_7_ = bf16[256,1024]{1,0:T(8,128)(2,1)S(1)} collective-permute-done((bf16[256,1024]{1,0:T(8,128)(2,1)S(1)}, bf16[256,1024]{1,0:T(8,128)(2,1)S(1)}, u32[]{:S(2)}, u32[]{:S(2)}) %collective-permute-start.9) | collective-permute-done | bytes 524320 | tf_op jit(solution)/shard_map/ppermute | solution.py:402
  63.9 1.8 %collective-permute-done.10.refs_8_ = bf16[256,1024]{1,0:T(8,128)(2,1)S(1)} collective-permute-done((bf16[256,1024]{1,0:T(8,128)(2,1)S(1)}, bf16[256,1024]{1,0:T(8,128)(2,1)S(1)}, u32[]{:S(2)}, u32[]{:S(2)}) %collective-permute-start.10) | collective-permute-done | bytes 524320 | tf_op jit(solution)/shard_map/ppermute | solution.py:402
  66.8 1.6 %collective-permute-start.20 = (bf16[256,1024]{1,0:T(8,128)(2,1)S(1)}, bf16[256,1024]{1,0:T(8,128)(2,1)S(1)}, u32[]{:S(2)}, u32[]{:S(2)}) collective-permute-start(bf16[256,1024]{1,0:T(8,128)(2,1)S(1)} %get-tuple-element.88.refs_0_), channel_id=1, source_target_pairs={{0,8},{8,16},{16,24},{24,28},{28,20},{20,12},{12,4},{4,0},{1,9},{9... | collective-permute-start | bytes 1572872 | tf_op jit(solution)/shard_map/ppermute | solution.py:402
  70.4 4.8 %collective-permute-done.16.refs_6_ = bf16[128,2048]{1,0:T(8,128)(2,1)S(1)} collective-permute-done((bf16[128,2048]{1,0:T(8,128)(2,1)S(1)}, bf16[128,2048]{1,0:T(8,128)(2,1)S(1)}, u32[]{:S(2)}, u32[]{:S(2)}) %collective-permute-start.16) | collective-permute-done | bytes 524320 | tf_op jit(solution)/shard_map/ppermute | solution.py:402
  75.2 1.8 %collective-permute-done.17.refs_7_ = bf16[128,2048]{1,0:T(8,128)(2,1)S(1)} collective-permute-done((bf16[128,2048]{1,0:T(8,128)(2,1)S(1)}, bf16[128,2048]{1,0:T(8,128)(2,1)S(1)}, u32[]{:S(2)}, u32[]{:S(2)}) %collective-permute-start.17) | collective-permute-done | bytes 524320 | tf_op jit(solution)/shard_map/ppermute | solution.py:402
  78.0 1.6 %collective-permute-start.18 = (bf16[128,2048]{1,0:T(8,128)(2,1)S(1)}, bf16[128,2048]{1,0:T(8,128)(2,1)S(1)}, u32[]{:S(2)}, u32[]{:S(2)}) collective-permute-start(bf16[128,2048]{1,0:T(8,128)(2,1)S(1)} %get-tuple-element.90.refs_9_), channel_id=1, source_target_pairs={{0,8},{8,16},{16,24},{24,28},{28,20},{20,12},{12,4},{4,0},{1,9},{9... | collective-permute-start | bytes 1572872 | tf_op jit(solution)/shard_map/ppermute | solution.py:402
  80.1 6.3 %collective-permute-done.20.refs_7_ = bf16[256,1024]{1,0:T(8,128)(2,1)S(1)} collective-permute-done((bf16[256,1024]{1,0:T(8,128)(2,1)S(1)}, bf16[256,1024]{1,0:T(8,128)(2,1)S(1)}, u32[]{:S(2)}, u32[]{:S(2)}) %collective-permute-start.20) | collective-permute-done | bytes 524320 | tf_op jit(solution)/shard_map/ppermute | solution.py:402
  86.4 1.8 %collective-permute-done.21.refs_8_ = bf16[256,1024]{1,0:T(8,128)(2,1)S(1)} collective-permute-done((bf16[256,1024]{1,0:T(8,128)(2,1)S(1)}, bf16[256,1024]{1,0:T(8,128)(2,1)S(1)}, u32[]{:S(2)}, u32[]{:S(2)}) %collective-permute-start.21) | collective-permute-done | bytes 524320 | tf_op jit(solution)/shard_map/ppermute | solution.py:402
  88.8 1.6 %collective-permute-start.25 = (bf16[256,512]{1,0:T(8,128)(2,1)S(1)}, bf16[256,512]{1,0:T(8,128)(2,1)S(1)}, u32[]{:S(2)}, u32[]{:S(2)}) collective-permute-start(bf16[256,512]{1,0:T(8,128)(2,1)S(1)} %get-tuple-element.92.refs_9_), channel_id=1, source_target_pairs={{0,8},{8,16},{16,24},{24,28},{28,20},{20,12},{12,4},{4,0},{1,9},{9... | collective-permute-start | bytes 786440 | tf_op jit(solution)/shard_map/ppermute | solution.py:402
  91.5 6.2 %collective-permute-done.18.refs_6_ = bf16[128,2048]{1,0:T(8,128)(2,1)S(1)} collective-permute-done((bf16[128,2048]{1,0:T(8,128)(2,1)S(1)}, bf16[128,2048]{1,0:T(8,128)(2,1)S(1)}, u32[]{:S(2)}, u32[]{:S(2)}) %collective-permute-start.18) | collective-permute-done | bytes 524320 | tf_op jit(solution)/shard_map/ppermute | solution.py:402
  97.6 1.8 %collective-permute-done.19.refs_7_ = bf16[128,2048]{1,0:T(8,128)(2,1)S(1)} collective-permute-done((bf16[128,2048]{1,0:T(8,128)(2,1)S(1)}, bf16[128,2048]{1,0:T(8,128)(2,1)S(1)}, u32[]{:S(2)}, u32[]{:S(2)}) %collective-permute-start.19) | collective-permute-done | bytes 524320 | tf_op jit(solution)/shard_map/ppermute | solution.py:402
  100.1 1.6 %collective-permute-start.23 = (bf16[128,1024]{1,0:T(8,128)(2,1)S(1)}, bf16[128,1024]{1,0:T(8,128)(2,1)S(1)}, u32[]{:S(2)}, u32[]{:S(2)}) collective-permute-start(bf16[128,1024]{1,0:T(8,128)(2,1)S(1)} %get-tuple-element.94.refs_8_), channel_id=1, source_target_pairs={{0,8},{8,16},{16,24},{24,28},{28,20},{20,12},{12,4},{4,0},{1,9},{9... | collective-permute-start | bytes 786440 | tf_op jit(solution)/shard_map/ppermute | solution.py:402
  106.8 1.8 %collective-permute-done.23.arrived_ref = bf16[128,1024]{1,0:T(8,128)(2,1)S(1)} collective-permute-done((bf16[128,1024]{1,0:T(8,128)(2,1)S(1)}, bf16[128,1024]{1,0:T(8,128)(2,1)S(1)}, u32[]{:S(2)}, u32[]{:S(2)}) %collective-permute-start.23) | collective-permute-done | bytes 262176 | tf_op jit(solution)/shard_map/ppermute | solution.py:402
  (58 shorter events, 29.7 us)
Async XLA Ops:
  0.6 16.0 %collective-permute-start.3 = (bf16[256,1024]{1,0:T(8,128)(2,1)}, bf16[256,1024]{1,0:T(8,128)(2,1)S(1)}, u32[]{:S(2)}, u32[]{:S(2)}) collective-permute-start(bf16[256,1024]{1,0:T(8,128)(2,1)} %refs_3_.1), channel_id=1, source_target_pairs={{0,2},{1,3},{2,0},{3,1},{4,6},{5,7},{6,4},{7,5},{8,10},{9,11},{10,... | collective-permute-start | bytes 1572872 | tf_op jit(solution)/shard_map/ppermute | solution.py:328
  5.5 2.6 %collective-permute-start.1 = (bf16[128,1024]{1,0:T(8,128)(2,1)S(1)}, bf16[128,1024]{1,0:T(8,128)(2,1)S(1)}, u32[]{:S(2)}, u32[]{:S(2)}) collective-permute-start(bf16[128,1024]{1,0:T(8,128)(2,1)S(1)} %get-tuple-element.55), channel_id=1, source_target_pairs={{0,1},{1,0},{2,3},{3,2},{4,5},{5,4},{6,7},{7,6},{8,9},{9,8},{10,11... | collective-permute-start | bytes 786440 | tf_op jit(solution)/shard_map/ppermute | solution.py:323
  5.6 6.7 %collective-permute-start = (bf16[128,1024]{1,0:T(8,128)(2,1)S(1)}, bf16[128,1024]{1,0:T(8,128)(2,1)S(1)}, u32[]{:S(2)}, u32[]{:S(2)}) collective-permute-start(bf16[128,1024]{1,0:T(8,128)(2,1)S(1)} %get-tuple-element.53), channel_id=1, source_target_pairs={{0,1},{1,0},{2,3},{3,2},{4,5},{5,4},{6,7},{7,6},{8,9},{9,8},{10,11... | collective-permute-start | bytes 786440 | tf_op jit(solution)/shard_map/ppermute | solution.py:323
  6.1 10.6 %collective-permute-start.2 = (s32[1,256]{1,0:T(1,128)}, s32[1,256]{1,0:T(1,128)S(1)}, u32[]{:S(2)}, u32[]{:S(2)}) collective-permute-start(s32[1,256]{1,0:T(1,128)} %bitcast.1), channel_id=1, source_target_pairs={{0,2},{1,3},{2,0},{3,1},{4,6},{5,7},{6,4},{7,5},{8,10},{9,11},{10,... | collective-permute-start | bytes 3080 | tf_op jit(solution)/shard_map/ppermute | solution.py:329
  6.1 16.0 %collective-permute-start.5 = (bf16[128,1024]{1,0:T(8,128)(2,1)S(1)}, bf16[128,1024]{1,0:T(8,128)(2,1)S(1)}, u32[]{:S(2)}, u32[]{:S(2)}) collective-permute-start(bf16[128,1024]{1,0:T(8,128)(2,1)S(1)} %get-tuple-element.64), channel_id=1, source_target_pairs={{0,2},{1,3},{2,0},{3,1},{4,6},{5,7},{6,4},{7,5},{8,10},{9,11},{10,... | collective-permute-start | bytes 786440 | tf_op jit(solution)/shard_map/ppermute | solution.py:323
  8.1 2.2 %copy-start = (bf16[1,1024,2048]{2,1,0:T(8,128)(2,1)S(1)}, bf16[1,1024,2048]{2,1,0:T(8,128)(2,1)}, u32[]{:S(2)}) copy-start(bf16[1,1024,2048]{2,1,0:T(8,128)(2,1)} %up_ref.7) | copy-start | bytes 12582916
  10.3 2.2 %copy-start.2 = (bf16[1,2048,1024]{2,1,0:T(8,128)(2,1)S(1)}, bf16[1,2048,1024]{2,1,0:T(8,128)(2,1)}, u32[]{:S(2)}) copy-start(bf16[1,2048,1024]{2,1,0:T(8,128)(2,1)} %refs_1_.9) | copy-start | bytes 12582916
  12.3 7.1 %copy-start.1 = (bf16[1,1024,2048]{2,1,0:T(8,128)(2,1)S(1)}, bf16[1,1024,2048]{2,1,0:T(8,128)(2,1)}, u32[]{:S(2)}) copy-start(bf16[1,1024,2048]{2,1,0:T(8,128)(2,1)} %up_ref.7) | copy-start | bytes 12582916
  17.1 6.7 %collective-permute-start.4 = (bf16[128,1024]{1,0:T(8,128)(2,1)S(1)}, bf16[128,1024]{1,0:T(8,128)(2,1)S(1)}, u32[]{:S(2)}, u32[]{:S(2)}) collective-permute-start(bf16[128,1024]{1,0:T(8,128)(2,1)S(1)} %get-tuple-element.63), channel_id=1, source_target_pairs={{0,1},{1,0},{2,3},{3,2},{4,5},{5,4},{6,7},{7,6},{8,9},{9,8},{10,11... | collective-permute-start | bytes 786440 | tf_op jit(solution)/shard_map/ppermute | solution.py:323
  17.2 9.1 %collective-permute-start.6 = (bf16[128,1024]{1,0:T(8,128)(2,1)S(1)}, bf16[128,1024]{1,0:T(8,128)(2,1)S(1)}, u32[]{:S(2)}, u32[]{:S(2)}) collective-permute-start(bf16[128,1024]{1,0:T(8,128)(2,1)S(1)} %get-tuple-element.69), channel_id=1, source_target_pairs={{0,3},{1,2},{2,1},{3,0},{4,7},{5,6},{6,5},{7,4},{8,11},{9,10},{10,... | collective-permute-start | bytes 786440 | tf_op jit(solution)/shard_map/ppermute | solution.py:323
  26.7 14.8 %collective-permute-start.7 = (bf16[256,1024]{1,0:T(8,128)(2,1)S(1)}, bf16[256,1024]{1,0:T(8,128)(2,1)S(1)}, u32[]{:S(2)}, u32[]{:S(2)}) collective-permute-start(bf16[256,1024]{1,0:T(8,128)(2,1)S(1)} %get-tuple-element.73.refs_4_), channel_id=1, source_target_pairs={{0,8},{8,16},{16,24},{24,28},{28,20},{20,12},{12,4},{4,0},{1,9},{9... | collective-permute-start | bytes 1572872 | tf_op jit(solution)/shard_map/ppermute | solution.py:402
  28.6 14.7 %collective-permute-start.8 = (bf16[256,1024]{1,0:T(8,128)(2,1)S(1)}, bf16[256,1024]{1,0:T(8,128)(2,1)S(1)}, u32[]{:S(2)}, u32[]{:S(2)}) collective-permute-start(bf16[256,1024]{1,0:T(8,128)(2,1)S(1)} %get-tuple-element.74.refs_5_), channel_id=1, source_target_pairs={{8,0},{16,8},{24,16},{28,24},{20,28},{12,20},{4,12},{0,4},{9,1},{1... | collective-permute-start | bytes 1572872 | tf_op jit(solution)/shard_map/ppermute | solution.py:402
  31.4 21.3 %collective-permute-start.11 = (bf16[128,2048]{1,0:T(8,128)(2,1)S(1)}, bf16[128,2048]{1,0:T(8,128)(2,1)S(1)}, u32[]{:S(2)}, u32[]{:S(2)}) collective-permute-start(bf16[128,2048]{1,0:T(8,128)(2,1)S(1)} %get-tuple-element.82.refs_0_), channel_id=1, source_target_pairs={{0,8},{8,16},{16,24},{24,28},{28,20},{20,12},{12,4},{4,0},{1,9},{9... | collective-permute-start | bytes 1572872 | tf_op jit(solution)/shard_map/ppermute | solution.py:402
  33.2 21.3 %collective-permute-start.12 = (bf16[128,2048]{1,0:T(8,128)(2,1)S(1)}, bf16[128,2048]{1,0:T(8,128)(2,1)S(1)}, u32[]{:S(2)}, u32[]{:S(2)}) collective-permute-start(bf16[128,2048]{1,0:T(8,128)(2,1)S(1)} %get-tuple-element.83.refs_1_), channel_id=1, source_target_pairs={{8,0},{16,8},{24,16},{28,24},{20,28},{12,20},{4,12},{0,4},{9,1},{1... | collective-permute-start | bytes 1572872 | tf_op jit(solution)/shard_map/ppermute | solution.py:402
  35.0 9.3 %collective-permute-start.13 = (bf16[128,1152]{1,0:T(8,128)(2,1)S(1)}, bf16[128,1152]{1,0:T(8,128)(2,1)S(1)}, u32[]{:S(2)}, u32[]{:S(2)}) collective-permute-start(bf16[128,1152]{1,0:T(8,128)(2,1)S(1)} %feat_grad.4.refs_9_), channel_id=1, source_target_pairs={{0,2},{1,3},{2,0},{3,1},{4,6},{5,7},{6,4},{7,5},{8,10},{9,11},{10,... | collective-permute-start | bytes 884744 | tf_op jit(solution)/shard_map/ppermute | solution.py:426
  45.8 11.8 %collective-permute-start.14 = (bf16[128,1152]{1,0:T(8,128)(2,1)S(1)}, bf16[128,1152]{1,0:T(8,128)(2,1)S(1)}, u32[]{:S(2)}, u32[]{:S(2)}) collective-permute-start(bf16[128,1152]{1,0:T(8,128)(2,1)S(1)} %feat_grad.5.refs_8_), channel_id=1, source_target_pairs={{0,3},{1,2},{2,1},{3,0},{4,7},{5,6},{6,5},{7,4},{8,11},{9,10},{10,... | collective-permute-start | bytes 884744 | tf_op jit(solution)/shard_map/ppermute | solution.py:426
  45.9 18.0 %collective-permute-start.9 = (bf16[256,1024]{1,0:T(8,128)(2,1)S(1)}, bf16[256,1024]{1,0:T(8,128)(2,1)S(1)}, u32[]{:S(2)}, u32[]{:S(2)}) collective-permute-start(bf16[256,1024]{1,0:T(8,128)(2,1)S(1)} %get-tuple-element.84.refs_0_), channel_id=1, source_target_pairs={{0,8},{8,16},{16,24},{24,28},{28,20},{20,12},{12,4},{4,0},{1,9},{9... | collective-permute-start | bytes 1572872 | tf_op jit(solution)/shard_map/ppermute | solution.py:402
  47.5 18.3 %collective-permute-start.10 = (bf16[256,1024]{1,0:T(8,128)(2,1)S(1)}, bf16[256,1024]{1,0:T(8,128)(2,1)S(1)}, u32[]{:S(2)}, u32[]{:S(2)}) collective-permute-start(bf16[256,1024]{1,0:T(8,128)(2,1)S(1)} %get-tuple-element.85.refs_1_), channel_id=1, source_target_pairs={{8,0},{16,8},{24,16},{28,24},{20,28},{12,20},{4,12},{0,4},{9,1},{1... | collective-permute-start | bytes 1572872 | tf_op jit(solution)/shard_map/ppermute | solution.py:402
  55.5 19.6 %collective-permute-start.16 = (bf16[128,2048]{1,0:T(8,128)(2,1)S(1)}, bf16[128,2048]{1,0:T(8,128)(2,1)S(1)}, u32[]{:S(2)}, u32[]{:S(2)}) collective-permute-start(bf16[128,2048]{1,0:T(8,128)(2,1)S(1)} %get-tuple-element.86.refs_0_), channel_id=1, source_target_pairs={{0,8},{8,16},{16,24},{24,28},{28,20},{20,12},{12,4},{4,0},{1,9},{9... | collective-permute-start | bytes 1572872 | tf_op jit(solution)/shard_map/ppermute | solution.py:402
  57.2 19.8 %collective-permute-start.17 = (bf16[128,2048]{1,0:T(8,128)(2,1)S(1)}, bf16[128,2048]{1,0:T(8,128)(2,1)S(1)}, u32[]{:S(2)}, u32[]{:S(2)}) collective-permute-start(bf16[128,2048]{1,0:T(8,128)(2,1)S(1)} %get-tuple-element.87.refs_1_), channel_id=1, source_target_pairs={{8,0},{16,8},{24,16},{28,24},{20,28},{12,20},{4,12},{0,4},{9,1},{1... | collective-permute-start | bytes 1572872 | tf_op jit(solution)/shard_map/ppermute | solution.py:402
  59.1 9.7 %collective-permute-start.15 = (bf16[128,1152]{1,0:T(8,128)(2,1)S(1)}, bf16[128,1152]{1,0:T(8,128)(2,1)S(1)}, u32[]{:S(2)}, u32[]{:S(2)}) collective-permute-start(bf16[128,1152]{1,0:T(8,128)(2,1)S(1)} %feat_grad.6.refs_9_), channel_id=1, source_target_pairs={{0,1},{1,0},{2,3},{3,2},{4,5},{5,4},{6,7},{7,6},{8,9},{9,8},{10,11... | collective-permute-start | bytes 884744 | tf_op jit(solution)/shard_map/ppermute | solution.py:426
  66.8 19.7 %collective-permute-start.20 = (bf16[256,1024]{1,0:T(8,128)(2,1)S(1)}, bf16[256,1024]{1,0:T(8,128)(2,1)S(1)}, u32[]{:S(2)}, u32[]{:S(2)}) collective-permute-start(bf16[256,1024]{1,0:T(8,128)(2,1)S(1)} %get-tuple-element.88.refs_0_), channel_id=1, source_target_pairs={{0,8},{8,16},{16,24},{24,28},{28,20},{20,12},{12,4},{4,0},{1,9},{9... | collective-permute-start | bytes 1572872 | tf_op jit(solution)/shard_map/ppermute | solution.py:402
  68.4 19.9 %collective-permute-start.21 = (bf16[256,1024]{1,0:T(8,128)(2,1)S(1)}, bf16[256,1024]{1,0:T(8,128)(2,1)S(1)}, u32[]{:S(2)}, u32[]{:S(2)}) collective-permute-start(bf16[256,1024]{1,0:T(8,128)(2,1)S(1)} %get-tuple-element.89.refs_1_), channel_id=1, source_target_pairs={{8,0},{16,8},{24,16},{28,24},{20,28},{12,20},{4,12},{0,4},{9,1},{1... | collective-permute-start | bytes 1572872 | tf_op jit(solution)/shard_map/ppermute | solution.py:402
  78.0 19.6 %collective-permute-start.18 = (bf16[128,2048]{1,0:T(8,128)(2,1)S(1)}, bf16[128,2048]{1,0:T(8,128)(2,1)S(1)}, u32[]{:S(2)}, u32[]{:S(2)}) collective-permute-start(bf16[128,2048]{1,0:T(8,128)(2,1)S(1)} %get-tuple-element.90.refs_9_), channel_id=1, source_target_pairs={{0,8},{8,16},{16,24},{24,28},{28,20},{20,12},{12,4},{4,0},{1,9},{9... | collective-permute-start | bytes 1572872 | tf_op jit(solution)/shard_map/ppermute | solution.py:402
  79.6 19.8 %collective-permute-start.19 = (bf16[128,2048]{1,0:T(8,128)(2,1)S(1)}, bf16[128,2048]{1,0:T(8,128)(2,1)S(1)}, u32[]{:S(2)}, u32[]{:S(2)}) collective-permute-start(bf16[128,2048]{1,0:T(8,128)(2,1)S(1)} %get-tuple-element.91.refs_10_), channel_id=1, source_target_pairs={{8,0},{16,8},{24,16},{28,24},{20,28},{12,20},{4,12},{0,4},{9,1},{1... | collective-permute-start | bytes 1572872 | tf_op jit(solution)/shard_map/ppermute | solution.py:402
  88.8 16.2 %collective-permute-start.25 = (bf16[256,512]{1,0:T(8,128)(2,1)S(1)}, bf16[256,512]{1,0:T(8,128)(2,1)S(1)}, u32[]{:S(2)}, u32[]{:S(2)}) collective-permute-start(bf16[256,512]{1,0:T(8,128)(2,1)S(1)} %get-tuple-element.92.refs_9_), channel_id=1, source_target_pairs={{0,8},{8,16},{16,24},{24,28},{28,20},{20,12},{12,4},{4,0},{1,9},{9... | collective-permute-start | bytes 786440 | tf_op jit(solution)/shard_map/ppermute | solution.py:402
  90.5 15.5 %collective-permute-start.24 = (bf16[256,512]{1,0:T(8,128)(2,1)S(1)}, bf16[256,512]{1,0:T(8,128)(2,1)S(1)}, u32[]{:S(2)}, u32[]{:S(2)}) collective-permute-start(bf16[256,512]{1,0:T(8,128)(2,1)S(1)} %get-tuple-element.93.refs_10_), channel_id=1, source_target_pairs={{8,0},{16,8},{24,16},{28,24},{20,28},{12,20},{4,12},{0,4},{9,1},{1... | collective-permute-start | bytes 786440 | tf_op jit(solution)/shard_map/ppermute | solution.py:402
  100.1 4.5 %copy-start.3 = (bf16[256]{0:T(256)(128)(2,1)S(1)}, bf16[256]{0:T(256)(128)(2,1)}, u32[]{:S(2)}) copy-start(bf16[256]{0:T(256)(128)(2,1)} %refs_1_.5) | copy-start | bytes 1540
  100.1 8.5 %collective-permute-start.23 = (bf16[128,1024]{1,0:T(8,128)(2,1)S(1)}, bf16[128,1024]{1,0:T(8,128)(2,1)S(1)}, u32[]{:S(2)}, u32[]{:S(2)}) collective-permute-start(bf16[128,1024]{1,0:T(8,128)(2,1)S(1)} %get-tuple-element.94.refs_8_), channel_id=1, source_target_pairs={{0,8},{8,16},{16,24},{24,28},{28,20},{20,12},{12,4},{4,0},{1,9},{9... | collective-permute-start | bytes 786440 | tf_op jit(solution)/shard_map/ppermute | solution.py:402
  101.7 8.4 %collective-permute-start.22 = (bf16[128,1024]{1,0:T(8,128)(2,1)S(1)}, bf16[128,1024]{1,0:T(8,128)(2,1)S(1)}, u32[]{:S(2)}, u32[]{:S(2)}) collective-permute-start(bf16[128,1024]{1,0:T(8,128)(2,1)S(1)} %get-tuple-element.95.refs_9_), channel_id=1, source_target_pairs={{8,0},{16,8},{24,16},{28,24},{20,28},{12,20},{4,12},{0,4},{9,1},{1... | collective-permute-start | bytes 786440 | tf_op jit(solution)/shard_map/ppermute | solution.py:402

commit v7 on v5

--- a/solution.py
+++ b/solution.py
@@ -10,6 +10,7 @@
 SQRT_HALF = 0.7071067811865476
 INV_ROOT_TAU = 0.3989422804014327
 LANES = 128
+PIECES = 4
 VMEM_LIMIT = 16 * 1024 * 1024
 F32 = jnp.float32
 BF16 = jnp.bfloat16
@@ -235,12 +236,17 @@
 
 
 def last_kernel(way, count, arrived_ref, own_ref, *refs):
-    out, held, sem = refs[-3:]
-    half = held.shape[1]
-    held[...] = (own_ref[...] + arrived_ref[...].astype(F32)) * (1.0 / count)
-    copy = pltpu.make_async_copy(held, out.at[0, :, way * half : (way + 1) * half], sem)
-    copy.start()
-    copy.wait()
+    out, held, sems = refs[-3:]
+    rows, half = held.shape
+    copies = []
+    for i in range(PIECES):
+        part = slice(i * rows // PIECES, (i + 1) * rows // PIECES)
+        held[part] = (own_ref[part] + arrived_ref[part].astype(F32)) * (1.0 / count)
+        target = out.at[0, part, way * half : (way + 1) * half]
+        copies.append(pltpu.make_async_copy(held.at[part], target, sems.at[i]))
+        copies[-1].start()
+    for copy in copies:
+        copy.wait()
 
 
 def last_call(name, count, arrived, own, after):
@@ -256,7 +262,7 @@
                 out_specs=pl.BlockSpec(memory_space=pltpu.HBM),
                 out_shape=pltpu.HBM((1, rows, 2 * half), F32),
                 input_output_aliases={2: 0} if out else {},
-                scratch_shapes=[pltpu.VMEM((rows, half), F32), pltpu.SemaphoreType.DMA],
+                scratch_shapes=[pltpu.VMEM((rows, half), F32), pltpu.SemaphoreType.DMA((PIECES,))],
                 compiler_params=params(),
                 name=name,
             )(arrived[way], own[way], *(in_hbm(a) for a in out), *after)

time: 111 us -> 111 us (level)
  no operation moved by 1% of the time
where the time goes in v7:
time: 111 us
  starting transfers between devices  38.8 us (35%)
  waiting for transfers between devices  36.6 us (33%)
  Pallas kernels  31.5 us (28%)
  local copies, waits for them, and re-layouts  2.35 us (2%)
    ppermute x14, starting transfers between devices, send(): lax.ppermute(pair[0], 'dp', forward)  22.1 us
    ppermute x14, waiting for transfers between devices, send(): lax.ppermute(pair[1], 'dp', backward)  17.7 us
    pallas_call x10, Pallas kernels, call(): pl.pallas_call(body, in_specs=[WHOLE] * len(inputs) + [LATER] * len(after...  14.9 us
    ppermute x14, waiting for transfers between devices, send(): lax.ppermute(pair[0], 'dp', forward)  13 us
    pallas_call x17, Pallas kernels, ring_step(): pl.pallas_call(functools.partial(step_kernel, [len(group) for group in ri...  9.32 us
    ppermute x14, starting transfers between devices, send(): lax.ppermute(pair[1], 'dp', backward)  7 us
    ppermute x5, starting transfers between devices, exchange(): return {k: lax.ppermute(outs[k], 'expert', sources[k]) for k in reach}  4.82 us
    pallas_call x4, Pallas kernels, last_call(): pl.pallas_call(functools.partial(last_kernel, way, count), in_specs=[WHOL...  3.34 us
  transfers between devices with their start and end apart: 38, of which 28 were waited for; matrix products, arithmetic and copies ran while one was open for 1% of the time, Pallas kernels for 27%

profile of v7, /device:TPU:0, one launch (start us, length us, event | category | flops | bytes accessed | tf_op | source)
XLA Modules:
  0.0 111.0 jit_solution(1107850089096005347)
XLA Ops:
  0.6 3.0 %collective-permute-start.3 = (bf16[256,1024]{1,0:T(8,128)(2,1)}, bf16[256,1024]{1,0:T(8,128)(2,1)S(1)}, u32[]{:S(2)}, u32[]{:S(2)}) collective-permute-start(bf16[256,1024]{1,0:T(8,128)(2,1)} %refs_3_.1), channel_id=1, source_target_pairs={{0,2},{1,3},{2,0},{3,1},{4,6},{5,7},{6,4},{7,5},{8,10},{9,11},{10,... | collective-permute-start | bytes 1572872 | tf_op jit(solution)/shard_map/ppermute | solution.py:304
  3.6 1.9 %pack.1 = (s32[1,256]{1,0:T(1,128)S(1)}, bf16[128,1024]{1,0:T(8,128)(2,1)S(1)}, bf16[128,1024]{1,0:T(8,128)(2,1)S(1)}, bf16[128,1024]{1,0:T(8,128)(2,1)S(1)}, bf...) custom-call(s32[256]{0:T(256)} %refs_0_.1, bf16[256]{0:T(256)(128)(2,1)} %refs_1_.5, ...), custom_call_target="tpu_custom_call" | custom-call | tf_op jit(solution)/shard_map/pack/pallas_call | solution.py:308
  6.1 2.0 %collective-permute-start.5 = (bf16[128,1024]{1,0:T(8,128)(2,1)S(1)}, bf16[128,1024]{1,0:T(8,128)(2,1)S(1)}, u32[]{:S(2)}, u32[]{:S(2)}) collective-permute-start(bf16[128,1024]{1,0:T(8,128)(2,1)S(1)} %get-tuple-element.80), channel_id=1, source_target_pairs={{0,2},{1,3},{2,0},{3,1},{4,6},{5,7},{6,4},{7,5},{8,10},{9,11},{10,... | collective-permute-start | bytes 786440 | tf_op jit(solution)/shard_map/ppermute | solution.py:299
  8.1 2.2 %copy-done = bf16[1,1024,2048]{2,1,0:T(8,128)(2,1)S(1)} copy-done((bf16[1,1024,2048]{2,1,0:T(8,128)(2,1)S(1)}, bf16[1,1024,2048]{2,1,0:T(8,128)(2,1)}, u32[]{:S(2)}) %copy-start) | copy-done | bytes 4194328
  10.3 2.0 %hidden.3 = (bf16[1024,256]{1,0:T(8,128)(2,1)S(1)}, bf16[256,2048]{1,0:T(8,128)(2,1)S(1)}, bf16[2048,256]{1,0:T(8,128)(2,1)S(1)}, bf16[256,2048]{1,0:T(8,128)(2,1)S(1)}) custom-call(bf16[128,1024]{1,0:T(8,128)(2,1)S(1)} %get-tuple-element.70.refs_0_, bf16[128,1024]{1,0:T(8,128)(2,1)S(1)} %collective-permute-done.1.refs_1_, bf16[1,1024,2048]{2,1,0:T(8,128)(2,1)S(1)} %copy-done), custom_call_target="tpu_custom_call" | custom-call | tf_op jit(solution)/shard_map/hidden/pallas_call | solution.py:101
  14.0 2.7 %collective-permute-done.2.id_ref = s32[1,256]{1,0:T(1,128)S(1)} collective-permute-done((s32[1,256]{1,0:T(1,128)}, s32[1,256]{1,0:T(1,128)S(1)}, u32[]{:S(2)}, u32[]{:S(2)}) %collective-permute-start.2) | collective-permute-done | bytes 1056 | tf_op jit(solution)/shard_map/ppermute | solution.py:305
  17.2 2.2 %collective-permute-start.6 = (bf16[128,1024]{1,0:T(8,128)(2,1)S(1)}, bf16[128,1024]{1,0:T(8,128)(2,1)S(1)}, u32[]{:S(2)}, u32[]{:S(2)}) collective-permute-start(bf16[128,1024]{1,0:T(8,128)(2,1)S(1)} %get-tuple-element.86), channel_id=1, source_target_pairs={{0,3},{1,2},{2,1},{3,0},{4,7},{5,6},{6,5},{7,4},{8,11},{9,10},{10,... | collective-permute-start | bytes 786440 | tf_op jit(solution)/shard_map/ppermute | solution.py:299
  20.4 1.7 %collective-permute-done.5.refs_0_.refs_4_.refs_5_ = bf16[128,1024]{1,0:T(8,128)(2,1)S(1)} collective-permute-done((bf16[128,1024]{1,0:T(8,128)(2,1)S(1)}, bf16[128,1024]{1,0:T(8,128)(2,1)S(1)}, u32[]{:S(2)}, u32[]{:S(2)}) %collective-permute-start.5) | collective-permute-done | bytes 262176 | tf_op jit(solution)/shard_map/ppermute | solution.py:299
  22.1 1.6 %pre_grad.4 = (bf16[128,2048]{1,0:T(8,128)(2,1)S(1)}, f32[128,128]{1,0:T(8,128)S(1)}) custom-call(bf16[128,1024]{1,0:T(8,128)(2,1)S(1)} %collective-permute-done.5.refs_0_.refs_4_.refs_5_, bf16[1,2048,1024]{2,1,0:T(8,128)(2,1)S(1)} %copy-done.2, bf16[128,2048]{1,0:T(8,128)(2,1)S(1)} %get-tuple-element.81.refs_2_.refs_4_, ...), custom_call_target="tpu_custom_call" | custom-call | tf_op jit(solution)/shard_map/pre_grad/pallas_call | solution.py:101
  26.6 1.8 %collective-permute-start.9 = (bf16[256,512]{1,0:T(8,128)(2,1)S(1)}, bf16[256,512]{1,0:T(8,128)(2,1)S(1)}, u32[]{:S(2)}, u32[]{:S(2)}) collective-permute-start(bf16[256,512]{1,0:T(8,128)(2,1)S(1)} %get-tuple-element.94.refs_4_), channel_id=1, source_target_pairs={{0,8},{8,16},{16,24},{24,28},{28,20},{20,12},{12,4},{4,0},{1,9},{9... | collective-permute-start | bytes 786440 | tf_op jit(solution)/shard_map/ppermute | solution.py:376
  28.7 1.6 %pre_grad.5 = (bf16[128,2048]{1,0:T(8,128)(2,1)S(1)}, f32[128,128]{1,0:T(8,128)S(1)}) custom-call(bf16[128,1024]{1,0:T(8,128)(2,1)S(1)} %collective-permute-done.6.refs_1_.refs_0_.refs_6_, bf16[1,2048,1024]{2,1,0:T(8,128)(2,1)S(1)} %copy-done.2, bf16[128,2048]{1,0:T(8,128)(2,1)S(1)} %get-tuple-element.87.refs_5_.refs_2_, ...), custom_call_target="tpu_custom_call" | custom-call | tf_op jit(solution)/shard_map/pre_grad/pallas_call | solution.py:101
  30.9 1.8 %collective-permute-start.7 = (bf16[128,1024]{1,0:T(8,128)(2,1)S(1)}, bf16[128,1024]{1,0:T(8,128)(2,1)S(1)}, u32[]{:S(2)}, u32[]{:S(2)}) collective-permute-start(bf16[128,1024]{1,0:T(8,128)(2,1)S(1)} %get-tuple-element.98.refs_9_), channel_id=1, source_target_pairs={{0,8},{8,16},{16,24},{24,28},{28,20},{20,12},{12,4},{4,0},{1,9},{9... | collective-permute-start | bytes 786440 | tf_op jit(solution)/shard_map/ppermute | solution.py:376
  33.0 2.8 %collective-permute-done.9.refs_7_ = bf16[256,512]{1,0:T(8,128)(2,1)S(1)} collective-permute-done((bf16[256,512]{1,0:T(8,128)(2,1)S(1)}, bf16[256,512]{1,0:T(8,128)(2,1)S(1)}, u32[]{:S(2)}, u32[]{:S(2)}) %collective-permute-start.9) | collective-permute-done | bytes 262176 | tf_op jit(solution)/shard_map/ppermute | solution.py:376
  35.7 1.8 %collective-permute-done.10.refs_8_ = bf16[256,512]{1,0:T(8,128)(2,1)S(1)} collective-permute-done((bf16[256,512]{1,0:T(8,128)(2,1)S(1)}, bf16[256,512]{1,0:T(8,128)(2,1)S(1)}, u32[]{:S(2)}, u32[]{:S(2)}) %collective-permute-start.10) | collective-permute-done | bytes 262176 | tf_op jit(solution)/shard_map/ppermute | solution.py:376
  38.1 1.6 %collective-permute-start.13 = (bf16[256,512]{1,0:T(8,128)(2,1)S(1)}, bf16[256,512]{1,0:T(8,128)(2,1)S(1)}, u32[]{:S(2)}, u32[]{:S(2)}) collective-permute-start(bf16[256,512]{1,0:T(8,128)(2,1)S(1)} %get-tuple-element.100.refs_8_), channel_id=1, source_target_pairs={{0,8},{8,16},{16,24},{24,28},{28,20},{20,12},{12,4},{4,0},{1,9},{9... | collective-permute-start | bytes 786440 | tf_op jit(solution)/shard_map/ppermute | solution.py:376
  41.3 1.8 %collective-permute-done.8.refs_7_ = bf16[128,1024]{1,0:T(8,128)(2,1)S(1)} collective-permute-done((bf16[128,1024]{1,0:T(8,128)(2,1)S(1)}, bf16[128,1024]{1,0:T(8,128)(2,1)S(1)}, u32[]{:S(2)}, u32[]{:S(2)}) %collective-permute-start.8) | collective-permute-done | bytes 262176 | tf_op jit(solution)/shard_map/ppermute | solution.py:376
  43.8 1.6 %collective-permute-start.11 = (bf16[128,1024]{1,0:T(8,128)(2,1)S(1)}, bf16[128,1024]{1,0:T(8,128)(2,1)S(1)}, u32[]{:S(2)}, u32[]{:S(2)}) collective-permute-start(bf16[128,1024]{1,0:T(8,128)(2,1)S(1)} %get-tuple-element.102.refs_0_), channel_id=1, source_target_pairs={{0,8},{8,16},{16,24},{24,28},{28,20},{20,12},{12,4},{4,0},{1,9},{9... | collective-permute-start | bytes 786440 | tf_op jit(solution)/shard_map/ppermute | solution.py:376
  47.3 1.6 %collective-permute-start.19 = (bf16[128,1152]{1,0:T(8,128)(2,1)S(1)}, bf16[128,1152]{1,0:T(8,128)(2,1)S(1)}, u32[]{:S(2)}, u32[]{:S(2)}) collective-permute-start(bf16[128,1152]{1,0:T(8,128)(2,1)S(1)} %feat_grad.4.refs_9_), channel_id=1, source_target_pairs={{0,2},{1,3},{2,0},{3,1},{4,6},{5,7},{6,4},{7,5},{8,10},{9,11},{10,... | collective-permute-start | bytes 884744 | tf_op jit(solution)/shard_map/ppermute | solution.py:418
  49.6 1.6 %collective-permute-start.17 = (bf16[256,512]{1,0:T(8,128)(2,1)S(1)}, bf16[256,512]{1,0:T(8,128)(2,1)S(1)}, u32[]{:S(2)}, u32[]{:S(2)}) collective-permute-start(bf16[256,512]{1,0:T(8,128)(2,1)S(1)} %get-tuple-element.104.refs_8_), channel_id=1, source_target_pairs={{0,8},{8,16},{16,24},{24,28},{28,20},{20,12},{12,4},{4,0},{1,9},{9... | collective-permute-start | bytes 786440 | tf_op jit(solution)/shard_map/ppermute | solution.py:376
  53.0 1.6 %collective-permute-done.12.refs_7_ = bf16[128,1024]{1,0:T(8,128)(2,1)S(1)} collective-permute-done((bf16[128,1024]{1,0:T(8,128)(2,1)S(1)}, bf16[128,1024]{1,0:T(8,128)(2,1)S(1)}, u32[]{:S(2)}, u32[]{:S(2)}) %collective-permute-start.12) | collective-permute-done | bytes 262176 | tf_op jit(solution)/shard_map/ppermute | solution.py:376
  55.2 1.6 %collective-permute-start.15 = (bf16[128,1024]{1,0:T(8,128)(2,1)S(1)}, bf16[128,1024]{1,0:T(8,128)(2,1)S(1)}, u32[]{:S(2)}, u32[]{:S(2)}) collective-permute-start(bf16[128,1024]{1,0:T(8,128)(2,1)S(1)} %get-tuple-element.106.refs_0_), channel_id=1, source_target_pairs={{0,8},{8,16},{16,24},{24,28},{28,20},{20,12},{12,4},{4,0},{1,9},{9... | collective-permute-start | bytes 786440 | tf_op jit(solution)/shard_map/ppermute | solution.py:376
  58.9 1.6 %collective-permute-done.18.refs_8_ = bf16[256,512]{1,0:T(8,128)(2,1)S(1)} collective-permute-done((bf16[256,512]{1,0:T(8,128)(2,1)S(1)}, bf16[256,512]{1,0:T(8,128)(2,1)S(1)}, u32[]{:S(2)}, u32[]{:S(2)}) %collective-permute-start.18) | collective-permute-done | bytes 262176 | tf_op jit(solution)/shard_map/ppermute | solution.py:376
  61.0 1.6 %collective-permute-start.22 = (bf16[256,512]{1,0:T(8,128)(2,1)S(1)}, bf16[256,512]{1,0:T(8,128)(2,1)S(1)}, u32[]{:S(2)}, u32[]{:S(2)}) collective-permute-start(bf16[256,512]{1,0:T(8,128)(2,1)S(1)} %get-tuple-element.108.refs_8_), channel_id=1, source_target_pairs={{0,8},{8,16},{16,24},{24,28},{28,20},{20,12},{12,4},{4,0},{1,9},{9... | collective-permute-start | bytes 786440 | tf_op jit(solution)/shard_map/ppermute | solution.py:376
  63.5 1.5 %collective-permute-done.16.refs_7_ = bf16[128,1024]{1,0:T(8,128)(2,1)S(1)} collective-permute-done((bf16[128,1024]{1,0:T(8,128)(2,1)S(1)}, bf16[128,1024]{1,0:T(8,128)(2,1)S(1)}, u32[]{:S(2)}, u32[]{:S(2)}) %collective-permute-start.16) | collective-permute-done | bytes 262176 | tf_op jit(solution)/shard_map/ppermute | solution.py:376
  65.6 1.6 %collective-permute-start.20 = (bf16[128,1024]{1,0:T(8,128)(2,1)S(1)}, bf16[128,1024]{1,0:T(8,128)(2,1)S(1)}, u32[]{:S(2)}, u32[]{:S(2)}) collective-permute-start(bf16[128,1024]{1,0:T(8,128)(2,1)S(1)} %get-tuple-element.110.refs_0_), channel_id=1, source_target_pairs={{0,8},{8,16},{16,24},{24,28},{28,20},{20,12},{12,4},{4,0},{1,9},{9... | collective-permute-start | bytes 786440 | tf_op jit(solution)/shard_map/ppermute | solution.py:376
  70.3 1.6 %collective-permute-done.23.refs_8_ = bf16[256,512]{1,0:T(8,128)(2,1)S(1)} collective-permute-done((bf16[256,512]{1,0:T(8,128)(2,1)S(1)}, bf16[256,512]{1,0:T(8,128)(2,1)S(1)}, u32[]{:S(2)}, u32[]{:S(2)}) %collective-permute-start.23) | collective-permute-done | bytes 262176 | tf_op jit(solution)/shard_map/ppermute | solution.py:376
  72.4 1.5 %collective-permute-start.28 = (bf16[256,512]{1,0:T(8,128)(2,1)S(1)}, bf16[256,512]{1,0:T(8,128)(2,1)S(1)}, u32[]{:S(2)}, u32[]{:S(2)}) collective-permute-start(bf16[256,512]{1,0:T(8,128)(2,1)S(1)} %get-tuple-element.112.refs_8_), channel_id=1, source_target_pairs={{0,8},{8,16},{16,24},{24,28},{28,20},{20,12},{12,4},{4,0},{1,9},{9... | collective-permute-start | bytes 786440 | tf_op jit(solution)/shard_map/ppermute | solution.py:376
  75.9 1.6 %collective-permute-done.21.refs_7_ = bf16[128,1024]{1,0:T(8,128)(2,1)S(1)} collective-permute-done((bf16[128,1024]{1,0:T(8,128)(2,1)S(1)}, bf16[128,1024]{1,0:T(8,128)(2,1)S(1)}, u32[]{:S(2)}, u32[]{:S(2)}) %collective-permute-start.21) | collective-permute-done | bytes 262176 | tf_op jit(solution)/shard_map/ppermute | solution.py:376
  78.0 1.5 %collective-permute-start.26 = (bf16[128,1024]{1,0:T(8,128)(2,1)S(1)}, bf16[128,1024]{1,0:T(8,128)(2,1)S(1)}, u32[]{:S(2)}, u32[]{:S(2)}) collective-permute-start(bf16[128,1024]{1,0:T(8,128)(2,1)S(1)} %get-tuple-element.114.refs_0_), channel_id=1, source_target_pairs={{0,8},{8,16},{16,24},{24,28},{28,20},{20,12},{12,4},{4,0},{1,9},{9... | collective-permute-start | bytes 786440 | tf_op jit(solution)/shard_map/ppermute | solution.py:376
  97.1 1.6 %collective-permute-done.30.refs_6_ = bf16[128,1024]{1,0:T(8,128)(2,1)S(1)} collective-permute-done((bf16[128,1024]{1,0:T(8,128)(2,1)S(1)}, bf16[128,1024]{1,0:T(8,128)(2,1)S(1)}, u32[]{:S(2)}, u32[]{:S(2)}) %collective-permute-start.30) | collective-permute-done | bytes 262176 | tf_op jit(solution)/shard_map/ppermute | solution.py:376
  102.7 1.6 %unpack.1 = (bf16[256,1024]{1,0:T(8,128)(2,1)}, f32[256,128]{1,0:T(8,128)S(1)}) custom-call(s32[1,256]{1,0:T(1,128)S(1)} %get-tuple-element.67.slot_ref, bf16[128,1152]{1,0:T(8,128)(2,1)S(1)} %feat_grad.7.refs_9_.refs_0_, bf16[128,1152]{1,0:T(8,128)(2,1)S(1)} %collective-permute-done.25.refs_2_.refs_1_, ...), custom_call_target="tpu_custom_call" | custom-call | tf_op jit(solution)/shard_map/unpack/pallas_call | solution.py:446
  106.7 1.9 %collective-permute-done.35.arrived_ref = bf16[128,1024]{1,0:T(8,128)(2,1)S(1)} collective-permute-done((bf16[128,1024]{1,0:T(8,128)(2,1)S(1)}, bf16[128,1024]{1,0:T(8,128)(2,1)S(1)}, u32[]{:S(2)}, u32[]{:S(2)}) %collective-permute-start.35) | collective-permute-done | bytes 262176 | tf_op jit(solution)/shard_map/ppermute | solution.py:376
  (88 shorter events, 51.7 us)
Async XLA Ops:
  0.6 16.0 %collective-permute-start.3 = (bf16[256,1024]{1,0:T(8,128)(2,1)}, bf16[256,1024]{1,0:T(8,128)(2,1)S(1)}, u32[]{:S(2)}, u32[]{:S(2)}) collective-permute-start(bf16[256,1024]{1,0:T(8,128)(2,1)} %refs_3_.1), channel_id=1, source_target_pairs={{0,2},{1,3},{2,0},{3,1},{4,6},{5,7},{6,4},{7,5},{8,10},{9,11},{10,... | collective-permute-start | bytes 1572872 | tf_op jit(solution)/shard_map/ppermute | solution.py:304
  6.1 10.6 %collective-permute-start.2 = (s32[1,256]{1,0:T(1,128)}, s32[1,256]{1,0:T(1,128)S(1)}, u32[]{:S(2)}, u32[]{:S(2)}) collective-permute-start(s32[1,256]{1,0:T(1,128)} %bitcast.1), channel_id=1, source_target_pairs={{0,2},{1,3},{2,0},{3,1},{4,6},{5,7},{6,4},{7,5},{8,10},{9,11},{10,... | collective-permute-start | bytes 3080 | tf_op jit(solution)/shard_map/ppermute | solution.py:305
  6.1 16.0 %collective-permute-start.5 = (bf16[128,1024]{1,0:T(8,128)(2,1)S(1)}, bf16[128,1024]{1,0:T(8,128)(2,1)S(1)}, u32[]{:S(2)}, u32[]{:S(2)}) collective-permute-start(bf16[128,1024]{1,0:T(8,128)(2,1)S(1)} %get-tuple-element.80), channel_id=1, source_target_pairs={{0,2},{1,3},{2,0},{3,1},{4,6},{5,7},{6,4},{7,5},{8,10},{9,11},{10,... | collective-permute-start | bytes 786440 | tf_op jit(solution)/shard_map/ppermute | solution.py:299
  17.2 9.1 %collective-permute-start.6 = (bf16[128,1024]{1,0:T(8,128)(2,1)S(1)}, bf16[128,1024]{1,0:T(8,128)(2,1)S(1)}, u32[]{:S(2)}, u32[]{:S(2)}) collective-permute-start(bf16[128,1024]{1,0:T(8,128)(2,1)S(1)} %get-tuple-element.86), channel_id=1, source_target_pairs={{0,3},{1,2},{2,1},{3,0},{4,7},{5,6},{6,5},{7,4},{8,11},{9,10},{10,... | collective-permute-start | bytes 786440 | tf_op jit(solution)/shard_map/ppermute | solution.py:299
  26.6 9.1 %collective-permute-start.9 = (bf16[256,512]{1,0:T(8,128)(2,1)S(1)}, bf16[256,512]{1,0:T(8,128)(2,1)S(1)}, u32[]{:S(2)}, u32[]{:S(2)}) collective-permute-start(bf16[256,512]{1,0:T(8,128)(2,1)S(1)} %get-tuple-element.94.refs_4_), channel_id=1, source_target_pairs={{0,8},{8,16},{16,24},{24,28},{28,20},{20,12},{12,4},{4,0},{1,9},{9... | collective-permute-start | bytes 786440 | tf_op jit(solution)/shard_map/ppermute | solution.py:376
  28.4 9.1 %collective-permute-start.10 = (bf16[256,512]{1,0:T(8,128)(2,1)S(1)}, bf16[256,512]{1,0:T(8,128)(2,1)S(1)}, u32[]{:S(2)}, u32[]{:S(2)}) collective-permute-start(bf16[256,512]{1,0:T(8,128)(2,1)S(1)} %get-tuple-element.95.refs_5_), channel_id=1, source_target_pairs={{8,0},{16,8},{24,16},{28,24},{20,28},{12,20},{4,12},{0,4},{9,1},{1... | collective-permute-start | bytes 786440 | tf_op jit(solution)/shard_map/ppermute | solution.py:376
  30.9 10.5 %collective-permute-start.7 = (bf16[128,1024]{1,0:T(8,128)(2,1)S(1)}, bf16[128,1024]{1,0:T(8,128)(2,1)S(1)}, u32[]{:S(2)}, u32[]{:S(2)}) collective-permute-start(bf16[128,1024]{1,0:T(8,128)(2,1)S(1)} %get-tuple-element.98.refs_9_), channel_id=1, source_target_pairs={{0,8},{8,16},{16,24},{24,28},{28,20},{20,12},{12,4},{4,0},{1,9},{9... | collective-permute-start | bytes 786440 | tf_op jit(solution)/shard_map/ppermute | solution.py:376
  32.7 10.5 %collective-permute-start.8 = (bf16[128,1024]{1,0:T(8,128)(2,1)S(1)}, bf16[128,1024]{1,0:T(8,128)(2,1)S(1)}, u32[]{:S(2)}, u32[]{:S(2)}) collective-permute-start(bf16[128,1024]{1,0:T(8,128)(2,1)S(1)} %get-tuple-element.99.refs_10_), channel_id=1, source_target_pairs={{8,0},{16,8},{24,16},{28,24},{20,28},{12,20},{4,12},{0,4},{9,1},{1... | collective-permute-start | bytes 786440 | tf_op jit(solution)/shard_map/ppermute | solution.py:376
  38.1 10.8 %collective-permute-start.13 = (bf16[256,512]{1,0:T(8,128)(2,1)S(1)}, bf16[256,512]{1,0:T(8,128)(2,1)S(1)}, u32[]{:S(2)}, u32[]{:S(2)}) collective-permute-start(bf16[256,512]{1,0:T(8,128)(2,1)S(1)} %get-tuple-element.100.refs_8_), channel_id=1, source_target_pairs={{0,8},{8,16},{16,24},{24,28},{28,20},{20,12},{12,4},{4,0},{1,9},{9... | collective-permute-start | bytes 786440 | tf_op jit(solution)/shard_map/ppermute | solution.py:376
  39.8 9.2 %collective-permute-start.14 = (bf16[256,512]{1,0:T(8,128)(2,1)S(1)}, bf16[256,512]{1,0:T(8,128)(2,1)S(1)}, u32[]{:S(2)}, u32[]{:S(2)}) collective-permute-start(bf16[256,512]{1,0:T(8,128)(2,1)S(1)} %get-tuple-element.101.refs_9_), channel_id=1, source_target_pairs={{8,0},{16,8},{24,16},{28,24},{20,28},{12,20},{4,12},{0,4},{9,1},{1... | collective-permute-start | bytes 786440 | tf_op jit(solution)/shard_map/ppermute | solution.py:376
  43.8 9.3 %collective-permute-start.11 = (bf16[128,1024]{1,0:T(8,128)(2,1)S(1)}, bf16[128,1024]{1,0:T(8,128)(2,1)S(1)}, u32[]{:S(2)}, u32[]{:S(2)}) collective-permute-start(bf16[128,1024]{1,0:T(8,128)(2,1)S(1)} %get-tuple-element.102.refs_0_), channel_id=1, source_target_pairs={{0,8},{8,16},{16,24},{24,28},{28,20},{20,12},{12,4},{4,0},{1,9},{9... | collective-permute-start | bytes 786440 | tf_op jit(solution)/shard_map/ppermute | solution.py:376
  45.4 9.2 %collective-permute-start.12 = (bf16[128,1024]{1,0:T(8,128)(2,1)S(1)}, bf16[128,1024]{1,0:T(8,128)(2,1)S(1)}, u32[]{:S(2)}, u32[]{:S(2)}) collective-permute-start(bf16[128,1024]{1,0:T(8,128)(2,1)S(1)} %get-tuple-element.103.refs_1_), channel_id=1, source_target_pairs={{8,0},{16,8},{24,16},{28,24},{20,28},{12,20},{4,12},{0,4},{9,1},{1... | collective-permute-start | bytes 786440 | tf_op jit(solution)/shard_map/ppermute | solution.py:376
  47.3 10.0 %collective-permute-start.19 = (bf16[128,1152]{1,0:T(8,128)(2,1)S(1)}, bf16[128,1152]{1,0:T(8,128)(2,1)S(1)}, u32[]{:S(2)}, u32[]{:S(2)}) collective-permute-start(bf16[128,1152]{1,0:T(8,128)(2,1)S(1)} %feat_grad.4.refs_9_), channel_id=1, source_target_pairs={{0,2},{1,3},{2,0},{3,1},{4,6},{5,7},{6,4},{7,5},{8,10},{9,11},{10,... | collective-permute-start | bytes 884744 | tf_op jit(solution)/shard_map/ppermute | solution.py:418
  49.6 9.3 %collective-permute-start.17 = (bf16[256,512]{1,0:T(8,128)(2,1)S(1)}, bf16[256,512]{1,0:T(8,128)(2,1)S(1)}, u32[]{:S(2)}, u32[]{:S(2)}) collective-permute-start(bf16[256,512]{1,0:T(8,128)(2,1)S(1)} %get-tuple-element.104.refs_8_), channel_id=1, source_target_pairs={{0,8},{8,16},{16,24},{24,28},{28,20},{20,12},{12,4},{4,0},{1,9},{9... | collective-permute-start | bytes 786440 | tf_op jit(solution)/shard_map/ppermute | solution.py:376
  51.2 9.2 %collective-permute-start.18 = (bf16[256,512]{1,0:T(8,128)(2,1)S(1)}, bf16[256,512]{1,0:T(8,128)(2,1)S(1)}, u32[]{:S(2)}, u32[]{:S(2)}) collective-permute-start(bf16[256,512]{1,0:T(8,128)(2,1)S(1)} %get-tuple-element.105.refs_9_), channel_id=1, source_target_pairs={{8,0},{16,8},{24,16},{28,24},{20,28},{12,20},{4,12},{0,4},{9,1},{1... | collective-permute-start | bytes 786440 | tf_op jit(solution)/shard_map/ppermute | solution.py:376
  55.2 8.3 %collective-permute-start.15 = (bf16[128,1024]{1,0:T(8,128)(2,1)S(1)}, bf16[128,1024]{1,0:T(8,128)(2,1)S(1)}, u32[]{:S(2)}, u32[]{:S(2)}) collective-permute-start(bf16[128,1024]{1,0:T(8,128)(2,1)S(1)} %get-tuple-element.106.refs_0_), channel_id=1, source_target_pairs={{0,8},{8,16},{16,24},{24,28},{28,20},{20,12},{12,4},{4,0},{1,9},{9... | collective-permute-start | bytes 786440 | tf_op jit(solution)/shard_map/ppermute | solution.py:376
  58.8 9.3 %collective-permute-start.24 = (bf16[128,1152]{1,0:T(8,128)(2,1)S(1)}, bf16[128,1152]{1,0:T(8,128)(2,1)S(1)}, u32[]{:S(2)}, u32[]{:S(2)}) collective-permute-start(bf16[128,1152]{1,0:T(8,128)(2,1)S(1)} %feat_grad.5.refs_9_), channel_id=1, source_target_pairs={{0,3},{1,2},{2,1},{3,0},{4,7},{5,6},{6,5},{7,4},{8,11},{9,10},{10,... | collective-permute-start | bytes 884744 | tf_op jit(solution)/shard_map/ppermute | solution.py:418
  61.0 9.2 %collective-permute-start.22 = (bf16[256,512]{1,0:T(8,128)(2,1)S(1)}, bf16[256,512]{1,0:T(8,128)(2,1)S(1)}, u32[]{:S(2)}, u32[]{:S(2)}) collective-permute-start(bf16[256,512]{1,0:T(8,128)(2,1)S(1)} %get-tuple-element.108.refs_8_), channel_id=1, source_target_pairs={{0,8},{8,16},{16,24},{24,28},{28,20},{20,12},{12,4},{4,0},{1,9},{9... | collective-permute-start | bytes 786440 | tf_op jit(solution)/shard_map/ppermute | solution.py:376
  62.6 9.2 %collective-permute-start.23 = (bf16[256,512]{1,0:T(8,128)(2,1)S(1)}, bf16[256,512]{1,0:T(8,128)(2,1)S(1)}, u32[]{:S(2)}, u32[]{:S(2)}) collective-permute-start(bf16[256,512]{1,0:T(8,128)(2,1)S(1)} %get-tuple-element.109.refs_9_), channel_id=1, source_target_pairs={{8,0},{16,8},{24,16},{28,24},{20,28},{12,20},{4,12},{0,4},{9,1},{1... | collective-permute-start | bytes 786440 | tf_op jit(solution)/shard_map/ppermute | solution.py:376
  65.6 10.3 %collective-permute-start.20 = (bf16[128,1024]{1,0:T(8,128)(2,1)S(1)}, bf16[128,1024]{1,0:T(8,128)(2,1)S(1)}, u32[]{:S(2)}, u32[]{:S(2)}) collective-permute-start(bf16[128,1024]{1,0:T(8,128)(2,1)S(1)} %get-tuple-element.110.refs_0_), channel_id=1, source_target_pairs={{0,8},{8,16},{16,24},{24,28},{28,20},{20,12},{12,4},{4,0},{1,9},{9... | collective-permute-start | bytes 786440 | tf_op jit(solution)/shard_map/ppermute | solution.py:376
  67.3 10.2 %collective-permute-start.21 = (bf16[128,1024]{1,0:T(8,128)(2,1)S(1)}, bf16[128,1024]{1,0:T(8,128)(2,1)S(1)}, u32[]{:S(2)}, u32[]{:S(2)}) collective-permute-start(bf16[128,1024]{1,0:T(8,128)(2,1)S(1)} %get-tuple-element.111.refs_1_), channel_id=1, source_target_pairs={{8,0},{16,8},{24,16},{28,24},{20,28},{12,20},{4,12},{0,4},{9,1},{1... | collective-permute-start | bytes 786440 | tf_op jit(solution)/shard_map/ppermute | solution.py:376
  69.6 10.5 %collective-permute-start.25 = (bf16[128,1152]{1,0:T(8,128)(2,1)S(1)}, bf16[128,1152]{1,0:T(8,128)(2,1)S(1)}, u32[]{:S(2)}, u32[]{:S(2)}) collective-permute-start(bf16[128,1152]{1,0:T(8,128)(2,1)S(1)} %feat_grad.6.refs_9_), channel_id=1, source_target_pairs={{0,1},{1,0},{2,3},{3,2},{4,5},{5,4},{6,7},{7,6},{8,9},{9,8},{10,11... | collective-permute-start | bytes 884744 | tf_op jit(solution)/shard_map/ppermute | solution.py:418
  72.4 9.3 %collective-permute-start.28 = (bf16[256,512]{1,0:T(8,128)(2,1)S(1)}, bf16[256,512]{1,0:T(8,128)(2,1)S(1)}, u32[]{:S(2)}, u32[]{:S(2)}) collective-permute-start(bf16[256,512]{1,0:T(8,128)(2,1)S(1)} %get-tuple-element.112.refs_8_), channel_id=1, source_target_pairs={{0,8},{8,16},{16,24},{24,28},{28,20},{20,12},{12,4},{4,0},{1,9},{9... | collective-permute-start | bytes 786440 | tf_op jit(solution)/shard_map/ppermute | solution.py:376
  73.9 9.2 %collective-permute-start.29 = (bf16[256,512]{1,0:T(8,128)(2,1)S(1)}, bf16[256,512]{1,0:T(8,128)(2,1)S(1)}, u32[]{:S(2)}, u32[]{:S(2)}) collective-permute-start(bf16[256,512]{1,0:T(8,128)(2,1)S(1)} %get-tuple-element.113.refs_9_), channel_id=1, source_target_pairs={{8,0},{16,8},{24,16},{28,24},{20,28},{12,20},{4,12},{0,4},{9,1},{1... | collective-permute-start | bytes 786440 | tf_op jit(solution)/shard_map/ppermute | solution.py:376
  78.0 9.3 %collective-permute-start.26 = (bf16[128,1024]{1,0:T(8,128)(2,1)S(1)}, bf16[128,1024]{1,0:T(8,128)(2,1)S(1)}, u32[]{:S(2)}, u32[]{:S(2)}) collective-permute-start(bf16[128,1024]{1,0:T(8,128)(2,1)S(1)} %get-tuple-element.114.refs_0_), channel_id=1, source_target_pairs={{0,8},{8,16},{16,24},{24,28},{28,20},{20,12},{12,4},{4,0},{1,9},{9... | collective-permute-start | bytes 786440 | tf_op jit(solution)/shard_map/ppermute | solution.py:376
  79.5 9.2 %collective-permute-start.27 = (bf16[128,1024]{1,0:T(8,128)(2,1)S(1)}, bf16[128,1024]{1,0:T(8,128)(2,1)S(1)}, u32[]{:S(2)}, u32[]{:S(2)}) collective-permute-start(bf16[128,1024]{1,0:T(8,128)(2,1)S(1)} %get-tuple-element.115.refs_1_), channel_id=1, source_target_pairs={{8,0},{16,8},{24,16},{28,24},{20,28},{12,20},{4,12},{0,4},{9,1},{1... | collective-permute-start | bytes 786440 | tf_op jit(solution)/shard_map/ppermute | solution.py:376
  83.7 9.3 %collective-permute-start.32 = (bf16[256,512]{1,0:T(8,128)(2,1)S(1)}, bf16[256,512]{1,0:T(8,128)(2,1)S(1)}, u32[]{:S(2)}, u32[]{:S(2)}) collective-permute-start(bf16[256,512]{1,0:T(8,128)(2,1)S(1)} %get-tuple-element.116.refs_8_), channel_id=1, source_target_pairs={{0,8},{8,16},{16,24},{24,28},{28,20},{20,12},{12,4},{4,0},{1,9},{9... | collective-permute-start | bytes 786440 | tf_op jit(solution)/shard_map/ppermute | solution.py:376
  85.2 9.2 %collective-permute-start.33 = (bf16[256,512]{1,0:T(8,128)(2,1)S(1)}, bf16[256,512]{1,0:T(8,128)(2,1)S(1)}, u32[]{:S(2)}, u32[]{:S(2)}) collective-permute-start(bf16[256,512]{1,0:T(8,128)(2,1)S(1)} %get-tuple-element.117.refs_9_), channel_id=1, source_target_pairs={{8,0},{16,8},{24,16},{28,24},{20,28},{12,20},{4,12},{0,4},{9,1},{1... | collective-permute-start | bytes 786440 | tf_op jit(solution)/shard_map/ppermute | solution.py:376
  89.4 9.3 %collective-permute-start.30 = (bf16[128,1024]{1,0:T(8,128)(2,1)S(1)}, bf16[128,1024]{1,0:T(8,128)(2,1)S(1)}, u32[]{:S(2)}, u32[]{:S(2)}) collective-permute-start(bf16[128,1024]{1,0:T(8,128)(2,1)S(1)} %get-tuple-element.118.refs_7_), channel_id=1, source_target_pairs={{0,8},{8,16},{16,24},{24,28},{28,20},{20,12},{12,4},{4,0},{1,9},{9... | collective-permute-start | bytes 786440 | tf_op jit(solution)/shard_map/ppermute | solution.py:376
  90.8 9.2 %collective-permute-start.31 = (bf16[128,1024]{1,0:T(8,128)(2,1)S(1)}, bf16[128,1024]{1,0:T(8,128)(2,1)S(1)}, u32[]{:S(2)}, u32[]{:S(2)}) collective-permute-start(bf16[128,1024]{1,0:T(8,128)(2,1)S(1)} %get-tuple-element.119.refs_8_), channel_id=1, source_target_pairs={{8,0},{16,8},{24,16},{28,24},{20,28},{12,20},{4,12},{0,4},{9,1},{1... | collective-permute-start | bytes 786440 | tf_op jit(solution)/shard_map/ppermute | solution.py:376
  95.0 10.0 %collective-permute-start.37 = (bf16[256,512]{1,0:T(8,128)(2,1)S(1)}, bf16[256,512]{1,0:T(8,128)(2,1)S(1)}, u32[]{:S(2)}, u32[]{:S(2)}) collective-permute-start(bf16[256,512]{1,0:T(8,128)(2,1)S(1)} %get-tuple-element.122.refs_8_), channel_id=1, source_target_pairs={{0,8},{8,16},{16,24},{24,28},{28,20},{20,12},{12,4},{4,0},{1,9},{9... | collective-permute-start | bytes 786440 | tf_op jit(solution)/shard_map/ppermute | solution.py:376
  96.4 9.5 %collective-permute-start.36 = (bf16[256,512]{1,0:T(8,128)(2,1)S(1)}, bf16[256,512]{1,0:T(8,128)(2,1)S(1)}, u32[]{:S(2)}, u32[]{:S(2)}) collective-permute-start(bf16[256,512]{1,0:T(8,128)(2,1)S(1)} %get-tuple-element.123.refs_9_), channel_id=1, source_target_pairs={{8,0},{16,8},{24,16},{28,24},{20,28},{12,20},{4,12},{0,4},{9,1},{1... | collective-permute-start | bytes 786440 | tf_op jit(solution)/shard_map/ppermute | solution.py:376
  (10 other events, 61.7 us)

commit v8 on v5

--- a/solution.py
+++ b/solution.py
@@ -196,18 +196,18 @@
 def ring_chunk(step, count):
     index = lax.axis_index("dp")
     half = lax.div(index, 2)
-    place = jnp.where(lax.rem(index, 2) == 0, half, count - 1 - half)
+    place = jnp.where(lax.rem(index, 2) == 0, count - 1 - half, half)
     chunks = []
     for move in (count - step, step):
         position = lax.rem(place + move, count)
-        mirror = 2 * (count - 1 - position) + 1
-        chunks.append(jnp.where(position < count // 2, 2 * position, mirror))
+        mirror = 2 * (count - 1 - position)
+        chunks.append(jnp.where(position < count // 2, 2 * position + 1, mirror))
     return chunks
 
 
 def ring_pairs(count):
     half = count // 2
-    ring = [2 * p if p < half else 2 * (count - 1 - p) + 1 for p in range(count)]
+    ring = [2 * p + 1 if p < half else 2 * (count - 1 - p) for p in range(count)]
     return [(ring[p], ring[(p + 1) % count]) for p in range(count)]
 
 

time: 111 us -> 111 us (level)
  no operation moved by 1% of the time
where the time goes in v8:
time: 111 us
  starting transfers between devices  38.8 us (35%)
  waiting for transfers between devices  36.4 us (33%)
  Pallas kernels  31.6 us (28%)
  local copies, waits for them, and re-layouts  2.35 us (2%)
    ppermute x14, starting transfers between devices, send(): lax.ppermute(pair[0], 'dp', forward)  22 us
    ppermute x14, waiting for transfers between devices, send(): lax.ppermute(pair[1], 'dp', backward)  17.4 us
    pallas_call x10, Pallas kernels, call(): pl.pallas_call(body, in_specs=[WHOLE] * len(inputs) + [LATER] * len(after...  14.9 us
    ppermute x14, waiting for transfers between devices, send(): lax.ppermute(pair[0], 'dp', forward)  13.2 us
    pallas_call x17, Pallas kernels, ring_step(): pl.pallas_call(functools.partial(step_kernel, [len(group) for group in ri...  9.32 us
    ppermute x14, starting transfers between devices, send(): lax.ppermute(pair[1], 'dp', backward)  7.06 us
    ppermute x5, starting transfers between devices, exchange(): return {k: lax.ppermute(outs[k], 'expert', sources[k]) for k in reach}  4.82 us
    pallas_call x4, Pallas kernels, last_call(): pl.pallas_call(functools.partial(last_kernel, way, count), in_specs=[WHOL...  3.44 us
  transfers between devices with their start and end apart: 38, of which 28 were waited for; matrix products, arithmetic and copies ran while one was open for 1% of the time, Pallas kernels for 27%

profile of v8, /device:TPU:0, one launch (start us, length us, event | category | flops | bytes accessed | tf_op | source)
XLA Modules:
  0.0 110.9 jit_solution(16797111341322940424)
XLA Ops:
  0.6 3.0 %collective-permute-start.3 = (bf16[256,1024]{1,0:T(8,128)(2,1)}, bf16[256,1024]{1,0:T(8,128)(2,1)S(1)}, u32[]{:S(2)}, u32[]{:S(2)}) collective-permute-start(bf16[256,1024]{1,0:T(8,128)(2,1)} %refs_3_.1), channel_id=1, source_target_pairs={{0,2},{1,3},{2,0},{3,1},{4,6},{5,7},{6,4},{7,5},{8,10},{9,11},{10,... | collective-permute-start | bytes 1572872 | tf_op jit(solution)/shard_map/ppermute | solution.py:298
  3.6 1.9 %pack.1 = (s32[1,256]{1,0:T(1,128)S(1)}, bf16[128,1024]{1,0:T(8,128)(2,1)S(1)}, bf16[128,1024]{1,0:T(8,128)(2,1)S(1)}, bf16[128,1024]{1,0:T(8,128)(2,1)S(1)}, bf...) custom-call(s32[256]{0:T(256)} %refs_0_.1, bf16[256]{0:T(256)(128)(2,1)} %refs_1_.5, ...), custom_call_target="tpu_custom_call" | custom-call | tf_op jit(solution)/shard_map/pack/pallas_call | solution.py:302
  6.1 2.0 %collective-permute-start.5 = (bf16[128,1024]{1,0:T(8,128)(2,1)S(1)}, bf16[128,1024]{1,0:T(8,128)(2,1)S(1)}, u32[]{:S(2)}, u32[]{:S(2)}) collective-permute-start(bf16[128,1024]{1,0:T(8,128)(2,1)S(1)} %get-tuple-element.80), channel_id=1, source_target_pairs={{0,2},{1,3},{2,0},{3,1},{4,6},{5,7},{6,4},{7,5},{8,10},{9,11},{10,... | collective-permute-start | bytes 786440 | tf_op jit(solution)/shard_map/ppermute | solution.py:293
  8.1 2.2 %copy-done = bf16[1,1024,2048]{2,1,0:T(8,128)(2,1)S(1)} copy-done((bf16[1,1024,2048]{2,1,0:T(8,128)(2,1)S(1)}, bf16[1,1024,2048]{2,1,0:T(8,128)(2,1)}, u32[]{:S(2)}) %copy-start) | copy-done | bytes 4194328
  10.3 2.0 %hidden.3 = (bf16[1024,256]{1,0:T(8,128)(2,1)S(1)}, bf16[256,2048]{1,0:T(8,128)(2,1)S(1)}, bf16[2048,256]{1,0:T(8,128)(2,1)S(1)}, bf16[256,2048]{1,0:T(8,128)(2,1)S(1)}) custom-call(bf16[128,1024]{1,0:T(8,128)(2,1)S(1)} %get-tuple-element.70.refs_0_, bf16[128,1024]{1,0:T(8,128)(2,1)S(1)} %collective-permute-done.1.refs_1_, bf16[1,1024,2048]{2,1,0:T(8,128)(2,1)S(1)} %copy-done), custom_call_target="tpu_custom_call" | custom-call | tf_op jit(solution)/shard_map/hidden/pallas_call | solution.py:100
  14.0 2.7 %collective-permute-done.2.id_ref = s32[1,256]{1,0:T(1,128)S(1)} collective-permute-done((s32[1,256]{1,0:T(1,128)}, s32[1,256]{1,0:T(1,128)S(1)}, u32[]{:S(2)}, u32[]{:S(2)}) %collective-permute-start.2) | collective-permute-done | bytes 1056 | tf_op jit(solution)/shard_map/ppermute | solution.py:299
  17.2 2.2 %collective-permute-start.6 = (bf16[128,1024]{1,0:T(8,128)(2,1)S(1)}, bf16[128,1024]{1,0:T(8,128)(2,1)S(1)}, u32[]{:S(2)}, u32[]{:S(2)}) collective-permute-start(bf16[128,1024]{1,0:T(8,128)(2,1)S(1)} %get-tuple-element.86), channel_id=1, source_target_pairs={{0,3},{1,2},{2,1},{3,0},{4,7},{5,6},{6,5},{7,4},{8,11},{9,10},{10,... | collective-permute-start | bytes 786440 | tf_op jit(solution)/shard_map/ppermute | solution.py:293
  20.4 1.7 %collective-permute-done.5.refs_0_.refs_4_.refs_5_ = bf16[128,1024]{1,0:T(8,128)(2,1)S(1)} collective-permute-done((bf16[128,1024]{1,0:T(8,128)(2,1)S(1)}, bf16[128,1024]{1,0:T(8,128)(2,1)S(1)}, u32[]{:S(2)}, u32[]{:S(2)}) %collective-permute-start.5) | collective-permute-done | bytes 262176 | tf_op jit(solution)/shard_map/ppermute | solution.py:293
  22.1 1.6 %pre_grad.4 = (bf16[128,2048]{1,0:T(8,128)(2,1)S(1)}, f32[128,128]{1,0:T(8,128)S(1)}) custom-call(bf16[128,1024]{1,0:T(8,128)(2,1)S(1)} %collective-permute-done.5.refs_0_.refs_4_.refs_5_, bf16[1,2048,1024]{2,1,0:T(8,128)(2,1)S(1)} %copy-done.2, bf16[128,2048]{1,0:T(8,128)(2,1)S(1)} %get-tuple-element.81.refs_2_.refs_4_, ...), custom_call_target="tpu_custom_call" | custom-call | tf_op jit(solution)/shard_map/pre_grad/pallas_call | solution.py:100
  26.6 1.8 %collective-permute-start.9 = (bf16[256,512]{1,0:T(8,128)(2,1)S(1)}, bf16[256,512]{1,0:T(8,128)(2,1)S(1)}, u32[]{:S(2)}, u32[]{:S(2)}) collective-permute-start(bf16[256,512]{1,0:T(8,128)(2,1)S(1)} %get-tuple-element.94.refs_4_), channel_id=1, source_target_pairs={{4,12},{12,20},{20,28},{28,24},{24,16},{16,8},{8,0},{0,4},{5,13},{... | collective-permute-start | bytes 786440 | tf_op jit(solution)/shard_map/ppermute | solution.py:370
  28.7 1.6 %pre_grad.5 = (bf16[128,2048]{1,0:T(8,128)(2,1)S(1)}, f32[128,128]{1,0:T(8,128)S(1)}) custom-call(bf16[128,1024]{1,0:T(8,128)(2,1)S(1)} %collective-permute-done.6.refs_1_.refs_0_.refs_6_, bf16[1,2048,1024]{2,1,0:T(8,128)(2,1)S(1)} %copy-done.2, bf16[128,2048]{1,0:T(8,128)(2,1)S(1)} %get-tuple-element.87.refs_5_.refs_2_, ...), custom_call_target="tpu_custom_call" | custom-call | tf_op jit(solution)/shard_map/pre_grad/pallas_call | solution.py:100
  30.9 1.8 %collective-permute-start.7 = (bf16[128,1024]{1,0:T(8,128)(2,1)S(1)}, bf16[128,1024]{1,0:T(8,128)(2,1)S(1)}, u32[]{:S(2)}, u32[]{:S(2)}) collective-permute-start(bf16[128,1024]{1,0:T(8,128)(2,1)S(1)} %get-tuple-element.98.refs_9_), channel_id=1, source_target_pairs={{4,12},{12,20},{20,28},{28,24},{24,16},{16,8},{8,0},{0,4},{5,13},{... | collective-permute-start | bytes 786440 | tf_op jit(solution)/shard_map/ppermute | solution.py:370
  32.9 2.9 %collective-permute-done.9.refs_7_ = bf16[256,512]{1,0:T(8,128)(2,1)S(1)} collective-permute-done((bf16[256,512]{1,0:T(8,128)(2,1)S(1)}, bf16[256,512]{1,0:T(8,128)(2,1)S(1)}, u32[]{:S(2)}, u32[]{:S(2)}) %collective-permute-start.9) | collective-permute-done | bytes 262176 | tf_op jit(solution)/shard_map/ppermute | solution.py:370
  35.8 1.7 %collective-permute-done.10.refs_8_ = bf16[256,512]{1,0:T(8,128)(2,1)S(1)} collective-permute-done((bf16[256,512]{1,0:T(8,128)(2,1)S(1)}, bf16[256,512]{1,0:T(8,128)(2,1)S(1)}, u32[]{:S(2)}, u32[]{:S(2)}) %collective-permute-start.10) | collective-permute-done | bytes 262176 | tf_op jit(solution)/shard_map/ppermute | solution.py:370
  38.1 1.6 %collective-permute-start.13 = (bf16[256,512]{1,0:T(8,128)(2,1)S(1)}, bf16[256,512]{1,0:T(8,128)(2,1)S(1)}, u32[]{:S(2)}, u32[]{:S(2)}) collective-permute-start(bf16[256,512]{1,0:T(8,128)(2,1)S(1)} %get-tuple-element.100.refs_8_), channel_id=1, source_target_pairs={{4,12},{12,20},{20,28},{28,24},{24,16},{16,8},{8,0},{0,4},{5,13},{... | collective-permute-start | bytes 786440 | tf_op jit(solution)/shard_map/ppermute | solution.py:370
  41.4 1.7 %collective-permute-done.8.refs_7_ = bf16[128,1024]{1,0:T(8,128)(2,1)S(1)} collective-permute-done((bf16[128,1024]{1,0:T(8,128)(2,1)S(1)}, bf16[128,1024]{1,0:T(8,128)(2,1)S(1)}, u32[]{:S(2)}, u32[]{:S(2)}) %collective-permute-start.8) | collective-permute-done | bytes 262176 | tf_op jit(solution)/shard_map/ppermute | solution.py:370
  43.7 1.6 %collective-permute-start.11 = (bf16[128,1024]{1,0:T(8,128)(2,1)S(1)}, bf16[128,1024]{1,0:T(8,128)(2,1)S(1)}, u32[]{:S(2)}, u32[]{:S(2)}) collective-permute-start(bf16[128,1024]{1,0:T(8,128)(2,1)S(1)} %get-tuple-element.102.refs_0_), channel_id=1, source_target_pairs={{4,12},{12,20},{20,28},{28,24},{24,16},{16,8},{8,0},{0,4},{5,13},{... | collective-permute-start | bytes 786440 | tf_op jit(solution)/shard_map/ppermute | solution.py:370
  47.3 1.6 %collective-permute-start.19 = (bf16[128,1152]{1,0:T(8,128)(2,1)S(1)}, bf16[128,1152]{1,0:T(8,128)(2,1)S(1)}, u32[]{:S(2)}, u32[]{:S(2)}) collective-permute-start(bf16[128,1152]{1,0:T(8,128)(2,1)S(1)} %feat_grad.4.refs_9_), channel_id=1, source_target_pairs={{0,2},{1,3},{2,0},{3,1},{4,6},{5,7},{6,4},{7,5},{8,10},{9,11},{10,... | collective-permute-start | bytes 884744 | tf_op jit(solution)/shard_map/ppermute | solution.py:412
  49.5 1.6 %collective-permute-start.17 = (bf16[256,512]{1,0:T(8,128)(2,1)S(1)}, bf16[256,512]{1,0:T(8,128)(2,1)S(1)}, u32[]{:S(2)}, u32[]{:S(2)}) collective-permute-start(bf16[256,512]{1,0:T(8,128)(2,1)S(1)} %get-tuple-element.104.refs_8_), channel_id=1, source_target_pairs={{4,12},{12,20},{20,28},{28,24},{24,16},{16,8},{8,0},{0,4},{5,13},{... | collective-permute-start | bytes 786440 | tf_op jit(solution)/shard_map/ppermute | solution.py:370
  53.0 1.6 %collective-permute-done.12.refs_7_ = bf16[128,1024]{1,0:T(8,128)(2,1)S(1)} collective-permute-done((bf16[128,1024]{1,0:T(8,128)(2,1)S(1)}, bf16[128,1024]{1,0:T(8,128)(2,1)S(1)}, u32[]{:S(2)}, u32[]{:S(2)}) %collective-permute-start.12) | collective-permute-done | bytes 262176 | tf_op jit(solution)/shard_map/ppermute | solution.py:370
  55.1 1.6 %collective-permute-start.15 = (bf16[128,1024]{1,0:T(8,128)(2,1)S(1)}, bf16[128,1024]{1,0:T(8,128)(2,1)S(1)}, u32[]{:S(2)}, u32[]{:S(2)}) collective-permute-start(bf16[128,1024]{1,0:T(8,128)(2,1)S(1)} %get-tuple-element.106.refs_0_), channel_id=1, source_target_pairs={{4,12},{12,20},{20,28},{28,24},{24,16},{16,8},{8,0},{0,4},{5,13},{... | collective-permute-start | bytes 786440 | tf_op jit(solution)/shard_map/ppermute | solution.py:370
  58.8 1.6 %collective-permute-done.18.refs_8_ = bf16[256,512]{1,0:T(8,128)(2,1)S(1)} collective-permute-done((bf16[256,512]{1,0:T(8,128)(2,1)S(1)}, bf16[256,512]{1,0:T(8,128)(2,1)S(1)}, u32[]{:S(2)}, u32[]{:S(2)}) %collective-permute-start.18) | collective-permute-done | bytes 262176 | tf_op jit(solution)/shard_map/ppermute | solution.py:370
  61.0 1.6 %collective-permute-start.22 = (bf16[256,512]{1,0:T(8,128)(2,1)S(1)}, bf16[256,512]{1,0:T(8,128)(2,1)S(1)}, u32[]{:S(2)}, u32[]{:S(2)}) collective-permute-start(bf16[256,512]{1,0:T(8,128)(2,1)S(1)} %get-tuple-element.108.refs_8_), channel_id=1, source_target_pairs={{4,12},{12,20},{20,28},{28,24},{24,16},{16,8},{8,0},{0,4},{5,13},{... | collective-permute-start | bytes 786440 | tf_op jit(solution)/shard_map/ppermute | solution.py:370
  65.6 1.6 %collective-permute-start.20 = (bf16[128,1024]{1,0:T(8,128)(2,1)S(1)}, bf16[128,1024]{1,0:T(8,128)(2,1)S(1)}, u32[]{:S(2)}, u32[]{:S(2)}) collective-permute-start(bf16[128,1024]{1,0:T(8,128)(2,1)S(1)} %get-tuple-element.110.refs_0_), channel_id=1, source_target_pairs={{4,12},{12,20},{20,28},{28,24},{24,16},{16,8},{8,0},{0,4},{5,13},{... | collective-permute-start | bytes 786440 | tf_op jit(solution)/shard_map/ppermute | solution.py:370
  70.2 1.6 %collective-permute-done.23.refs_8_ = bf16[256,512]{1,0:T(8,128)(2,1)S(1)} collective-permute-done((bf16[256,512]{1,0:T(8,128)(2,1)S(1)}, bf16[256,512]{1,0:T(8,128)(2,1)S(1)}, u32[]{:S(2)}, u32[]{:S(2)}) %collective-permute-start.23) | collective-permute-done | bytes 262176 | tf_op jit(solution)/shard_map/ppermute | solution.py:370
  72.4 1.5 %collective-permute-start.28 = (bf16[256,512]{1,0:T(8,128)(2,1)S(1)}, bf16[256,512]{1,0:T(8,128)(2,1)S(1)}, u32[]{:S(2)}, u32[]{:S(2)}) collective-permute-start(bf16[256,512]{1,0:T(8,128)(2,1)S(1)} %get-tuple-element.112.refs_8_), channel_id=1, source_target_pairs={{4,12},{12,20},{20,28},{28,24},{24,16},{16,8},{8,0},{0,4},{5,13},{... | collective-permute-start | bytes 786440 | tf_op jit(solution)/shard_map/ppermute | solution.py:370
  75.8 1.6 %collective-permute-done.21.refs_7_ = bf16[128,1024]{1,0:T(8,128)(2,1)S(1)} collective-permute-done((bf16[128,1024]{1,0:T(8,128)(2,1)S(1)}, bf16[128,1024]{1,0:T(8,128)(2,1)S(1)}, u32[]{:S(2)}, u32[]{:S(2)}) %collective-permute-start.21) | collective-permute-done | bytes 262176 | tf_op jit(solution)/shard_map/ppermute | solution.py:370
  78.0 1.5 %collective-permute-start.26 = (bf16[128,1024]{1,0:T(8,128)(2,1)S(1)}, bf16[128,1024]{1,0:T(8,128)(2,1)S(1)}, u32[]{:S(2)}, u32[]{:S(2)}) collective-permute-start(bf16[128,1024]{1,0:T(8,128)(2,1)S(1)} %get-tuple-element.114.refs_0_), channel_id=1, source_target_pairs={{4,12},{12,20},{20,28},{28,24},{24,16},{16,8},{8,0},{0,4},{5,13},{... | collective-permute-start | bytes 786440 | tf_op jit(solution)/shard_map/ppermute | solution.py:370
  80.1 1.5 %feat_grad.7.refs_9_.refs_0_ = bf16[128,1152]{1,0:T(8,128)(2,1)S(1)} custom-call(bf16[256,2048]{1,0:T(8,128)(2,1)S(1)} %get-tuple-element.74.refs_3_.pre_ref, bf16[1,1024,2048]{2,1,0:T(8,128)(2,1)S(1)} %copy-done.1, f32[256,128]{1,0:T(8,128)S(1)} %get-tuple-element.75._.sum_ref, bf16[128,1024]{1,0:T(8,128)(2,1)S(1)} %get-tuple-element.114.refs_0_, ...), custom_call_target="tpu_custom_call" | custom-call | tf_op jit(solution)/shard_map/feat_grad/pallas_call | solution.py:100
  97.1 1.6 %collective-permute-done.30.refs_6_ = bf16[128,1024]{1,0:T(8,128)(2,1)S(1)} collective-permute-done((bf16[128,1024]{1,0:T(8,128)(2,1)S(1)}, bf16[128,1024]{1,0:T(8,128)(2,1)S(1)}, u32[]{:S(2)}, u32[]{:S(2)}) %collective-permute-start.30) | collective-permute-done | bytes 262176 | tf_op jit(solution)/shard_map/ppermute | solution.py:370
  102.7 1.6 %unpack.1 = (bf16[256,1024]{1,0:T(8,128)(2,1)}, f32[256,128]{1,0:T(8,128)S(1)}) custom-call(s32[1,256]{1,0:T(1,128)S(1)} %get-tuple-element.67.slot_ref, bf16[128,1152]{1,0:T(8,128)(2,1)S(1)} %feat_grad.7.refs_9_.refs_0_, bf16[128,1152]{1,0:T(8,128)(2,1)S(1)} %collective-permute-done.25.refs_2_.refs_1_, ...), custom_call_target="tpu_custom_call" | custom-call | tf_op jit(solution)/shard_map/unpack/pallas_call | solution.py:440
  106.7 1.8 %collective-permute-done.35.arrived_ref = bf16[128,1024]{1,0:T(8,128)(2,1)S(1)} collective-permute-done((bf16[128,1024]{1,0:T(8,128)(2,1)S(1)}, bf16[128,1024]{1,0:T(8,128)(2,1)S(1)}, u32[]{:S(2)}, u32[]{:S(2)}) %collective-permute-start.35) | collective-permute-done | bytes 262176 | tf_op jit(solution)/shard_map/ppermute | solution.py:370
  (88 shorter events, 51.9 us)
Async XLA Ops:
  0.6 16.0 %collective-permute-start.3 = (bf16[256,1024]{1,0:T(8,128)(2,1)}, bf16[256,1024]{1,0:T(8,128)(2,1)S(1)}, u32[]{:S(2)}, u32[]{:S(2)}) collective-permute-start(bf16[256,1024]{1,0:T(8,128)(2,1)} %refs_3_.1), channel_id=1, source_target_pairs={{0,2},{1,3},{2,0},{3,1},{4,6},{5,7},{6,4},{7,5},{8,10},{9,11},{10,... | collective-permute-start | bytes 1572872 | tf_op jit(solution)/shard_map/ppermute | solution.py:298
  6.1 10.6 %collective-permute-start.2 = (s32[1,256]{1,0:T(1,128)}, s32[1,256]{1,0:T(1,128)S(1)}, u32[]{:S(2)}, u32[]{:S(2)}) collective-permute-start(s32[1,256]{1,0:T(1,128)} %bitcast.1), channel_id=1, source_target_pairs={{0,2},{1,3},{2,0},{3,1},{4,6},{5,7},{6,4},{7,5},{8,10},{9,11},{10,... | collective-permute-start | bytes 3080 | tf_op jit(solution)/shard_map/ppermute | solution.py:299
  6.1 16.0 %collective-permute-start.5 = (bf16[128,1024]{1,0:T(8,128)(2,1)S(1)}, bf16[128,1024]{1,0:T(8,128)(2,1)S(1)}, u32[]{:S(2)}, u32[]{:S(2)}) collective-permute-start(bf16[128,1024]{1,0:T(8,128)(2,1)S(1)} %get-tuple-element.80), channel_id=1, source_target_pairs={{0,2},{1,3},{2,0},{3,1},{4,6},{5,7},{6,4},{7,5},{8,10},{9,11},{10,... | collective-permute-start | bytes 786440 | tf_op jit(solution)/shard_map/ppermute | solution.py:293
  17.2 9.1 %collective-permute-start.6 = (bf16[128,1024]{1,0:T(8,128)(2,1)S(1)}, bf16[128,1024]{1,0:T(8,128)(2,1)S(1)}, u32[]{:S(2)}, u32[]{:S(2)}) collective-permute-start(bf16[128,1024]{1,0:T(8,128)(2,1)S(1)} %get-tuple-element.86), channel_id=1, source_target_pairs={{0,3},{1,2},{2,1},{3,0},{4,7},{5,6},{6,5},{7,4},{8,11},{9,10},{10,... | collective-permute-start | bytes 786440 | tf_op jit(solution)/shard_map/ppermute | solution.py:293
  26.6 9.2 %collective-permute-start.9 = (bf16[256,512]{1,0:T(8,128)(2,1)S(1)}, bf16[256,512]{1,0:T(8,128)(2,1)S(1)}, u32[]{:S(2)}, u32[]{:S(2)}) collective-permute-start(bf16[256,512]{1,0:T(8,128)(2,1)S(1)} %get-tuple-element.94.refs_4_), channel_id=1, source_target_pairs={{4,12},{12,20},{20,28},{28,24},{24,16},{16,8},{8,0},{0,4},{5,13},{... | collective-permute-start | bytes 786440 | tf_op jit(solution)/shard_map/ppermute | solution.py:370
  28.4 9.1 %collective-permute-start.10 = (bf16[256,512]{1,0:T(8,128)(2,1)S(1)}, bf16[256,512]{1,0:T(8,128)(2,1)S(1)}, u32[]{:S(2)}, u32[]{:S(2)}) collective-permute-start(bf16[256,512]{1,0:T(8,128)(2,1)S(1)} %get-tuple-element.95.refs_5_), channel_id=1, source_target_pairs={{12,4},{20,12},{28,20},{24,28},{16,24},{8,16},{0,8},{4,0},{13,5},{... | collective-permute-start | bytes 786440 | tf_op jit(solution)/shard_map/ppermute | solution.py:370
  30.9 10.5 %collective-permute-start.7 = (bf16[128,1024]{1,0:T(8,128)(2,1)S(1)}, bf16[128,1024]{1,0:T(8,128)(2,1)S(1)}, u32[]{:S(2)}, u32[]{:S(2)}) collective-permute-start(bf16[128,1024]{1,0:T(8,128)(2,1)S(1)} %get-tuple-element.98.refs_9_), channel_id=1, source_target_pairs={{4,12},{12,20},{20,28},{28,24},{24,16},{16,8},{8,0},{0,4},{5,13},{... | collective-permute-start | bytes 786440 | tf_op jit(solution)/shard_map/ppermute | solution.py:370
  32.7 10.5 %collective-permute-start.8 = (bf16[128,1024]{1,0:T(8,128)(2,1)S(1)}, bf16[128,1024]{1,0:T(8,128)(2,1)S(1)}, u32[]{:S(2)}, u32[]{:S(2)}) collective-permute-start(bf16[128,1024]{1,0:T(8,128)(2,1)S(1)} %get-tuple-element.99.refs_10_), channel_id=1, source_target_pairs={{12,4},{20,12},{28,20},{24,28},{16,24},{8,16},{0,8},{4,0},{13,5},{... | collective-permute-start | bytes 786440 | tf_op jit(solution)/shard_map/ppermute | solution.py:370
  38.1 10.8 %collective-permute-start.13 = (bf16[256,512]{1,0:T(8,128)(2,1)S(1)}, bf16[256,512]{1,0:T(8,128)(2,1)S(1)}, u32[]{:S(2)}, u32[]{:S(2)}) collective-permute-start(bf16[256,512]{1,0:T(8,128)(2,1)S(1)} %get-tuple-element.100.refs_8_), channel_id=1, source_target_pairs={{4,12},{12,20},{20,28},{28,24},{24,16},{16,8},{8,0},{0,4},{5,13},{... | collective-permute-start | bytes 786440 | tf_op jit(solution)/shard_map/ppermute | solution.py:370
  39.7 9.2 %collective-permute-start.14 = (bf16[256,512]{1,0:T(8,128)(2,1)S(1)}, bf16[256,512]{1,0:T(8,128)(2,1)S(1)}, u32[]{:S(2)}, u32[]{:S(2)}) collective-permute-start(bf16[256,512]{1,0:T(8,128)(2,1)S(1)} %get-tuple-element.101.refs_9_), channel_id=1, source_target_pairs={{12,4},{20,12},{28,20},{24,28},{16,24},{8,16},{0,8},{4,0},{13,5},{... | collective-permute-start | bytes 786440 | tf_op jit(solution)/shard_map/ppermute | solution.py:370
  43.7 9.3 %collective-permute-start.11 = (bf16[128,1024]{1,0:T(8,128)(2,1)S(1)}, bf16[128,1024]{1,0:T(8,128)(2,1)S(1)}, u32[]{:S(2)}, u32[]{:S(2)}) collective-permute-start(bf16[128,1024]{1,0:T(8,128)(2,1)S(1)} %get-tuple-element.102.refs_0_), channel_id=1, source_target_pairs={{4,12},{12,20},{20,28},{28,24},{24,16},{16,8},{8,0},{0,4},{5,13},{... | collective-permute-start | bytes 786440 | tf_op jit(solution)/shard_map/ppermute | solution.py:370
  45.3 9.2 %collective-permute-start.12 = (bf16[128,1024]{1,0:T(8,128)(2,1)S(1)}, bf16[128,1024]{1,0:T(8,128)(2,1)S(1)}, u32[]{:S(2)}, u32[]{:S(2)}) collective-permute-start(bf16[128,1024]{1,0:T(8,128)(2,1)S(1)} %get-tuple-element.103.refs_1_), channel_id=1, source_target_pairs={{12,4},{20,12},{28,20},{24,28},{16,24},{8,16},{0,8},{4,0},{13,5},{... | collective-permute-start | bytes 786440 | tf_op jit(solution)/shard_map/ppermute | solution.py:370
  47.3 9.9 %collective-permute-start.19 = (bf16[128,1152]{1,0:T(8,128)(2,1)S(1)}, bf16[128,1152]{1,0:T(8,128)(2,1)S(1)}, u32[]{:S(2)}, u32[]{:S(2)}) collective-permute-start(bf16[128,1152]{1,0:T(8,128)(2,1)S(1)} %feat_grad.4.refs_9_), channel_id=1, source_target_pairs={{0,2},{1,3},{2,0},{3,1},{4,6},{5,7},{6,4},{7,5},{8,10},{9,11},{10,... | collective-permute-start | bytes 884744 | tf_op jit(solution)/shard_map/ppermute | solution.py:412
  49.5 9.3 %collective-permute-start.17 = (bf16[256,512]{1,0:T(8,128)(2,1)S(1)}, bf16[256,512]{1,0:T(8,128)(2,1)S(1)}, u32[]{:S(2)}, u32[]{:S(2)}) collective-permute-start(bf16[256,512]{1,0:T(8,128)(2,1)S(1)} %get-tuple-element.104.refs_8_), channel_id=1, source_target_pairs={{4,12},{12,20},{20,28},{28,24},{24,16},{16,8},{8,0},{0,4},{5,13},{... | collective-permute-start | bytes 786440 | tf_op jit(solution)/shard_map/ppermute | solution.py:370
  51.1 9.2 %collective-permute-start.18 = (bf16[256,512]{1,0:T(8,128)(2,1)S(1)}, bf16[256,512]{1,0:T(8,128)(2,1)S(1)}, u32[]{:S(2)}, u32[]{:S(2)}) collective-permute-start(bf16[256,512]{1,0:T(8,128)(2,1)S(1)} %get-tuple-element.105.refs_9_), channel_id=1, source_target_pairs={{12,4},{20,12},{28,20},{24,28},{16,24},{8,16},{0,8},{4,0},{13,5},{... | collective-permute-start | bytes 786440 | tf_op jit(solution)/shard_map/ppermute | solution.py:370
  55.1 8.4 %collective-permute-start.15 = (bf16[128,1024]{1,0:T(8,128)(2,1)S(1)}, bf16[128,1024]{1,0:T(8,128)(2,1)S(1)}, u32[]{:S(2)}, u32[]{:S(2)}) collective-permute-start(bf16[128,1024]{1,0:T(8,128)(2,1)S(1)} %get-tuple-element.106.refs_0_), channel_id=1, source_target_pairs={{4,12},{12,20},{20,28},{28,24},{24,16},{16,8},{8,0},{0,4},{5,13},{... | collective-permute-start | bytes 786440 | tf_op jit(solution)/shard_map/ppermute | solution.py:370
  58.7 9.3 %collective-permute-start.24 = (bf16[128,1152]{1,0:T(8,128)(2,1)S(1)}, bf16[128,1152]{1,0:T(8,128)(2,1)S(1)}, u32[]{:S(2)}, u32[]{:S(2)}) collective-permute-start(bf16[128,1152]{1,0:T(8,128)(2,1)S(1)} %feat_grad.5.refs_9_), channel_id=1, source_target_pairs={{0,3},{1,2},{2,1},{3,0},{4,7},{5,6},{6,5},{7,4},{8,11},{9,10},{10,... | collective-permute-start | bytes 884744 | tf_op jit(solution)/shard_map/ppermute | solution.py:412
  61.0 9.2 %collective-permute-start.22 = (bf16[256,512]{1,0:T(8,128)(2,1)S(1)}, bf16[256,512]{1,0:T(8,128)(2,1)S(1)}, u32[]{:S(2)}, u32[]{:S(2)}) collective-permute-start(bf16[256,512]{1,0:T(8,128)(2,1)S(1)} %get-tuple-element.108.refs_8_), channel_id=1, source_target_pairs={{4,12},{12,20},{20,28},{28,24},{24,16},{16,8},{8,0},{0,4},{5,13},{... | collective-permute-start | bytes 786440 | tf_op jit(solution)/shard_map/ppermute | solution.py:370
  62.6 9.2 %collective-permute-start.23 = (bf16[256,512]{1,0:T(8,128)(2,1)S(1)}, bf16[256,512]{1,0:T(8,128)(2,1)S(1)}, u32[]{:S(2)}, u32[]{:S(2)}) collective-permute-start(bf16[256,512]{1,0:T(8,128)(2,1)S(1)} %get-tuple-element.109.refs_9_), channel_id=1, source_target_pairs={{12,4},{20,12},{28,20},{24,28},{16,24},{8,16},{0,8},{4,0},{13,5},{... | collective-permute-start | bytes 786440 | tf_op jit(solution)/shard_map/ppermute | solution.py:370
  65.6 10.2 %collective-permute-start.20 = (bf16[128,1024]{1,0:T(8,128)(2,1)S(1)}, bf16[128,1024]{1,0:T(8,128)(2,1)S(1)}, u32[]{:S(2)}, u32[]{:S(2)}) collective-permute-start(bf16[128,1024]{1,0:T(8,128)(2,1)S(1)} %get-tuple-element.110.refs_0_), channel_id=1, source_target_pairs={{4,12},{12,20},{20,28},{28,24},{24,16},{16,8},{8,0},{0,4},{5,13},{... | collective-permute-start | bytes 786440 | tf_op jit(solution)/shard_map/ppermute | solution.py:370
  67.2 10.2 %collective-permute-start.21 = (bf16[128,1024]{1,0:T(8,128)(2,1)S(1)}, bf16[128,1024]{1,0:T(8,128)(2,1)S(1)}, u32[]{:S(2)}, u32[]{:S(2)}) collective-permute-start(bf16[128,1024]{1,0:T(8,128)(2,1)S(1)} %get-tuple-element.111.refs_1_), channel_id=1, source_target_pairs={{12,4},{20,12},{28,20},{24,28},{16,24},{8,16},{0,8},{4,0},{13,5},{... | collective-permute-start | bytes 786440 | tf_op jit(solution)/shard_map/ppermute | solution.py:370
  69.6 10.5 %collective-permute-start.25 = (bf16[128,1152]{1,0:T(8,128)(2,1)S(1)}, bf16[128,1152]{1,0:T(8,128)(2,1)S(1)}, u32[]{:S(2)}, u32[]{:S(2)}) collective-permute-start(bf16[128,1152]{1,0:T(8,128)(2,1)S(1)} %feat_grad.6.refs_9_), channel_id=1, source_target_pairs={{0,1},{1,0},{2,3},{3,2},{4,5},{5,4},{6,7},{7,6},{8,9},{9,8},{10,11... | collective-permute-start | bytes 884744 | tf_op jit(solution)/shard_map/ppermute | solution.py:412
  72.4 9.3 %collective-permute-start.28 = (bf16[256,512]{1,0:T(8,128)(2,1)S(1)}, bf16[256,512]{1,0:T(8,128)(2,1)S(1)}, u32[]{:S(2)}, u32[]{:S(2)}) collective-permute-start(bf16[256,512]{1,0:T(8,128)(2,1)S(1)} %get-tuple-element.112.refs_8_), channel_id=1, source_target_pairs={{4,12},{12,20},{20,28},{28,24},{24,16},{16,8},{8,0},{0,4},{5,13},{... | collective-permute-start | bytes 786440 | tf_op jit(solution)/shard_map/ppermute | solution.py:370
  73.9 9.2 %collective-permute-start.29 = (bf16[256,512]{1,0:T(8,128)(2,1)S(1)}, bf16[256,512]{1,0:T(8,128)(2,1)S(1)}, u32[]{:S(2)}, u32[]{:S(2)}) collective-permute-start(bf16[256,512]{1,0:T(8,128)(2,1)S(1)} %get-tuple-element.113.refs_9_), channel_id=1, source_target_pairs={{12,4},{20,12},{28,20},{24,28},{16,24},{8,16},{0,8},{4,0},{13,5},{... | collective-permute-start | bytes 786440 | tf_op jit(solution)/shard_map/ppermute | solution.py:370
  78.0 9.3 %collective-permute-start.26 = (bf16[128,1024]{1,0:T(8,128)(2,1)S(1)}, bf16[128,1024]{1,0:T(8,128)(2,1)S(1)}, u32[]{:S(2)}, u32[]{:S(2)}) collective-permute-start(bf16[128,1024]{1,0:T(8,128)(2,1)S(1)} %get-tuple-element.114.refs_0_), channel_id=1, source_target_pairs={{4,12},{12,20},{20,28},{28,24},{24,16},{16,8},{8,0},{0,4},{5,13},{... | collective-permute-start | bytes 786440 | tf_op jit(solution)/shard_map/ppermute | solution.py:370
  79.5 9.2 %collective-permute-start.27 = (bf16[128,1024]{1,0:T(8,128)(2,1)S(1)}, bf16[128,1024]{1,0:T(8,128)(2,1)S(1)}, u32[]{:S(2)}, u32[]{:S(2)}) collective-permute-start(bf16[128,1024]{1,0:T(8,128)(2,1)S(1)} %get-tuple-element.115.refs_1_), channel_id=1, source_target_pairs={{12,4},{20,12},{28,20},{24,28},{16,24},{8,16},{0,8},{4,0},{13,5},{... | collective-permute-start | bytes 786440 | tf_op jit(solution)/shard_map/ppermute | solution.py:370
  83.7 9.3 %collective-permute-start.32 = (bf16[256,512]{1,0:T(8,128)(2,1)S(1)}, bf16[256,512]{1,0:T(8,128)(2,1)S(1)}, u32[]{:S(2)}, u32[]{:S(2)}) collective-permute-start(bf16[256,512]{1,0:T(8,128)(2,1)S(1)} %get-tuple-element.116.refs_8_), channel_id=1, source_target_pairs={{4,12},{12,20},{20,28},{28,24},{24,16},{16,8},{8,0},{0,4},{5,13},{... | collective-permute-start | bytes 786440 | tf_op jit(solution)/shard_map/ppermute | solution.py:370
  85.1 9.2 %collective-permute-start.33 = (bf16[256,512]{1,0:T(8,128)(2,1)S(1)}, bf16[256,512]{1,0:T(8,128)(2,1)S(1)}, u32[]{:S(2)}, u32[]{:S(2)}) collective-permute-start(bf16[256,512]{1,0:T(8,128)(2,1)S(1)} %get-tuple-element.117.refs_9_), channel_id=1, source_target_pairs={{12,4},{20,12},{28,20},{24,28},{16,24},{8,16},{0,8},{4,0},{13,5},{... | collective-permute-start | bytes 786440 | tf_op jit(solution)/shard_map/ppermute | solution.py:370
  89.4 9.3 %collective-permute-start.30 = (bf16[128,1024]{1,0:T(8,128)(2,1)S(1)}, bf16[128,1024]{1,0:T(8,128)(2,1)S(1)}, u32[]{:S(2)}, u32[]{:S(2)}) collective-permute-start(bf16[128,1024]{1,0:T(8,128)(2,1)S(1)} %get-tuple-element.118.refs_7_), channel_id=1, source_target_pairs={{4,12},{12,20},{20,28},{28,24},{24,16},{16,8},{8,0},{0,4},{5,13},{... | collective-permute-start | bytes 786440 | tf_op jit(solution)/shard_map/ppermute | solution.py:370
  90.8 9.2 %collective-permute-start.31 = (bf16[128,1024]{1,0:T(8,128)(2,1)S(1)}, bf16[128,1024]{1,0:T(8,128)(2,1)S(1)}, u32[]{:S(2)}, u32[]{:S(2)}) collective-permute-start(bf16[128,1024]{1,0:T(8,128)(2,1)S(1)} %get-tuple-element.119.refs_8_), channel_id=1, source_target_pairs={{12,4},{20,12},{28,20},{24,28},{16,24},{8,16},{0,8},{4,0},{13,5},{... | collective-permute-start | bytes 786440 | tf_op jit(solution)/shard_map/ppermute | solution.py:370
  95.0 10.0 %collective-permute-start.37 = (bf16[256,512]{1,0:T(8,128)(2,1)S(1)}, bf16[256,512]{1,0:T(8,128)(2,1)S(1)}, u32[]{:S(2)}, u32[]{:S(2)}) collective-permute-start(bf16[256,512]{1,0:T(8,128)(2,1)S(1)} %get-tuple-element.122.refs_8_), channel_id=1, source_target_pairs={{4,12},{12,20},{20,28},{28,24},{24,16},{16,8},{8,0},{0,4},{5,13},{... | collective-permute-start | bytes 786440 | tf_op jit(solution)/shard_map/ppermute | solution.py:370
  96.4 9.5 %collective-permute-start.36 = (bf16[256,512]{1,0:T(8,128)(2,1)S(1)}, bf16[256,512]{1,0:T(8,128)(2,1)S(1)}, u32[]{:S(2)}, u32[]{:S(2)}) collective-permute-start(bf16[256,512]{1,0:T(8,128)(2,1)S(1)} %get-tuple-element.123.refs_9_), channel_id=1, source_target_pairs={{12,4},{20,12},{28,20},{24,28},{16,24},{8,16},{0,8},{4,0},{13,5},{... | collective-permute-start | bytes 786440 | tf_op jit(solution)/shard_map/ppermute | solution.py:370
  (10 other events, 61.6 us)
